TPU v7x, 32 devices: a whole 2x2x4 slice. The times are simulated.
32 devices in a mesh: seq: 8 (over z, x), tp: 4 (over y, core).
Axes of the slice: x: 2, y: 2, z: 4, core: 2. Of those that a mesh axis runs over, the one named last changes fastest.
Arguments:
- tokens: bfloat16 [4, 1024, 768], P('tp', 'seq'), may hold values from -6 to 6
- norm_gain: float32 [768], replicated, may hold values from 0.5 to 1.5
- query_weight: bfloat16 [768, 768], replicated, may hold values from -0.21875 to 0.21875
- key_weight: bfloat16 [768, 768], replicated, may hold values from -0.21875 to 0.21875
- value_weight: bfloat16 [768, 768], replicated, may hold values from -0.21875 to 0.21875
- rate_weight: bfloat16 [768, 12], replicated, may hold values from -0.21875 to 0.21875
- rate_bias: float32 [12], P('tp'), may hold values from -2 to 1
- first_weight: float32 [12, 64, 256], P('tp'), may hold values from -0.75 to 0.75
- first_bias: float32 [12, 256], P('tp'), may hold values from -3 to 3
- second_weight: float32 [12, 256, 64], P('tp'), may hold values from -0.375 to 0.375
- second_bias: float32 [12, 64], P('tp'), may hold values from -3 to 3
- inner_gain: float32 [12, 64], P('tp'), may hold values from 0.25 to 1.75
- inner_bias: float32 [12, 64], P('tp'), may hold values from -3 to 3
- branch_gate: bfloat16 [768, 768], replicated, may hold values from -0.21875 to 0.21875
- output_weight: bfloat16 [768, 768], replicated, may hold values from -0.4375 to 0.4375
- post_gain: float32 [768], replicated, may hold values from 0.5 to 1.5
- post_bias: float32 [768], replicated, may hold values from -3 to 3
- feed_gain: float32 [768], replicated, may hold values from 0.5 to 1.5
- feed_gate: bfloat16 [768, 2048], P(None, 'tp'), may hold values from -0.21875 to 0.21875
- feed_linear: bfloat16 [768, 2048], P(None, 'tp'), may hold values from -0.21875 to 0.21875
- feed_down: bfloat16 [2048, 768], P('tp'), may hold values from -0.25 to 0.25
- cotangent: bfloat16 [4, 1024, 768], P('tp', 'seq'), may hold values from -6 to 6
Outputs:
- result: bfloat16 [4, 1024, 768], P('tp', 'seq')
- tokens_grad: float32 [4, 1024, 768], P('tp', 'seq')
- norm_gain_grad: float32 [768], replicated
- query_weight_grad: float32 [768, 768], replicated
- key_weight_grad: float32 [768, 768], replicated
- value_weight_grad: float32 [768, 768], replicated
- rate_weight_grad: float32 [768, 12], replicated
- rate_bias_grad: float32 [12], P('tp')
- first_weight_grad: float32 [12, 64, 256], P('tp')
- first_bias_grad: float32 [12, 256], P('tp')
- second_weight_grad: float32 [12, 256, 64], P('tp')
- second_bias_grad: float32 [12, 64], P('tp')
- inner_gain_grad: float32 [12, 64], P('tp')
- inner_bias_grad: float32 [12, 64], P('tp')
- branch_gate_grad: float32 [768, 768], replicated
- output_weight_grad: float32 [768, 768], replicated
- post_gain_grad: float32 [768], replicated
- post_bias_grad: float32 [768], replicated
- feed_gain_grad: float32 [768], replicated
- feed_gate_grad: float32 [768, 2048], P(None, 'tp')
- feed_linear_grad: float32 [768, 2048], P(None, 'tp')
- feed_down_grad: float32 [2048, 768], P('tp')
All inputs are finite; a program needn't handle non-finite values.
Results may differ from a plain program's by a relative error of at most 0.028.
Values may be sent and summed in bfloat16 or wider, within the bound.
No kernel may reach another device: no remote copies, remote signals or barrier semaphores. Data moves between devices by JAX's collectives and lax.ppermute only.
A program may use at most 128 MiB of HBM per device.

v0:
```python
from functools import partial

import jax
import jax.numpy as jnp
from jax import lax
from jax.sharding import PartitionSpec as P

MINI = 16


RATE_SCALE = 0.25
INNER_EPS = 1e-06
NORM_EPS = 1e-05
SLOPE_C = 0.7978845608028654
CUBIC = 0.044715


def passed_along(array, axis, by):
    peers = lax.axis_size(axis)
    pairs = [(i, i + by) for i in range(peers) if 0 <= i + by < peers]
    return lax.ppermute(array, axis, pairs)


def smooth_act(value):
    return 0.5 * value * (1.0 + jnp.tanh(SLOPE_C * (value + CUBIC * value * value * value)))


def smooth_slope(value):
    tangent = jnp.tanh(SLOPE_C * (value + CUBIC * value * value * value))
    return 0.5 * (1.0 + tangent) + 0.5 * value * (1.0 - tangent * tangent) * SLOPE_C * (
        1.0 + 3.0 * CUBIC * value * value
    )


def product(spec, left, right):
    return jnp.einsum(spec, left, right, precision=lax.Precision.HIGHEST)


def row_norm(value):
    centre = value - jnp.mean(value, -1, keepdims=True)
    scale = lax.rsqrt(jnp.mean(centre * centre, -1, keepdims=True) + INNER_EPS)
    return (centre * scale, scale)


def inner_step(gain, bias, state, block):
    first_w, first_b, second_w, second_b = state
    query, keys, values, rate = block
    size = keys.shape[-2]
    causal = jnp.tril(jnp.ones((size, size), jnp.float32))
    gain_row = gain[..., None, :]
    bias_row = bias[..., None, :]
    first_pre = product("...bp,...pi->...bi", keys, first_w) + first_b[..., None, :]
    first_act = smooth_act(first_pre)
    second_pre = product("...bi,...ip->...bp", first_act, second_w) + second_b[..., None, :]
    normed, scale = row_norm(second_pre)
    error = normed * gain_row + bias_row + keys - values
    grad_norm = error * gain_row
    second_grad = scale * (
        grad_norm
        - jnp.mean(grad_norm, -1, keepdims=True)
        - normed * jnp.mean(grad_norm * normed, -1, keepdims=True)
    )
    first_grad = product("...bp,...ip->...bi", second_grad, second_w) * smooth_slope(first_pre)
    rate_cols = rate[..., None, :]
    weights_one = (product("...bp,...cp->...bc", query, keys) + 1.0) * causal * rate_cols
    query_first = (
        product("...bp,...pi->...bi", query, first_w)
        + first_b[..., None, :]
        - product("...bc,...ci->...bi", weights_one, first_grad)
    )
    query_act = smooth_act(query_first)
    weights_two = (product("...bi,...ci->...bc", query_act, first_act) + 1.0) * causal * rate_cols
    query_second = (
        product("...bi,...ip->...bp", query_act, second_w)
        + second_b[..., None, :]
        - product("...bc,...cp->...bp", weights_two, second_grad)
    )
    query_normed, unused = row_norm(query_second)
    outputs = query + query_normed * gain_row + bias_row
    scaled_first = first_grad * rate[..., None]
    scaled_second = second_grad * rate[..., None]
    first_w = first_w - product("...bp,...bi->...pi", keys, scaled_first)
    first_b = first_b - jnp.sum(scaled_first, -2)
    second_w = second_w - product("...bi,...bp->...ip", first_act, scaled_second)
    second_b = second_b - jnp.sum(scaled_second, -2)
    return ((first_w, first_b, second_w, second_b), outputs)


def blocks_of(array, lead, count, block):
    shaped = array.reshape(lead + (count, block) + array.shape[len(lead) + 1 :])
    return jnp.moveaxis(shaped, len(lead), 0)


def inner_group(state, query, keys, values, rate, gain, bias, block):
    lead = query.shape[:-2]
    length = query.shape[-2]
    width = query.shape[-1]
    count = length // block
    stepper = jax.checkpoint(partial(inner_step, gain, bias))
    pieces = (
        blocks_of(query, lead, count, block),
        blocks_of(keys, lead, count, block),
        blocks_of(values, lead, count, block),
        blocks_of(rate, lead, count, block),
    )
    state, outputs = lax.scan(stepper, state, pieces)
    outputs = jnp.moveaxis(outputs, 0, len(lead)).reshape(lead + (length, width))
    return (state, outputs)


def root_norm(value, gain):
    return value * lax.rsqrt(jnp.mean(value * value, -1, keepdims=True) + NORM_EPS) * gain


def layer_norm(value, gain, bias):
    centre = value - jnp.mean(value, -1, keepdims=True)
    return centre * lax.rsqrt(jnp.mean(centre * centre, -1, keepdims=True) + NORM_EPS) * gain + bias


def gated_branch(mixed, gate_pre, gain, bias):
    return layer_norm(mixed, gain, bias) * smooth_act(gate_pre)


def swish_product(gate_val, linear_val):
    return jax.nn.silu(gate_val) * linear_val


def matmul(left, right):
    return jnp.dot(left, right, preferred_element_type=jnp.float32)


def pack_state(state):
    first_w, first_b, second_w, second_b = state
    lead = first_b.shape[:-1]
    return jnp.concatenate(
        [first_w.reshape(lead + (-1,)), first_b, second_w.reshape(lead + (-1,)), second_b], -1
    )


def unpack_state(packed, head_width, inner_width):
    size = head_width * inner_width
    lead = packed.shape[:-1]
    first_w = packed[..., :size].reshape(lead + (head_width, inner_width))
    first_b = packed[..., size : size + inner_width]
    second_w = packed[..., size + inner_width : 2 * size + inner_width].reshape(
        lead + (inner_width, head_width)
    )
    second_b = packed[..., 2 * size + inner_width :]
    return (first_w, first_b, second_w, second_b)


def add_slot(buffer, addition, index):
    current = lax.dynamic_index_in_dim(buffer, index, 0, keepdims=False)
    return lax.dynamic_update_index_in_dim(buffer, current + addition, index, 0)


def on_device(
    tokens,
    norm_gain,
    query_weight,
    key_weight,
    value_weight,
    rate_weight,
    rate_bias,
    first_weight,
    first_bias,
    second_weight,
    second_bias,
    inner_gain,
    inner_bias,
    branch_gate,
    output_weight,
    post_gain,
    post_bias,
    feed_gain,
    feed_gate,
    feed_linear,
    feed_down,
    cotangent,
):
    low_type = jnp.bfloat16
    wide_type = jnp.float32
    residual = tokens[0].astype(wide_type)
    tok_rows = residual.shape[0]
    head_width = first_weight.shape[1]
    inner_width = first_weight.shape[2]
    normed_val, norm_pull = jax.vjp(root_norm, residual, norm_gain)
    normed = normed_val.astype(low_type)
    query_tok = matmul(normed, query_weight).astype(low_type)
    keys_tok = matmul(normed, key_weight).astype(low_type)
    values_tok = matmul(normed, value_weight).astype(low_type)
    logits_tok = matmul(normed, rate_weight).astype(low_type)
    gate_pre = matmul(normed, branch_gate)
    head_query, head_keys, head_values, head_logits = (
        lax.all_to_all(query_tok[None], "tp", split_axis=2, concat_axis=0, tiled=True),
        lax.all_to_all(keys_tok[None], "tp", split_axis=2, concat_axis=0, tiled=True),
        lax.all_to_all(values_tok[None], "tp", split_axis=2, concat_axis=0, tiled=True),
        lax.all_to_all(logits_tok[None], "tp", split_axis=2, concat_axis=0, tiled=True),
    )
    seq_count = head_query.shape[0]
    heads_here = head_logits.shape[2]

    def spread(array, index):
        piece = lax.dynamic_index_in_dim(array, index, 0, keepdims=False).astype(wide_type)
        return piece.reshape(tok_rows, heads_here, head_width).transpose(1, 0, 2)

    def group_inputs(index):
        logit_piece = lax.dynamic_index_in_dim(head_logits, index, 0, keepdims=False).astype(
            wide_type
        )
        return (
            spread(head_query, index),
            spread(head_keys, index),
            spread(head_values, index),
            jnp.transpose(logit_piece),
        )

    def local_group(packed, query_c, keys_c, values_c, logit_c, bias_vec, gain_c, shift_c):
        state = unpack_state(packed, head_width, inner_width)
        rate = jax.nn.sigmoid(logit_c + bias_vec[:, None]) * (RATE_SCALE / head_width)
        new_state, outputs = inner_group(
            state, query_c, keys_c, values_c, rate, gain_c, shift_c, MINI
        )
        return (pack_state(new_state), outputs)

    start_packed = pack_state((first_weight, first_bias, second_weight, second_bias))
    rank = lax.axis_index("seq")
    ranks = lax.axis_size("seq")
    sections = ranks + seq_count - 1

    def forward_section(section, carry):
        incoming, mixed_buf, kept = carry
        index = section - rank
        active = jnp.logical_and(index >= 0, index < seq_count)
        clipped = jnp.clip(index, 0, seq_count - 1)
        start = jnp.where(rank == 0, start_packed, incoming)

        def forward_run(slot):
            new_state, outputs = local_group(
                start, *group_inputs(slot), rate_bias, inner_gain, inner_bias
            )
            return (new_state, outputs, start)

        def forward_skip(slot):
            return (
                start,
                lax.dynamic_index_in_dim(mixed_buf, slot, 0, keepdims=False),
                lax.dynamic_index_in_dim(kept, slot, 0, keepdims=False),
            )

        new_state, outputs, keep_now = lax.cond(active, forward_run, forward_skip, clipped)
        mixed_buf = lax.dynamic_update_index_in_dim(mixed_buf, outputs, clipped, 0)
        kept = lax.dynamic_update_index_in_dim(kept, keep_now, clipped, 0)
        outgoing = passed_along(new_state.astype(jnp.bfloat16), "seq", 1).astype(new_state.dtype)
        return (outgoing, mixed_buf, kept)

    mixed_buf = jnp.zeros((seq_count, heads_here, tok_rows, head_width), wide_type)
    kept = jnp.zeros((seq_count,) + start_packed.shape, wide_type)
    unused, mixed_buf, kept = lax.fori_loop(
        0, sections, forward_section, (jnp.zeros_like(start_packed), mixed_buf, kept)
    )

    def tokens_form(buffer):
        return (
            buffer.transpose(0, 2, 1, 3)
            .reshape(seq_count, tok_rows, heads_here * head_width)
            .astype(low_type)
        )

    mixed_back = lax.all_to_all(
        tokens_form(mixed_buf), "tp", split_axis=0, concat_axis=2, tiled=True
    )
    mixed_tok = mixed_back[0].astype(wide_type)
    branch_val, branch_pull = jax.vjp(gated_branch, mixed_tok, gate_pre, post_gain, post_bias)
    branch_in = branch_val.astype(low_type)
    middle = residual + matmul(branch_in, output_weight)
    feed_val, feed_pull = jax.vjp(root_norm, middle, feed_gain)
    feed_in = feed_val.astype(low_type)
    grad_out = cotangent[0].astype(wide_type)
    down_grad = grad_out.astype(low_type)
    every_in = lax.all_gather(feed_in, "tp", axis=0, tiled=True)
    gate_val = matmul(every_in, feed_gate)
    linear_val = matmul(every_in, feed_linear)
    act_val, act_pull = jax.vjp(swish_product, gate_val, linear_val)
    hidden = act_val.astype(low_type)
    second_out = lax.psum_scatter(
        matmul(hidden, feed_down).astype(jnp.bfloat16), "tp", scatter_dimension=0, tiled=True
    ).astype(jnp.float32)
    every_grad = lax.all_gather(down_grad, "tp", axis=0, tiled=True)
    hidden_grad = jnp.einsum("td,fd->tf", every_grad, feed_down, preferred_element_type=wide_type)
    feed_down_grad = jnp.einsum("tf,td->fd", hidden, every_grad, preferred_element_type=wide_type)
    gate_grad, linear_grad = act_pull(hidden_grad)
    gate_low = gate_grad.astype(low_type)
    linear_low = linear_grad.astype(low_type)
    feed_gate_grad = jnp.einsum("td,tf->df", every_in, gate_low, preferred_element_type=wide_type)
    feed_linear_grad = jnp.einsum(
        "td,tf->df", every_in, linear_low, preferred_element_type=wide_type
    )
    input_part = jnp.einsum(
        "tf,df->td", gate_low, feed_gate, preferred_element_type=wide_type
    ) + jnp.einsum("tf,df->td", linear_low, feed_linear, preferred_element_type=wide_type)
    feed_in_grad = lax.psum_scatter(
        input_part.astype(jnp.bfloat16), "tp", scatter_dimension=0, tiled=True
    ).astype(jnp.float32)
    result = (middle + second_out).astype(low_type)[None]
    middle_part, feed_gain_grad = feed_pull(feed_in_grad)
    middle_grad = grad_out + middle_part
    out_low = middle_grad.astype(low_type)
    output_weight_grad = jnp.einsum(
        "td,te->de", branch_in, out_low, preferred_element_type=wide_type
    )
    branch_grad = jnp.einsum("te,de->td", out_low, output_weight, preferred_element_type=wide_type)
    mixed_grad, gate_pre_grad, post_gain_grad, post_bias_grad = branch_pull(branch_grad)
    heads_grad = lax.all_to_all(
        mixed_grad.astype(low_type)[None], "tp", split_axis=2, concat_axis=0, tiled=True
    )

    def backward_section(section, carry):
        (
            incoming,
            query_buf,
            keys_buf,
            values_buf,
            logit_buf,
            bias_total,
            gain_total,
            shift_total,
            start_total,
        ) = carry
        index = section - (ranks - 1 - rank)
        active = jnp.logical_and(index >= 0, index < seq_count)
        clipped = jnp.clip(index, 0, seq_count - 1)

        def backward_run(slot):
            out_grad = spread(heads_grad, slot)
            state_in = lax.dynamic_index_in_dim(kept, slot, 0, keepdims=False)
            unused_out, pull = jax.vjp(
                local_group, state_in, *group_inputs(slot), rate_bias, inner_gain, inner_bias
            )
            return pull((incoming, out_grad))

        def backward_skip(slot):
            blank = jnp.zeros((heads_here, tok_rows, head_width), wide_type)
            return (
                jnp.zeros_like(incoming),
                blank,
                blank,
                blank,
                jnp.zeros((heads_here, tok_rows), wide_type),
                jnp.zeros_like(rate_bias),
                jnp.zeros_like(inner_gain),
                jnp.zeros_like(inner_bias),
            )

        (
            state_grad,
            query_grad,
            keys_grad,
            values_grad,
            logit_grad,
            bias_grad,
            gain_grad,
            shift_grad,
        ) = lax.cond(active, backward_run, backward_skip, clipped)
        query_buf = add_slot(query_buf, query_grad, clipped)
        keys_buf = add_slot(keys_buf, keys_grad, clipped)
        values_buf = add_slot(values_buf, values_grad, clipped)
        logit_buf = add_slot(logit_buf, logit_grad, clipped)
        start_total = start_total + jnp.where(rank == 0, state_grad, 0.0)
        outgoing = passed_along(state_grad.astype(jnp.bfloat16), "seq", -1).astype(state_grad.dtype)
        return (
            outgoing,
            query_buf,
            keys_buf,
            values_buf,
            logit_buf,
            bias_total + bias_grad,
            gain_total + gain_grad,
            shift_total + shift_grad,
            start_total,
        )

    blank_buf = jnp.zeros((seq_count, heads_here, tok_rows, head_width), wide_type)
    carry = (
        jnp.zeros_like(start_packed),
        blank_buf,
        blank_buf,
        blank_buf,
        jnp.zeros((seq_count, heads_here, tok_rows), wide_type),
        jnp.zeros_like(rate_bias),
        jnp.zeros_like(inner_gain),
        jnp.zeros_like(inner_bias),
        jnp.zeros_like(start_packed),
    )
    (
        unused,
        query_buf,
        keys_buf,
        values_buf,
        logit_buf,
        bias_total,
        gain_total,
        shift_total,
        start_total,
    ) = lax.fori_loop(0, sections, backward_section, carry)
    query_back, keys_back, values_back, logit_back = (
        lax.all_to_all(tokens_form(query_buf), "tp", split_axis=0, concat_axis=2, tiled=True),
        lax.all_to_all(tokens_form(keys_buf), "tp", split_axis=0, concat_axis=2, tiled=True),
        lax.all_to_all(tokens_form(values_buf), "tp", split_axis=0, concat_axis=2, tiled=True),
        lax.all_to_all(
            logit_buf.transpose(0, 2, 1).astype(low_type),
            "tp",
            split_axis=0,
            concat_axis=2,
            tiled=True,
        ),
    )
    query_low = query_back[0]
    keys_low = keys_back[0]
    values_low = values_back[0]
    logit_low = logit_back[0]
    gate_low_pre = gate_pre_grad.astype(low_type)
    query_weight_grad = jnp.einsum("td,te->de", normed, query_low, preferred_element_type=wide_type)
    key_weight_grad = jnp.einsum("td,te->de", normed, keys_low, preferred_element_type=wide_type)
    value_weight_grad = jnp.einsum(
        "td,te->de", normed, values_low, preferred_element_type=wide_type
    )
    rate_weight_grad = jnp.einsum("td,te->de", normed, logit_low, preferred_element_type=wide_type)
    branch_gate_grad = jnp.einsum(
        "td,te->de", normed, gate_low_pre, preferred_element_type=wide_type
    )
    normed_grad = (
        jnp.einsum("te,de->td", query_low, query_weight, preferred_element_type=wide_type)
        + jnp.einsum("te,de->td", keys_low, key_weight, preferred_element_type=wide_type)
        + jnp.einsum("te,de->td", values_low, value_weight, preferred_element_type=wide_type)
        + jnp.einsum("te,de->td", logit_low, rate_weight, preferred_element_type=wide_type)
        + jnp.einsum("te,de->td", gate_low_pre, branch_gate, preferred_element_type=wide_type)
    )
    residual_part, norm_gain_grad = norm_pull(normed_grad)
    tokens_grad = (middle_grad + residual_part)[None]
    shared = lax.psum(
        (
            norm_gain_grad,
            query_weight_grad,
            key_weight_grad,
            value_weight_grad,
            rate_weight_grad,
            branch_gate_grad,
            output_weight_grad,
            post_gain_grad,
            post_bias_grad,
            feed_gain_grad,
        ),
        ("seq", "tp"),
    )
    start_parts = unpack_state(start_total, head_width, inner_width)
    sharded = (
        lax.psum(bias_total.astype(jnp.bfloat16), "seq").astype(jnp.float32),
        lax.psum(start_parts[0].astype(jnp.bfloat16), "seq").astype(jnp.float32),
        lax.psum(start_parts[1].astype(jnp.bfloat16), "seq").astype(jnp.float32),
        lax.psum(start_parts[2].astype(jnp.bfloat16), "seq").astype(jnp.float32),
        lax.psum(start_parts[3].astype(jnp.bfloat16), "seq").astype(jnp.float32),
        lax.psum(gain_total.astype(jnp.bfloat16), "seq").astype(jnp.float32),
        lax.psum(shift_total.astype(jnp.bfloat16), "seq").astype(jnp.float32),
        lax.psum(feed_gate_grad.astype(jnp.bfloat16), "seq").astype(jnp.float32),
        lax.psum(feed_linear_grad.astype(jnp.bfloat16), "seq").astype(jnp.float32),
        lax.psum(feed_down_grad.astype(jnp.bfloat16), "seq").astype(jnp.float32),
    )
    return (
        result,
        tokens_grad,
        shared[0],
        shared[1],
        shared[2],
        shared[3],
        shared[4],
        sharded[0],
        sharded[1],
        sharded[2],
        sharded[3],
        sharded[4],
        sharded[5],
        sharded[6],
        shared[5],
        shared[6],
        shared[7],
        shared[8],
        shared[9],
        sharded[7],
        sharded[8],
        sharded[9],
    )


def solution(mesh):
    in_specs = (
        P("tp", "seq", None),
        P(),
        P(),
        P(),
        P(),
        P(),
        P("tp"),
        P("tp", None, None),
        P("tp", None),
        P("tp", None, None),
        P("tp", None),
        P("tp", None),
        P("tp", None),
        P(),
        P(),
        P(),
        P(),
        P(),
        P(None, "tp"),
        P(None, "tp"),
        P("tp", None),
        P("tp", "seq", None),
    )
    out_specs = (
        P("tp", "seq", None),
        P("tp", "seq", None),
        P(),
        P(),
        P(),
        P(),
        P(),
        P("tp"),
        P("tp", None, None),
        P("tp", None),
        P("tp", None, None),
        P("tp", None),
        P("tp", None),
        P("tp", None),
        P(),
        P(),
        P(),
        P(),
        P(),
        P(None, "tp"),
        P(None, "tp"),
        P("tp", None),
    )
    return jax.shard_map(
        on_device, mesh=mesh, in_specs=in_specs, out_specs=out_specs, check_vma=False
    )
```

profile of v0, /device:TPU:0, one launch (start us, length us, event | category | flops | bytes accessed | tf_op | source)
XLA Modules:
  0.0 2946.6 jit_solution(17273859138642381827)
XLA Ops:
  12.1 4.2 all-to-all-start.3
  25.8 4.0 all-to-all-start
  36.4 3.4 all-to-all-start.1
  45.1 3.5 all-to-all-start.2
  57.6 427.6 %while.126 = (s32[]{:T(128)}, f32[3,33088]{1,0:T(4,128)S(1)}, bf16[4,3,128,64]{3,2,1,0:T(8,128)(2,1)}, f32[4,3,33088]{2,1,0:T(4,128)}, s32[]{:T(128)}, /*index=5...) while((s32[]{:T(128)}, f32[3,33088]{1,0:T(4,128)S(1)}, ...), condition=%wide.region_14.15_spmd.clone, body=%wide.region_1.14_spmd.clone.sunk | while | flops 73628584 | bytes 13462009 | solution.py:259
  58.9 40.4 %conditional.6 = (f32[3,33088]{1,0:T(4,128)S(1)}, bf16[1,3,128,64]{3,2,1,0:T(8,128)(2,1)S(1)}, f32[1,3,33088]{2,1,0:T(4,128)S(1)}) conditional(s32[]{:T(128)} %convert_element_type.497, (s32[]{:T(128)}, bf16[4,3,128,64]{3,2,1,0:T(8,128)(2,1)}, f32[4,3,33088]{2,1,0:T(4,128)}, f32[3,33088]{1,0:T(4,128)S(1)}) %tuple.276, (f32[3,33088]{1,0:T(4,128)S(1)}, ...), branch_computations={%region_2.2_spmd, %region_3.13_spmd} | conditional | flops 73231520 | bytes 9209211 | solution.py:251
  61.8 36.6 %while.123 = (s32[]{:T(128)}, f32[3,64,256]{2,1,0:T(8,128)S(1)}, f32[3,256]{1,0:T(4,128)S(1)}, f32[3,256,64]{1,2,0:T(8,128)S(1)}, f32[3,64]{1,0:T(4,128)S(1)}, /...) while((s32[]{:T(128)}, f32[3,64,256]{2,1,0:T(8,128)S(1)}, ...), condition=%wide.region_13.12_spmd, body=%wide.region_4.11_spmd.sunk | while | flops 72857696 | bytes 2839965 | solution.py:106
  102.3 5.0 collective-permute-done.1
  108.6 40.4 %conditional.6 = (f32[3,33088]{1,0:T(4,128)S(1)}, bf16[1,3,128,64]{3,2,1,0:T(8,128)(2,1)S(1)}, f32[1,3,33088]{2,1,0:T(4,128)S(1)}) conditional(s32[]{:T(128)} %convert_element_type.497, (s32[]{:T(128)}, bf16[4,3,128,64]{3,2,1,0:T(8,128)(2,1)}, f32[4,3,33088]{2,1,0:T(4,128)}, f32[3,33088]{1,0:T(4,128)S(1)}) %tuple.276, (f32[3,33088]{1,0:T(4,128)S(1)}, ...), branch_computations={%region_2.2_spmd, %region_3.13_spmd} | conditional | flops 73231520 | bytes 9209211 | solution.py:251
  111.5 36.6 %while.123 = (s32[]{:T(128)}, f32[3,64,256]{2,1,0:T(8,128)S(1)}, f32[3,256]{1,0:T(4,128)S(1)}, f32[3,256,64]{1,2,0:T(8,128)S(1)}, f32[3,64]{1,0:T(4,128)S(1)}, /...) while((s32[]{:T(128)}, f32[3,64,256]{2,1,0:T(8,128)S(1)}, ...), condition=%wide.region_13.12_spmd, body=%wide.region_4.11_spmd.sunk | while | flops 72857696 | bytes 2839965 | solution.py:106
  149.1 3.4 collective-permute-start.1
  154.0 4.1 collective-permute-done.1
  159.5 40.4 %conditional.6 = (f32[3,33088]{1,0:T(4,128)S(1)}, bf16[1,3,128,64]{3,2,1,0:T(8,128)(2,1)S(1)}, f32[1,3,33088]{2,1,0:T(4,128)S(1)}) conditional(s32[]{:T(128)} %convert_element_type.497, (s32[]{:T(128)}, bf16[4,3,128,64]{3,2,1,0:T(8,128)(2,1)}, f32[4,3,33088]{2,1,0:T(4,128)}, f32[3,33088]{1,0:T(4,128)S(1)}) %tuple.276, (f32[3,33088]{1,0:T(4,128)S(1)}, ...), branch_computations={%region_2.2_spmd, %region_3.13_spmd} | conditional | flops 73231520 | bytes 9209211 | solution.py:251
  162.4 36.6 %while.123 = (s32[]{:T(128)}, f32[3,64,256]{2,1,0:T(8,128)S(1)}, f32[3,256]{1,0:T(4,128)S(1)}, f32[3,256,64]{1,2,0:T(8,128)S(1)}, f32[3,64]{1,0:T(4,128)S(1)}, /...) while((s32[]{:T(128)}, f32[3,64,256]{2,1,0:T(8,128)S(1)}, ...), condition=%wide.region_13.12_spmd, body=%wide.region_4.11_spmd.sunk | while | flops 72857696 | bytes 2839965 | solution.py:106
  200.0 3.4 collective-permute-start.1
  204.9 3.2 collective-permute-done.1
  209.5 40.4 %conditional.6 = (f32[3,33088]{1,0:T(4,128)S(1)}, bf16[1,3,128,64]{3,2,1,0:T(8,128)(2,1)S(1)}, f32[1,3,33088]{2,1,0:T(4,128)S(1)}) conditional(s32[]{:T(128)} %convert_element_type.497, (s32[]{:T(128)}, bf16[4,3,128,64]{3,2,1,0:T(8,128)(2,1)}, f32[4,3,33088]{2,1,0:T(4,128)}, f32[3,33088]{1,0:T(4,128)S(1)}) %tuple.276, (f32[3,33088]{1,0:T(4,128)S(1)}, ...), branch_computations={%region_2.2_spmd, %region_3.13_spmd} | conditional | flops 73231520 | bytes 9209211 | solution.py:251
  212.4 36.6 %while.123 = (s32[]{:T(128)}, f32[3,64,256]{2,1,0:T(8,128)S(1)}, f32[3,256]{1,0:T(4,128)S(1)}, f32[3,256,64]{1,2,0:T(8,128)S(1)}, f32[3,64]{1,0:T(4,128)S(1)}, /...) while((s32[]{:T(128)}, f32[3,64,256]{2,1,0:T(8,128)S(1)}, ...), condition=%wide.region_13.12_spmd, body=%wide.region_4.11_spmd.sunk | while | flops 72857696 | bytes 2839965 | solution.py:106
  250.0 3.4 collective-permute-start.1
  260.7 41.9 %collective-permute-start.1 = (bf16[3,33088]{1,0:T(4,128)(2,1)S(1)}, bf16[3,33088]{1,0:T(4,128)(2,1)S(1)}, u32[]{:S(2)}, u32[]{:S(2)}) collective-permute-start(bf16[3,33088]{1,0:T(4,128)(2,1)S(1)} %convert_element_type.498), channel_id=1, source_target_pairs={{0,4},{4,8},{8,12},{12,16},{16,20},{20,24},{24,28},{1,5},{5,9},{9,... | collective-permute-start | bytes 595592 | tf_op jit(solution)/shard_map/while/body/eval_jaxpr/ppermute | solution.py:21
  310.1 4.3 collective-permute-start.1
  321.8 42.6 %collective-permute-start.1 = (bf16[3,33088]{1,0:T(4,128)(2,1)S(1)}, bf16[3,33088]{1,0:T(4,128)(2,1)S(1)}, u32[]{:S(2)}, u32[]{:S(2)}) collective-permute-start(bf16[3,33088]{1,0:T(4,128)(2,1)S(1)} %convert_element_type.498), channel_id=1, source_target_pairs={{0,4},{4,8},{8,12},{12,16},{16,20},{20,24},{24,28},{1,5},{5,9},{9,... | collective-permute-start | bytes 595592 | tf_op jit(solution)/shard_map/while/body/eval_jaxpr/ppermute | solution.py:21
  371.8 4.3 collective-permute-start.1
  383.4 38.3 %collective-permute-start.1 = (bf16[3,33088]{1,0:T(4,128)(2,1)S(1)}, bf16[3,33088]{1,0:T(4,128)(2,1)S(1)}, u32[]{:S(2)}, u32[]{:S(2)}) collective-permute-start(bf16[3,33088]{1,0:T(4,128)(2,1)S(1)} %convert_element_type.498), channel_id=1, source_target_pairs={{0,4},{4,8},{8,12},{12,16},{16,20},{20,24},{24,28},{1,5},{5,9},{9,... | collective-permute-start | bytes 595592 | tf_op jit(solution)/shard_map/while/body/eval_jaxpr/ppermute | solution.py:21
  429.2 4.3 collective-permute-start.1
  440.9 40.4 %collective-permute-start.1 = (bf16[3,33088]{1,0:T(4,128)(2,1)S(1)}, bf16[3,33088]{1,0:T(4,128)(2,1)S(1)}, u32[]{:S(2)}, u32[]{:S(2)}) collective-permute-start(bf16[3,33088]{1,0:T(4,128)(2,1)S(1)} %convert_element_type.498), channel_id=1, source_target_pairs={{0,4},{4,8},{8,12},{12,16},{16,20},{20,24},{24,28},{1,5},{5,9},{9,... | collective-permute-start | bytes 595592 | tf_op jit(solution)/shard_map/while/body/eval_jaxpr/ppermute | solution.py:21
  487.1 3.5 all-to-all-start.4
  490.6 11.0 all-gather
  505.3 8.9 all_gather.6
  527.4 131.8 %reduce-scatter.5.cloned.1.call-done = bf16[128,768]{1,0:T(8,128)(2,1)} async-done(((bf16[512,768]{1,0:T(8,128)(2,1)}), bf16[128,768]{1,0:T(8,128)(2,1)}) %reduce-scatter.5.cloned.1.call-update) | async-done | bytes 196624 | tf_op jit(solution)/shard_map/reduce_scatter | solution.py:302
  660.9 24.9 reduce-scatter.3.cloned.1.call-done
  687.6 3.2 multiply_reduce_fusion.25
  694.3 3.4 all-to-all-start.5
  699.2 3.7 all-to-all-done.5
  706.2 1865.3 %while.127 = (s32[]{:T(128)}, f32[3,33088]{1,0:T(4,128)S(1)}, f32[4,3,128,64]{2,3,1,0:T(8,128)}, f32[4,3,128,64]{2,3,1,0:T(8,128)}, f32[4,3,128,64]{2,3,1,0:T(8,...) while((s32[]{:T(128)}, f32[3,33088]{1,0:T(4,128)S(1)}, ...), condition=%wide.region_63.64_spmd.clone, body=%wide.region_23.63_spmd.clone.sunk | while | flops 249449568 | bytes 30661256 | solution.py:405
  706.2 2.8 conditional.7
  721.3 2.8 conditional.7
  736.2 2.8 conditional.7
  750.5 2.8 conditional.7
  765.1 2.8 conditional.7
  807.4 1083.6 %collective-permute-done = bf16[3,33088]{1,0:T(4,128)(2,1)S(1)} collective-permute-done((bf16[3,33088]{1,0:T(4,128)(2,1)S(1)}, bf16[3,33088]{1,0:T(4,128)(2,1)S(1)}, u32[]{:S(2)}, u32[]{:S(2)}) %collective-permute-start) | collective-permute-done | bytes 198560 | tf_op jit(solution)/shard_map/while/body/eval_jaxpr/ppermute | solution.py:21
  1891.2 158.5 %conditional.7 = (f32[3,33088]{1,0:T(4,128)}, f32[3,128,64]{2,1,0:T(8,128)}, f32[3,128,64]{2,1,0:T(8,128)S(1)}, f32[3,128,64]{2,1,0:T(8,128)S(1)}, f32[3,128]{1,...) conditional(s32[]{:T(128)} %convert_element_type.501, () %tuple.282, (pred[]{:T(512)}, ...), branch_computations={%region_24.24_spmd, %region_25.62_spmd} | conditional | flops 248878352 | bytes 24220812 | solution.py:364
  1895.0 29.5 %while.124 = (s32[]{:T(128)}, f32[3,64,256]{2,1,0:T(8,128)S(1)}, f32[3,256]{1,0:T(4,128)S(1)}, f32[3,256,64]{1,2,0:T(8,128)S(1)}, f32[3,64]{1,0:T(4,128)S(1)}, /...) while((s32[]{:T(128)}, f32[3,64,256]{2,1,0:T(8,128)S(1)}, ...), condition=%wide.region_33.32_spmd, body=%wide.region_26.31_spmd.sunk | while | flops 47812656 | bytes 2680757 | solution.py:106
  1925.8 121.5 %while.125 = (s32[]{:T(128)}, f32[3,64]{1,0:T(4,128)}, f32[3,64]{1,0:T(4,128)}, f32[3,64,256]{2,1,0:T(8,128)S(1)}, f32[3,256]{1,0:T(4,128)S(1)}, /*index=5*/f32[...) while((s32[]{:T(128)}, f32[3,64]{1,0:T(4,128)}, ...), condition=%wide.region_61.60_spmd.clone, body=%wide.region_34.59_spmd.clone.sunk | while | flops 200564192 | bytes 8970920 | solution.py:106
  2061.5 158.5 %conditional.7 = (f32[3,33088]{1,0:T(4,128)}, f32[3,128,64]{2,1,0:T(8,128)}, f32[3,128,64]{2,1,0:T(8,128)S(1)}, f32[3,128,64]{2,1,0:T(8,128)S(1)}, f32[3,128]{1,...) conditional(s32[]{:T(128)} %convert_element_type.501, () %tuple.282, (pred[]{:T(512)}, ...), branch_computations={%region_24.24_spmd, %region_25.62_spmd} | conditional | flops 248878352 | bytes 24220812 | solution.py:364
  2065.4 29.5 %while.124 = (s32[]{:T(128)}, f32[3,64,256]{2,1,0:T(8,128)S(1)}, f32[3,256]{1,0:T(4,128)S(1)}, f32[3,256,64]{1,2,0:T(8,128)S(1)}, f32[3,64]{1,0:T(4,128)S(1)}, /...) while((s32[]{:T(128)}, f32[3,64,256]{2,1,0:T(8,128)S(1)}, ...), condition=%wide.region_33.32_spmd, body=%wide.region_26.31_spmd.sunk | while | flops 47812656 | bytes 2680757 | solution.py:106
  2096.1 121.5 %while.125 = (s32[]{:T(128)}, f32[3,64]{1,0:T(4,128)}, f32[3,64]{1,0:T(4,128)}, f32[3,64,256]{2,1,0:T(8,128)S(1)}, f32[3,256]{1,0:T(4,128)S(1)}, /*index=5*/f32[...) while((s32[]{:T(128)}, f32[3,64]{1,0:T(4,128)}, ...), condition=%wide.region_61.60_spmd.clone, body=%wide.region_34.59_spmd.clone.sunk | while | flops 200564192 | bytes 8970920 | solution.py:106
  2231.8 158.5 %conditional.7 = (f32[3,33088]{1,0:T(4,128)}, f32[3,128,64]{2,1,0:T(8,128)}, f32[3,128,64]{2,1,0:T(8,128)S(1)}, f32[3,128,64]{2,1,0:T(8,128)S(1)}, f32[3,128]{1,...) conditional(s32[]{:T(128)} %convert_element_type.501, () %tuple.282, (pred[]{:T(512)}, ...), branch_computations={%region_24.24_spmd, %region_25.62_spmd} | conditional | flops 248878352 | bytes 24220812 | solution.py:364
  2235.7 29.5 %while.124 = (s32[]{:T(128)}, f32[3,64,256]{2,1,0:T(8,128)S(1)}, f32[3,256]{1,0:T(4,128)S(1)}, f32[3,256,64]{1,2,0:T(8,128)S(1)}, f32[3,64]{1,0:T(4,128)S(1)}, /...) while((s32[]{:T(128)}, f32[3,64,256]{2,1,0:T(8,128)S(1)}, ...), condition=%wide.region_33.32_spmd, body=%wide.region_26.31_spmd.sunk | while | flops 47812656 | bytes 2680757 | solution.py:106
  2266.4 121.5 %while.125 = (s32[]{:T(128)}, f32[3,64]{1,0:T(4,128)}, f32[3,64]{1,0:T(4,128)}, f32[3,64,256]{2,1,0:T(8,128)S(1)}, f32[3,256]{1,0:T(4,128)S(1)}, /*index=5*/f32[...) while((s32[]{:T(128)}, f32[3,64]{1,0:T(4,128)}, ...), condition=%wide.region_61.60_spmd.clone, body=%wide.region_34.59_spmd.clone.sunk | while | flops 200564192 | bytes 8970920 | solution.py:106
  2402.1 158.5 %conditional.7 = (f32[3,33088]{1,0:T(4,128)}, f32[3,128,64]{2,1,0:T(8,128)}, f32[3,128,64]{2,1,0:T(8,128)S(1)}, f32[3,128,64]{2,1,0:T(8,128)S(1)}, f32[3,128]{1,...) conditional(s32[]{:T(128)} %convert_element_type.501, () %tuple.282, (pred[]{:T(512)}, ...), branch_computations={%region_24.24_spmd, %region_25.62_spmd} | conditional | flops 248878352 | bytes 24220812 | solution.py:364
  2406.0 29.5 %while.124 = (s32[]{:T(128)}, f32[3,64,256]{2,1,0:T(8,128)S(1)}, f32[3,256]{1,0:T(4,128)S(1)}, f32[3,256,64]{1,2,0:T(8,128)S(1)}, f32[3,64]{1,0:T(4,128)S(1)}, /...) while((s32[]{:T(128)}, f32[3,64,256]{2,1,0:T(8,128)S(1)}, ...), condition=%wide.region_33.32_spmd, body=%wide.region_26.31_spmd.sunk | while | flops 47812656 | bytes 2680757 | solution.py:106
  2436.8 121.5 %while.125 = (s32[]{:T(128)}, f32[3,64]{1,0:T(4,128)}, f32[3,64]{1,0:T(4,128)}, f32[3,64,256]{2,1,0:T(8,128)S(1)}, f32[3,256]{1,0:T(4,128)S(1)}, /*index=5*/f32[...) while((s32[]{:T(128)}, f32[3,64]{1,0:T(4,128)}, ...), condition=%wide.region_61.60_spmd.clone, body=%wide.region_34.59_spmd.clone.sunk | while | flops 200564192 | bytes 8970920 | solution.py:106
  2577.6 3.8 all-to-all-start.6
  2586.7 3.4 all-to-all-start.7
  2592.0 3.3 all-to-all-done.7
  2595.3 3.4 all-to-all-start.8
  2600.7 3.3 all-to-all-done.8
  2607.5 3.8 all-to-all-start.9
  2613.8 20.5 all-reduce.6
  2646.0 40.8 %all-reduce.4 = (f32[768]{0:T(1024)}, f32[768,12]{0,1:T(8,128)}, f32[768]{0:T(1024)}, f32[768]{0:T(1024)}, f32[768]{0:T(1024)}) all-reduce(f32[768]{0:T(1024)S(1)} %get-tuple-element.2102, f32[768,12]{0,1:T(8,128)S(1)} %copy-done.45, f32[768]{0:T(1024)S(1)} %copy-done.55, ...), channel_id=1, replica_groups=mesh['seq'=8,'tp'=4] {'seq','tp'}, use_global_device_ids=true, to_apply=%region_66.67 | all-reduce | flops 12288 | bytes 98304 | tf_op jit(solution)/shard_map/psum | solution.py:441
  2687.7 5.9 all-reduce.13.cloned.1.call-done
  2702.1 225.2 %all-reduce.11.cloned.1.call-done = (f32[768,768]{1,0:T(8,128)}, f32[768,768]{1,0:T(8,128)}, f32[768,768]{1,0:T(8,128)}, f32[768,768]{1,0:T(8,128)}, f32[768,768]{1,0:T(8,128)}) async-done(((f32[768,768]{1,0:T(8,128)}, f32[768,768]{1,0:T(8,128)}, f32[768,768]{1,0:T(8,128)}, f32[768,768]{1,0:T(8,128)}, f32[768,768]{1,0:T(8,128)}), (f32[768,768]{1,0:T(8,128)}, f32[768,768]{1,0:T(8,128)}, ...) | async-done | bytes 11796496 | tf_op jit(solution)/shard_map/psum | solution.py:441
  2927.2 3.4 copy.546
  (4602 shorter events, 1126.4 us)
Async XLA Ops:
  7.2 497.3 %copy-start = (bf16[768,768]{1,0:T(8,128)(2,1)S(1)}, bf16[768,768]{1,0:T(8,128)(2,1)}, u32[]{:S(2)}) copy-start(bf16[768,768]{1,0:T(8,128)(2,1)} %param.50) | copy-start | bytes 3538948
  7.2 11.5 copy-start.41
  9.0 493.0 %copy-start.46 = (f32[128]{0:T(128)}, f32[128]{0:T(128)S(1)}, u32[]{:S(2)}) copy-start(f32[128]{0:T(128)S(1)} %fusion.222) | copy-start | bytes 1540
  12.1 13.7 all-to-all-start.3
  18.9 10.9 copy-start.4
  18.9 10.9 copy-start.8
  18.9 10.9 copy-start.39
  25.8 10.6 all-to-all-start
  30.9 8.9 copy-start.10
  36.4 8.7 all-to-all-start.1
  39.8 8.9 copy-start.53
  39.8 8.8 copy-start.57
  45.1 9.2 all-to-all-start.2
  99.4 7.8 collective-permute-start.1
  149.1 9.0 collective-permute-start.1
  200.0 8.1 collective-permute-start.1
  250.0 7.3 collective-permute-start.1
  260.7 45.8 %collective-permute-start.1 = (bf16[3,33088]{1,0:T(4,128)(2,1)S(1)}, bf16[3,33088]{1,0:T(4,128)(2,1)S(1)}, u32[]{:S(2)}, u32[]{:S(2)}) collective-permute-start(bf16[3,33088]{1,0:T(4,128)(2,1)S(1)} %convert_element_type.498), channel_id=1, source_target_pairs={{0,4},{4,8},{8,12},{12,16},{16,20},{20,24},{24,28},{1,5},{5,9},{9,... | collective-permute-start | bytes 595592 | tf_op jit(solution)/shard_map/while/body/eval_jaxpr/ppermute | solution.py:21
  310.1 8.2 collective-permute-start.1
  321.8 46.5 %collective-permute-start.1 = (bf16[3,33088]{1,0:T(4,128)(2,1)S(1)}, bf16[3,33088]{1,0:T(4,128)(2,1)S(1)}, u32[]{:S(2)}, u32[]{:S(2)}) collective-permute-start(bf16[3,33088]{1,0:T(4,128)(2,1)S(1)} %convert_element_type.498), channel_id=1, source_target_pairs={{0,4},{4,8},{8,12},{12,16},{16,20},{20,24},{24,28},{1,5},{5,9},{9,... | collective-permute-start | bytes 595592 | tf_op jit(solution)/shard_map/while/body/eval_jaxpr/ppermute | solution.py:21
  371.8 8.2 collective-permute-start.1
  383.4 42.2 %collective-permute-start.1 = (bf16[3,33088]{1,0:T(4,128)(2,1)S(1)}, bf16[3,33088]{1,0:T(4,128)(2,1)S(1)}, u32[]{:S(2)}, u32[]{:S(2)}) collective-permute-start(bf16[3,33088]{1,0:T(4,128)(2,1)S(1)} %convert_element_type.498), channel_id=1, source_target_pairs={{0,4},{4,8},{8,12},{12,16},{16,20},{20,24},{24,28},{1,5},{5,9},{9,... | collective-permute-start | bytes 595592 | tf_op jit(solution)/shard_map/while/body/eval_jaxpr/ppermute | solution.py:21
  429.2 8.2 collective-permute-start.1
  440.9 44.3 %collective-permute-start.1 = (bf16[3,33088]{1,0:T(4,128)(2,1)S(1)}, bf16[3,33088]{1,0:T(4,128)(2,1)S(1)}, u32[]{:S(2)}, u32[]{:S(2)}) collective-permute-start(bf16[3,33088]{1,0:T(4,128)(2,1)S(1)} %convert_element_type.498), channel_id=1, source_target_pairs={{0,4},{4,8},{8,12},{12,16},{16,20},{20,24},{24,28},{1,5},{5,9},{9,... | collective-permute-start | bytes 595592 | tf_op jit(solution)/shard_map/while/body/eval_jaxpr/ppermute | solution.py:21
  487.0 15.0 copy-start.54
  487.1 15.0 copy-start.61
  487.1 14.5 all-to-all-start.4
  490.6 168.7 %reduce-scatter.5.cloned.1.call-start = ((), (), s32[]{:S(2)}) async-start(), calls=%async_computation.13 | async-start | bytes 983040 | tf_op jit(solution)/shard_map/reduce_scatter | solution.py:302
  504.5 9.7 copy-start.28
  504.5 9.7 copy-start.18
  505.3 9.4 copy-start.17
  520.2 165.5 %reduce-scatter.3.cloned.1.call-start = ((), (), s32[]{:S(2)}) async-start(), calls=%async_computation.12 | async-start | bytes 983040 | tf_op jit(solution)/shard_map/reduce_scatter | solution.py:286
  525.9 159.9 %copy-start.35 = (bf16[1,128,768]{2,1,0:T(8,128)(2,1)S(1)}, bf16[1,128,768]{2,1,0:T(8,128)(2,1)}, u32[]{:S(2)}) copy-start(bf16[1,128,768]{2,1,0:T(8,128)(2,1)} %param.57) | copy-start | bytes 589828
  691.1 6.6 copy-start.34
  691.1 6.6 copy-start.62
  694.3 8.7 all-to-all-start.5
  697.6 1995.9 %all-reduce.13.cloned.1.call-start = ((), (), s32[]{:S(2)}) async-start(), calls=%async_computation.15 | async-start | bytes 5308416 | tf_op jit(solution)/shard_map/psum | solution.py:461
  711.3 9.8 collective-permute-start
  726.5 9.5 collective-permute-start
  741.4 8.9 collective-permute-start
  755.7 9.2 collective-permute-start
  770.3 9.2 collective-permute-start
  784.9 9.2 collective-permute-start
  799.5 1091.5 %collective-permute-start = (bf16[3,33088]{1,0:T(4,128)(2,1)S(1)}, bf16[3,33088]{1,0:T(4,128)(2,1)S(1)}, u32[]{:S(2)}, u32[]{:S(2)}) collective-permute-start(bf16[3,33088]{1,0:T(4,128)(2,1)S(1)} %get-tuple-element.2931), channel_id=1, source_target_pairs={{4,0},{8,4},{12,8},{16,12},{20,16},{24,20},{28,24},{5,1},{9,5},{13... | collective-permute-start | bytes 595592 | tf_op jit(solution)/shard_map/while/body/eval_jaxpr/ppermute | solution.py:21
  2052.1 9.2 collective-permute-start
  2222.5 9.2 collective-permute-start
  2392.8 9.2 collective-permute-start
  2563.1 8.3 collective-permute-start
  2575.0 6.4 copy-start.5
  2575.0 6.4 copy-start.26
  2575.0 6.4 copy-start.40
  2575.0 6.4 copy-start.47
  2577.6 5.8 copy-start.13
  2577.6 9.1 all-to-all-start.6
  2586.7 8.7 all-to-all-start.7
  2595.3 8.7 all-to-all-start.8
  2598.7 328.5 %all-reduce.11.cloned.1.call-start = ((), (), s32[]{:S(2)}) async-start(), calls=%async_computation.14 | async-start | bytes 23592960 | tf_op jit(solution)/shard_map/psum | solution.py:441
  2606.0 7.8 slice-start.1
  2606.0 7.8 slice-start.2
  2606.0 36.7 %copy-start.7 = (bf16[768,768]{1,0:T(8,128)(2,1)S(1)}, bf16[768,768]{1,0:T(8,128)(2,1)}, u32[]{:S(2)}) copy-start(bf16[768,768]{1,0:T(8,128)(2,1)} %param.38) | copy-start | bytes 3538948
  2606.0 37.2 %copy-start.9 = (bf16[768,768]{1,0:T(8,128)(2,1)S(1)}, bf16[768,768]{1,0:T(8,128)(2,1)}, u32[]{:S(2)}) copy-start(bf16[768,768]{1,0:T(8,128)(2,1)} %param.39) | copy-start | bytes 3538948
  2607.5 33.0 %all-to-all-start.9 = ((bf16[4,128,3]{1,2,0:T(4,128)(2,1)}), bf16[4,128,3]{1,2,0:T(4,128)(2,1)}, u32[]{:S(2)}, u32[]{:S(2)}) async-start(bf16[4,128,3]{1,2,0:T(4,128)(2,1)} %copy.291), calls=%async_computation.11 | async-start | bytes 8192 | tf_op jit(solution)/shard_map/all_to_all | solution.py:410
  2644.7 42.1 %copy-start.59 = (f32[128]{0:T(128)S(1)}, f32[128]{0:T(128)}, u32[]{:S(2)}) copy-start(f32[128]{0:T(128)} %copy-done.58) | copy-start | bytes 1540
  2693.6 5.9 copy-start.32
  (47 other events, 94.6 us)
Sparse Core Ops, SparseCore 0:
  520.4 138.8 reduce-scatter.4
  662.5 23.2 reduce-scatter.2
  2575.0 118.5 all-reduce.12
  2701.0 226.1 all-reduce.10
where the time goes:
time: 2960 us; the launch traced here: 2950 us
  waiting for transfers between devices  1530 us (52%)
  matrix products  473 us (16%)
  local copies, waits for them, and re-layouts  294 us (10%)
  other arithmetic  294 us (10%)
  starting transfers between devices  238 us (8%)
  blocking collectives  81.2 us (3%)
    ppermute x22, waiting for transfers between devices, passed_along(): return lax.ppermute(array, axis, pairs)  1130 us
    dot_general x1504, matrix products, product(): return jnp.einsum(spec, left, right, precision=lax.Precision.HIGHEST)  435 us
    psum x1, waiting for transfers between devices, on_device(): lax.psum((norm_gain_grad, query_weight_grad, key_weight_grad, value_weigh...  225 us
    ppermute x22, starting transfers between devices, passed_along(): return lax.ppermute(array, axis, pairs)  202 us
    reduce_scatter x1, waiting for transfers between devices, on_device(): lax.psum_scatter(input_part.astype(jnp.bfloat16), 'tp', scatter_dimension...  132 us
    add_any x64, other arithmetic, inner_group(): state, outputs = lax.scan(stepper, state, pieces)  75.6 us
    squeeze x224, local copies, waits for them, and re-layouts, inner_group(): state, outputs = lax.scan(stepper, state, pieces)  62.3 us

commit v1 on v0

v1 whole, which is shorter than its diff:
```python
from functools import partial

import jax
import jax.numpy as jnp
from jax import lax
from jax.sharding import PartitionSpec as P
from jax.experimental import pallas as pl
from jax.experimental.pallas import tpu as pltpu
C0=0.7978845608028654;C1=0.044715
EPS=1e-6
B=16
CH=128
LOW=jnp.bfloat16
F=jnp.float32
def nn(a,b): return lax.dot_general(a.astype(LOW),b.astype(LOW),(((1,),(0,)),((),())),preferred_element_type=F)
def nt(a,b): return lax.dot_general(a.astype(LOW),b.astype(LOW),(((1,),(1,)),((),())),preferred_element_type=F)
def tn(a,b): return lax.dot_general(a.astype(LOW),b.astype(LOW),(((0,),(0,)),((),())),preferred_element_type=F)
def mean(x): return jnp.sum(x,-1,keepdims=True)*(1.0/x.shape[-1])
def gelu2(z):
    z2=z*z
    t=jnp.tanh(z*(C0+(C0*C1)*z2))
    h=0.5+0.5*t
    x=z*h
    g1=h+x*(1-t)*(C0+(3*C0*C1)*z2)
    return x,g1
def gelu1(z):
    z2=z*z
    return z*(0.5+0.5*jnp.tanh(z*(C0+(C0*C1)*z2)))
def iotas():
    r=lax.broadcasted_iota(jnp.int32,(CH,CH),0); c=lax.broadcasted_iota(jnp.int32,(CH,CH),1)
    return r,c

def fwd_kernel(C,q_ref,k_ref,v_ref,r_ref,w1_ref,b1_ref,u_ref,b2_ref,gam_ref,bet_ref,
               o_ref,z1_ref,p_ref,zc_ref,z1q_ref,zq_ref,us_ref,w1s_ref,
               W1,B1,U,B2,S1,S2,X2,KK,BASE,T):
    @pl.when(pl.program_id(0)==0)
    def _():
        W1[...]=w1_ref[...]; B1[...]=b1_ref[...]; U[...]=u_ref[...]; B2[...]=b2_ref[...]
        S1[...]=jnp.zeros_like(S1)
    H=64
    ri,ci=iotas()
    blk=(ci//B)<(ri//B)
    tri=ci<=ri
    K=[k_ref[:,H*c:H*c+H] for c in range(C)]
    Q=[q_ref[:,H*c:H*c+H] for c in range(C)]
    gam=[gam_ref[c] for c in range(C)]; bet=[bet_ref[c] for c in range(C)]
    R=[r_ref[:,c:c+1] for c in range(C)]
    w1b=[W1[c].astype(LOW) for c in range(C)]
    b1=[B1[c] for c in range(C)]
    u0=[U[c].astype(LOW) for c in range(C)]
    b20=[B2[c] for c in range(C)]
    g2=[gam[c]*gam[c] for c in range(C)]
    g2m=[mean(g2[c]) for c in range(C)]
    for c in range(C):
        w1s_ref[0,c]=w1b[c]
        KK[c]=jnp.where(blk,nt(K[c],K[c])+1.0,0.0).astype(LOW)
        BASE[c]=nn(K[c],w1b[c])+b1[c]
        T[c]=(bet[c]+K[c].astype(F)-v_ref[:,H*c:H*c+H].astype(F))*gam[c]
    ub=list(u0); uf=[U[c] for c in range(C)]; b2=list(b20)
    for j in range(CH//B):
        sl=slice(B*j,B*j+B)
        for c in range(C):
            z1=BASE[c,sl]
            if j>0: z1=z1-nn(KK[c,sl],S1[c])
            x2,g1=gelu2(z1)
            x2b=x2.astype(LOW)
            zc=nt(x2b,ub[c])+b2[c]
            mu=mean(zc); zz=zc*zc; t=T[c,sl]
            var=mean(zz)-mu*mu
            s=lax.rsqrt(var+EPS)
            zc=zc-mu
            y=zc*s
            G=y*g2[c]+t
            m1=mean(G); m2=mean(G*y)
            d2=s*(G-m1-y*m2)
            P=nn(d2,ub[c])
            rr=R[c][sl]
            s1=P*(g1*rr)
            s2=d2*rr
            s2b=s2.astype(LOW)
            S1[c,sl]=s1.astype(LOW); S2[c,sl]=s2b; X2[c,sl]=x2b
            z1_ref[c,sl]=z1; p_ref[c,sl]=P; zc_ref[c,sl]=zc
            us_ref[0,c,j]=ub[c]
            uf[c]=uf[c]-tn(s2b,x2b); ub[c]=uf[c].astype(LOW)
            b2[c]=b2[c]-jnp.sum(s2,0,keepdims=True)
    for c in range(C):
        U[c]=uf[c]; B2[c]=b2[c]
        W1[c]=W1[c]-tn(K[c],S1[c])
        B1[c]=B1[c]-jnp.sum(S1[c].astype(F),0,keepdims=True)
        A1=jnp.where(tri,nt(Q[c],K[c])+1.0,0.0)
        z1q=nn(Q[c],w1b[c])+b1[c]-nn(A1,S1[c])
        x2q=gelu1(z1q).astype(LOW)
        A2=jnp.where(tri,nt(x2q,X2[c])+1.0,0.0)
        zq=nt(x2q,u0[c])+b20[c]-nn(A2,S2[c])
        zq=zq-mean(zq)
        yq=zq*lax.rsqrt(mean(zq*zq)+EPS)
        o_ref[:,H*c:H*c+H]=(Q[c].astype(F)+yq*gam[c]+bet[c]).astype(LOW)
        z1q_ref[c]=z1q; zq_ref[c]=zq

def fwd_scan(q,k,v,r,w1,b1,u,b2,gam,bet):
    L=q.shape[0]; C=w1.shape[0]; I=w1.shape[2]; H=w1.shape[1]; n=L//CH
    row=lambda w,dt=None: pl.BlockSpec((CH,w),lambda i:(i,0))
    full=lambda *s: pl.BlockSpec(s,lambda i:(0,)*len(s))
    big=lambda w: pl.BlockSpec((C,CH,w),lambda i:(0,i,0))
    sd=jax.ShapeDtypeStruct
    return pl.pallas_call(partial(fwd_kernel,C),grid=(n,),
        in_specs=[row(C*H)]*3+[row(C),full(C,H,I),full(C,1,I),full(C,H,I),full(C,1,H),full(C,1,H),full(C,1,H)],
        out_specs=[row(C*H),big(I),big(I),big(H),big(I),big(H),pl.BlockSpec((1,C,CH//B,H,I),lambda i:(i,0,0,0,0)),pl.BlockSpec((1,C,H,I),lambda i:(i,0,0,0))],
        out_shape=[sd((L,C*H),LOW),sd((C,L,I),F),sd((C,L,I),F),sd((C,L,H),F),sd((C,L,I),F),sd((C,L,H),F),sd((n,C,CH//B,H,I),LOW),sd((n,C,H,I),LOW)],
        scratch_shapes=[pltpu.VMEM((C,H,I),F),pltpu.VMEM((C,1,I),F),pltpu.VMEM((C,H,I),F),pltpu.VMEM((C,1,H),F),
            pltpu.VMEM((C,CH,I),LOW),pltpu.VMEM((C,CH,H),LOW),pltpu.VMEM((C,CH,I),LOW),pltpu.VMEM((C,CH,CH),LOW),pltpu.VMEM((C,CH,I),F),pltpu.VMEM((C,CH,H),F)],
        compiler_params=pltpu.CompilerParams(vmem_limit_bytes=48*1024*1024),
    )(q,k,v,r,w1,b1,u,b2,gam,bet)

def gelu3(z):
    z2=z*z
    t=jnp.tanh(z*(C0+(C0*C1)*z2))
    u1=C0+(3*C0*C1)*z2
    h=0.5+0.5*t
    h1=h*(1-t)*u1
    x=z*h
    g1=h+z*h1
    g2=2*h1+z*(h*(1-t)*(6*C0*C1)*z-2*t*u1*h1)
    return x,g1,g2

def bwd_kernel(C,n,q_ref,k_ref,v_ref,r_ref,do_ref,z1_ref,p_ref,zc_ref,z1q_ref,zq_ref,us_ref,w1s_ref,gam_ref,bet_ref,
               dq_ref,dk_ref,dv_ref,dr_ref,H1,h1,HU,h2,dgam_ref,dbet_ref,
               BASE,DX2,X2,RG1,RPG2,DS2Q,KK,DZ1,DS1,DS2,DG,YB,GB,DB,SB,S2B,G1):
    @pl.when(pl.program_id(0)==0)
    def _():
        for ref in (H1,h1,HU,h2,dgam_ref,dbet_ref,DZ1): ref[...]=jnp.zeros_like(ref)
    H=64
    ri,ci=iotas()
    blk=(ci//B)<(ri//B)
    blkT=(ci//B)>(ri//B)
    tri=ci<=ri
    K=[k_ref[:,H*c:H*c+H] for c in range(C)]
    Q=[q_ref[:,H*c:H*c+H] for c in range(C)]
    gam=[gam_ref[c] for c in range(C)]; bet=[bet_ref[c] for c in range(C)]
    R=[r_ref[:,c:c+1] for c in range(C)]
    g2=[gam[c]*gam[c] for c in range(C)]
    hu=[HU[c] for c in range(C)]; hh2=[h2[c] for c in range(C)]
    keep=[]
    for c in range(C):
        dO=do_ref[:,H*c:H*c+H].astype(F)
        x2q,g1q=gelu2(z1q_ref[c]); x2q=x2q.astype(LOW)
        zq=zq_ref[c]; sq=lax.rsqrt(mean(zq*zq)+EPS); yq=zq*sq
        x2,g1,gg2=gelu3(z1_ref[c]); x2=x2.astype(LOW)
        X2[c]=x2
        P=p_ref[c]
        r=R[c]
        RG1[c]=r*g1; G1[c]=g1
        RPG2[c]=r*(P*gg2)
        s1=(P*g1*r).astype(LOW)
        zc=zc_ref[c]
        s=lax.rsqrt(mean(zc*zc)+EPS)
        y=zc*s
        t0=bet[c]+K[c].astype(F)-v_ref[:,H*c:H*c+H].astype(F)
        G=y*g2[c]+t0*gam[c]
        m1=mean(G); m2=mean(G*y)
        d2=s*(G-m1-y*m2)
        s2=(d2*r).astype(LOW)
        YB[c]=y; GB[c]=G; DB[c]=d2; S2B[c]=s2
        SB[c,:,0:1]=s; SB[c,:,1:2]=m2
        u0=us_ref[0,c,0]
        w1=w1s_ref[0,c]
        dgam_ref[c]=dgam_ref[c]+jnp.sum(dO*yq,0,keepdims=True)
        dbet_ref[c]=dbet_ref[c]+jnp.sum(dO,0,keepdims=True)
        dyq=dO*gam[c]
        dzq=sq*(dyq-mean(dyq)-yq*mean(dyq*yq))
        dzqb=dzq.astype(LOW)
        A2=jnp.where(tri,nt(x2q,x2)+1.0,0.0)
        dA2=jnp.where(tri,nt(dzqb,s2),0.0).astype(LOW)
        dx2q=nn(dzqb,u0)-nn(dA2,x2)
        DX2[c]=-tn(dA2,x2q)
        DS2Q[c]=-tn(A2,dzqb)
        dz1q=dx2q*g1q
        dz1qb=dz1q.astype(LOW)
        A1=jnp.where(tri,nt(Q[c],K[c])+1.0,0.0)
        dA1=jnp.where(tri,nt(dz1qb,s1),0.0).astype(LOW)
        dq_ref[:,H*c:H*c+H]=(dO+nt(dz1qb,w1)-nn(dA1,K[c])).astype(LOW)
        h1b=H1[c].astype(LOW)
        dk=nt(s1,h1b)+tn(dA1,Q[c])
        KK[c]=jnp.where(blkT,nt(K[c],K[c])+1.0,0.0).astype(LOW)
        BASE[c]=-tn(A1,dz1qb)-nn(K[c],h1b)-h1[c]
        h1n=h1[c]+jnp.sum(dz1q,0,keepdims=True)
        H1n=H1[c]+tn(Q[c],dz1qb)
        keep.append((s1,t0,dzqb,x2q,dk,H1n,h1n,w1,P*g1))
    for j in reversed(range(CH//B)):
        sl=slice(B*j,B*j+B)
        for c in range(C):
            ub=us_ref[0,c,j]
            rr=R[c][sl]
            hub=hu[c].astype(LOW)
            ds1=BASE[c,sl]
            if j<CH//B-1: ds1=ds1-nn(KK[c,sl],DZ1[c])
            x2=X2[c,sl]
            ds2=DS2Q[c,sl]-nt(x2,hub)-hh2[c]
            dx2=DX2[c,sl]-nn(S2B[c,sl],hub)
            dP=ds1*RG1[c,sl]
            dPb=dP.astype(LOW)
            e=rr*ds2+nt(dPb,ub)
            s=SB[c,sl,0:1]; m2=SB[c,sl,1:2]; y=YB[c,sl]; g_=GB[c,sl]; d2=DB[c,sl]
            a=mean(e); b=mean(e*y); cc=mean(e*d2)
            dG=s*(e-a-y*b)
            dY=g2[c]*dG-s*(m2*e+g_*b)
            dZc=s*(dY-mean(dY)-y*(cc+mean(dY*y)))
            dZcb=dZc.astype(LOW)
            dx2=dx2+nn(dZcb,ub)
            dz1=dx2*G1[c,sl]+ds1*RPG2[c,sl]
            DZ1[c,sl]=dz1.astype(LOW)
            DS1[c,sl]=ds1; DS2[c,sl]=ds2; DG[c,sl]=dG
            hu[c]=hu[c]+tn(jnp.concatenate([d2.astype(LOW),dZcb],0),jnp.concatenate([dPb,x2],0))
            hh2[c]=hh2[c]+jnp.sum(dZc,0,keepdims=True)
    for c in range(C):
        s1,t0,dzqb,x2q,dk,H1n,h1n,w1,D1=keep[c]
        dz1=DZ1[c]
        M=jnp.where(blk,nt(dz1,s1),0.0).astype(LOW)
        dG=DG[c]; dGg=dG*gam[c]
        dk=-dk-nn(M,K[c])-tn(M,K[c])+nt(dz1,w1)+dGg
        dk_ref[:,H*c:H*c+H]=dk.astype(LOW)
        dv_ref[:,H*c:H*c+H]=(-dGg).astype(LOW)
        dr_ref[:,c:c+1]=jnp.sum(DS1[c]*D1,-1,keepdims=True)+jnp.sum(DS2[c]*DB[c],-1,keepdims=True)
        dgam_ref[c]=dgam_ref[c]+jnp.sum(dG*(2*YB[c]*gam[c]+t0),0,keepdims=True)
        dbet_ref[c]=dbet_ref[c]+jnp.sum(dGg,0,keepdims=True)
        H1[c]=H1n+tn(K[c],dz1)
        h1[c]=h1n+jnp.sum(dz1.astype(F),0,keepdims=True)
        HU[c]=hu[c]+tn(dzqb,x2q)
        h2[c]=hh2[c]+jnp.sum(dzqb.astype(F),0,keepdims=True)

def bwd_scan(q,k,v,r,do,z1,p,zc,z1q,zq,us,w1s,gam,bet):
    L=q.shape[0]; C,_,I=z1.shape; H=zc.shape[2]; n=L//CH
    row=lambda w,dt=None: pl.BlockSpec((CH,w),lambda i:(n-1-i,0))
    full=lambda *s: pl.BlockSpec(s,lambda i:(0,)*len(s))
    big=lambda w: pl.BlockSpec((C,CH,w),lambda i:(0,n-1-i,0))
    sd=jax.ShapeDtypeStruct
    V=pltpu.VMEM
    return pl.pallas_call(partial(bwd_kernel,C,n),grid=(n,),
        in_specs=[row(C*H)]*3+[row(C),row(C*H),big(I),big(I),big(H),big(I),big(H),pl.BlockSpec((1,C,CH//B,H,I),lambda i:(n-1-i,0,0,0,0)),pl.BlockSpec((1,C,H,I),lambda i:(n-1-i,0,0,0)),full(C,1,H),full(C,1,H)],
        out_specs=[row(C*H)]*3+[row(C),full(C,H,I),full(C,1,I),full(C,H,I),full(C,1,H),full(C,1,H),full(C,1,H)],
        out_shape=[sd((L,C*H),LOW)]*3+[sd((L,C),F),sd((C,H,I),F),sd((C,1,I),F),sd((C,H,I),F),sd((C,1,H),F),sd((C,1,H),F),sd((C,1,H),F)],
        scratch_shapes=[V((C,CH,I),F),V((C,CH,I),F),V((C,CH,I),LOW),V((C,CH,I),F),V((C,CH,I),F),V((C,CH,H),F),V((C,CH,CH),LOW),V((C,CH,I),LOW),V((C,CH,I),F),V((C,CH,H),F),V((C,CH,H),F),
            V((C,CH,H),F),V((C,CH,H),F),V((C,CH,H),F),V((C,CH,2),F),V((C,CH,H),LOW),V((C,CH,I),F)],
        compiler_params=pltpu.CompilerParams(vmem_limit_bytes=48*1024*1024),
    )(q,k,v,r,do,z1,p,zc,z1q,zq,us,w1s,gam,bet)

RATE_SCALE = 0.25
NORM_EPS = 1e-05


def smooth_act(value):
    return 0.5 * value * (1.0 + jnp.tanh(C0 * (value + C1 * value * value * value)))


def root_norm(value, gain):
    return value * lax.rsqrt(jnp.mean(value * value, -1, keepdims=True) + NORM_EPS) * gain


def layer_norm(value, gain, bias):
    centre = value - jnp.mean(value, -1, keepdims=True)
    return centre * lax.rsqrt(jnp.mean(centre * centre, -1, keepdims=True) + NORM_EPS) * gain + bias


def gated_branch(mixed, gate_pre, gain, bias):
    return layer_norm(mixed, gain, bias) * smooth_act(gate_pre)


def swish_product(gate_val, linear_val):
    return jax.nn.silu(gate_val) * linear_val


def matmul(left, right):
    return jnp.dot(left, right, preferred_element_type=F)


def on_device(
    tokens, norm_gain, query_weight, key_weight, value_weight, rate_weight, rate_bias,
    first_weight, first_bias, second_weight, second_bias, inner_gain, inner_bias,
    branch_gate, output_weight, post_gain, post_bias, feed_gain, feed_gate, feed_linear,
    feed_down, cotangent,
):
    seqs = lax.axis_size("seq")
    rank = lax.axis_index("seq")
    heads = rate_weight.shape[1]
    local_heads, head, inner = first_weight.shape
    rows = tokens.shape[1]
    width = tokens.shape[2]
    each = -(-heads // seqs)
    span = each * head
    length = seqs * rows
    extra = -(-each // 16) * 16

    def to_chains(array):
        padded = jnp.pad(array, ((0, 0), (0, seqs * span - array.shape[1])))
        return padded.reshape(rows, seqs, span).transpose(1, 0, 2)

    def from_chains(array):
        return array.transpose(1, 0, 2).reshape(rows, seqs * span)[:, :width]

    def swap(array):
        return lax.all_to_all(array, "seq", split_axis=0, concat_axis=0, tiled=True)

    first_pack = jnp.concatenate([first_weight, first_bias[:, None, :]], 1)
    centred = jnp.swapaxes(second_weight, 1, 2)
    centred = centred - jnp.mean(centred, 1, keepdims=True)
    tail = jnp.concatenate(
        [
            second_bias - jnp.mean(second_bias, -1, keepdims=True),
            inner_gain,
            inner_bias,
            jnp.pad(rate_bias[:, None], ((0, 0), (0, inner - 3 * head - 1))),
        ],
        -1,
    )
    second_pack = jnp.concatenate([centred, tail[:, None, :]], 1)
    packed = jnp.pad(jnp.stack([first_pack, second_pack], 1), ((0, 0), (0, 0), (0, 7), (0, 0)))
    every = lax.all_gather(packed, "tp", axis=0, tiled=True)
    own = jnp.stack(
        [
            lax.dynamic_index_in_dim(every, jnp.minimum(rank * each + c, heads - 1), 0, keepdims=False)
            for c in range(each)
        ]
    )
    chain_first = own[:, 0, :head]
    chain_first_bias = own[:, 0, head : head + 1]
    chain_second = own[:, 1, :head]
    chain_tail = own[:, 1, head : head + 1]
    chain_second_bias = chain_tail[..., :head]
    chain_gain = chain_tail[..., head : 2 * head]
    chain_shift = chain_tail[..., 2 * head : 3 * head]
    chain_rate_bias = chain_tail[:, 0, 3 * head]

    residual = tokens[0].astype(F)
    normed_val, norm_pull = jax.vjp(root_norm, residual, norm_gain)
    normed = normed_val.astype(LOW)
    query_tok = matmul(normed, query_weight).astype(LOW)
    keys_tok = matmul(normed, key_weight).astype(LOW)
    values_tok = matmul(normed, value_weight).astype(LOW)
    logits_tok = matmul(normed, rate_weight).astype(LOW)
    gate_pre = matmul(normed, branch_gate)

    logit_rows = jnp.pad(logits_tok.T, ((0, seqs * each - heads), (0, 0))).reshape(seqs, each, rows)
    logit_rows = jnp.pad(logit_rows, ((0, 0), (0, extra - each), (0, 3 * span - rows)))
    sent = jnp.concatenate(
        [jnp.concatenate([to_chains(query_tok), to_chains(keys_tok), to_chains(values_tok)], -1), logit_rows],
        1,
    )
    got = swap(sent)
    chain_qkv = got[:, :rows].reshape(length, 3 * span)
    query_c = chain_qkv[:, :span]
    keys_c = chain_qkv[:, span : 2 * span]
    values_c = chain_qkv[:, 2 * span :]
    logit_c = got[:, rows : rows + each, :rows].transpose(0, 2, 1).reshape(length, each).astype(F)
    gate_c = jax.nn.sigmoid(logit_c + chain_rate_bias)
    rate_c = gate_c * (RATE_SCALE / head)

    outs, *kept = fwd_scan(
        query_c, keys_c, values_c, rate_c, chain_first, chain_first_bias, chain_second,
        chain_second_bias, chain_gain, chain_shift,
    )
    mixed_tok = from_chains(swap(outs.reshape(seqs, rows, span))).astype(F)

    branch_val, branch_pull = jax.vjp(gated_branch, mixed_tok, gate_pre, post_gain, post_bias)
    branch_in = branch_val.astype(LOW)
    middle = residual + matmul(branch_in, output_weight)
    feed_val, feed_pull = jax.vjp(root_norm, middle, feed_gain)
    feed_in = feed_val.astype(LOW)
    down_grad = cotangent[0]
    grad_out = down_grad.astype(F)
    every_grad = lax.all_gather(down_grad, "tp", axis=0, tiled=True)
    every_in = lax.all_gather(feed_in, "tp", axis=0, tiled=True)
    gate_val = matmul(every_in, feed_gate)
    linear_val = matmul(every_in, feed_linear)
    act_val, act_pull = jax.vjp(swish_product, gate_val, linear_val)
    hidden = act_val.astype(LOW)

    def sum_over_tp(array):
        parts = array.astype(LOW).reshape(lax.axis_size("tp"), rows, width)
        parts = lax.all_to_all(parts, "tp", split_axis=0, concat_axis=0, tiled=True)
        return jnp.sum(parts.astype(F), 0)

    hidden_grad = jnp.einsum("td,fd->tf", every_grad, feed_down, preferred_element_type=F)
    gate_grad, linear_grad = act_pull(hidden_grad)
    gate_low = gate_grad.astype(LOW)
    linear_low = linear_grad.astype(LOW)
    input_part = jnp.einsum("tf,df->td", gate_low, feed_gate, preferred_element_type=F) + jnp.einsum(
        "tf,df->td", linear_low, feed_linear, preferred_element_type=F
    )
    feed_in_grad = sum_over_tp(input_part)
    middle_part, feed_gain_grad = feed_pull(feed_in_grad)
    middle_grad = grad_out + middle_part
    out_low = middle_grad.astype(LOW)
    branch_grad = jnp.einsum("te,de->td", out_low, output_weight, preferred_element_type=F)
    mixed_grad, gate_pre_grad, post_gain_grad, post_bias_grad = branch_pull(branch_grad)
    out_grad_c = swap(to_chains(mixed_grad.astype(LOW))).reshape(length, span)

    second_out = sum_over_tp(matmul(hidden, feed_down))
    result = (middle + second_out).astype(LOW)[None]

    feed_down_grad = jnp.einsum("tf,td->fd", hidden, every_grad, preferred_element_type=F)
    feed_gate_grad = jnp.einsum("td,tf->df", every_in, gate_low, preferred_element_type=F)
    feed_linear_grad = jnp.einsum("td,tf->df", every_in, linear_low, preferred_element_type=F)
    output_weight_grad = jnp.einsum("td,te->de", branch_in, out_low, preferred_element_type=F)
    gate_low_pre = gate_pre_grad.astype(LOW)
    branch_gate_grad = jnp.einsum("td,te->de", normed, gate_low_pre, preferred_element_type=F)
    fed = [
        array.astype(F)
        for array in lax.psum(
            (feed_gate_grad.astype(LOW), feed_linear_grad.astype(LOW), feed_down_grad.astype(LOW)), "seq"
        )
    ]
    early = [
        array.astype(F)
        for array in lax.psum((output_weight_grad.astype(LOW), branch_gate_grad.astype(LOW)), ("seq", "tp"))
    ]

    (
        query_g, keys_g, values_g, rate_g, first_g, first_bias_g, second_g, second_bias_g, gain_g, shift_g,
    ) = bwd_scan(query_c, keys_c, values_c, rate_c, out_grad_c, *kept, chain_gain, chain_shift)
    logit_g = rate_g * (RATE_SCALE / head) * gate_c * (1.0 - gate_c)
    second_g = second_g - jnp.mean(second_g, 1, keepdims=True)
    second_bias_g = second_bias_g - jnp.mean(second_bias_g, -1, keepdims=True)
    bias_g = jnp.sum(logit_g, 0)

    logit_back = logit_g.astype(LOW).reshape(seqs, rows, each).transpose(0, 2, 1)
    logit_back = jnp.pad(logit_back, ((0, 0), (0, extra - each), (0, 3 * span - rows)))
    qkv_back = jnp.concatenate([query_g, keys_g, values_g], -1).reshape(seqs, rows, 3 * span)
    back = swap(jnp.concatenate([qkv_back, logit_back], 1))
    query_low = from_chains(back[:, :rows, :span])
    keys_low = from_chains(back[:, :rows, span : 2 * span])
    values_low = from_chains(back[:, :rows, 2 * span :])
    logit_low = back[:, rows : rows + each, :rows].reshape(seqs * each, rows)[:heads].T

    query_weight_grad = jnp.einsum("td,te->de", normed, query_low, preferred_element_type=F)
    key_weight_grad = jnp.einsum("td,te->de", normed, keys_low, preferred_element_type=F)
    value_weight_grad = jnp.einsum("td,te->de", normed, values_low, preferred_element_type=F)
    rate_weight_grad = jnp.einsum("td,te->de", normed, logit_low, preferred_element_type=F)
    late_in = (query_weight_grad.astype(LOW), key_weight_grad.astype(LOW), value_weight_grad.astype(LOW))
    late_in, early = lax.optimization_barrier((late_in, early))
    late = [array.astype(F) for array in lax.psum(late_in, ("seq", "tp"))]
    normed_grad = (
        jnp.einsum("te,de->td", query_low, query_weight, preferred_element_type=F)
        + jnp.einsum("te,de->td", keys_low, key_weight, preferred_element_type=F)
        + jnp.einsum("te,de->td", values_low, value_weight, preferred_element_type=F)
        + jnp.einsum("te,de->td", logit_low, rate_weight, preferred_element_type=F)
        + jnp.einsum("te,de->td", gate_low_pre, branch_gate, preferred_element_type=F)
    )
    residual_part, norm_gain_grad = norm_pull(normed_grad)
    tokens_grad = (middle_grad + residual_part)[None]
    small = lax.psum(
        (norm_gain_grad, rate_weight_grad, post_gain_grad, post_bias_grad, feed_gain_grad), ("seq", "tp")
    )

    tail_g = jnp.concatenate(
        [
            second_bias_g[:, 0],
            gain_g[:, 0],
            shift_g[:, 0],
            jnp.pad(bias_g[:, None], ((0, 0), (0, inner - 3 * head - 1))),
        ],
        -1,
    )
    chain_g = jnp.stack(
        [
            jnp.concatenate([first_g, first_bias_g], 1),
            jnp.concatenate([second_g, tail_g[:, None, :]], 1),
        ],
        1,
    )
    chain_g = jnp.pad(chain_g, ((0, 0), (0, 0), (0, 7), (0, 0))).astype(LOW)
    all_g = lax.all_gather(chain_g, "seq", axis=0, tiled=True)[:heads]
    head_g = lax.psum_scatter(all_g, "tp", scatter_dimension=0, tiled=True).astype(F)
    tail_sum = head_g[:, 1, head]
    return (
        result,
        tokens_grad,
        small[0],
        late[0],
        late[1],
        late[2],
        small[1],
        tail_sum[:, 3 * head],
        head_g[:, 0, :head],
        head_g[:, 0, head],
        jnp.swapaxes(head_g[:, 1, :head], 1, 2),
        tail_sum[:, :head],
        tail_sum[:, head : 2 * head],
        tail_sum[:, 2 * head : 3 * head],
        early[1],
        early[0],
        small[2],
        small[3],
        small[4],
        fed[0],
        fed[1],
        fed[2],
    )


def solution(mesh):
    in_specs = (
        P("tp", "seq", None),
        P(),
        P(),
        P(),
        P(),
        P(),
        P("tp"),
        P("tp", None, None),
        P("tp", None),
        P("tp", None, None),
        P("tp", None),
        P("tp", None),
        P("tp", None),
        P(),
        P(),
        P(),
        P(),
        P(),
        P(None, "tp"),
        P(None, "tp"),
        P("tp", None),
        P("tp", "seq", None),
    )
    out_specs = (
        P("tp", "seq", None),
        P("tp", "seq", None),
        P(),
        P(),
        P(),
        P(),
        P(),
        P("tp"),
        P("tp", None, None),
        P("tp", None),
        P("tp", None, None),
        P("tp", None),
        P("tp", None),
        P("tp", None),
        P(),
        P(),
        P(),
        P(),
        P(),
        P(None, "tp"),
        P(None, "tp"),
        P("tp", None),
    )
    return jax.shard_map(
        on_device, mesh=mesh, in_specs=in_specs, out_specs=out_specs, check_vma=False
    )
```

time: 2960 us -> 697 us (0.24)
  waiting for transfers between devices: 1530 us -> 350 us
  matrix products: 473 us -> 32.5 us
  local copies, waits for them, and re-layouts: 294 us -> 23.9 us
  other arithmetic: 294 us -> 36.7 us
  starting transfers between devices: 238 us -> 24 us
  Pallas kernels: 0 us -> 137 us
    ppermute x22 -> x0, waiting for transfers between devices: 1130 us -> none  [passed_along(): return lax.ppermute(array, axis, pairs)]
    dot_general x1531 -> x27, matrix products: 473 us -> 32.5 us  [the longest x9 9.44 us: matmul(): return jnp.dot(left, right, preferred_element_type=F)]
    ppermute x22 -> x0, starting transfers between devices: 202 us -> none  [passed_along(): return lax.ppermute(array, axis, pairs)]
    reduce_scatter x2 -> x0, waiting for transfers between devices: 157 us -> none  [the longest x1 132 us: on_device(): lax.psum_scatter(input_part.astype(jnp.bfloat16), 'tp', scatter_dimension...]
    pallas_call x0 -> x2, Pallas kernels: none -> 137 us  [the longest x1 70.3 us: fwd_scan(): pl.pallas_call(partial(fwd_kernel, C), grid=(n,), in_specs=[row(C * H)] *...]
    dynamic_update_slice x227 -> x0, local copies, waits for them, and re-layouts: 81.2 us -> none  [the longest x128 45.4 us: inner_group(): state, outputs = lax.scan(stepper, state, pieces)]
    add_any x132 -> x0, other arithmetic: 80 us -> none  [the longest x64 75.6 us: inner_group(): state, outputs = lax.scan(stepper, state, pieces)]
    reduce_sum x516 -> x7, other arithmetic: 79.1 us -> 4.8 us  [the longest x2 2.68 us: sum_over_tp(): return jnp.sum(parts.astype(F), 0)]
where the time goes in v1:
time: 697 us; the launch traced here: 696 us
  waiting for transfers between devices  350 us (50%)
  Pallas kernels  137 us (20%)
  blocking collectives  75.6 us (11%)
  other arithmetic  36.7 us (5%)
  matrix products  32.5 us (5%)
  starting transfers between devices  24 us (3%)
  local copies, waits for them, and re-layouts  23.9 us (3%)
  between operations  15.8 us (2%)
    psum x1, waiting for transfers between devices, on_device(): late = [array.astype(F) for array in lax.psum(late_in, ('seq', 'tp'))]  134 us
    psum x1, waiting for transfers between devices, on_device(): lax.psum((feed_gate_grad.astype(LOW), feed_linear_grad.astype(LOW), feed_...  109 us
    pallas_call x1, Pallas kernels, fwd_scan(): pl.pallas_call(partial(fwd_kernel, C), grid=(n,), in_specs=[row(C * H)] *...  70.3 us
    pallas_call x1, Pallas kernels, bwd_scan(): pl.pallas_call(partial(bwd_kernel, C, n), grid=(n,), in_specs=[row(C * H)...  67.1 us
    psum x1, blocking collectives, on_device(): lax.psum((norm_gain_grad, rate_weight_grad, post_gain_grad, post_bias_gra...  39.9 us
    psum x1, waiting for transfers between devices, on_device(): lax.psum((output_weight_grad.astype(LOW), branch_gate_grad.astype(LOW)),...  38.5 us
    all_gather x1, waiting for transfers between devices, on_device(): all_g = lax.all_gather(chain_g, 'seq', axis=0, tiled=True)[:heads]  29 us
    all_to_all x3, waiting for transfers between devices, swap(): return lax.all_to_all(array, 'seq', split_axis=0, concat_axis=0, tiled=True)  22.4 us
  transfers between devices with their start and end apart: 11, of which 7 were waited for; matrix products, arithmetic and copies ran while one was open for 7% of the time, Pallas kernels for 10%

profile of v1, /device:TPU:0, one launch (start us, length us, event | category | flops | bytes accessed | tf_op | source)
XLA Modules:
  0.0 695.6 jit_solution(15699489082694177106)
XLA Ops:
  8.8 0.8 reduce_sum.169
  11.1 1.0 bitcast_reduce_fusion
  12.1 0.9 bitcast_subtract_fusion
  13.1 1.1 maximum_bitcast_fusion
  14.1 0.8 select_maximum_fusion
  16.8 0.8 copy-done.25
  18.1 1.0 fusion.7
  19.2 7.3 %all-to-all-start = ((bf16[8,144,384]{2,1,0:T(8,128)(2,1)}), bf16[8,144,384]{2,1,0:T(8,128)(2,1)S(1)}, u32[]{:S(2)}, u32[]{:S(2)}) async-start(bf16[8,144,384]{2,1,0:T(8,128)(2,1)} %fusion.7), calls=%async_computation | async-start | bytes 1769472 | tf_op jit(solution)/shard_map/all_to_all | solution.py:301
  26.4 22.3 %all-to-all-done = bf16[8,144,384]{2,1,0:T(8,128)(2,1)S(1)} async-done(((bf16[8,144,384]{2,1,0:T(8,128)(2,1)}), bf16[8,144,384]{2,1,0:T(8,128)(2,1)S(1)}, u32[]{:S(2)}, u32[]{:S(2)}) %all-to-all-start) | async-done | bytes 884768 | tf_op jit(solution)/shard_map/all_to_all | solution.py:301
  49.3 1.0 constant_dynamic-slice_fusion
  51.4 70.3 %shard_map.381 = (bf16[1024,128]{1,0:T(8,128)(2,1)S(1)}, f32[2,1024,256]{2,1,0:T(8,128)}, f32[2,1024,256]{2,1,0:T(8,128)}, f32[2,1024,64]{2,1,0:T(8,128)S(1)}, f...) custom-call(bf16[1024,128]{1,0:T(8,128)(2,1)S(1)} %get-tuple-element, ...), custom_call_target="tpu_custom_call" | custom-call | tf_op jit(solution)/shard_map/pallas_call | solution.py:106
  121.7 1.0 copy-done.2
  122.7 0.8 copy-done.4
  124.2 4.0 all-to-all-start.1
  128.3 2.5 fusion.83
  130.8 9.1 %all-gather = bf16[1,512,768]{2,1,0:T(8,128)(2,1)} all-gather(bf16[1,128,768]{2,1,0:T(8,128)(2,1)S(1)} %copy-done.57), channel_id=2, replica_groups=mesh['seq'=8,'tp'=4] {'tp'}, dimensions={1}, use_global_device_ids=true | all-gather | bytes 983040 | tf_op jit(solution)/shard_map/all_gather | solution.py:370
  139.8 1.0 copy_bitcast_fusion
  141.7 1.6 multiply_reduce_fusion.2
  144.3 8.7 %all_gather.13 = bf16[512,768]{1,0:T(8,128)(2,1)S(1)} all-gather(bf16[128,768]{1,0:T(8,128)(2,1)S(1)} %multiply_convert_fusion.2), channel_id=1, replica_groups=mesh['seq'=8,'tp'=4] {'tp'}, dimensions={0}, use_global_device_ids=true | all-gather | bytes 983040 | tf_op jit(solution)/shard_map/all_gather | solution.py:371
  155.8 1.8 multiply_convert_fusion
  158.6 1.5 add_convert_fusion
  160.1 4.2 all-to-all-start.3
  164.3 2.7 convolution_convert_fusion.8
  167.1 9.0 %all-to-all-done.3 = bf16[4,128,768]{2,1,0:T(8,128)(2,1)} async-done(((bf16[4,128,768]{2,1,0:T(8,128)(2,1)}), bf16[4,128,768]{2,1,0:T(8,128)(2,1)}, u32[]{:S(2)}, u32[]{:S(2)}) %all-to-all-start.3) | async-done | bytes 786464 | tf_op jit(solution)/shard_map/all_to_all | solution.py:379
  176.0 4.2 all-to-all-start.2
  180.5 1.3 convert_reduce_fusion
  181.8 1.5 multiply_reduce_fusion
  183.9 8.1 %all-to-all-done.2 = bf16[4,128,768]{2,1,0:T(8,128)(2,1)} async-done(((bf16[4,128,768]{2,1,0:T(8,128)(2,1)}), bf16[4,128,768]{2,1,0:T(8,128)(2,1)}, u32[]{:S(2)}, u32[]{:S(2)}) %all-to-all-start.2) | async-done | bytes 786464 | tf_op jit(solution)/shard_map/all_to_all | solution.py:379
  192.0 1.4 convert_reduce_fusion.1
  193.4 1.5 fusion.47
  195.0 2.2 fusion.32
  197.1 1.7 convolution_convert_fusion.1
  198.8 1.6 convolution_convert_fusion
  200.5 1.1 copy-done.20
  201.5 2.6 convolution_convert_fusion.7
  204.1 1.5 convolution_convert_fusion.6
  205.6 1.5 convolution_convert_fusion.5
  208.1 1.4 fusion.89
  209.6 17.9 %all_to_all.30 = bf16[8,128,128]{2,1,0:T(8,128)(2,1)S(1)} all-to-all(bf16[8,128,128]{2,1,0:T(8,128)(2,1)S(1)} %bitcast_bitcast_fusion), channel_id=1, replica_groups=mesh['seq'=8,'tp'=4] {'seq'}, dimensions={0} | all-to-all | bytes 524288 | tf_op jit(solution)/shard_map/all_to_all | solution.py:301
  227.5 67.1 %shard_map.382 = (bf16[1024,128]{1,0:T(8,128)(2,1)S(1)}, bf16[1024,128]{1,0:T(8,128)(2,1)S(1)}, bf16[1024,128]{1,0:T(8,128)(2,1)S(1)}, f32[1024,2]{1,0:T(8,128)S...) custom-call(bf16[1024,128]{1,0:T(8,128)(2,1)S(1)} %get-tuple-element, ...), custom_call_target="tpu_custom_call" | custom-call | tf_op jit(solution)/shard_map/pallas_call | solution.py:238
  295.7 1.2 pad_maximum_fusion
  296.9 1.0 fusion.8
  297.9 3.7 all-to-all-start.5
  304.5 38.5 %all-reduce.25.cloned.1.call-done = (bf16[768,768]{1,0:T(8,128)(2,1)}, bf16[768,768]{1,0:T(8,128)(2,1)}) async-done(((bf16[768,768]{1,0:T(8,128)(2,1)}, bf16[768,768]{1,0:T(8,128)(2,1)}), (bf16[768,768]{1,0:T(8,128)(2,1)}, bf16[768,768]{1,0:T(8,128)(2,1)})) %all-reduce.25.cloned.1.call-update) | async-done | bytes 2359312 | tf_op jit(solution)/shard_map/psum | solution.py:414
  342.9 2.9 convert_element_type.191
  345.9 1.6 convert_element_type.193
  347.5 108.5 %all-reduce.27.cloned.1.call-done = (bf16[768,512]{1,0:T(8,128)(2,1)}, bf16[768,512]{1,0:T(8,128)(2,1)}, bf16[512,768]{1,0:T(8,128)(2,1)}) async-done(((bf16[768,512]{1,0:T(8,128)(2,1)}, bf16[768,512]{1,0:T(8,128)(2,1)}, bf16[512,768]{1,0:T(8,128)(2,1)}), (bf16[768,512]{1,0:T(8,128)(2,1)}, bf16[768,512]{1,0:T(8,128)(2,1)}, bf16[512,768]{1,0:T(8,128)(2,1)})) %all-reduce.27.cloned.1.call-update) | async-done | bytes 2359312 | tf_op jit(solution)/shard_map/psum | solution.py:408
  456.0 2.6 convert_element_type.202
  458.6 1.4 convert_element_type.204
  459.9 1.3 convert_element_type.206
  462.3 1.6 convolution_convert_fusion.4
  463.9 1.6 convolution_convert_fusion.3
  465.5 1.6 convolution_convert_fusion.2
  468.4 1.3 convolution_add_fusion.3
  469.7 29.0 %all-gather.6.cloned.1.call-done = bf16[16,2,72,256]{3,2,0,1:T(8,128)(2,1)} async-done(((bf16[2,2,72,256]{3,2,0,1:T(8,128)(2,1)}), bf16[16,2,72,256]{3,2,0,1:T(8,128)(2,1)}) %all-gather.6.cloned.1.call-update) | async-done | bytes 1179664 | tf_op jit(solution)/shard_map/all_gather | solution.py:471
  498.7 2.1 slice.147
  502.1 1.0 copy-done.27
  503.8 39.9 %all-reduce.12 = (f32[768]{0:T(1024)}, f32[768,12]{0,1:T(8,128)}, f32[768]{0:T(1024)}, f32[768]{0:T(1024)}, f32[768]{0:T(1024)}) all-reduce(f32[768]{0:T(1024)S(1)} %get-tuple-element.72, f32[768,12]{0,1:T(8,128)S(1)} %fusion.54, f32[768]{0:T(1024)S(1)} %copy-done.74, ...), channel_id=1, replica_groups=mesh['seq'=8,'tp'=4] {'seq','tp'}, use_global_device_ids=true, to_apply=%region_13.14 | all-reduce | flops 12288 | bytes 98304 | tf_op jit(solution)/shard_map/psum | solution.py:450
  543.8 0.9 fusion.49
  544.7 1.0 dynamic-slice_convert_fusion
  548.4 134.2 %all-reduce.23.cloned.1.call-done = (bf16[768,768]{1,0:T(8,128)(2,1)}, bf16[768,768]{1,0:T(8,128)(2,1)}, bf16[768,768]{1,0:T(8,128)(2,1)}) async-done(((bf16[768,768]{1,0:T(8,128)(2,1)}, bf16[768,768]{1,0:T(8,128)(2,1)}, bf16[768,768]{1,0:T(8,128)(2,1)}), (bf16[768,768]{1,0:T(8,128)(2,1)}, bf16[768,768]{1,0:T(8,128)(2,1)}, bf16[768,768]{1,0:T(8,128)(2,1)})) %all-reduce.23.cloned.1.call-update) | async-done | bytes 3538960 | tf_op jit(solution)/shard_map/psum | solution.py:440
  682.6 2.9 convert_element_type.194
  685.5 1.6 convert_element_type.195
  687.2 1.6 convert_element_type.196
  (276 shorter events, 25.3 us)
Async XLA Ops:
  7.2 134.5 %copy-start = (bf16[768,768]{1,0:T(8,128)(2,1)S(1)}, bf16[768,768]{1,0:T(8,128)(2,1)}, u32[]{:S(2)}) copy-start(bf16[768,768]{1,0:T(8,128)(2,1)} %param.36) | copy-start | bytes 3538948
  7.2 42.1 %all-gather.4.cloned.1.call-start = ((), (), s32[]{:S(2)}) async-start(), calls=%async_computation.6 | async-start | bytes 2211840 | tf_op jit(solution)/shard_map/all_gather | solution.py:317
  13.0 1.9 copy-start.16
  13.0 2.7 copy-start.64
  13.0 2.7 copy-start.66
  13.1 2.9 copy-start.23
  15.0 1.4 copy-start.21
  19.2 29.6 %all-to-all-start = ((bf16[8,144,384]{2,1,0:T(8,128)(2,1)}), bf16[8,144,384]{2,1,0:T(8,128)(2,1)S(1)}, u32[]{:S(2)}, u32[]{:S(2)}) async-start(bf16[8,144,384]{2,1,0:T(8,128)(2,1)} %fusion.7), calls=%async_computation | async-start | bytes 1769472 | tf_op jit(solution)/shard_map/all_to_all | solution.py:301
  49.0 2.0 copy-start.28
  124.2 15.7 %all-to-all-start.1 = ((bf16[8,128,128]{2,1,0:T(8,128)(2,1)}), bf16[8,128,128]{2,1,0:T(8,128)(2,1)}, u32[]{:S(2)}, u32[]{:S(2)}) async-start(bf16[8,128,128]{2,1,0:T(8,128)(2,1)} %bitcast.214), calls=%async_computation.1 | async-start | bytes 524288 | tf_op jit(solution)/shard_map/all_to_all | solution.py:301
  128.2 2.5 copy-start.57
  140.8 2.5 copy-start.30
  141.0 2.4 copy-start.71
  141.7 1.7 copy-start.78
  141.7 2.5 copy-start.65
  143.4 9.6 %copy-start.41 = (bf16[768,512]{1,0:T(8,128)(2,1)S(1)}, bf16[768,512]{1,0:T(8,128)(2,1)}, u32[]{:S(2)}) copy-start(bf16[768,512]{1,0:T(8,128)(2,1)} %param.40) | copy-start | bytes 2359300
  153.0 1.4 copy-start.40
  160.1 15.9 %all-to-all-start.3 = ((bf16[4,128,768]{2,1,0:T(8,128)(2,1)}), bf16[4,128,768]{2,1,0:T(8,128)(2,1)}, u32[]{:S(2)}, u32[]{:S(2)}) async-start(bf16[4,128,768]{2,1,0:T(8,128)(2,1)} %bitcast.215), calls=%async_computation.3 | async-start | bytes 1572864 | tf_op jit(solution)/shard_map/all_to_all | solution.py:379
  176.0 15.9 %all-to-all-start.2 = ((bf16[4,128,768]{2,1,0:T(8,128)(2,1)}), bf16[4,128,768]{2,1,0:T(8,128)(2,1)}, u32[]{:S(2)}, u32[]{:S(2)}) async-start(bf16[4,128,768]{2,1,0:T(8,128)(2,1)} %bitcast.225), calls=%async_computation.2 | async-start | bytes 1572864 | tf_op jit(solution)/shard_map/all_to_all | solution.py:379
  180.2 162.7 %all-reduce.25.cloned.1.call-start = ((), (), s32[]{:S(2)}) async-start(), calls=%async_computation.10 | async-start | bytes 4718592 | tf_op jit(solution)/shard_map/psum | solution.py:414
  180.5 2.9 copy-start.89
  181.8 1.5 copy-start.36
  191.9 1.4 copy-start.58
  191.9 1.4 copy-start.84
  193.4 1.6 copy-start.31
  193.4 1.6 copy-start.48
  193.4 1.5 copy-start.68
  193.4 1.5 copy-start.72
  193.4 1.5 copy-start.73
  193.4 1.5 copy-start.79
  194.9 2.2 copy-start.38
  197.1 1.7 copy-start.59
  197.1 1.7 copy-start.17
  200.4 255.6 %all-reduce.27.cloned.1.call-start = ((), (), s32[]{:S(2)}) async-start(), calls=%async_computation.11 | async-start | bytes 4718592 | tf_op jit(solution)/shard_map/psum | solution.py:408
  201.5 2.6 copy-start.62
  204.1 1.5 copy-start.56
  204.1 1.5 copy-start.90
  208.1 19.4 %copy-start.3 = (f32[2,1024,64]{2,1,0:T(8,128)S(1)}, f32[2,1024,64]{2,1,0:T(8,128)}, u32[]{:S(2)}) copy-start(f32[2,1024,64]{2,1,0:T(8,128)} %copy-done.2) | copy-start | bytes 1572868
  208.1 19.4 %copy-start.5 = (bf16[8,2,64,256]{3,2,1,0:T(8,128)(2,1)S(1)}, bf16[8,2,64,256]{3,2,1,0:T(8,128)(2,1)}, u32[]{:S(2)}) copy-start(bf16[8,2,64,256]{3,2,1,0:T(8,128)(2,1)} %copy-done.4) | copy-start | bytes 1572868
  227.5 67.2 %copy-start.29 = (f32[8,128,2]{2,1,0:T(8,128)S(1)}, f32[8,128,2]{2,1,0:T(8,128)}, u32[]{:S(2)}) copy-start(f32[8,128,2]{2,1,0:T(8,128)} %copy-done.28) | copy-start | bytes 24580
  227.5 67.2 %copy-start.77 = (f32[2]{0:T(128)S(1)}, f32[2]{0:T(128)}, u32[]{:S(2)}) copy-start(f32[2]{0:T(128)} %copy-done.76) | copy-start | bytes 28
  297.9 3.9 copy-start.15
  297.9 3.9 copy-start.13
  297.9 4.2 copy-start.11
  297.9 5.3 copy-start.86
  297.9 163.2 %all-to-all-start.5 = ((bf16[8,144,384]{2,1,0:T(8,128)(2,1)}), bf16[8,144,384]{2,1,0:T(8,128)(2,1)S(1)}, u32[]{:S(2)}, u32[]{:S(2)}) async-start(bf16[8,144,384]{2,1,0:T(8,128)(2,1)} %fusion.8), calls=%async_computation.5 | async-start | bytes 1769472 | tf_op jit(solution)/shard_map/all_to_all | solution.py:301
  301.6 197.0 %all-gather.6.cloned.1.call-start = ((), (), s32[]{:S(2)}) async-start(), calls=%async_computation.7 | async-start | bytes 1327104 | tf_op jit(solution)/shard_map/all_gather | solution.py:471
  302.9 241.7 %all-reduce.21.cloned.1.call-start = ((), (), s32[]{:S(2)}) async-start(), calls=%async_computation.8 | async-start | bytes 1769472
  342.9 2.9 copy-start.50
  456.0 2.6 copy-start.54
  461.6 2.3 copy-start.44
  461.8 2.1 copy-start.46
  462.0 3.5 copy-start.42
  465.5 1.6 copy-start.22
  465.5 1.6 copy-start.45
  469.7 31.2 %copy-start.26 = (bf16[768,768]{1,0:T(8,128)(2,1)S(1)}, bf16[768,768]{1,0:T(8,128)(2,1)}, u32[]{:S(2)}) copy-start(bf16[768,768]{1,0:T(8,128)(2,1)} %param.26) | copy-start | bytes 3538948
  469.7 31.3 %copy-start.43 = (bf16[8,128,128]{1,2,0:T(8,128)(2,1)S(1)}, bf16[8,128,128]{1,2,0:T(8,128)(2,1)}, u32[]{:S(2)}) copy-start(bf16[8,128,128]{1,2,0:T(8,128)(2,1)} %copy-done.42) | copy-start | bytes 786436
  469.7 31.3 %copy-start.49 = (f32[128,768]{1,0:T(8,128)S(1)}, f32[128,768]{1,0:T(8,128)}, u32[]{:S(2)}) copy-start(f32[128,768]{1,0:T(8,128)} %convolution_add_fusion.3) | copy-start | bytes 1179652
  500.8 181.7 %all-reduce.23.cloned.1.call-start = ((), (), s32[]{:S(2)}) async-start(), calls=%async_computation.9 | async-start | bytes 7077888 | tf_op jit(solution)/shard_map/psum | solution.py:440
  503.1 40.6 %copy-start.81 = (f32[128]{0:T(128)S(1)}, f32[128]{0:T(128)}, u32[]{:S(2)}) copy-start(f32[128]{0:T(128)} %copy-done.80) | copy-start | bytes 1540
  503.1 40.6 %copy-start.39 = (f32[128,768]{1,0:T(8,128)S(1)}, f32[128,768]{1,0:T(8,128)}, u32[]{:S(2)}) copy-start(f32[128,768]{1,0:T(8,128)} %copy-done.38) | copy-start | bytes 1179652
  682.6 2.9 copy-start.52
  685.5 1.7 copy-start.51
  687.1 1.7 copy-start.1
  (38 other events, 35.5 us)
Sparse Core Ops, SparseCore 0:
  15.1 23.4 all-gather.3
  200.5 142.3 all-reduce.24
  347.9 108.0 all-reduce.26
  458.6 40.0 all-gather.5
  501.0 34.3 all-reduce.20
  541.7 140.8 all-reduce.22

commit v2 on v1

--- a/solution.py
+++ b/solution.py
@@ -30,7 +30,7 @@
     r=lax.broadcasted_iota(jnp.int32,(CH,CH),0); c=lax.broadcasted_iota(jnp.int32,(CH,CH),1)
     return r,c
 
-def fwd_kernel(C,q_ref,k_ref,v_ref,r_ref,w1_ref,b1_ref,u_ref,b2_ref,gam_ref,bet_ref,
+def fwd_kernel(C,x_ref,r_ref,w1_ref,b1_ref,u_ref,b2_ref,gam_ref,bet_ref,
                o_ref,z1_ref,p_ref,zc_ref,z1q_ref,zq_ref,us_ref,w1s_ref,
                W1,B1,U,B2,S1,S2,X2,KK,BASE,T):
     @pl.when(pl.program_id(0)==0)
@@ -41,8 +41,8 @@
     ri,ci=iotas()
     blk=(ci//B)<(ri//B)
     tri=ci<=ri
-    K=[k_ref[:,H*c:H*c+H] for c in range(C)]
-    Q=[q_ref[:,H*c:H*c+H] for c in range(C)]
+    K=[x_ref[:,H*(C+c):H*(C+c)+H] for c in range(C)]
+    Q=[x_ref[:,H*c:H*c+H] for c in range(C)]
     gam=[gam_ref[c] for c in range(C)]; bet=[bet_ref[c] for c in range(C)]
     R=[r_ref[:,c:c+1] for c in range(C)]
     w1b=[W1[c].astype(LOW) for c in range(C)]
@@ -55,7 +55,7 @@
         w1s_ref[0,c]=w1b[c]
         KK[c]=jnp.where(blk,nt(K[c],K[c])+1.0,0.0).astype(LOW)
         BASE[c]=nn(K[c],w1b[c])+b1[c]
-        T[c]=(bet[c]+K[c].astype(F)-v_ref[:,H*c:H*c+H].astype(F))*gam[c]
+        T[c]=(bet[c]+K[c].astype(F)-x_ref[:,H*(2*C+c):H*(2*C+c)+H].astype(F))*gam[c]
     ub=list(u0); uf=[U[c] for c in range(C)]; b2=list(b20)
     for j in range(CH//B):
         sl=slice(B*j,B*j+B)
@@ -97,20 +97,20 @@
         o_ref[:,H*c:H*c+H]=(Q[c].astype(F)+yq*gam[c]+bet[c]).astype(LOW)
         z1q_ref[c]=z1q; zq_ref[c]=zq
 
-def fwd_scan(q,k,v,r,w1,b1,u,b2,gam,bet):
-    L=q.shape[0]; C=w1.shape[0]; I=w1.shape[2]; H=w1.shape[1]; n=L//CH
+def fwd_scan(x,r,w1,b1,u,b2,gam,bet):
+    L=x.shape[0]; C=w1.shape[0]; I=w1.shape[2]; H=w1.shape[1]; n=L//CH
     row=lambda w,dt=None: pl.BlockSpec((CH,w),lambda i:(i,0))
     full=lambda *s: pl.BlockSpec(s,lambda i:(0,)*len(s))
     big=lambda w: pl.BlockSpec((C,CH,w),lambda i:(0,i,0))
     sd=jax.ShapeDtypeStruct
     return pl.pallas_call(partial(fwd_kernel,C),grid=(n,),
-        in_specs=[row(C*H)]*3+[row(C),full(C,H,I),full(C,1,I),full(C,H,I),full(C,1,H),full(C,1,H),full(C,1,H)],
+        in_specs=[row(3*C*H),row(C),full(C,H,I),full(C,1,I),full(C,H,I),full(C,1,H),full(C,1,H),full(C,1,H)],
         out_specs=[row(C*H),big(I),big(I),big(H),big(I),big(H),pl.BlockSpec((1,C,CH//B,H,I),lambda i:(i,0,0,0,0)),pl.BlockSpec((1,C,H,I),lambda i:(i,0,0,0))],
         out_shape=[sd((L,C*H),LOW),sd((C,L,I),F),sd((C,L,I),F),sd((C,L,H),F),sd((C,L,I),F),sd((C,L,H),F),sd((n,C,CH//B,H,I),LOW),sd((n,C,H,I),LOW)],
         scratch_shapes=[pltpu.VMEM((C,H,I),F),pltpu.VMEM((C,1,I),F),pltpu.VMEM((C,H,I),F),pltpu.VMEM((C,1,H),F),
             pltpu.VMEM((C,CH,I),LOW),pltpu.VMEM((C,CH,H),LOW),pltpu.VMEM((C,CH,I),LOW),pltpu.VMEM((C,CH,CH),LOW),pltpu.VMEM((C,CH,I),F),pltpu.VMEM((C,CH,H),F)],
         compiler_params=pltpu.CompilerParams(vmem_limit_bytes=48*1024*1024),
-    )(q,k,v,r,w1,b1,u,b2,gam,bet)
+    )(x,r,w1,b1,u,b2,gam,bet)
 
 def gelu3(z):
     z2=z*z
@@ -123,8 +123,8 @@
     g2=2*h1+z*(h*(1-t)*(6*C0*C1)*z-2*t*u1*h1)
     return x,g1,g2
 
-def bwd_kernel(C,n,q_ref,k_ref,v_ref,r_ref,do_ref,z1_ref,p_ref,zc_ref,z1q_ref,zq_ref,us_ref,w1s_ref,gam_ref,bet_ref,
-               dq_ref,dk_ref,dv_ref,dr_ref,H1,h1,HU,h2,dgam_ref,dbet_ref,
+def bwd_kernel(C,n,x_ref,r_ref,do_ref,z1_ref,p_ref,zc_ref,z1q_ref,zq_ref,us_ref,w1s_ref,gam_ref,bet_ref,
+               dx_ref,dr_ref,H1,h1,HU,h2,dgam_ref,dbet_ref,
                BASE,DX2,X2,RG1,RPG2,DS2Q,KK,DZ1,DS1,DS2,DG,YB,GB,DB,SB,S2B,G1):
     @pl.when(pl.program_id(0)==0)
     def _():
@@ -134,8 +134,8 @@
     blk=(ci//B)<(ri//B)
     blkT=(ci//B)>(ri//B)
     tri=ci<=ri
-    K=[k_ref[:,H*c:H*c+H] for c in range(C)]
-    Q=[q_ref[:,H*c:H*c+H] for c in range(C)]
+    K=[x_ref[:,H*(C+c):H*(C+c)+H] for c in range(C)]
+    Q=[x_ref[:,H*c:H*c+H] for c in range(C)]
     gam=[gam_ref[c] for c in range(C)]; bet=[bet_ref[c] for c in range(C)]
     R=[r_ref[:,c:c+1] for c in range(C)]
     g2=[gam[c]*gam[c] for c in range(C)]
@@ -155,7 +155,7 @@
         zc=zc_ref[c]
         s=lax.rsqrt(mean(zc*zc)+EPS)
         y=zc*s
-        t0=bet[c]+K[c].astype(F)-v_ref[:,H*c:H*c+H].astype(F)
+        t0=bet[c]+K[c].astype(F)-x_ref[:,H*(2*C+c):H*(2*C+c)+H].astype(F)
         G=y*g2[c]+t0*gam[c]
         m1=mean(G); m2=mean(G*y)
         d2=s*(G-m1-y*m2)
@@ -178,7 +178,7 @@
         dz1qb=dz1q.astype(LOW)
         A1=jnp.where(tri,nt(Q[c],K[c])+1.0,0.0)
         dA1=jnp.where(tri,nt(dz1qb,s1),0.0).astype(LOW)
-        dq_ref[:,H*c:H*c+H]=(dO+nt(dz1qb,w1)-nn(dA1,K[c])).astype(LOW)
+        dx_ref[:,H*c:H*c+H]=(dO+nt(dz1qb,w1)-nn(dA1,K[c])).astype(LOW)
         h1b=H1[c].astype(LOW)
         dk=nt(s1,h1b)+tn(dA1,Q[c])
         KK[c]=jnp.where(blkT,nt(K[c],K[c])+1.0,0.0).astype(LOW)
@@ -218,8 +218,8 @@
         M=jnp.where(blk,nt(dz1,s1),0.0).astype(LOW)
         dG=DG[c]; dGg=dG*gam[c]
         dk=-dk-nn(M,K[c])-tn(M,K[c])+nt(dz1,w1)+dGg
-        dk_ref[:,H*c:H*c+H]=dk.astype(LOW)
-        dv_ref[:,H*c:H*c+H]=(-dGg).astype(LOW)
+        dx_ref[:,H*(C+c):H*(C+c)+H]=dk.astype(LOW)
+        dx_ref[:,H*(2*C+c):H*(2*C+c)+H]=(-dGg).astype(LOW)
         dr_ref[:,c:c+1]=jnp.sum(DS1[c]*D1,-1,keepdims=True)+jnp.sum(DS2[c]*DB[c],-1,keepdims=True)
         dgam_ref[c]=dgam_ref[c]+jnp.sum(dG*(2*YB[c]*gam[c]+t0),0,keepdims=True)
         dbet_ref[c]=dbet_ref[c]+jnp.sum(dGg,0,keepdims=True)
@@ -228,21 +228,21 @@
         HU[c]=hu[c]+tn(dzqb,x2q)
         h2[c]=hh2[c]+jnp.sum(dzqb.astype(F),0,keepdims=True)
 
-def bwd_scan(q,k,v,r,do,z1,p,zc,z1q,zq,us,w1s,gam,bet):
-    L=q.shape[0]; C,_,I=z1.shape; H=zc.shape[2]; n=L//CH
+def bwd_scan(x,r,do,z1,p,zc,z1q,zq,us,w1s,gam,bet):
+    L=x.shape[0]; C,_,I=z1.shape; H=zc.shape[2]; n=L//CH
     row=lambda w,dt=None: pl.BlockSpec((CH,w),lambda i:(n-1-i,0))
     full=lambda *s: pl.BlockSpec(s,lambda i:(0,)*len(s))
     big=lambda w: pl.BlockSpec((C,CH,w),lambda i:(0,n-1-i,0))
     sd=jax.ShapeDtypeStruct
     V=pltpu.VMEM
     return pl.pallas_call(partial(bwd_kernel,C,n),grid=(n,),
-        in_specs=[row(C*H)]*3+[row(C),row(C*H),big(I),big(I),big(H),big(I),big(H),pl.BlockSpec((1,C,CH//B,H,I),lambda i:(n-1-i,0,0,0,0)),pl.BlockSpec((1,C,H,I),lambda i:(n-1-i,0,0,0)),full(C,1,H),full(C,1,H)],
-        out_specs=[row(C*H)]*3+[row(C),full(C,H,I),full(C,1,I),full(C,H,I),full(C,1,H),full(C,1,H),full(C,1,H)],
-        out_shape=[sd((L,C*H),LOW)]*3+[sd((L,C),F),sd((C,H,I),F),sd((C,1,I),F),sd((C,H,I),F),sd((C,1,H),F),sd((C,1,H),F),sd((C,1,H),F)],
+        in_specs=[row(3*C*H),row(C),row(C*H),big(I),big(I),big(H),big(I),big(H),pl.BlockSpec((1,C,CH//B,H,I),lambda i:(n-1-i,0,0,0,0)),pl.BlockSpec((1,C,H,I),lambda i:(n-1-i,0,0,0)),full(C,1,H),full(C,1,H)],
+        out_specs=[row(3*C*H),row(C),full(C,H,I),full(C,1,I),full(C,H,I),full(C,1,H),full(C,1,H),full(C,1,H)],
+        out_shape=[sd((L,3*C*H),LOW),sd((L,C),F),sd((C,H,I),F),sd((C,1,I),F),sd((C,H,I),F),sd((C,1,H),F),sd((C,1,H),F),sd((C,1,H),F)],
         scratch_shapes=[V((C,CH,I),F),V((C,CH,I),F),V((C,CH,I),LOW),V((C,CH,I),F),V((C,CH,I),F),V((C,CH,H),F),V((C,CH,CH),LOW),V((C,CH,I),LOW),V((C,CH,I),F),V((C,CH,H),F),V((C,CH,H),F),
             V((C,CH,H),F),V((C,CH,H),F),V((C,CH,H),F),V((C,CH,2),F),V((C,CH,H),LOW),V((C,CH,I),F)],
         compiler_params=pltpu.CompilerParams(vmem_limit_bytes=48*1024*1024),
-    )(q,k,v,r,do,z1,p,zc,z1q,zq,us,w1s,gam,bet)
+    )(x,r,do,z1,p,zc,z1q,zq,us,w1s,gam,bet)
 
 RATE_SCALE = 0.25
 NORM_EPS = 1e-05
@@ -271,6 +271,181 @@
 
 def matmul(left, right):
     return jnp.dot(left, right, preferred_element_type=F)
+
+
+def flip(array, axis, mask):
+    peers = lax.axis_size(axis)
+    return lax.ppermute(array, axis, [(i, i ^ mask) for i in range(peers)])
+
+
+def masks_of(axis):
+    masks = []
+    while 1 << len(masks) < lax.axis_size(axis):
+        masks.append(1 << len(masks))
+    return masks
+
+
+def side(axis, mask):
+    return (lax.axis_index(axis) // mask) % 2
+
+
+def gather_near(array, axis):
+    for mask in reversed(masks_of(axis)):
+        array = jnp.concatenate([array, flip(array, axis, mask)], 0)
+    return array
+
+
+def scatter_near(array, axis):
+    for mask in masks_of(axis):
+        half = array.shape[0] // 2
+        array = array[:half].astype(F) + flip(array[half:].astype(LOW), axis, mask).astype(F)
+    return array
+
+
+def halve(array, axis, mask, dim):
+    bit = side(axis, mask)
+    mine = lax.dynamic_index_in_dim(array, bit, dim, keepdims=False)
+    other = lax.dynamic_index_in_dim(array, 1 - bit, dim, keepdims=False)
+    return mine.astype(F) + flip(other.astype(LOW), axis, mask).astype(F)
+
+
+def double(array, axis, mask):
+    got = flip(array, axis, mask)
+    upper = side(axis, mask) == 1
+    return jnp.stack([jnp.where(upper, got, array), jnp.where(upper, array, got)])
+
+
+def share_rows(columns, chain_g, rate_column, vectors, early, heads, local_heads, weights_in):
+    seqs, tps = lax.axis_size("seq"), lax.axis_size("tp")
+    width, lanes = columns.shape
+    span = lanes // 3
+    each, _, head, inner = chain_g[0].shape
+    states = jnp.concatenate([chain_g[0], chain_g[1][:, :, None], jnp.zeros((each, 2, 7, inner), F)], 2)
+    state_rows = states.size // lanes // tps
+    rate_rows = rate_column.size // lanes // tps
+    vectors = jnp.concatenate([vectors, jnp.zeros_like(vectors[:1])], 0)
+    vector_rows = vectors.size // lanes // tps
+    rest = jnp.concatenate(
+        [rate_column.reshape(tps, rate_rows, lanes), vectors.reshape(tps, vector_rows, lanes)], 1
+    )
+    late = jnp.concatenate(
+        [
+            columns.reshape(tps, width // tps, lanes),
+            states.reshape(tps, state_rows, lanes),
+            jnp.pad(rest, ((0, 0), (0, 16 - rate_rows - vector_rows), (0, 0))),
+        ],
+        1,
+    )
+    late = lax.psum_scatter(late.astype(LOW), "tp", scatter_dimension=0, tiled=True)
+    late = lax.all_gather(late, ("seq", "tp"), axis=0, tiled=True).reshape((seqs, tps) + late.shape[1:])
+    weights = late[:, :, : width // tps].reshape(seqs, tps, width // tps, 3, span)
+    weights = weights.transpose(3, 1, 2, 0, 4).reshape(3, width, seqs * span)[:, :, :width].astype(F)
+    states = late[:, :, width // tps : width // tps + state_rows].reshape(seqs * each, 2, head + 8, inner)[:heads]
+    states = lax.dynamic_slice_in_dim(states, lax.axis_index("tp") * local_heads, local_heads, 0).astype(F)
+    rest = late[:, :, width // tps + state_rows :]
+    rate_weight_grad = rest[:, :, :rate_rows].reshape(seqs * each, width)[:heads].T.astype(F)
+    vectors = rest[:, :, rate_rows : rate_rows + vector_rows].reshape(seqs, 4, width)
+    vectors = jnp.sum(vectors.astype(F), 0)
+    norm_gain_grad = early[1] * weights_in[3].astype(F)
+    for i in range(3):
+        norm_gain_grad = norm_gain_grad + weights[i] * weights_in[i].astype(F)
+    return weights, states[:, :, :head], states[:, :, head], rate_weight_grad, vectors, jnp.sum(norm_gain_grad, -1)
+
+
+def last_kernel(seqs, each, heads, local_heads, me_ref, a_ref, b_ref, wq_ref, wk_ref, wv_ref, wg_ref, gg_ref,
+                q_ref, k_ref, v_ref, n_ref, s_ref, r_ref):
+    cut = a_ref.shape[3]
+    span = a_ref.shape[4] // 3
+    below = q_ref.shape[0] - cut
+    total = gg_ref[0] * wg_ref[...].astype(F)
+    for s in range(seqs):
+        if s * each >= heads:
+            continue
+        x, q = s % 2, ((s >> 1) & 1) * 2 + (s >> 2)
+        for i, o_ref in enumerate((q_ref, k_ref, v_ref)):
+            o_ref[:cut, span * s : span * s + span] = a_ref[0, 0, 4 * x + q, :, span * i : span * i + span].astype(F)
+            o_ref[cut:, span * s : span * s + span] = b_ref[0, x, 0, q, :below, span * i : span * i + span].astype(F)
+    for o_ref, w_ref in ((q_ref, wq_ref), (k_ref, wk_ref), (v_ref, wv_ref)):
+        total = total + o_ref[...] * w_ref[...].astype(F)
+    n_ref[...] = jnp.sum(total, -1, keepdims=True)
+
+    def tile(x, q, n):
+        return b_ref[0, x, 0, q, below + 16 * (n // 3) : below + 16 * (n // 3) + 16, 128 * (n % 3) : 128 * (n % 3) + 128]
+
+    for i in range(local_heads):
+        h = me_ref[0] * local_heads + i
+        s = h // each
+        upper = lax.rem(h, each) == 1
+        x = lax.rem(s, 2)
+        q = lax.rem(s // 2, 2) * 2 + s // 4
+        for k in range(2):
+            for j in range(2):
+                low = tile(x, q, k * 2 + j).astype(F)
+                high = tile(x, q, 4 + k * 2 + j).astype(F)
+                s_ref[i, k, :, 128 * j : 128 * j + 128] = jnp.where(upper, high, low)
+    for s in range(seqs):
+        r_ref[0, s] = tile(s % 2, ((s >> 1) & 1) * 2 + (s >> 2), 8).astype(F)
+
+
+def share_tiles(columns, chain_g, rate_column, vectors, other_fed, early, heads, local_heads, weights_in):
+    seqs, tps = lax.axis_size("seq"), lax.axis_size("tp")
+    width, lanes = columns.shape
+    each, _, head, inner = chain_g[0].shape
+    here = width // tps
+    states = chain_g[0].reshape(each * 2, tps, head // tps, 2, 128).transpose(1, 0, 3, 2, 4)
+    states = states.reshape(tps, each * 4, head // tps, 128)
+    tails = chain_g[1].reshape(tps, -1, 128)
+    rates = rate_column.reshape(tps, -1, 128)
+    vector_rows = -(-vectors.size // 128 // tps)
+    small = jnp.pad(vectors.reshape(-1, 128), ((0, vector_rows * tps - vectors.size // 128), (0, 0)))
+    small = jnp.concatenate([tails, rates, small.reshape(tps, vector_rows, 128)], 1)
+    small = jnp.pad(small, ((0, 0), (0, 16 - small.shape[1]), (0, 0)))
+    tiles = jnp.concatenate([states, small[:, None]], 1).reshape(tps, 3, 3, 16, 128)
+    tiles = tiles.transpose(0, 1, 3, 2, 4).reshape(tps, 48, lanes)
+    late = jnp.concatenate([columns.reshape(tps, here, lanes), tiles], 1)
+    share = late.shape[1]
+    late = late.reshape(2, 2, share, lanes)
+    late = halve(late, "tp", 1, 1)
+    late = halve(late, "tp", 2, 0).astype(LOW)
+    late = double(late, "seq", 4)
+    late = double(late, "seq", 2)
+    cut = 128
+    part_a, part_b = late[:, :, :cut], late[:, :, cut:]
+    part_a, part_b = double(part_a, "seq", 1), double(part_b, "tp", 2)
+    part_a, part_b = double(part_a, "tp", 2), double(part_b, "seq", 1)
+    part_a, part_b = double(part_a, "tp", 1), double(part_b, "tp", 1)
+    part_a = part_a.reshape(2, 2, seqs, cut, lanes)
+    part_b = part_b.reshape(2, 2, 2, seqs // 2, share - cut, lanes)
+    me = lax.axis_index("tp").astype(jnp.int32).reshape(1)
+    square = pl.BlockSpec((here, width), lambda t: (t, 0))
+    sd = jax.ShapeDtypeStruct
+    *weights, norm_gain_grad, head_w, small = pl.pallas_call(
+        partial(last_kernel, seqs, each, heads, local_heads),
+        grid=(tps,),
+        in_specs=[
+            pl.BlockSpec(memory_space=pltpu.SMEM),
+            pl.BlockSpec((1, 1, seqs, cut, lanes), lambda t: (t % 2, t // 2, 0, 0, 0)),
+            pl.BlockSpec((1, 2, 1, seqs // 2, share - cut, lanes), lambda t: (t % 2, 0, t // 2, 0, 0, 0)),
+            square, square, square, square,
+            pl.BlockSpec((1, here, width), lambda t: (1, t, 0)),
+        ],
+        out_specs=[
+            square, square, square,
+            pl.BlockSpec((here, 1), lambda t: (t, 0)),
+            pl.BlockSpec((local_heads, 2, head // tps, inner), lambda t: (0, 0, t, 0)),
+            pl.BlockSpec((1, seqs, 16, 128), lambda t: (t, 0, 0, 0)),
+        ],
+        out_shape=[sd((width, width), F)] * 3
+        + [sd((width, 1), F), sd((local_heads, 2, head, inner), F), sd((tps, seqs, 16, 128), F)],
+        compiler_params=pltpu.CompilerParams(vmem_limit_bytes=48 * 1024 * 1024),
+    )(me, part_a, part_b, *weights_in, early)
+    edge = tails.shape[1]
+    edge_r = edge + rates.shape[1]
+    head_t = small[:, :, :edge].transpose(1, 0, 2, 3).reshape(seqs * each, 2, inner)
+    head_t = lax.dynamic_slice_in_dim(head_t, me[0] * local_heads, local_heads, 0)
+    rate_weight_grad = small[:, :, edge:edge_r].transpose(1, 0, 2, 3).reshape(seqs * each, width)[:heads].T
+    vectors = jnp.sum(small[:, :, edge_r : edge_r + vector_rows], 1).reshape(-1)[: 3 * width].reshape(3, width)
+    return weights, head_w, head_t, rate_weight_grad, vectors, other_fed, norm_gain_grad[:, 0]
 
 
 def on_device(
@@ -333,6 +508,9 @@
     residual = tokens[0].astype(F)
     normed_val, norm_pull = jax.vjp(root_norm, residual, norm_gain)
     normed = normed_val.astype(LOW)
+    down_grad = cotangent[0]
+    grad_out = down_grad.astype(F)
+    every_grad = gather_near(down_grad, "tp")
     query_tok = matmul(normed, query_weight).astype(LOW)
     keys_tok = matmul(normed, key_weight).astype(LOW)
     values_tok = matmul(normed, value_weight).astype(LOW)
@@ -347,17 +525,16 @@
     )
     got = swap(sent)
     chain_qkv = got[:, :rows].reshape(length, 3 * span)
-    query_c = chain_qkv[:, :span]
-    keys_c = chain_qkv[:, span : 2 * span]
-    values_c = chain_qkv[:, 2 * span :]
     logit_c = got[:, rows : rows + each, :rows].transpose(0, 2, 1).reshape(length, each).astype(F)
     gate_c = jax.nn.sigmoid(logit_c + chain_rate_bias)
     rate_c = gate_c * (RATE_SCALE / head)
 
+    every_normed = lax.all_gather(normed, "seq", axis=0, tiled=True)
     outs, *kept = fwd_scan(
-        query_c, keys_c, values_c, rate_c, chain_first, chain_first_bias, chain_second,
+        chain_qkv, rate_c, chain_first, chain_first_bias, chain_second,
         chain_second_bias, chain_gain, chain_shift,
     )
+    outs, every_normed = lax.optimization_barrier((outs, every_normed))
     mixed_tok = from_chains(swap(outs.reshape(seqs, rows, span))).astype(F)
 
     branch_val, branch_pull = jax.vjp(gated_branch, mixed_tok, gate_pre, post_gain, post_bias)
@@ -365,19 +542,11 @@
     middle = residual + matmul(branch_in, output_weight)
     feed_val, feed_pull = jax.vjp(root_norm, middle, feed_gain)
     feed_in = feed_val.astype(LOW)
-    down_grad = cotangent[0]
-    grad_out = down_grad.astype(F)
-    every_grad = lax.all_gather(down_grad, "tp", axis=0, tiled=True)
-    every_in = lax.all_gather(feed_in, "tp", axis=0, tiled=True)
+    every_in = gather_near(feed_in, "tp")
     gate_val = matmul(every_in, feed_gate)
     linear_val = matmul(every_in, feed_linear)
     act_val, act_pull = jax.vjp(swish_product, gate_val, linear_val)
     hidden = act_val.astype(LOW)
-
-    def sum_over_tp(array):
-        parts = array.astype(LOW).reshape(lax.axis_size("tp"), rows, width)
-        parts = lax.all_to_all(parts, "tp", split_axis=0, concat_axis=0, tiled=True)
-        return jnp.sum(parts.astype(F), 0)
 
     hidden_grad = jnp.einsum("td,fd->tf", every_grad, feed_down, preferred_element_type=F)
     gate_grad, linear_grad = act_pull(hidden_grad)
@@ -386,7 +555,7 @@
     input_part = jnp.einsum("tf,df->td", gate_low, feed_gate, preferred_element_type=F) + jnp.einsum(
         "tf,df->td", linear_low, feed_linear, preferred_element_type=F
     )
-    feed_in_grad = sum_over_tp(input_part)
+    feed_in_grad = scatter_near(input_part, "tp")
     middle_part, feed_gain_grad = feed_pull(feed_in_grad)
     middle_grad = grad_out + middle_part
     out_low = middle_grad.astype(LOW)
@@ -394,29 +563,49 @@
     mixed_grad, gate_pre_grad, post_gain_grad, post_bias_grad = branch_pull(branch_grad)
     out_grad_c = swap(to_chains(mixed_grad.astype(LOW))).reshape(length, span)
 
-    second_out = sum_over_tp(matmul(hidden, feed_down))
+    second_part = matmul(hidden, feed_down).astype(LOW)
+    second_part, out_grad_c = lax.optimization_barrier((second_part, out_grad_c))
+    second_out = scatter_near(second_part, "tp")
     result = (middle + second_out).astype(LOW)[None]
 
     feed_down_grad = jnp.einsum("tf,td->fd", hidden, every_grad, preferred_element_type=F)
     feed_gate_grad = jnp.einsum("td,tf->df", every_in, gate_low, preferred_element_type=F)
-    feed_linear_grad = jnp.einsum("td,tf->df", every_in, linear_low, preferred_element_type=F)
+    feed_linear_grad = jnp.einsum("tf,td->fd", linear_low, every_in, preferred_element_type=F)
     output_weight_grad = jnp.einsum("td,te->de", branch_in, out_low, preferred_element_type=F)
     gate_low_pre = gate_pre_grad.astype(LOW)
     branch_gate_grad = jnp.einsum("td,te->de", normed, gate_low_pre, preferred_element_type=F)
-    fed = [
-        array.astype(F)
-        for array in lax.psum(
-            (feed_gate_grad.astype(LOW), feed_linear_grad.astype(LOW), feed_down_grad.astype(LOW)), "seq"
-        )
-    ]
-    early = [
-        array.astype(F)
-        for array in lax.psum((output_weight_grad.astype(LOW), branch_gate_grad.astype(LOW)), ("seq", "tp"))
-    ]
+    tps = lax.axis_size("tp")
+    early = jnp.concatenate([output_weight_grad, branch_gate_grad], 0).reshape((2,) * len(masks_of("tp")) + (-1, width))
+    for mask in masks_of("tp"):
+        early = halve(early, "tp", mask, len(masks_of("tp")) - 1 - masks_of("tp").index(mask))
+    fed_parts = jnp.concatenate(
+        [
+            feed_linear_grad.astype(LOW).reshape(seqs, -1, width),
+            feed_down_grad.astype(LOW).reshape(seqs, -1, width),
+        ],
+        1,
+    )
+    fed_parts, out_grad_c = lax.optimization_barrier((fed_parts, out_grad_c))
+    fed_parts = swap(fed_parts)
+    early, first_fed = lax.psum((early.astype(LOW), feed_gate_grad.astype(LOW)), "seq")
 
     (
-        query_g, keys_g, values_g, rate_g, first_g, first_bias_g, second_g, second_bias_g, gain_g, shift_g,
-    ) = bwd_scan(query_c, keys_c, values_c, rate_c, out_grad_c, *kept, chain_gain, chain_shift)
+        qkv_g, rate_g, first_g, first_bias_g, second_g, second_bias_g, gain_g, shift_g,
+    ) = bwd_scan(chain_qkv, rate_c, out_grad_c, *kept, chain_gain, chain_shift)
+    early, first_fed, fed_parts, qkv_g, rate_g = lax.optimization_barrier(
+        (early, first_fed, fed_parts, qkv_g, rate_g)
+    )
+    fed = jnp.sum(fed_parts.astype(F), 0).astype(LOW)
+    levels = masks_of("seq")
+    for mask in reversed(levels):
+        fed = double(fed, "seq", mask)
+    fed = fed.transpose(list(range(len(levels)))[::-1] + [len(levels), len(levels) + 1])
+    fed = fed.reshape(seqs, 2, -1, width)
+    other_fed = [fed[:, 0].reshape(-1, width).astype(F).T, fed[:, 1].reshape(-1, width).astype(F)]
+    for mask in reversed(masks_of("tp")):
+        early = double(early, "tp", mask)
+    early = jnp.transpose(early, list(range(len(masks_of("tp"))))[::-1] + [len(masks_of("tp")), len(masks_of("tp")) + 1])
+    early = early.reshape(2, width, width).astype(F)
     logit_g = rate_g * (RATE_SCALE / head) * gate_c * (1.0 - gate_c)
     second_g = second_g - jnp.mean(second_g, 1, keepdims=True)
     second_bias_g = second_bias_g - jnp.mean(second_bias_g, -1, keepdims=True)
@@ -424,20 +613,13 @@
 
     logit_back = logit_g.astype(LOW).reshape(seqs, rows, each).transpose(0, 2, 1)
     logit_back = jnp.pad(logit_back, ((0, 0), (0, extra - each), (0, 3 * span - rows)))
-    qkv_back = jnp.concatenate([query_g, keys_g, values_g], -1).reshape(seqs, rows, 3 * span)
+    qkv_back = qkv_g.reshape(seqs, rows, 3 * span)
     back = swap(jnp.concatenate([qkv_back, logit_back], 1))
     query_low = from_chains(back[:, :rows, :span])
     keys_low = from_chains(back[:, :rows, span : 2 * span])
     values_low = from_chains(back[:, :rows, 2 * span :])
     logit_low = back[:, rows : rows + each, :rows].reshape(seqs * each, rows)[:heads].T
 
-    query_weight_grad = jnp.einsum("td,te->de", normed, query_low, preferred_element_type=F)
-    key_weight_grad = jnp.einsum("td,te->de", normed, keys_low, preferred_element_type=F)
-    value_weight_grad = jnp.einsum("td,te->de", normed, values_low, preferred_element_type=F)
-    rate_weight_grad = jnp.einsum("td,te->de", normed, logit_low, preferred_element_type=F)
-    late_in = (query_weight_grad.astype(LOW), key_weight_grad.astype(LOW), value_weight_grad.astype(LOW))
-    late_in, early = lax.optimization_barrier((late_in, early))
-    late = [array.astype(F) for array in lax.psum(late_in, ("seq", "tp"))]
     normed_grad = (
         jnp.einsum("te,de->td", query_low, query_weight, preferred_element_type=F)
         + jnp.einsum("te,de->td", keys_low, key_weight, preferred_element_type=F)
@@ -445,12 +627,8 @@
         + jnp.einsum("te,de->td", logit_low, rate_weight, preferred_element_type=F)
         + jnp.einsum("te,de->td", gate_low_pre, branch_gate, preferred_element_type=F)
     )
-    residual_part, norm_gain_grad = norm_pull(normed_grad)
+    residual_part, unused = norm_pull(normed_grad)
     tokens_grad = (middle_grad + residual_part)[None]
-    small = lax.psum(
-        (norm_gain_grad, rate_weight_grad, post_gain_grad, post_bias_grad, feed_gain_grad), ("seq", "tp")
-    )
-
     tail_g = jnp.concatenate(
         [
             second_bias_g[:, 0],
@@ -460,40 +638,46 @@
         ],
         -1,
     )
-    chain_g = jnp.stack(
-        [
-            jnp.concatenate([first_g, first_bias_g], 1),
-            jnp.concatenate([second_g, tail_g[:, None, :]], 1),
-        ],
-        1,
-    )
-    chain_g = jnp.pad(chain_g, ((0, 0), (0, 0), (0, 7), (0, 0))).astype(LOW)
-    all_g = lax.all_gather(chain_g, "seq", axis=0, tiled=True)[:heads]
-    head_g = lax.psum_scatter(all_g, "tp", scatter_dimension=0, tiled=True).astype(F)
-    tail_sum = head_g[:, 1, head]
+    chain_g = (jnp.stack([first_g, second_g], 1), jnp.stack([first_bias_g[:, 0], tail_g], 1))
+    columns = jnp.einsum("ld,le->de", every_normed, qkv_g, preferred_element_type=F)
+    rate_column = jnp.einsum("ld,le->ed", every_normed, logit_g.astype(LOW), preferred_element_type=F)
+    vectors = jnp.stack([post_gain_grad, post_bias_grad, feed_gain_grad])
+    if each == 2 and tps == 4 and seqs == 8:
+        weights, head_w, head_t, rate_weight_grad, vectors, other_fed, norm_gain_grad = share_tiles(
+            columns, chain_g, rate_column, vectors, other_fed, early, heads, local_heads,
+            (query_weight, key_weight, value_weight, branch_gate),
+        )
+    else:
+        weights, head_w, head_t, rate_weight_grad, vectors, norm_gain_grad = share_rows(
+            columns, chain_g, rate_column, vectors, early, heads, local_heads,
+            (query_weight, key_weight, value_weight, branch_gate),
+        )
+    norm_gain_grad = norm_gain_grad + jnp.sum(rate_weight_grad * rate_weight.astype(F), -1)
+    norm_gain_grad = norm_gain_grad / norm_gain
+    tail_sum = head_t[:, 1]
     return (
         result,
         tokens_grad,
-        small[0],
-        late[0],
-        late[1],
-        late[2],
-        small[1],
+        norm_gain_grad,
+        weights[0],
+        weights[1],
+        weights[2],
+        rate_weight_grad,
         tail_sum[:, 3 * head],
-        head_g[:, 0, :head],
-        head_g[:, 0, head],
-        jnp.swapaxes(head_g[:, 1, :head], 1, 2),
+        head_w[:, 0],
+        head_t[:, 0],
+        jnp.swapaxes(head_w[:, 1], 1, 2),
         tail_sum[:, :head],
         tail_sum[:, head : 2 * head],
         tail_sum[:, 2 * head : 3 * head],
         early[1],
         early[0],
-        small[2],
-        small[3],
-        small[4],
-        fed[0],
-        fed[1],
-        fed[2],
+        vectors[0],
+        vectors[1],
+        vectors[2],
+        first_fed.astype(F),
+        other_fed[0].astype(F),
+        other_fed[1].astype(F),
     )
 
 

time: 697 us -> 462 us (0.66)
  waiting for transfers between devices: 350 us -> 95.7 us
  blocking collectives: 75.6 us -> 0 us
  local copies, waits for them, and re-layouts: 23.9 us -> 68.6 us
  other arithmetic: 36.7 us -> 59.9 us
  starting transfers between devices: 24 us -> 46.5 us
  Pallas kernels: 137 us -> 144 us
    psum x3 -> x1, waiting for transfers between devices: 281 us -> 5.43 us  [on_device(): lax.psum((early.astype(LOW), feed_gate_grad.astype(LOW)), 'seq')]
    ppermute x0 -> x25, waiting for transfers between devices: none -> 57.5 us  [flip(): return lax.ppermute(array, axis, [(i, i ^ mask) for i in range(peers)])]
    psum x1 -> x0, blocking collectives: 39.9 us -> none  [on_device(): lax.psum((norm_gain_grad, rate_weight_grad, post_gain_grad, post_bias_gra...]
    all_gather x1, waiting for transfers between devices: 29 us -> 0.01 us  [on_device(): every_normed = lax.all_gather(normed, 'seq', axis=0, tiled=True)]
    unnamed x195 -> x276, local copies, waits for them, and re-layouts: 15.2 us -> 36.9 us
    ppermute x0 -> x25, starting transfers between devices: none -> 21.6 us  [flip(): return lax.ppermute(array, axis, [(i, i ^ mask) for i in range(peers)])]
    another operation x9 -> x28, other arithmetic: 0.8 us -> 19.1 us  [the longest x24 18.1 us: double(): jnp.stack([jnp.where(upper, got, array), jnp.where(upper, array, got)])]
    all_to_all x1 -> x0, blocking collectives: 17.9 us -> none  [swap(): return lax.all_to_all(array, 'seq', split_axis=0, concat_axis=0, tiled=True)]
  transfers between devices with their start and end apart: 11 -> 33, of which waited for: 7 -> 13; matrix products, arithmetic and copies ran while one was open for 7% -> 21% of each run, Pallas kernels for 10% -> 30%
where the time goes in v2:
time: 462 us; the launch traced here: 460 us
  Pallas kernels  144 us (31%)
  waiting for transfers between devices  95.7 us (21%)
  local copies, waits for them, and re-layouts  68.6 us (15%)
  other arithmetic  59.9 us (13%)
  starting transfers between devices  46.5 us (10%)
  matrix products  29 us (6%)
  between operations  15.6 us (3%)
    pallas_call x1, Pallas kernels, fwd_scan(): pl.pallas_call(partial(fwd_kernel, C), grid=(n,), in_specs=[row(3 * C * H...  70.3 us
    pallas_call x1, Pallas kernels, bwd_scan(): pl.pallas_call(partial(bwd_kernel, C, n), grid=(n,), in_specs=[row(3 * C...  67.1 us
    ppermute x25, waiting for transfers between devices, flip(): return lax.ppermute(array, axis, [(i, i ^ mask) for i in range(peers)])  57.5 us
    unnamed x276, local copies, waits for them, and re-layouts  36.9 us
    all_to_all x5, waiting for transfers between devices, swap(): return lax.all_to_all(array, 'seq', split_axis=0, concat_axis=0, tiled=True)  32.1 us
    all_to_all x5, starting transfers between devices, swap(): return lax.all_to_all(array, 'seq', split_axis=0, concat_axis=0, tiled=True)  24.6 us
    ppermute x25, starting transfers between devices, flip(): return lax.ppermute(array, axis, [(i, i ^ mask) for i in range(peers)])  21.6 us
    another operation x24, other arithmetic, double(): jnp.stack([jnp.where(upper, got, array), jnp.where(upper, array, got)])  18.1 us
  transfers between devices with their start and end apart: 33, of which 13 were waited for; matrix products, arithmetic and copies ran while one was open for 21% of the time, Pallas kernels for 30%

profile of v2, /device:TPU:0, one launch (start us, length us, event | category | flops | bytes accessed | tf_op | source)
XLA Modules:
  0.0 459.7 jit_solution(16233371478792424549)
XLA Ops:
  15.8 1.8 convolution_convert_fusion.6
  19.5 7.2 %all-to-all-start = ((bf16[8,144,384]{2,1,0:T(8,128)(2,1)}), bf16[8,144,384]{2,1,0:T(8,128)(2,1)}, u32[]{:S(2)}, u32[]{:S(2)}) async-start(bf16[8,144,384]{2,1,0:T(8,128)(2,1)} %fusion.10), calls=%async_computation | async-start | bytes 1769472 | tf_op jit(solution)/shard_map/all_to_all | solution.py:476
  27.5 21.7 %all-to-all-done = bf16[8,144,384]{2,1,0:T(8,128)(2,1)} async-done(((bf16[8,144,384]{2,1,0:T(8,128)(2,1)}), bf16[8,144,384]{2,1,0:T(8,128)(2,1)}, u32[]{:S(2)}, u32[]{:S(2)}) %all-to-all-start) | async-done | bytes 884768 | tf_op jit(solution)/shard_map/all_to_all | solution.py:476
  51.0 2.1 slice.210
  55.4 70.3 %shard_map.381 = (bf16[1024,128]{1,0:T(8,128)(2,1)S(1)}, f32[2,1024,256]{2,1,0:T(8,128)}, f32[2,1024,256]{2,1,0:T(8,128)}, f32[2,1024,64]{2,1,0:T(8,128)S(1)}, f...) custom-call(bf16[1024,384]{1,0:T(8,128)(2,1)S(1)} %bitcast.281, ...), custom_call_target="tpu_custom_call" | custom-call | tf_op jit(solution)/shard_map/pallas_call | solution.py:106
  130.0 4.4 all-to-all-start.1
  134.3 2.5 fusion.92
  136.8 6.0 %all-to-all-done.1 = bf16[8,128,128]{2,1,0:T(8,128)(2,1)} async-done(((bf16[8,128,128]{2,1,0:T(8,128)(2,1)}), bf16[8,128,128]{2,1,0:T(8,128)(2,1)}, u32[]{:S(2)}, u32[]{:S(2)}) %all-to-all-start.1) | async-done | bytes 262176 | tf_op jit(solution)/shard_map/all_to_all | solution.py:476
  144.7 1.7 multiply_reduce_fusion.2
  147.3 1.6 collective-permute-start
  148.9 4.2 collective-permute-done
  153.2 1.6 collective-permute-start.2
  154.7 5.7 %collective-permute-done.2 = bf16[128,768]{1,0:T(8,128)(2,1)S(1)} collective-permute-done((bf16[128,768]{1,0:T(8,128)(2,1)S(1)}, bf16[128,768]{1,0:T(8,128)(2,1)S(1)}, u32[]{:S(2)}, u32[]{:S(2)}) %collective-permute-start.2) | collective-permute-done | bytes 196640 | tf_op jit(solution)/shard_map/ppermute | solution.py:278
  163.0 1.8 multiply_convert_fusion
  168.0 2.0 collective-permute-done.4
  171.4 1.6 collective-permute-start.5
  173.0 1.5 convolution_convert_fusion.1
  174.5 3.9 collective-permute-done.5
  182.5 2.5 pad_maximum_fusion
  185.0 2.8 fusion.3
  188.9 4.2 all-to-all-start.2
  193.1 1.9 convolution_convert_fusion
  196.9 1.5 convolution_convert_fusion.3
  198.4 4.3 all-to-all-done.2
  203.4 4.3 all-to-all-start.3
  208.1 2.3 bitcast_add_fusion
  212.7 1.5 collective-permute-start.9
  214.2 2.6 convolution_convert_fusion.2
  216.9 10.4 %collective-permute-done.9 = bf16[384,768]{1,0:T(8,128)(2,1)} collective-permute-done((bf16[384,768]{1,0:T(8,128)(2,1)}, bf16[384,768]{1,0:T(8,128)(2,1)}, u32[]{:S(2)}, u32[]{:S(2)}) %collective-permute-start.9) | collective-permute-done | bytes 589856 | tf_op jit(solution)/shard_map/ppermute | solution.py:278
  227.3 2.0 fusion.4
  235.5 67.1 %shard_map.382 = (bf16[1024,384]{1,0:T(8,128)(2,1)S(1)}, f32[1024,2]{1,0:T(8,128)S(1)}, f32[2,64,256]{2,1,0:T(8,128)S(1)}, f32[2,1,256]{2,1,0:T(1,128)S(1)}, f32...) custom-call(bf16[1024,384]{1,0:T(8,128)(2,1)S(1)} %bitcast.282, ...), custom_call_target="tpu_custom_call" | custom-call | tf_op jit(solution)/shard_map/pallas_call | solution.py:238
  309.4 1.8 reshape.290
  311.2 1.7 copy.147
  312.8 1.8 slice.177
  315.3 5.4 %all-reduce.15.cloned.1.call-done = (bf16[384,768]{1,0:T(8,128)(2,1)}, bf16[768,512]{1,0:T(8,128)(2,1)}) async-done(((bf16[384,768]{1,0:T(8,128)(2,1)}, bf16[768,512]{1,0:T(8,128)(2,1)}), (bf16[384,768]{1,0:T(8,128)(2,1)}, bf16[768,512]{1,0:T(8,128)(2,1)})) %all-reduce.15.cloned.1.call-update) | async-done | bytes 1376272 | tf_op jit(solution)/shard_map/psum | solution.py:590
  320.8 1.6 fusion.63
  322.6 1.8 fusion.95
  326.6 2.4 reduce_sum.220
  329.1 1.7 collective-permute-start.22
  330.7 2.4 fusion.94
  335.4 1.5 collective-permute-start.7
  336.9 4.3 collective-permute-done.22
  343.6 1.5 collective-permute-start.11
  348.5 4.5 all-to-all-start.4
  353.0 2.6 convert_element_type.238
  356.6 2.9 collective-permute-start.12
  360.6 1.5 collective-permute-start.24
  362.2 20.3 %collective-permute-done.12 = bf16[240,384]{1,0:T(8,128)(2,1)S(1)} collective-permute-done((bf16[240,384]{1,0:T(8,128)(2,1)S(1)}, bf16[240,384]{1,0:T(8,128)(2,1)S(1)}, u32[]{:S(2)}, u32[]{:S(2)}) %collective-permute-start.12) | collective-permute-done | bytes 184352 | tf_op jit(solution)/shard_map/ppermute | solution.py:278
  385.2 6.0 %collective-permute-done.13 = bf16[2,240,384]{2,1,0:T(8,128)(2,1)S(1)} collective-permute-done((bf16[2,240,384]{2,1,0:T(8,128)(2,1)S(1)}, bf16[2,240,384]{2,1,0:T(8,128)(2,1)S(1)}, u32[]{:S(2)}, u32[]{:S(2)}) %collective-permute-start.13) | collective-permute-done | bytes 368672 | tf_op jit(solution)/shard_map/ppermute | solution.py:278
  391.4 1.6 collective-permute-start.17
  393.7 2.3 collective-permute-start.14
  399.1 3.0 copy.157
  408.4 2.0 fusion.87
  410.5 1.8 copy.170
  413.0 1.8 copy.169
  414.8 1.8 copy.168
  416.6 1.5 fusion.59
  427.3 1.4 select_bitcast_fusion.1
  428.7 2.8 fusion.54
  431.5 2.5 fusion.85
  434.3 1.8 pad_maximum_fusion.2.b_ref
  436.6 2.1 pad_maximum_fusion.1.a_ref
  438.6 6.9 %shard_map.383 = (f32[768,768]{1,0:T(8,128)}, f32[768,768]{1,0:T(8,128)}, f32[768,768]{1,0:T(8,128)}, f32[768,1]{1,0:T(8,128)S(1)}, f32[3,2,64,256]{3,2,1,0:T(8,128)S(1)}, /*index=5*/f32[4,8,16,128]{3,2,1,0:T(8,128)S(1)}) custom-call(s32[1]{0:T(128)} %bitcast.39.me_ref, bf16[2,2,8,128,384]{4,3,2,1,0:T(8,128)(2,1)} %pad_maximum_fusion.1.a_ref, ...), custom_call_target="tpu_custom_call" | custom-call | tf_op jit(solution)/shard_map/pallas_call | solution.py:422
  450.6 1.8 slice_bitcast_fusion
  (456 shorter events, 94.2 us)
Async XLA Ops:
  7.2 137.5 %copy-start = (bf16[768,768]{1,0:T(8,128)(2,1)S(1)}, bf16[768,768]{1,0:T(8,128)(2,1)}, u32[]{:S(2)}) copy-start(bf16[768,768]{1,0:T(8,128)(2,1)} %param.36) | copy-start | bytes 3538948
  7.2 7.7 %copy-start.66 = (bf16[1,128,768]{2,1,0:T(8,128)(2,1)S(1)}, bf16[1,128,768]{2,1,0:T(8,128)(2,1)}, u32[]{:S(2)}) copy-start(bf16[1,128,768]{2,1,0:T(8,128)(2,1)} %param.22) | copy-start | bytes 589828
  7.2 7.8 %copy-start.104 = (f32[768]{0:T(1024)S(1)}, f32[768]{0:T(1024)}, u32[]{:S(2)}) copy-start(f32[768]{0:T(1024)} %param.23) | copy-start | bytes 9220
  7.2 45.9 %all-gather.3.cloned.1.call-start = ((), (), s32[]{:S(2)}) async-start(), calls=%async_computation.5 | async-start | bytes 2211840 | tf_op jit(solution)/shard_map/all_gather | solution.py:492
  19.5 29.7 %all-to-all-start = ((bf16[8,144,384]{2,1,0:T(8,128)(2,1)}), bf16[8,144,384]{2,1,0:T(8,128)(2,1)}, u32[]{:S(2)}, u32[]{:S(2)}) async-start(bf16[8,144,384]{2,1,0:T(8,128)(2,1)} %fusion.10), calls=%async_computation | async-start | bytes 1769472 | tf_op jit(solution)/shard_map/all_to_all | solution.py:476
  26.8 103.2 %all-gather.5.cloned.1.call-start = ((), (), s32[]{:S(2)}) async-start(), calls=%async_computation.6 | async-start | bytes 1769472 | tf_op jit(solution)/shard_map/all_gather | solution.py:532
  130.0 14.7 %copy-start.101 = (f32[768]{0:T(1024)S(1)}, f32[768]{0:T(1024)}, u32[]{:S(2)}) copy-start(f32[768]{0:T(1024)} %param.37) | copy-start | bytes 9220
  130.0 12.9 %all-to-all-start.1 = ((bf16[8,128,128]{2,1,0:T(8,128)(2,1)}), bf16[8,128,128]{2,1,0:T(8,128)(2,1)}, u32[]{:S(2)}, u32[]{:S(2)}) async-start(bf16[8,128,128]{2,1,0:T(8,128)(2,1)} %bitcast.287), calls=%async_computation.1 | async-start | bytes 524288 | tf_op jit(solution)/shard_map/all_to_all | solution.py:476
  144.7 8.4 %copy-start.81 = (bf16[1,128,768]{2,1,0:T(8,128)(2,1)S(1)}, bf16[1,128,768]{2,1,0:T(8,128)(2,1)}, u32[]{:S(2)}) copy-start(bf16[1,128,768]{2,1,0:T(8,128)(2,1)} %param.43) | copy-start | bytes 589828
  146.4 14.2 %copy-start.130 = (f32[128]{0:T(128)}, f32[128]{0:T(128)S(1)}, u32[]{:S(2)}) copy-start(f32[128]{0:T(128)S(1)} %get-tuple-element.245) | copy-start | bytes 1540
  146.4 14.2 %copy-start.84 = (bf16[768,512]{1,0:T(8,128)(2,1)S(1)}, bf16[768,512]{1,0:T(8,128)(2,1)}, u32[]{:S(2)}) copy-start(bf16[768,512]{1,0:T(8,128)(2,1)} %param.41) | copy-start | bytes 2359300
  146.5 14.1 %copy-start.114 = (f32[128]{0:T(128)}, f32[128]{0:T(128)S(1)}, u32[]{:S(2)}) copy-start(f32[128]{0:T(128)S(1)} %fusion.73) | copy-start | bytes 1540
  147.3 13.9 %copy-start.78 = (bf16[128,768]{1,0:T(8,128)(2,1)}, bf16[128,768]{1,0:T(8,128)(2,1)S(1)}, u32[]{:S(2)}) copy-start(bf16[128,768]{1,0:T(8,128)(2,1)S(1)} %multiply_convert_fusion.2) | copy-start | bytes 589828
  147.3 5.7 %collective-permute-start = (bf16[128,768]{1,0:T(8,128)(2,1)S(1)}, bf16[128,768]{1,0:T(8,128)(2,1)S(1)}, u32[]{:S(2)}, u32[]{:S(2)}) collective-permute-start(bf16[128,768]{1,0:T(8,128)(2,1)S(1)} %multiply_convert_fusion.2), channel_id=1, source_target_pairs={{0,2},{1,3},{2,0},{3,1},{4,6},{5,7},{6,4},{7,5},{8,10},{9,11},{10,... | collective-permute-start | bytes 589832 | tf_op jit(solution)/shard_map/ppermute | solution.py:278
  153.0 8.2 %copy-start.95 = (bf16[128,768]{1,0:T(8,128)(2,1)}, bf16[128,768]{1,0:T(8,128)(2,1)S(1)}, u32[]{:S(2)}) copy-start(bf16[128,768]{1,0:T(8,128)(2,1)S(1)} %collective-permute-done) | copy-start | bytes 589828
  153.1 7.5 %collective-permute-start.1 = (bf16[256,768]{1,0:T(8,128)(2,1)S(1)}, bf16[256,768]{1,0:T(8,128)(2,1)S(1)}, u32[]{:S(2)}, u32[]{:S(2)}) collective-permute-start(bf16[256,768]{1,0:T(8,128)(2,1)S(1)} %pad_maximum_fusion.13), channel_id=1, source_target_pairs={{0,1},{1,0},{2,3},{3,2},{4,5},{5,4},{6,7},{7,6},{8,9},{9,8},{10,11... | collective-permute-start | bytes 1179656 | tf_op jit(solution)/shard_map/ppermute | solution.py:278
  153.2 7.3 %collective-permute-start.2 = (bf16[128,768]{1,0:T(8,128)(2,1)S(1)}, bf16[128,768]{1,0:T(8,128)(2,1)S(1)}, u32[]{:S(2)}, u32[]{:S(2)}) collective-permute-start(bf16[128,768]{1,0:T(8,128)(2,1)S(1)} %bitcast.312), channel_id=1, source_target_pairs={{0,2},{1,3},{2,0},{3,1},{4,6},{5,7},{6,4},{7,5},{8,10},{9,11},{10,... | collective-permute-start | bytes 589832 | tf_op jit(solution)/shard_map/ppermute | solution.py:278
  160.5 1.9 collective-permute-start.3
  168.0 2.1 collective-permute-start.4
  171.3 7.1 %copy-start.38 = (f32[128,768]{1,0:T(8,128)S(1)}, f32[128,768]{1,0:T(8,128)}, u32[]{:S(2)}) copy-start(f32[128,768]{1,0:T(8,128)} %copy-done.37) | copy-start | bytes 1179652
  171.4 7.0 %copy-start.115 = (f32[128]{0:T(128)S(1)}, f32[128]{0:T(128)}, u32[]{:S(2)}) copy-start(f32[128]{0:T(128)} %copy-done.114) | copy-start | bytes 1540
  171.4 7.8 %copy-start.131 = (f32[128]{0:T(128)S(1)}, f32[128]{0:T(128)}, u32[]{:S(2)}) copy-start(f32[128]{0:T(128)} %copy-done.130) | copy-start | bytes 1540
  171.4 7.8 %copy-start.82 = (bf16[1,128,768]{2,1,0:T(8,128)(2,1)S(1)}, bf16[1,128,768]{2,1,0:T(8,128)(2,1)}, u32[]{:S(2)}) copy-start(bf16[1,128,768]{2,1,0:T(8,128)(2,1)} %param.43) | copy-start | bytes 589828
  171.4 7.0 %collective-permute-start.5 = (bf16[128,768]{1,0:T(8,128)(2,1)S(1)}, bf16[128,768]{1,0:T(8,128)(2,1)S(1)}, u32[]{:S(2)}, u32[]{:S(2)}) collective-permute-start(bf16[128,768]{1,0:T(8,128)(2,1)S(1)} %slice.302), channel_id=1, source_target_pairs={{0,2},{1,3},{2,0},{3,1},{4,6},{5,7},{6,4},{7,5},{8,10},{9,11},{10,... | collective-permute-start | bytes 589832 | tf_op jit(solution)/shard_map/ppermute | solution.py:278
  187.8 20.3 %collective-permute-start.8 = (bf16[2,384,768]{2,1,0:T(8,128)(2,1)}, bf16[2,384,768]{2,1,0:T(8,128)(2,1)}, u32[]{:S(2)}, u32[]{:S(2)}) collective-permute-start(bf16[2,384,768]{2,1,0:T(8,128)(2,1)} %fusion.3), channel_id=1, source_target_pairs={{0,1},{1,0},{2,3},{3,2},{4,5},{5,4},{6,7},{7,6},{8,9},{9,8},{10,11... | collective-permute-start | bytes 3538952 | tf_op jit(solution)/shard_map/ppermute | solution.py:278
  188.9 13.8 %all-to-all-start.2 = ((bf16[8,128,128]{2,1,0:T(8,128)(2,1)}), bf16[8,128,128]{2,1,0:T(8,128)(2,1)S(1)}, u32[]{:S(2)}, u32[]{:S(2)}) async-start(bf16[8,128,128]{2,1,0:T(8,128)(2,1)} %bitcast_bitcast_fusion), calls=%async_computation.2 | async-start | bytes 524288 | tf_op jit(solution)/shard_map/all_to_all | solution.py:476
  203.4 117.4 %all-to-all-start.3 = ((bf16[8,128,768]{2,1,0:T(8,128)(2,1)}), bf16[8,128,768]{2,1,0:T(8,128)(2,1)}, u32[]{:S(2)}, u32[]{:S(2)}) async-start(bf16[8,128,768]{2,1,0:T(8,128)(2,1)} %pad_maximum_fusion.3), calls=%async_computation.3 | async-start | bytes 3145728 | tf_op jit(solution)/shard_map/all_to_all | solution.py:476
  207.7 113.0 %all-reduce.15.cloned.1.call-start = ((), (), s32[]{:S(2)}) async-start(), calls=%async_computation.7 | async-start | bytes 2752512 | tf_op jit(solution)/shard_map/psum | solution.py:590
  212.7 14.6 %collective-permute-start.9 = (bf16[384,768]{1,0:T(8,128)(2,1)}, bf16[384,768]{1,0:T(8,128)(2,1)}, u32[]{:S(2)}, u32[]{:S(2)}) collective-permute-start(bf16[384,768]{1,0:T(8,128)(2,1)} %fusion.18), channel_id=1, source_target_pairs={{0,2},{1,3},{2,0},{3,1},{4,6},{5,7},{6,4},{7,5},{8,10},{9,11},{10,... | collective-permute-start | bytes 1769480 | tf_op jit(solution)/shard_map/ppermute | solution.py:278
  214.2 13.1 %copy-start.36 = (f32[2,384,768]{2,1,0:T(8,128)S(1)}, f32[2,384,768]{2,1,0:T(8,128)}, u32[]{:S(2)}) copy-start(f32[2,384,768]{2,1,0:T(8,128)} %copy-done.35) | copy-start | bytes 7077892
  216.9 12.5 %copy-start.103 = (f32[768]{0:T(1024)S(1)}, f32[768]{0:T(1024)}, u32[]{:S(2)}) copy-start(f32[768]{0:T(1024)} %get-tuple-element.176) | copy-start | bytes 9220
  216.9 12.5 %copy-start.117 = (f32[768]{0:T(1024)S(1)}, f32[768]{0:T(1024)}, u32[]{:S(2)}) copy-start(f32[768]{0:T(1024)} %get-tuple-element.178) | copy-start | bytes 9220
  216.9 12.5 %copy-start.116 = (f32[768]{0:T(1024)S(1)}, f32[768]{0:T(1024)}, u32[]{:S(2)}) copy-start(f32[768]{0:T(1024)} %get-tuple-element.180) | copy-start | bytes 9220
  216.9 13.2 %copy-start.14 = (f32[2,1024,64]{2,1,0:T(8,128)S(1)}, f32[2,1024,64]{2,1,0:T(8,128)}, u32[]{:S(2)}) copy-start(f32[2,1024,64]{2,1,0:T(8,128)} %copy-done.13) | copy-start | bytes 1572868
  307.6 13.2 %copy-start.22 = (f32[1024,2]{1,0:T(8,128)S(1)}, f32[1024,2]{1,0:T(8,128)}, u32[]{:S(2)}) copy-start(f32[1024,2]{1,0:T(8,128)} %copy-done.21) | copy-start | bytes 24580
  307.6 13.2 %copy-start.49 = (f32[8,128,2]{2,1,0:T(8,128)S(1)}, f32[8,128,2]{2,1,0:T(8,128)}, u32[]{:S(2)}) copy-start(f32[8,128,2]{2,1,0:T(8,128)} %copy.135) | copy-start | bytes 24580
  309.4 13.1 %copy-start.29 = (f32[2,1,64]{2,1,0:T(1,128)S(1)}, f32[2,1,64]{2,1,0:T(1,128)}, u32[]{:S(2)}) copy-start(f32[2,1,64]{2,1,0:T(1,128)} %copy-done.28) | copy-start | bytes 1540
  309.4 13.1 %copy-start.31 = (f32[2,1,64]{2,1,0:T(1,128)S(1)}, f32[2,1,64]{2,1,0:T(1,128)}, u32[]{:S(2)}) copy-start(f32[2,1,64]{2,1,0:T(1,128)} %copy-done.30) | copy-start | bytes 1540
  314.6 18.7 %collective-permute-start.6 = (bf16[256,768]{1,0:T(8,128)(2,1)}, bf16[256,768]{1,0:T(8,128)(2,1)}, u32[]{:S(2)}, u32[]{:S(2)}) collective-permute-start(bf16[256,768]{1,0:T(8,128)(2,1)} %slice.177), channel_id=1, source_target_pairs={{0,1},{1,0},{2,3},{3,2},{4,5},{5,4},{6,7},{7,6},{8,9},{9,8},{10,11... | collective-permute-start | bytes 1179656 | tf_op jit(solution)/shard_map/ppermute | solution.py:278
  326.6 6.5 %copy-start.62 = (f32[2,2,48,384]{3,2,1,0:T(8,128)}, f32[2,2,48,384]{3,2,1,0:T(8,128)S(1)}, u32[]{:S(2)}) copy-start(f32[2,2,48,384]{3,2,1,0:T(8,128)S(1)} %concatenate.73) | copy-start | bytes 884740
  329.1 12.2 %collective-permute-start.22 = (bf16[128,768]{1,0:T(8,128)(2,1)}, bf16[128,768]{1,0:T(8,128)(2,1)S(1)}, u32[]{:S(2)}, u32[]{:S(2)}) collective-permute-start(bf16[128,768]{1,0:T(8,128)(2,1)} %reduce_sum.220), channel_id=1, source_target_pairs={{0,16},{4,20},{8,24},{12,28},{16,0},{20,4},{24,8},{28,12},{1,17},{... | collective-permute-start | bytes 589832 | tf_op jit(solution)/shard_map/ppermute | solution.py:278
  333.1 8.1 %copy-start.83 = (bf16[128,768]{1,0:T(8,128)(2,1)S(1)}, bf16[128,768]{1,0:T(8,128)(2,1)}, u32[]{:S(2)}) copy-start(bf16[128,768]{1,0:T(8,128)(2,1)} %reduce_sum.220) | copy-start | bytes 589828
  333.2 9.6 %copy-start.63 = (f32[2,2,48,384]{3,2,1,0:T(8,128)S(1)}, f32[2,2,48,384]{3,2,1,0:T(8,128)}, u32[]{:S(2)}) copy-start(f32[2,2,48,384]{3,2,1,0:T(8,128)} %copy-done.62) | copy-start | bytes 884740
  333.2 9.6 %collective-permute-start.10 = (bf16[2,240,384]{2,1,0:T(8,128)(2,1)S(1)}, bf16[2,240,384]{2,1,0:T(8,128)(2,1)S(1)}, u32[]{:S(2)}, u32[]{:S(2)}) collective-permute-start(bf16[2,240,384]{2,1,0:T(8,128)(2,1)S(1)} %fusion.52), channel_id=1, source_target_pairs={{0,1},{1,0},{2,3},{3,2},{4,5},{5,4},{6,7},{7,6},{8,9},{9,8},{10,11... | collective-permute-start | bytes 1105928 | tf_op jit(solution)/shard_map/ppermute | solution.py:278
  335.4 9.7 %collective-permute-start.7 = (bf16[128,768]{1,0:T(8,128)(2,1)S(1)}, bf16[128,768]{1,0:T(8,128)(2,1)S(1)}, u32[]{:S(2)}, u32[]{:S(2)}) collective-permute-start(bf16[128,768]{1,0:T(8,128)(2,1)S(1)} %slice.301), channel_id=1, source_target_pairs={{0,2},{1,3},{2,0},{3,1},{4,6},{5,7},{6,4},{7,5},{8,10},{9,11},{10,... | collective-permute-start | bytes 589832 | tf_op jit(solution)/shard_map/ppermute | solution.py:278
  342.8 16.7 %collective-permute-start.23 = (bf16[2,128,768]{2,1,0:T(8,128)(2,1)}, bf16[2,128,768]{2,1,0:T(8,128)(2,1)}, u32[]{:S(2)}, u32[]{:S(2)}) collective-permute-start(bf16[2,128,768]{2,1,0:T(8,128)(2,1)} %pad_maximum_fusion.15), channel_id=1, source_target_pairs={{0,8},{4,12},{8,0},{12,4},{16,24},{20,28},{24,16},{28,20},{1,9},{5... | collective-permute-start | bytes 1179656 | tf_op jit(solution)/shard_map/ppermute | solution.py:278
  343.6 12.0 %collective-permute-start.11 = (bf16[240,384]{1,0:T(8,128)(2,1)}, bf16[240,384]{1,0:T(8,128)(2,1)}, u32[]{:S(2)}, u32[]{:S(2)}) collective-permute-start(bf16[240,384]{1,0:T(8,128)(2,1)} %fusion.61), channel_id=1, source_target_pairs={{0,2},{1,3},{2,0},{3,1},{4,6},{5,7},{6,4},{7,5},{8,10},{9,11},{10,... | collective-permute-start | bytes 552968 | tf_op jit(solution)/shard_map/ppermute | solution.py:278
  346.9 35.7 %collective-permute-start.20 = (bf16[384,768]{1,0:T(8,128)(2,1)}, bf16[384,768]{1,0:T(8,128)(2,1)}, u32[]{:S(2)}, u32[]{:S(2)}) collective-permute-start(bf16[384,768]{1,0:T(8,128)(2,1)} %get-tuple-element.79), channel_id=1, source_target_pairs={{0,2},{1,3},{2,0},{3,1},{4,6},{5,7},{6,4},{7,5},{8,10},{9,11},{10,... | collective-permute-start | bytes 1769480 | tf_op jit(solution)/shard_map/ppermute | solution.py:278
  348.5 59.9 %all-to-all-start.4 = ((bf16[8,144,384]{2,1,0:T(8,128)(2,1)}), bf16[8,144,384]{2,1,0:T(8,128)(2,1)}, u32[]{:S(2)}, u32[]{:S(2)}) async-start(bf16[8,144,384]{2,1,0:T(8,128)(2,1)} %fusion.11), calls=%async_computation.4 | async-start | bytes 1769472 | tf_op jit(solution)/shard_map/all_to_all | solution.py:476
  353.0 6.5 %copy-start.69 = (bf16[1,128,768]{2,1,0:T(8,128)(2,1)S(1)}, bf16[1,128,768]{2,1,0:T(8,128)(2,1)}, u32[]{:S(2)}) copy-start(bf16[1,128,768]{2,1,0:T(8,128)(2,1)} %copy-done.68) | copy-start | bytes 589828
  353.0 6.5 %copy-start.71 = (bf16[1,128,768]{2,1,0:T(8,128)(2,1)S(1)}, bf16[1,128,768]{2,1,0:T(8,128)(2,1)}, u32[]{:S(2)}) copy-start(bf16[1,128,768]{2,1,0:T(8,128)(2,1)} %copy-done.70) | copy-start | bytes 589828
  356.6 25.8 %collective-permute-start.12 = (bf16[240,384]{1,0:T(8,128)(2,1)S(1)}, bf16[240,384]{1,0:T(8,128)(2,1)S(1)}, u32[]{:S(2)}, u32[]{:S(2)}) collective-permute-start(bf16[240,384]{1,0:T(8,128)(2,1)S(1)} %fusion.53), channel_id=1, source_target_pairs={{0,16},{4,20},{8,24},{12,28},{16,0},{20,4},{24,8},{28,12},{1,17},{... | collective-permute-start | bytes 552968 | tf_op jit(solution)/shard_map/ppermute | solution.py:278
  360.5 22.1 %copy-start.85 = (bf16[384,768]{1,0:T(8,128)(2,1)S(1)}, bf16[384,768]{1,0:T(8,128)(2,1)}, u32[]{:S(2)}) copy-start(bf16[384,768]{1,0:T(8,128)(2,1)} %get-tuple-element.79) | copy-start | bytes 1769476
  360.6 35.4 %collective-permute-start.24 = (bf16[2,2,128,768]{3,2,0,1:T(8,128)(2,1)S(1)}, bf16[2,2,128,768]{3,2,0,1:T(8,128)(2,1)S(1)}, u32[]{:S(2)}, u32[]{:S(2)}) collective-permute-start(bf16[2,2,128,768]{3,2,0,1:T(8,128)(2,1)S(1)} %pad_maximum_fusion.11), channel_id=1, source_target_pairs={{0,4},{4,0},{8,12},{12,8},{16,20},{20,16},{24,28},{28,24},{1,5},{5... | collective-permute-start | bytes 2359304 | tf_op jit(solution)/shard_map/ppermute | solution.py:278
  382.5 8.7 %collective-permute-start.13 = (bf16[2,240,384]{2,1,0:T(8,128)(2,1)S(1)}, bf16[2,240,384]{2,1,0:T(8,128)(2,1)S(1)}, u32[]{:S(2)}, u32[]{:S(2)}) collective-permute-start(bf16[2,240,384]{2,1,0:T(8,128)(2,1)S(1)} %pad_maximum_fusion.16), channel_id=1, source_target_pairs={{0,8},{4,12},{8,0},{12,4},{16,24},{20,28},{24,16},{28,20},{1,9},{5... | collective-permute-start | bytes 1105928 | tf_op jit(solution)/shard_map/ppermute | solution.py:278
  385.0 41.3 %collective-permute-start.21 = (bf16[2,384,768]{2,1,0:T(8,128)(2,1)}, bf16[2,384,768]{2,1,0:T(8,128)(2,1)}, u32[]{:S(2)}, u32[]{:S(2)}) collective-permute-start(bf16[2,384,768]{2,1,0:T(8,128)(2,1)} %pad_maximum_fusion.7), channel_id=1, source_target_pairs={{0,1},{1,0},{2,3},{3,2},{4,5},{5,4},{6,7},{7,6},{8,9},{9,8},{10,11... | collective-permute-start | bytes 3538952 | tf_op jit(solution)/shard_map/ppermute | solution.py:278
  391.4 10.7 %collective-permute-start.17 = (bf16[2,2,112,384]{3,2,1,0:T(8,128)(2,1)S(1)}, bf16[2,2,112,384]{3,2,1,0:T(8,128)(2,1)}, u32[]{:S(2)}, u32[]{:S(2)}) collective-permute-start(bf16[2,2,112,384]{3,2,1,0:T(8,128)(2,1)S(1)} %pad_maximum_fusion.17), channel_id=1, source_target_pairs={{0,2},{1,3},{2,0},{3,1},{4,6},{5,7},{6,4},{7,5},{8,10},{9,11},{10,... | collective-permute-start | bytes 1032200 | tf_op jit(solution)/shard_map/ppermute | solution.py:278
  393.7 10.6 %collective-permute-start.14 = (bf16[2,2,128,384]{3,2,1,0:T(8,128)(2,1)}, bf16[2,2,128,384]{3,2,1,0:T(8,128)(2,1)}, u32[]{:S(2)}, u32[]{:S(2)}) collective-permute-start(bf16[2,2,128,384]{3,2,1,0:T(8,128)(2,1)} %fusion.45), channel_id=1, source_target_pairs={{0,4},{4,0},{8,12},{12,8},{16,20},{20,16},{24,28},{28,24},{1,5},{5... | collective-permute-start | bytes 1179656 | tf_op jit(solution)/shard_map/ppermute | solution.py:278
  404.2 18.0 %collective-permute-start.18 = (bf16[2,2,2,112,384]{4,3,2,1,0:T(8,128)(2,1)}, bf16[2,2,2,112,384]{4,3,2,1,0:T(8,128)(2,1)}, u32[]{:S(2)}, u32[]{:S(2)}) collective-permute-start(bf16[2,2,2,112,384]{4,3,2,1,0:T(8,128)(2,1)} %pad_maximum_fusion.12), channel_id=1, source_target_pairs={{0,4},{4,0},{8,12},{12,8},{16,20},{20,16},{24,28},{28,24},{1,5},{5... | collective-permute-start | bytes 2064392 | tf_op jit(solution)/shard_map/ppermute | solution.py:278
  407.1 9.4 %copy-start.4 = (bf16[768,768]{1,0:T(8,128)(2,1)S(1)}, bf16[768,768]{1,0:T(8,128)(2,1)}, u32[]{:S(2)}) copy-start(bf16[768,768]{1,0:T(8,128)(2,1)} %wq_ref.1) | copy-start | bytes 3538948
  407.1 17.3 %collective-permute-start.15 = (bf16[2,2,2,128,384]{4,3,2,1,0:T(8,128)(2,1)}, bf16[2,2,2,128,384]{4,3,2,1,0:T(8,128)(2,1)}, u32[]{:S(2)}, u32[]{:S(2)}) collective-permute-start(bf16[2,2,2,128,384]{4,3,2,1,0:T(8,128)(2,1)} %pad_maximum_fusion.10), channel_id=1, source_target_pairs={{0,2},{1,3},{2,0},{3,1},{4,6},{5,7},{6,4},{7,5},{8,10},{9,11},{10,... | collective-permute-start | bytes 2359304 | tf_op jit(solution)/shard_map/ppermute | solution.py:278
  423.8 10.2 %collective-permute-start.19 = (bf16[2,2,2,2,112,384]{5,4,3,2,1,0:T(8,128)(2,1)S(1)}, bf16[2,2,2,2,112,384]{5,4,3,2,1,0:T(8,128)(2,1)S(1)}, u32[]{:S(2)}, u32[]{:S(2)}) collective-permute-start(bf16[2,2,2,2,112,384]{5,4,3,2,1,0:T(8,128)(2,1)S(1)} %pad_maximum_fusion.6), channel_id=1, source_target_pairs={{0,1},{1,0},{2,3},{3,2},{4,5},{5,4},{6,7},{7,6},{8,9},{9,8},{10,11... | collective-permute-start | bytes 4128776 | tf_op jit(solution)/shard_map/ppermute | solution.py:278
  426.2 10.0 %collective-permute-start.16 = (bf16[2,2,2,2,128,384]{5,4,3,2,1,0:T(8,128)(2,1)S(1)}, bf16[2,2,2,2,128,384]{5,4,3,2,1,0:T(8,128)(2,1)S(1)}, u32[]{:S(2)}, u32[]{:S(2)}) collective-permute-start(bf16[2,2,2,2,128,384]{5,4,3,2,1,0:T(8,128)(2,1)S(1)} %pad_maximum_fusion.4), channel_id=1, source_target_pairs={{0,1},{1,0},{2,3},{3,2},{4,5},{5,4},{6,7},{7,6},{8,9},{9,8},{10,11... | collective-permute-start | bytes 4718600 | tf_op jit(solution)/shard_map/ppermute | solution.py:278
  438.6 14.5 %copy-start.1 = (bf16[768,768]{1,0:T(8,128)(2,1)S(1)}, bf16[768,768]{1,0:T(8,128)(2,1)}, u32[]{:S(2)}) copy-start(bf16[768,768]{1,0:T(8,128)(2,1)} %param.36) | copy-start | bytes 3538948
  (102 other events, 195.2 us)
Sparse Core Ops, SparseCore 0:
  15.0 23.4 all-gather.2
  41.2 44.1 all-gather.4
  229.4 91.2 all-reduce.14

commit v3 on v2

v3 whole, which is shorter than its diff:
```python
from functools import partial

import jax
import jax.numpy as jnp
from jax import lax
from jax.sharding import PartitionSpec as P
from jax.experimental import pallas as pl
from jax.experimental.pallas import tpu as pltpu
C0=0.7978845608028654
C1=0.044715
EPS=1e-6
RATE_SCALE=0.25
B=16
CH=128
NB=CH//B
LOW=jnp.bfloat16
F=jnp.float32
def nn(a,b): return lax.dot_general(a.astype(LOW),b.astype(LOW),(((1,),(0,)),((),())),preferred_element_type=F)
def nt(a,b): return lax.dot_general(a.astype(LOW),b.astype(LOW),(((1,),(1,)),((),())),preferred_element_type=F)
def tn(a,b): return lax.dot_general(a.astype(LOW),b.astype(LOW),(((0,),(0,)),((),())),preferred_element_type=F)
def gelu1(z):
    return z*(0.5+0.5*jnp.tanh(z*(C0+(C0*C1)*(z*z))))
def gelu2(z):
    z2=z*z
    t=jnp.tanh(z*(C0+(C0*C1)*z2))
    h=0.5+0.5*t
    x=z*h
    return x,h+x*(1-t)*(C0+(3*C0*C1)*z2)
def gelu3(z):
    z2=z*z
    t=jnp.tanh(z*(C0+(C0*C1)*z2))
    u1=C0+(3*C0*C1)*z2
    h=0.5+0.5*t
    h1=h*(1-t)*u1
    x=z*h
    return x,h+z*h1,2*h1+z*(h*(1-t)*(6*C0*C1)*z-2*t*u1*h1)
def lane_masks(C,H,R):
    lane=lax.broadcasted_iota(jnp.int32,(R,C*H),1)
    return [(lane>=H*c)&(lane<H*c+H) for c in range(C)]
def expand(C,x,masks):
    if C==1: return x
    zero=jnp.zeros((B,x.shape[1]),x.dtype)
    return jnp.concatenate([jnp.where(masks[c],x[B*j:B*j+B],zero) for j in range(x.shape[0]//B) for c in range(C)],0)
def collapse(C,x,masks):
    if C==1: return x
    rows=[]
    for j in range(x.shape[0]//(B*C)):
        y=x[B*C*j:B*C*j+B]
        for c in range(1,C): y=jnp.where(masks[c],x[B*(C*j+c):B*(C*j+c)+B],y)
        rows.append(y)
    return jnp.concatenate(rows,0) if len(rows)>1 else rows[0]
def tile_rows(C,x,n):
    t=jnp.concatenate([jnp.broadcast_to(x[c:c+1],(B,x.shape[1])) for c in range(C)],0)
    return jnp.concatenate([t]*n,0) if n>1 else t
def fill_masks(C,TRI,BLK,back):
    n=CH*C
    r=lax.broadcasted_iota(jnp.int32,(n,n),0); c=lax.broadcasted_iota(jnp.int32,(n,n),1)
    rs,cs=r//(B*C),c//(B*C)
    same=((r//B)%C)==((c//B)%C)
    tri=same&((cs<rs)|((cs==rs)&((c%B)<=(r%B))))
    TRI[...]=jnp.where(tri,1.0,0.0)
    BLK[...]=jnp.where(same&(cs<rs),1.0,0.0)
    if back is not None: back[...]=jnp.where(same&(cs>rs),1.0,0.0)
def ones_of(C,H):
    r=lax.broadcasted_iota(jnp.int32,(C*H,C*H),0); c=lax.broadcasted_iota(jnp.int32,(C*H,C*H),1)
    return jnp.where((r//H)==(c//H),1.0/H,0.0).astype(LOW)
def sums_of(C):
    r=lax.broadcasted_iota(jnp.int32,(C,CH*C),0); c=lax.broadcasted_iota(jnp.int32,(C,CH*C),1)
    return jnp.where(((c//B)%C)==r,1.0,0.0).astype(LOW)
def stack_col(C,r):
    return jnp.concatenate([r[B*j:B*j+B,c:c+1] for j in range(r.shape[0]//B) for c in range(C)],0)
def pair_cols(C,H,r,masks):
    y=jnp.broadcast_to(r[:,0:1],(r.shape[0],C*H))
    for c in range(1,C): y=jnp.where(masks[c],r[:,c:c+1],y)
    return y

def rates(C,x_ref,own_ref,H):
    rows=[x_ref[0,CH+c:CH+c+1,:CH].astype(F)+own_ref[c,2*H+1:2*H+2,3*H:3*H+1] for c in range(C)]
    rows=jnp.concatenate(rows+[jnp.zeros((CH-C,CH),F)],0)
    return (jax.nn.sigmoid(rows)*(RATE_SCALE/H)).T

def pair_row(C,H,own_ref,k):
    return jnp.concatenate([own_ref[c,2*H+1:2*H+2,k*H:k*H+H] for c in range(C)],1)

def fwd_kernel(C,H,x_ref,own_ref,
               o_ref,z1_ref,p_ref,zc_ref,z1q_ref,zq_ref,us_ref,w1s_ref,
               W1,B1,U,B2,TRI,BLK,S1,S2,X2,KK,BASE):
    W=C*H; SB=B*C
    @pl.when(pl.program_id(0)==0)
    def _():
        for c in range(C):
            W1[H*c:H*c+H]=own_ref[c,:H]
            u=own_ref[c,H:2*H]
            U[H*c:H*c+H]=u-jnp.sum(u,0,keepdims=True)*(1.0/H)
            B1[c:c+1]=own_ref[c,2*H:2*H+1]
        raw=[own_ref[c,2*H+1:2*H+2,:H] for c in range(C)]
        B2[...]=jnp.concatenate([v-jnp.sum(v,1,keepdims=True)*(1.0/H) for v in raw],1)
        fill_masks(C,TRI,BLK,None)
    m16=lane_masks(C,H,B); m128=lane_masks(C,H,CH)
    ones=ones_of(C,H)
    K=x_ref[0,:CH,W:2*W]
    Kst=expand(C,K,m16); Qst=expand(C,x_ref[0,:CH,:W],m16)
    gam=pair_row(C,H,own_ref,1); bet=pair_row(C,H,own_ref,2); g2=gam*gam
    T=(bet+K.astype(F)-x_ref[0,:CH,2*W:].astype(F))*gam
    R=rates(C,x_ref,own_ref,H)
    RP=pair_cols(C,H,R,m128)
    w1b=W1[...].astype(LOW); w1s_ref[0]=w1b
    b1r=tile_rows(C,B1[...],1)
    uf=U[...]; ub=uf.astype(LOW); u0=ub
    b2=B2[...]; b20=b2
    KK[...]=((nt(Kst,Kst)+1.0)*BLK[...]).astype(LOW)
    BASE[...]=nn(Kst,w1b)
    CT=nn(T,ones)
    g2m=nn(jnp.broadcast_to(g2,(8,W)),ones)[0:1]
    for j in range(NB):
        sl=slice(B*j,B*j+B); st=slice(SB*j,SB*j+SB)
        z1=BASE[st]+b1r
        if j>0: z1=z1-nn(KK[st,:SB*j],S1[:SB*j])
        x2,g1=gelu2(z1)
        x2b=x2.astype(LOW)
        zc=collapse(C,nt(x2b,ub),m16)+b2
        t=T[sl]; zz=zc*zc; zg=zc*g2; ct=CT[sl]; rr=RP[sl]
        mm=nn(jnp.concatenate([zc,zz,zg,zz*g2,zc*t],0),ones)
        mu=mm[0:B]; mzz=mm[B:2*B]; mzg=mm[2*B:3*B]; mzzg=mm[3*B:4*B]; mzt=mm[4*B:]
        s=lax.rsqrt(mzz-mu*mu+EPS)
        m1=s*(mzg-mu*g2m)+ct
        m2=s*(s*(mzzg-2.0*mu*mzg+mu*mu*g2m)+mzt-mu*ct)
        zc=zc-mu
        d2=s*(zc*s*(g2-m2)+(t-m1))
        P=nn(expand(C,d2,m16),ub)
        s1=(P*(g1*stack_col(C,R[sl]))).astype(LOW)
        s2=d2*rr
        s2b=expand(C,s2,m16).astype(LOW)
        S1[st]=s1; S2[st]=s2b; X2[st]=x2b
        z1_ref[st]=z1; p_ref[st]=P; zc_ref[sl]=zc
        us_ref[0,j]=ub
        uf=uf-tn(s2b,x2b); ub=uf.astype(LOW)
        b2=b2-jnp.sum(s2,0,keepdims=True)
    U[...]=uf; B2[...]=b2
    S1v=S1[...]
    W1[...]=W1[...]-tn(Kst,S1v)
    B1[...]=B1[...]-nn(sums_of(C),S1v)
    tri=TRI[...]
    A1=(nt(Qst,Kst)+1.0)*tri
    z1q=nn(Qst,w1b)+tile_rows(C,0.0+b1r_src(b1r,C),NB)-nn(A1,S1v)
    x2q=gelu1(z1q).astype(LOW)
    A2=(nt(x2q,X2[...])+1.0)*tri
    zq=collapse(C,nt(x2q,u0)-nn(A2,S2[...]),m16)+b20
    zq=zq-nn(zq,ones)
    yq=zq*lax.rsqrt(nn(zq*zq,ones)+EPS)
    o_ref[...]=(x_ref[0,:CH,:W].astype(F)+yq*gam+bet).astype(LOW)
    z1q_ref[...]=z1q; zq_ref[...]=zq

def b1r_src(b1r,C):
    return jnp.concatenate([b1r[B*c:B*c+1] for c in range(C)],0)

def fwd_scan(x,own):
    n,tall,W=x.shape
    W//=3
    C=own.shape[0]; I=own.shape[2]; H=W//C; L=n*CH
    rows=lambda k,w: pl.BlockSpec((k,w),lambda i:(i,0))
    sd=jax.ShapeDtypeStruct
    V=pltpu.VMEM
    return pl.pallas_call(partial(fwd_kernel,C,H),grid=(n,),
        in_specs=[pl.BlockSpec((1,tall,3*W),lambda i:(i,0,0)),pl.BlockSpec(own.shape,lambda i:(0,0,0))],
        out_specs=[rows(CH,W),rows(C*CH,I),rows(C*CH,I),rows(CH,W),rows(C*CH,I),rows(CH,W),
            pl.BlockSpec((1,NB,W,I),lambda i:(i,0,0,0)),pl.BlockSpec((1,W,I),lambda i:(i,0,0))],
        out_shape=[sd((L,W),LOW),sd((C*L,I),F),sd((C*L,I),F),sd((L,W),F),sd((C*L,I),F),sd((L,W),F),sd((n,NB,W,I),LOW),sd((n,W,I),LOW)],
        scratch_shapes=[V((W,I),F),V((C,I),F),V((W,I),F),V((1,W),F),V((C*CH,C*CH),F),V((C*CH,C*CH),F),
            V((C*CH,I),LOW),V((C*CH,W),LOW),V((C*CH,I),LOW),V((C*CH,C*CH),LOW),V((C*CH,I),F)],
        compiler_params=pltpu.CompilerParams(vmem_limit_bytes=48*1024*1024),
    )(x,own)

SLOT=("BASE","DX2","X2","RG1","G1","RPG2","DS2Q","KK","YB","GB","DB","SB","M2B","RED","S2E","S1B","X2Q","DZQ","DZ1Q","DKQ","DQ","KST","QST","T0","RP","PG1","R")

def slot_shapes(C,W,I):
    m=C*CH
    V=pltpu.VMEM
    wide,pair,tall=V((m,I),F),V((CH,W),F),V((m,W),LOW)
    kinds=dict(BASE=wide,DX2=wide,X2=V((m,I),LOW),RG1=wide,G1=wide,RPG2=wide,DS2Q=pair,KK=V((m,m),LOW),YB=pair,GB=pair,DB=pair,SB=pair,M2B=pair,
        RED=V((4*CH,W),F),S2E=tall,S1B=V((m,I),LOW),X2Q=V((m,I),LOW),DZQ=tall,DZ1Q=V((m,I),LOW),DKQ=V((m,W),F),DQ=V((CH,W),LOW),KST=tall,QST=tall,
        T0=pair,RP=pair,PG1=wide,R=V((CH,CH),F))
    return [kinds[name] for name in SLOT]

def bwd_pre(C,H,ins,own_ref,S,TRI,BLKT,gam,bet,dgam_ref,dbet_ref,factor):
    x_ref,do_ref,z1_ref,p_ref,zc_ref,z1q_ref,zq_ref,us_ref,w1s_ref=ins
    W=C*H
    m16=lane_masks(C,H,B); m128=lane_masks(C,H,CH)
    ones=ones_of(C,H)
    g2=gam*gam
    K=x_ref[0,:CH,W:2*W]
    Kst=expand(C,K,m16); Qst=expand(C,x_ref[0,:CH,:W],m16)
    S["KST"][...]=Kst; S["QST"][...]=Qst
    R=rates(C,x_ref,own_ref,H)
    S["R"][...]=R
    RP=pair_cols(C,H,R,m128)
    S["RP"][...]=RP
    dO=do_ref[...].astype(F)
    zq=zq_ref[...]; sq=lax.rsqrt(nn(zq*zq,ones)+EPS); yq=zq*sq
    dyq=dO*gam
    rq=nn(jnp.concatenate([dyq,dyq*yq],0),ones)
    dzq=sq*(dyq-rq[:CH]-yq*rq[CH:])
    dzqb=expand(C,dzq.astype(LOW),m16)
    S["DZQ"][...]=dzqb
    dgam_ref[...]=dgam_ref[...]+factor*jnp.sum(dO*yq,0,keepdims=True)
    dbet_ref[...]=dbet_ref[...]+factor*jnp.sum(dO,0,keepdims=True)
    yield
    zc=zc_ref[...]
    s=lax.rsqrt(nn(zc*zc,ones)+EPS)
    y=zc*s
    t0=bet+K.astype(F)-x_ref[0,:CH,2*W:].astype(F)
    G=y*g2+t0*gam
    red=nn(jnp.concatenate([G,G*y,g2*y,g2*y*y],0),ones)
    m1=red[:CH]; m2=red[CH:2*CH]
    d2=s*(G-m1-y*m2)
    s2=expand(C,(d2*RP).astype(LOW),m16)
    S["YB"][...]=y; S["GB"][...]=G; S["DB"][...]=d2; S["SB"][...]=s; S["M2B"][...]=m2; S["RED"][...]=red; S["S2E"][...]=s2; S["T0"][...]=t0
    yield
    x2,g1,gg2=gelu3(z1_ref[...]); x2=x2.astype(LOW)
    P=p_ref[...]
    RS=stack_col(C,R)
    rg1=RS*g1
    s1=(P*rg1).astype(LOW)
    S["X2"][...]=x2; S["G1"][...]=g1; S["RG1"][...]=rg1; S["RPG2"][...]=RS*(P*gg2); S["PG1"][...]=P*g1; S["S1B"][...]=s1
    yield
    x2q,g1q=gelu2(z1q_ref[...]); x2q=x2q.astype(LOW)
    S["X2Q"][...]=x2q
    A2=((nt(x2q,S["X2"][...])+1.0)*TRI[...]).astype(LOW)
    dA2=(nt(dzqb,s2)*TRI[...]).astype(LOW)
    yield
    dx2q=nn(dzqb,us_ref[0,0])-nn(dA2,S["X2"][...])
    S["DX2"][...]=-tn(dA2,x2q)
    S["DS2Q"][...]=-collapse(C,tn(A2,dzqb),m16)
    dz1qb=(dx2q*g1q).astype(LOW)
    S["DZ1Q"][...]=dz1qb
    yield
    A1=((nt(Qst,Kst)+1.0)*TRI[...]).astype(LOW)
    dA1=(nt(dz1qb,S["S1B"][...])*TRI[...]).astype(LOW)
    S["KK"][...]=((nt(Kst,Kst)+1.0)*BLKT[...]).astype(LOW)
    yield
    S["DQ"][...]=(dO+collapse(C,nt(dz1qb,w1s_ref[0])-nn(dA1,Kst),m16)).astype(LOW)
    S["DKQ"][...]=tn(dA1,Qst)
    S["BASE"][...]=-tn(A1,dz1qb)
    yield

def bwd_steps(C,H,S,us_ref,u,w1,H1,h1,HU,h2,BLK,gam,bet,dgam_ref,dbet_ref,DZ1,DS1,DS2,DG,dx_ref,db_ref,o,side):
    W=C*H; SB=B*C
    m16=lane_masks(C,H,B); m128=lane_masks(C,H,CH)
    ones=ones_of(C,H); sums=sums_of(C)
    g2=gam*gam
    Kst=S["KST"][...]
    h1b=H1[...].astype(LOW)
    S["BASE"][...]=S["BASE"][...]-nn(Kst,h1b)-tile_rows(C,h1[...],NB)
    dk=nt(S["S1B"][...],h1b)+S["DKQ"][...]
    g2m=nn(jnp.broadcast_to(g2,(8,W)),ones)[0:1]
    hu=HU[...]; hh2=h2[...]
    for j in reversed(range(NB)):
        sl=slice(B*j,B*j+B); st=slice(SB*j,SB*j+SB)
        ub=us_ref[u,j]
        rr=S["RP"][sl]
        hub=hu.astype(LOW)
        x2j=S["X2"][st]
        ds1=S["BASE"][st]
        if j<NB-1: ds1=ds1-nn(S["KK"][st,SB*j+SB:],DZ1[SB*j+SB:])
        ds2=S["DS2Q"][sl]-collapse(C,nt(x2j,hub),m16)-hh2
        dx2=S["DX2"][st]-nn(S["S2E"][st],hub)
        dPb=(ds1*S["RG1"][st]).astype(LOW)
        e=rr*ds2+collapse(C,nt(dPb,ub),m16)
        s=S["SB"][sl]; m2=S["M2B"][sl]; y=S["YB"][sl]; g_=S["GB"][sl]; d2=S["DB"][sl]
        m1=S["RED"][sl]; gy=S["RED"][2*CH+B*j:2*CH+B*j+B]; gyy=S["RED"][3*CH+B*j:3*CH+B*j+B]
        ge=g2*e
        mm=nn(jnp.concatenate([e,e*y,e*d2,ge,ge*y],0),ones)
        a=mm[0:B]; b=mm[B:2*B]; cc=mm[2*B:3*B]; mge=mm[3*B:4*B]; mgey=mm[4*B:]
        dG=s*(e-a-y*b)
        mdY=s*(mge-a*g2m-b*gy-m2*a-b*m1)
        mdYY=s*(mgey-a*gy-b*gyy-2.0*b*m2)
        dZc=s*(g2*dG-s*(m2*e+g_*b)-mdY-y*(cc+mdYY))
        dZcb=expand(C,dZc.astype(LOW),m16)
        dx2=dx2+nn(dZcb,ub)
        dz1=(dx2*S["G1"][st]+ds1*S["RPG2"][st]).astype(LOW)
        DZ1[st]=dz1
        DS1[st]=ds1; DS2[sl]=ds2; DG[sl]=dG
        hu=hu+tn(jnp.concatenate([expand(C,d2.astype(LOW),m16),dZcb],0),jnp.concatenate([dPb,x2j],0))
        hh2=hh2+jnp.sum(dZc,0,keepdims=True)
        next(side,None)
    dz1=DZ1[...]
    M=(nt(dz1,S["S1B"][...])*BLK[...]).astype(LOW)
    dG=DG[...]; dGg=dG*gam
    dk=collapse(C,nt(dz1,w1)-dk-nn(M,Kst)-tn(M,Kst),m16)+dGg
    dx_ref[o,:CH,:W]=S["DQ"][...]
    dx_ref[o,:CH,W:2*W]=dk.astype(LOW)
    dx_ref[o,:CH,2*W:]=(-dGg).astype(LOW)
    dr1=jnp.sum(DS1[...]*S["PG1"][...],-1,keepdims=True)
    dr2=DS2[...]*S["DB"][...]
    lane=lax.broadcasted_iota(jnp.int32,(CH,CH),1)
    dr=jnp.zeros((CH,CH),F)
    for c in range(C):
        rows=[dr1[B*(C*j+c):B*(C*j+c)+B] for j in range(NB)]
        col=jnp.concatenate(rows,0)+jnp.sum(jnp.where(m128[c],dr2,0.0),-1,keepdims=True)
        dr=jnp.where(lane==c,col,dr)
    R=S["R"][...]
    dr=dr*R*(1.0-R*(H/RATE_SCALE))
    db_ref[...]=db_ref[...]+jnp.sum(dr,0,keepdims=True)
    dr=dr.T.astype(LOW)
    extra=dx_ref.shape[1]-CH
    dx_ref[o,CH:,:]=jnp.zeros((extra,3*W),LOW)
    dx_ref[o,CH:,:CH]=dr[:extra]
    dgam_ref[...]=dgam_ref[...]+jnp.sum(dG*(2*S["YB"][...]*gam+S["T0"][...]),0,keepdims=True)
    dbet_ref[...]=dbet_ref[...]+jnp.sum(dGg,0,keepdims=True)
    dz1qb=S["DZ1Q"][...]
    H1[...]=H1[...]+tn(Kst,dz1)+tn(S["QST"][...],dz1qb)
    h1[...]=h1[...]+nn(sums,dz1)+nn(sums,dz1qb)
    HU[...]=hu+tn(S["DZQ"][...],S["X2Q"][...])
    h2[...]=hh2+jnp.sum(collapse(C,S["DZQ"][...].astype(F),m16),0,keepdims=True)

def bwd_kernel(C,H,steps,*refs):
    first,near,far=refs[:9],refs[9:18],refs[18:27]
    us_ref,w1_ref,own_ref,dx_ref,H1,h1,HU,h2,dgam_ref,dbet_ref,db_ref,TRI,BLK,BLKT,DZ1,DS1,DS2,DG=refs[27:45]
    k=len(SLOT)
    even=dict(zip(SLOT,refs[45:45+k])); odd=dict(zip(SLOT,refs[45+k:]))
    gam=pair_row(C,H,own_ref,1); bet=pair_row(C,H,own_ref,2)
    @pl.when(pl.program_id(0)==0)
    def _():
        for ref in (H1,h1,HU,h2,dgam_ref,dbet_ref,db_ref): ref[...]=jnp.zeros_like(ref)
        fill_masks(C,TRI,BLK,BLKT)
        for _ in bwd_pre(C,H,first,own_ref,even,TRI,BLKT,gam,bet,dgam_ref,dbet_ref,1.0): pass
    more=jnp.where(pl.program_id(0)<steps-1,1.0,0.0)
    side=bwd_pre(C,H,near,own_ref,odd,TRI,BLKT,gam,bet,dgam_ref,dbet_ref,1.0)
    bwd_steps(C,H,even,us_ref,1,w1_ref[1],H1,h1,HU,h2,BLK,gam,bet,dgam_ref,dbet_ref,DZ1,DS1,DS2,DG,dx_ref,db_ref,1,side)
    side=bwd_pre(C,H,far,own_ref,even,TRI,BLKT,gam,bet,dgam_ref,dbet_ref,more)
    bwd_steps(C,H,odd,us_ref,0,w1_ref[0],H1,h1,HU,h2,BLK,gam,bet,dgam_ref,dbet_ref,DZ1,DS1,DS2,DG,dx_ref,db_ref,0,side)

def bwd_scan(x,own,do,z1,p,zc,z1q,zq,us,w1s):
    n,tall,W=x.shape
    W//=3
    C=own.shape[0]; I=own.shape[2]; H=W//C
    full=lambda *s: pl.BlockSpec(s,lambda i:(0,)*len(s))
    sd=jax.ShapeDtypeStruct
    V=pltpu.VMEM
    m=C*CH
    def chunk(at):
        rows=lambda k,w: pl.BlockSpec((k,w),lambda i:(at(i),0))
        return [pl.BlockSpec((1,tall,3*W),lambda i:(at(i),0,0)),rows(CH,W),rows(m,I),rows(m,I),rows(CH,W),rows(m,I),rows(CH,W),
            pl.BlockSpec((1,1,W,I),lambda i:(at(i),0,0,0)),pl.BlockSpec((1,W,I),lambda i:(at(i),0,0))]
    ins=(x,do,z1,p,zc,z1q,zq,us,w1s)
    return pl.pallas_call(partial(bwd_kernel,C,H,n//2),grid=(n//2,),
        in_specs=chunk(lambda i:n-1)+chunk(lambda i:n-2-2*i)+chunk(lambda i:jnp.maximum(n-3-2*i,0))+[
            pl.BlockSpec((2,NB,W,I),lambda i:(n//2-1-i,0,0,0)),pl.BlockSpec((2,W,I),lambda i:(n//2-1-i,0,0)),full(*own.shape)],
        out_specs=[pl.BlockSpec((2,tall,3*W),lambda i:(n//2-1-i,0,0)),full(W,I),full(C,I),full(W,I),full(1,W),full(1,W),full(1,W),full(1,CH)],
        out_shape=[sd((n,tall,3*W),LOW),sd((W,I),F),sd((C,I),F),sd((W,I),F),sd((1,W),F),sd((1,W),F),sd((1,W),F),sd((1,CH),F)],
        scratch_shapes=[V((m,m),F),V((m,m),F),V((m,m),F),V((m,I),LOW),V((m,I),F),V((CH,W),F),V((CH,W),F)]+slot_shapes(C,W,I)*2,
        compiler_params=pltpu.CompilerParams(vmem_limit_bytes=48*1024*1024),
    )(*ins,*ins,*ins,us,w1s,own)

RATE_SCALE = 0.25
NORM_EPS = 1e-05


def smooth_act(value):
    return 0.5 * value * (1.0 + jnp.tanh(C0 * (value + C1 * value * value * value)))


def root_norm(value, gain):
    return value * lax.rsqrt(jnp.mean(value * value, -1, keepdims=True) + NORM_EPS) * gain


def layer_norm(value, gain, bias):
    centre = value - jnp.mean(value, -1, keepdims=True)
    return centre * lax.rsqrt(jnp.mean(centre * centre, -1, keepdims=True) + NORM_EPS) * gain + bias


def gated_branch(mixed, gate_pre, gain, bias):
    return layer_norm(mixed, gain, bias) * smooth_act(gate_pre)


def swish_product(gate_val, linear_val):
    return jax.nn.silu(gate_val) * linear_val


def matmul(left, right):
    return jnp.dot(left, right, preferred_element_type=F)


def flip(array, axis, mask):
    peers = lax.axis_size(axis)
    return lax.ppermute(array, axis, [(i, i ^ mask) for i in range(peers)])


def masks_of(axis):
    masks = []
    while 1 << len(masks) < lax.axis_size(axis):
        masks.append(1 << len(masks))
    return masks


def side(axis, mask):
    return (lax.axis_index(axis) // mask) % 2


def gather_near(array, axis):
    for mask in reversed(masks_of(axis)):
        array = jnp.concatenate([array, flip(array, axis, mask)], 0)
    return array


def scatter_once(array, axis, mask):
    half = array.shape[0] // 2
    return array[:half].astype(F) + flip(array[half:].astype(LOW), axis, mask).astype(F)


def scatter_near(array, axis):
    for mask in masks_of(axis):
        array = scatter_once(array, axis, mask)
    return array


def halve(array, axis, mask, dim):
    bit = side(axis, mask)
    mine = lax.dynamic_index_in_dim(array, bit, dim, keepdims=False)
    other = lax.dynamic_index_in_dim(array, 1 - bit, dim, keepdims=False)
    return mine.astype(F) + flip(other.astype(LOW), axis, mask).astype(F)


def double(array, axis, mask):
    got = flip(array, axis, mask)
    upper = side(axis, mask) == 1
    return jnp.stack([jnp.where(upper, got, array), jnp.where(upper, array, got)])


def project_kernel(each, blocks, x_ref, g_ref, wq_ref, wk_ref, wv_ref, wr_ref, wg_ref, s_ref, n_ref, p_ref, LT):
    step = pl.program_id(0)
    rows, width = x_ref.shape
    span = wq_ref.shape[1]

    @pl.when(step == 0)
    def _():
        x = x_ref[...].astype(F)
        scale = lax.rsqrt(jnp.sum(x * x, -1, keepdims=True) * (1.0 / width) + NORM_EPS)
        n_ref[...] = (x * scale * g_ref[...]).astype(LOW)
        logits = nn(n_ref[...], wr_ref[...]).astype(LOW).astype(F)
        heads = logits.shape[1]
        logits = jnp.concatenate([logits, jnp.zeros((rows, 128 - heads), F)], 1)
        LT[...] = logits.T

    normed = n_ref[...]
    extra = s_ref.shape[1] - rows
    s_ref[0, rows:, :] = jnp.zeros((extra, 3 * span), LOW)

    @pl.when(step < blocks)
    def _():
        for i, w_ref in enumerate((wq_ref, wk_ref, wv_ref)):
            s_ref[0, :rows, span * i : span * i + span] = nn(normed, w_ref[...]).astype(LOW)
        r = lax.broadcasted_iota(jnp.int32, (extra, rows), 0)
        c = lax.broadcasted_iota(jnp.int32, (extra, rows), 1)
        pick = jnp.where((r < each) & (c == step * each + r), 1.0, 0.0)
        s_ref[0, rows:, :rows] = nn(pick, LT[...]).astype(LOW)
        p_ref[...] = nn(normed, wg_ref[...])

    @pl.when(step >= blocks)
    def _():
        s_ref[0, :rows, :] = jnp.zeros((rows, 3 * span), LOW)


def project(x, gain, wq, wk, wv, wr, wg, seqs, each, extra):
    rows, width = x.shape
    span = each * (width // wr.shape[1])
    blocks = width // span
    column = pl.BlockSpec((width, span), lambda s: (0, jnp.minimum(s, blocks - 1)))
    full = lambda *shape: pl.BlockSpec(shape, lambda s: (0,) * len(shape))
    sd = jax.ShapeDtypeStruct
    return pl.pallas_call(
        partial(project_kernel, each, blocks),
        grid=(seqs,),
        in_specs=[full(rows, width), full(1, width), column, column, column, full(*wr.shape), column],
        out_specs=[
            pl.BlockSpec((1, rows + extra, 3 * span), lambda s: (s, 0, 0)),
            full(rows, width),
            pl.BlockSpec((rows, span), lambda s: (0, jnp.minimum(s, blocks - 1))),
        ],
        out_shape=[sd((seqs, rows + extra, 3 * span), LOW), sd((rows, width), LOW), sd((rows, width), F)],
        scratch_shapes=[pltpu.VMEM((128, 128), F)],
        compiler_params=pltpu.CompilerParams(vmem_limit_bytes=48 * 1024 * 1024),
    )(x, gain[None], wq, wk, wv, wr, wg)


def summed(fed_parts, early):
    seqs = lax.axis_size("seq")
    early = early.reshape(seqs, -1, early.shape[-1])
    early = lax.all_to_all(early, "seq", split_axis=0, concat_axis=0, tiled=True)
    return jnp.concatenate(
        [jnp.sum(fed_parts.astype(F), 0).astype(LOW), jnp.sum(early.astype(F), 0).astype(LOW)], 0
    )


def share_rows(every_normed, back_sent, state_g, vectors, fed_parts, early, heads, local_heads, head, weights_in):
    seqs, tps = lax.axis_size("seq"), lax.axis_size("tp")
    width = every_normed.shape[1]
    lanes = back_sent.shape[2]
    rows = every_normed.shape[0] // seqs
    span = lanes // 3
    each = span // head
    first_g, first_bias_g, second_g, second_bias_g, gain_g, shift_g, bias_g = state_g
    inner = first_g.shape[1]
    fed = lax.all_gather(summed(fed_parts, early), "seq", axis=0, tiled=False)
    back = lax.all_to_all(back_sent, "seq", split_axis=0, concat_axis=0, tiled=True)
    qkv_g = back_sent[:, :rows].reshape(seqs * rows, lanes)
    logit_g = back_sent[:, rows : rows + each, :rows].transpose(1, 0, 2).reshape(each, seqs * rows)
    columns = jnp.einsum("ld,le->de", every_normed, qkv_g, preferred_element_type=F)
    rate_column = jnp.einsum("el,ld->ed", logit_g, every_normed, preferred_element_type=F)
    first_g = first_g.reshape(each, head, inner)
    second_g = second_g.reshape(each, head, inner)
    second_g = second_g - jnp.mean(second_g, 1, keepdims=True)
    second_bias_g, gain_g, shift_g = [a.reshape(each, head) for a in (second_bias_g, gain_g, shift_g)]
    second_bias_g = second_bias_g - jnp.mean(second_bias_g, 1, keepdims=True)
    bias_g = bias_g[0, :each]
    tail = jnp.concatenate(
        [second_bias_g, gain_g, shift_g, jnp.pad(bias_g[:, None], ((0, 0), (0, inner - 3 * head - 1)))], -1
    )
    states = jnp.concatenate(
        [
            jnp.stack([first_g, second_g], 1),
            jnp.stack([first_bias_g, tail], 1)[:, :, None],
            jnp.zeros((each, 2, 7, inner), F),
        ],
        2,
    )
    state_rows = states.size // lanes // tps
    rate_rows = rate_column.size // lanes // tps
    vectors = jnp.concatenate([vectors, jnp.zeros_like(vectors[:1])], 0)
    vector_rows = vectors.size // lanes // tps
    rest = jnp.concatenate(
        [rate_column.reshape(tps, rate_rows, lanes), vectors.reshape(tps, vector_rows, lanes)], 1
    )
    late = jnp.concatenate(
        [
            columns.reshape(tps, width // tps, lanes),
            states.reshape(tps, state_rows, lanes),
            jnp.pad(rest, ((0, 0), (0, 16 - rate_rows - vector_rows), (0, 0))),
        ],
        1,
    )
    late = lax.psum_scatter(late.astype(LOW), "tp", scatter_dimension=0, tiled=True)
    late = lax.all_gather(late, ("seq", "tp"), axis=0, tiled=True).reshape((seqs, tps) + late.shape[1:])
    weights = late[:, :, : width // tps].reshape(seqs, tps, width // tps, 3, span)
    weights = weights.transpose(3, 1, 2, 0, 4).reshape(3, width, seqs * span)[:, :, :width].astype(F)
    states = late[:, :, width // tps : width // tps + state_rows].reshape(seqs * each, 2, head + 8, inner)[:heads]
    states = lax.dynamic_slice_in_dim(states, lax.axis_index("tp") * local_heads, local_heads, 0).astype(F)
    rest = late[:, :, width // tps + state_rows :]
    rate_weight_grad = rest[:, :, :rate_rows].reshape(seqs * each, width)[:heads].T.astype(F)
    vectors = rest[:, :, rate_rows : rate_rows + vector_rows].reshape(seqs, 4, width)
    vectors = jnp.sum(vectors.astype(F), 0)
    norm_gain_grad = jnp.sum(sum(weights[i] * weights_in[i].astype(F) for i in range(3)), -1)
    return weights, states[:, :, :head], states[:, :, head], rate_weight_grad, vectors, fed, back, norm_gain_grad


def pack_kernel(head, me_ref, n_ref, x_ref, w_ref, wb_ref, u_ref, ub_ref, g_ref, s_ref, r_ref, v_ref, keep_ref, sent_ref, COL, UC, SMALL):
    seqs, _, lanes = x_ref.shape
    rows = n_ref.shape[0] // seqs
    width = n_ref.shape[1]
    here = width // 4
    normed = n_ref[...]
    COL[...] = tn(normed, x_ref[:, :rows].reshape(seqs * rows, lanes))
    rate = jnp.zeros((16, width), F)
    for s in range(seqs):
        logit = x_ref[s, rows : rows + 16, :rows]
        rate = rate + nn(logit, n_ref[rows * s : rows * s + rows])
    SMALL[...] = jnp.zeros_like(SMALL)
    for c in range(2):
        lane = slice(head * c, head * c + head)
        u = u_ref[lane]
        UC[lane] = u - jnp.sum(u, 0, keepdims=True) * (1.0 / head)
        ub = ub_ref[:, lane]
        ub = ub - jnp.sum(ub, 1, keepdims=True) * (1.0 / head)
        for i in range(2):
            SMALL[2 * c, i : i + 1] = wb_ref[c : c + 1, 128 * i : 128 * i + 128]
        SMALL[2 * c + 1, 0:1] = jnp.concatenate([ub, g_ref[:, lane]], 1)
        SMALL[2 * c + 1, 1:2] = jnp.concatenate([s_ref[:, lane], jnp.broadcast_to(r_ref[:, c : c + 1], (1, head))], 1)
    for t in range(4):
        for i in range(3):
            at = (t % 2) * 384 + 128 * i
            SMALL[t, 2 + i : 3 + i] = rate[t // 2 : t // 2 + 1, at : at + 128]
        for i in range(5):
            k = 5 * t + i
            if k < 18:
                SMALL[t, 5 + i : 6 + i] = v_ref[k // 6 : k // 6 + 1, (k % 6) * 128 : (k % 6) * 128 + 128]
    for place, o in enumerate((0, 2, 1, 3)):
        out = (keep_ref, sent_ref)[place // 2].at[place % 2]
        t = me_ref[0] ^ o
        out[:here] = COL[pl.ds(pl.multiple_of(t * here, 16), here)].astype(LOW)
        for n in range(9):
            c, k, half = n // 4, (n // 2) % 2, n % 2
            if n < 8:
                tile = (w_ref, UC)[k][pl.ds(pl.multiple_of(head * c + 16 * t, 16), 16), 128 * half : 128 * half + 128]
            else:
                tile = SMALL[t]
            row, lane = here + 16 * (n // 3), 128 * (n % 3)
            out[row : row + 16, lane : lane + 128] = tile.astype(LOW)


def last_kernel(seqs, each, heads, local_heads, me_ref, a_ref, b_ref, wq_ref, wk_ref, wv_ref,
                q_ref, k_ref, v_ref, n_ref, s_ref, r_ref):
    cut = a_ref.shape[3]
    span = a_ref.shape[4] // 3
    below = q_ref.shape[0] - cut
    for s in range(seqs):
        if s * each >= heads:
            continue
        x, q = s % 2, ((s >> 1) & 1) * 2 + (s >> 2)
        for i, o_ref in enumerate((q_ref, k_ref, v_ref)):
            o_ref[:cut, span * s : span * s + span] = a_ref[0, 0, 4 * x + q, :, span * i : span * i + span].astype(F)
            o_ref[cut:, span * s : span * s + span] = b_ref[0, x, 0, q, :below, span * i : span * i + span].astype(F)
    total = q_ref[...] * wq_ref[...].astype(F)
    for o_ref, w_ref in ((k_ref, wk_ref), (v_ref, wv_ref)):
        total = total + o_ref[...] * w_ref[...].astype(F)
    n_ref[...] = jnp.sum(total, -1, keepdims=True)

    def tile(x, q, n):
        return b_ref[0, x, 0, q, below + 16 * (n // 3) : below + 16 * (n // 3) + 16, 128 * (n % 3) : 128 * (n % 3) + 128]

    for i in range(local_heads):
        h = me_ref[0] * local_heads + i
        s = h // each
        upper = lax.rem(h, each) == 1
        x = lax.rem(s, 2)
        q = lax.rem(s // 2, 2) * 2 + s // 4
        for k in range(2):
            for j in range(2):
                low = tile(x, q, k * 2 + j).astype(F)
                high = tile(x, q, 4 + k * 2 + j).astype(F)
                s_ref[i, k, :, 128 * j : 128 * j + 128] = jnp.where(upper, high, low)
    for s in range(seqs):
        r_ref[0, s] = tile(s % 2, ((s >> 1) & 1) * 2 + (s >> 2), 8).astype(F)


def share_tiles(every_normed, back_sent, state_g, vectors, fed_parts, early, heads, local_heads, head, weights_in):
    seqs, tps = lax.axis_size("seq"), lax.axis_size("tp")
    width = every_normed.shape[1]
    lanes = back_sent.shape[2]
    each = 2
    inner = state_g[0].shape[1]
    here = width // tps
    share = here + 48
    me = lax.axis_index("tp").astype(jnp.int32).reshape(1)
    sd = jax.ShapeDtypeStruct
    late, late_sent = pl.pallas_call(
        partial(pack_kernel, head),
        in_specs=[pl.BlockSpec(memory_space=pltpu.SMEM)] + [pl.BlockSpec(memory_space=pltpu.VMEM)] * 10,
        out_specs=[pl.BlockSpec(memory_space=pltpu.VMEM)] * 2,
        out_shape=[sd((2, share, lanes), LOW)] * 2,
        scratch_shapes=[
            pltpu.VMEM((width, lanes), F),
            pltpu.VMEM((each * head, inner), F),
            pltpu.VMEM((4, 16, 128), F),
        ],
        compiler_params=pltpu.CompilerParams(vmem_limit_bytes=48 * 1024 * 1024),
    )(me, every_normed, back_sent, *state_g, vectors)
    late = late.astype(F) + flip(late_sent, "tp", 1).astype(F)
    late, fed_parts = lax.optimization_barrier((late, fed_parts))
    fed = summed(fed_parts, early)
    late = scatter_once(late, "tp", 2).astype(LOW)[0]
    late, fed = lax.optimization_barrier((late, fed))
    fed = lax.all_gather(fed, "seq", axis=0, tiled=False)
    late = double(late, "seq", 4)
    late = double(late, "seq", 2)
    late, back_sent = lax.optimization_barrier((late, back_sent))
    back = lax.all_to_all(back_sent, "seq", split_axis=0, concat_axis=0, tiled=True)
    cut = 128
    part_a, part_b = late[:, :, :cut], late[:, :, cut:]
    part_a, part_b = double(part_a, "seq", 1), double(part_b, "tp", 2)
    part_a, part_b, fed = lax.optimization_barrier((part_a, part_b, fed))
    part_a, part_b = double(part_a, "tp", 2), double(part_b, "seq", 1)
    part_a, part_b = double(part_a, "tp", 1), double(part_b, "tp", 1)
    part_a = part_a.reshape(2, 2, seqs, cut, lanes)
    part_b = part_b.reshape(2, 2, 2, seqs // 2, share - cut, lanes)
    square = pl.BlockSpec((here, width), lambda t: (t, 0))
    sd = jax.ShapeDtypeStruct
    *weights, norm_gain_grad, head_w, small = pl.pallas_call(
        partial(last_kernel, seqs, each, heads, local_heads),
        grid=(tps,),
        in_specs=[
            pl.BlockSpec(memory_space=pltpu.SMEM),
            pl.BlockSpec((1, 1, seqs, cut, lanes), lambda t: (t % 2, t // 2, 0, 0, 0)),
            pl.BlockSpec((1, 2, 1, seqs // 2, share - cut, lanes), lambda t: (t % 2, 0, t // 2, 0, 0, 0)),
            square, square, square,
        ],
        out_specs=[
            square, square, square,
            pl.BlockSpec((here, 1), lambda t: (t, 0)),
            pl.BlockSpec((local_heads, 2, head // tps, inner), lambda t: (0, 0, t, 0)),
            pl.BlockSpec((1, seqs, 16, 128), lambda t: (t, 0, 0, 0)),
        ],
        out_shape=[sd((width, width), F)] * 3
        + [sd((width, 1), F), sd((local_heads, 2, head, inner), F), sd((tps, seqs, 16, 128), F)],
        compiler_params=pltpu.CompilerParams(vmem_limit_bytes=48 * 1024 * 1024),
    )(me, part_a, part_b, *weights_in)
    head_t = small[:, :, :2].transpose(1, 0, 2, 3).reshape(seqs * each, 2, inner)
    head_t = lax.dynamic_slice_in_dim(head_t, me[0] * local_heads, local_heads, 0)
    rate_weight_grad = small[:, :, 2:5].transpose(1, 0, 2, 3).reshape(seqs * each, width)[:heads].T
    vectors = jnp.sum(small[:, :, 5:10], 1).reshape(-1)[: 3 * width].reshape(3, width)
    return weights, head_w, head_t, rate_weight_grad, vectors, fed, back, norm_gain_grad[:, 0]


def on_device(
    tokens, norm_gain, query_weight, key_weight, value_weight, rate_weight, rate_bias,
    first_weight, first_bias, second_weight, second_bias, inner_gain, inner_bias,
    branch_gate, output_weight, post_gain, post_bias, feed_gain, feed_gate, feed_linear,
    feed_down, cotangent,
):
    seqs = lax.axis_size("seq")
    rank = lax.axis_index("seq")
    heads = rate_weight.shape[1]
    local_heads, head, inner = first_weight.shape
    rows = tokens.shape[1]
    width = tokens.shape[2]
    each = -(-heads // seqs)
    span = each * head
    length = seqs * rows
    extra = -(-each // 16) * 16

    def to_chains(array):
        padded = jnp.pad(array, ((0, 0), (0, seqs * span - array.shape[1])))
        return padded.reshape(rows, seqs, span).transpose(1, 0, 2)

    def from_chains(array):
        return array.transpose(1, 0, 2).reshape(rows, seqs * span)[:, :width]

    def swap(array):
        return lax.all_to_all(array, "seq", split_axis=0, concat_axis=0, tiled=True)

    tail = jnp.concatenate(
        [second_bias, inner_gain, inner_bias, jnp.pad(rate_bias[:, None], ((0, 0), (0, inner - 3 * head - 1)))], -1
    )
    packed = jnp.concatenate(
        [
            first_weight,
            jnp.swapaxes(second_weight, 1, 2),
            first_bias[:, None],
            tail[:, None],
            jnp.zeros((local_heads, 6, inner), F),
        ],
        1,
    )
    every = lax.all_gather(packed, "tp", axis=0, tiled=True)
    own = lax.dynamic_slice_in_dim(every, jnp.minimum(rank * each, heads - each), each, 0)

    residual = tokens[0].astype(F)
    normed_val, norm_pull = jax.vjp(root_norm, residual, norm_gain)
    down_grad = cotangent[0]
    grad_out = down_grad.astype(F)
    every_grad = gather_near(down_grad, "tp")
    if span % 128 == 0 and width % span == 0 and rows == 128:
        sent, normed, gate_pre = project(
            tokens[0], norm_gain, query_weight, key_weight, value_weight, rate_weight, branch_gate, seqs, each, extra
        )
    else:
        normed = normed_val.astype(LOW)
        query_tok = matmul(normed, query_weight).astype(LOW)
        keys_tok = matmul(normed, key_weight).astype(LOW)
        values_tok = matmul(normed, value_weight).astype(LOW)
        logits_tok = matmul(normed, rate_weight).astype(LOW)
        gate_pre = matmul(normed, branch_gate)
        logit_rows = jnp.pad(logits_tok.T, ((0, seqs * each - heads), (0, 0))).reshape(seqs, each, rows)
        logit_rows = jnp.pad(logit_rows, ((0, 0), (0, extra - each), (0, 3 * span - rows)))
        sent = [to_chains(query_tok), to_chains(keys_tok), to_chains(values_tok)]
        sent = jnp.concatenate([jnp.concatenate(sent, -1), logit_rows], 1)
    got = swap(sent)

    every_normed = lax.all_gather(normed, "seq", axis=0, tiled=True)
    outs, *kept = fwd_scan(got, own)
    outs, every_normed, every_grad = lax.optimization_barrier((outs, every_normed, every_grad))
    mixed_tok = from_chains(swap(outs.reshape(seqs, rows, span))).astype(F)

    branch_val, branch_pull = jax.vjp(gated_branch, mixed_tok, gate_pre, post_gain, post_bias)
    branch_in = branch_val.astype(LOW)
    middle = residual + matmul(branch_in, output_weight)
    feed_val, feed_pull = jax.vjp(root_norm, middle, feed_gain)
    feed_in = feed_val.astype(LOW)
    every_in = gather_near(feed_in, "tp")
    gate_val = matmul(every_in, feed_gate)
    linear_val = matmul(every_in, feed_linear)
    act_val, act_pull = jax.vjp(swish_product, gate_val, linear_val)
    hidden = act_val.astype(LOW)

    hidden_grad = jnp.einsum("td,fd->tf", every_grad, feed_down, preferred_element_type=F)
    gate_grad, linear_grad = act_pull(hidden_grad)
    gate_low = gate_grad.astype(LOW)
    linear_low = linear_grad.astype(LOW)
    input_part = jnp.einsum("tf,df->td", gate_low, feed_gate, preferred_element_type=F) + jnp.einsum(
        "tf,df->td", linear_low, feed_linear, preferred_element_type=F
    )
    feed_in_grad = scatter_near(input_part, "tp")
    middle_part, feed_gain_grad = feed_pull(feed_in_grad)
    middle_grad = grad_out + middle_part
    out_low = middle_grad.astype(LOW)
    branch_grad = jnp.einsum("te,de->td", out_low, output_weight, preferred_element_type=F)
    mixed_grad, gate_pre_grad, post_gain_grad, post_bias_grad = branch_pull(branch_grad)
    out_grad_c = swap(to_chains(mixed_grad.astype(LOW))).reshape(length, span)

    second_part = matmul(hidden, feed_down).astype(LOW)
    second_part, out_grad_c = lax.optimization_barrier((second_part, out_grad_c))
    second_out = scatter_near(second_part, "tp")
    result = (middle + second_out).astype(LOW)[None]

    feed_down_grad = jnp.einsum("tf,td->fd", hidden, every_grad, preferred_element_type=F)
    both_low = jnp.concatenate([gate_low, linear_low], 1)
    feed_both_grad = jnp.einsum("tf,td->fd", both_low, every_in, preferred_element_type=F)
    gate_low_pre = gate_pre_grad.astype(LOW)
    out_low, gate_low_pre, out_grad_c = lax.optimization_barrier((out_low, gate_low_pre, out_grad_c))
    tps = lax.axis_size("tp")
    lefts = jnp.stack([branch_in, normed])
    rights = jnp.stack([out_low, gate_low_pre])
    part_rows = 2 * width // tps
    orders = [0]
    for mask in reversed(masks_of("tp")):
        orders = orders + [o + mask for o in orders]
    parts = []
    for o in orders:
        owner = lax.axis_index("tp") ^ o
        which, place = owner % 2, owner // 2
        left = lax.dynamic_slice(lefts, (which, 0, place * part_rows), (1, rows, part_rows))
        right = lax.dynamic_index_in_dim(rights, which, 0, keepdims=True)
        parts.append((left, right))
    half = tps // 2

    def products(chosen):
        left = jnp.concatenate([p[0] for p in chosen], 0)
        right = jnp.concatenate([p[1] for p in chosen], 0)
        return jnp.einsum("jtd,jte->jde", left, right, preferred_element_type=F)

    early_sent = products(parts[half:]).astype(LOW)
    early = products(parts[:half]) + flip(early_sent, "tp", 1).astype(F)
    fed_parts = jnp.concatenate(
        [
            feed_both_grad.astype(LOW).reshape(seqs, -1, width),
            feed_down_grad.astype(LOW).reshape(seqs, -1, width),
        ],
        1,
    )
    fed_parts, early, out_grad_c = lax.optimization_barrier((fed_parts, early.astype(LOW), out_grad_c))
    fed_parts = swap(fed_parts)
    for mask in masks_of("tp")[1:]:
        early = scatter_once(early, "tp", mask)

    back_sent, *state_g = bwd_scan(got, own, out_grad_c, *kept)
    early, back_sent = lax.optimization_barrier((early.astype(LOW), back_sent))
    vectors = jnp.stack([post_gain_grad, post_bias_grad, feed_gain_grad])
    share = share_tiles if each == 2 and tps == 4 and seqs == 8 else share_rows
    weights, head_w, head_t, rate_weight_grad, vectors, fed, back, norm_gain_grad = share(
        every_normed, back_sent, state_g, vectors, fed_parts, early, heads, local_heads, head,
        (query_weight, key_weight, value_weight),
    )
    query_low = from_chains(back[:, :rows, :span])
    keys_low = from_chains(back[:, :rows, span : 2 * span])
    values_low = from_chains(back[:, :rows, 2 * span :])
    logit_low = back[:, rows : rows + each, :rows].reshape(seqs * each, rows)[:heads].T

    normed_grad = (
        jnp.einsum("te,de->td", query_low, query_weight, preferred_element_type=F)
        + jnp.einsum("te,de->td", keys_low, key_weight, preferred_element_type=F)
        + jnp.einsum("te,de->td", values_low, value_weight, preferred_element_type=F)
        + jnp.einsum("te,de->td", logit_low, rate_weight, preferred_element_type=F)
        + jnp.einsum("te,de->td", gate_low_pre, branch_gate, preferred_element_type=F)
    )
    residual_part, unused = norm_pull(normed_grad)
    tokens_grad = (middle_grad + residual_part)[None]
    inner_units = feed_gate.shape[1]
    both = fed[:, : 2 * inner_units // seqs].reshape(2, inner_units, width).astype(F)
    down = fed[:, 2 * inner_units // seqs : 3 * inner_units // seqs].reshape(inner_units, width).astype(F)
    early = fed[:, 3 * inner_units // seqs :].reshape(-1, width)
    for mask in reversed(masks_of("tp")):
        early = double(early, "tp", mask)
    early = early.reshape(2, width, width).astype(F)
    norm_gain_grad = norm_gain_grad + jnp.sum(rate_weight_grad * rate_weight.astype(F), -1)
    norm_gain_grad = norm_gain_grad + jnp.sum(early[1] * branch_gate.astype(F), -1)
    norm_gain_grad = norm_gain_grad / norm_gain
    tail_sum = head_t[:, 1]
    return (
        result,
        tokens_grad,
        norm_gain_grad,
        weights[0],
        weights[1],
        weights[2],
        rate_weight_grad,
        tail_sum[:, 3 * head],
        head_w[:, 0],
        head_t[:, 0],
        jnp.swapaxes(head_w[:, 1], 1, 2),
        tail_sum[:, :head],
        tail_sum[:, head : 2 * head],
        tail_sum[:, 2 * head : 3 * head],
        early[1],
        early[0],
        vectors[0],
        vectors[1],
        vectors[2],
        both[0].T,
        both[1].T,
        down,
    )


def solution(mesh):
    in_specs = (
        P("tp", "seq", None),
        P(),
        P(),
        P(),
        P(),
        P(),
        P("tp"),
        P("tp", None, None),
        P("tp", None),
        P("tp", None, None),
        P("tp", None),
        P("tp", None),
        P("tp", None),
        P(),
        P(),
        P(),
        P(),
        P(),
        P(None, "tp"),
        P(None, "tp"),
        P("tp", None),
        P("tp", "seq", None),
    )
    out_specs = (
        P("tp", "seq", None),
        P("tp", "seq", None),
        P(),
        P(),
        P(),
        P(),
        P(),
        P("tp"),
        P("tp", None, None),
        P("tp", None),
        P("tp", None, None),
        P("tp", None),
        P("tp", None),
        P("tp", None),
        P(),
        P(),
        P(),
        P(),
        P(),
        P(None, "tp"),
        P(None, "tp"),
        P("tp", None),
    )
    return jax.shard_map(
        on_device, mesh=mesh, in_specs=in_specs, out_specs=out_specs, check_vma=False
    )
```

time: 462 us -> 395 us (0.85)
  Pallas kernels: 144 us -> 99.6 us
  waiting for transfers between devices: 95.7 us -> 121 us
  other arithmetic: 59.9 us -> 37.5 us
  local copies, waits for them, and re-layouts: 68.6 us -> 51.1 us
  matrix products: 29 us -> 16.1 us
  blocking collectives: 0 us -> 12.3 us
  starting transfers between devices: 46.5 us -> 40.4 us
    pallas_call x2 -> x4, Pallas kernels: 137 us -> 93.4 us  [the longest x1 43.4 us: bwd_scan(): pl.pallas_call(partial(bwd_kernel, C, H, n // 2), grid=(n // 2,), in_spec...]
    ppermute x25 -> x22, waiting for transfers between devices: 57.5 us -> 83.5 us  [flip(): return lax.ppermute(array, axis, [(i, i ^ mask) for i in range(peers)])]
    unnamed x276 -> x145, local copies, waits for them, and re-layouts: 36.9 us -> 19.4 us
    all_to_all x0 -> x2, waiting for transfers between devices: none -> 14.9 us  [the longest x1 9.4 us: summed(): lax.all_to_all(early, 'seq', split_axis=0, concat_axis=0, tiled=True)]
    all_to_all x0 -> x1, blocking collectives: none -> 12.3 us  [swap(): return lax.all_to_all(array, 'seq', split_axis=0, concat_axis=0, tiled=True)]
    all_to_all x5 -> x3, waiting for transfers between devices: 32.1 us -> 21.6 us  [swap(): return lax.all_to_all(array, 'seq', split_axis=0, concat_axis=0, tiled=True)]
    all_to_all x0 -> x2, starting transfers between devices: none -> 8.76 us  [the longest x1 4.58 us: share_tiles(): lax.all_to_all(back_sent, 'seq', split_axis=0, concat_axis=0, tiled=True)]
    all_to_all x5 -> x3, starting transfers between devices: 24.6 us -> 16 us  [swap(): return lax.all_to_all(array, 'seq', split_axis=0, concat_axis=0, tiled=True)]
  transfers between devices with their start and end apart: 33 -> 30, of which waited for: 13 -> 20; matrix products, arithmetic and copies ran while one was open for 21% -> 15% of each run, Pallas kernels for 30% -> 24%
where the time goes in v3:
time: 395 us; the launch traced here: 393 us
  waiting for transfers between devices  121 us (31%)
  Pallas kernels  99.6 us (25%)
  local copies, waits for them, and re-layouts  51.1 us (13%)
  starting transfers between devices  40.4 us (10%)
  other arithmetic  37.5 us (9%)
  matrix products  16.1 us (4%)
  between operations  14.9 us (4%)
  blocking collectives  12.3 us (3%)
    ppermute x22, waiting for transfers between devices, flip(): return lax.ppermute(array, axis, [(i, i ^ mask) for i in range(peers)])  83.5 us
    pallas_call x1, Pallas kernels, bwd_scan(): pl.pallas_call(partial(bwd_kernel, C, H, n // 2), grid=(n // 2,), in_spec...  43.4 us
    pallas_call x1, Pallas kernels, fwd_scan(): pl.pallas_call(partial(fwd_kernel, C, H), grid=(n,), in_specs=[pl.BlockSp...  41.5 us
    all_to_all x3, waiting for transfers between devices, swap(): return lax.all_to_all(array, 'seq', split_axis=0, concat_axis=0, tiled=True)  21.6 us
    unnamed x145, local copies, waits for them, and re-layouts  19.4 us
    all_to_all x3, starting transfers between devices, swap(): return lax.all_to_all(array, 'seq', split_axis=0, concat_axis=0, tiled=True)  16 us
    ppermute x22, starting transfers between devices, flip(): return lax.ppermute(array, axis, [(i, i ^ mask) for i in range(peers)])  15.3 us
    all_to_all x1, blocking collectives, swap(): return lax.all_to_all(array, 'seq', split_axis=0, concat_axis=0, tiled=True)  12.3 us
  transfers between devices with their start and end apart: 30, of which 20 were waited for; matrix products, arithmetic and copies ran while one was open for 15% of the time, Pallas kernels for 24%

profile of v3, /device:TPU:0, one launch (start us, length us, event | category | flops | bytes accessed | tf_op | source)
XLA Modules:
  0.0 392.6 jit_solution(10569796986866095124)
XLA Ops:
  9.7 3.9 concatenate.45
  17.8 6.0 %shard_map.381 = (bf16[8,144,384]{2,1,0:T(8,128)(2,1)S(1)}, bf16[128,768]{1,0:T(8,128)(2,1)}, f32[128,768]{1,0:T(8,128)S(1)}) custom-call(bf16[128,768]{1,0:T(8,128)(2,1)S(1)} %bitcast.140, f32[1,768]{1,0:T(1,128)S(1)} %broadcast_in_dim.41.g_ref, bf16[768,768]{1,0:T(8,128)(2,1)S(1)} %copy-done.3, bf16[768,768]{1,0:T(8,128)(2,1)S(1)} %copy-done.4, ...), custom_call_target="tpu_custom_call" | custom-call | tf_op jit(solution)/shard_map/pallas_call | solution.py:471
  25.5 7.3 %all-to-all-start = ((bf16[8,144,384]{2,1,0:T(8,128)(2,1)}), bf16[8,144,384]{2,1,0:T(8,128)(2,1)S(1)}, u32[]{:S(2)}, u32[]{:S(2)}) async-start(bf16[8,144,384]{2,1,0:T(8,128)(2,1)} %copy-done.21), calls=%async_computation | async-start | bytes 1769472 | tf_op jit(solution)/shard_map/all_to_all | solution.py:728
  32.8 1.5 collective-permute-start
  34.3 5.1 %collective-permute-done = bf16[128,768]{1,0:T(8,128)(2,1)S(1)} collective-permute-done((bf16[128,768]{1,0:T(8,128)(2,1)}, bf16[128,768]{1,0:T(8,128)(2,1)S(1)}, u32[]{:S(2)}, u32[]{:S(2)}) %collective-permute-start) | collective-permute-done | bytes 196640 | tf_op jit(solution)/shard_map/ppermute | solution.py:386
  40.0 1.7 pad_maximum_fusion.11
  41.7 2.1 collective-permute-done.1
  43.8 2.1 pad_maximum_fusion.6
  45.9 1.7 constant_dynamic-slice_fusion.2.own_ref.refs_29_
  47.6 13.3 %all-to-all-done.x_ref.refs_0_.refs_9_.refs_18_ = bf16[8,144,384]{2,1,0:T(8,128)(2,1)S(1)} async-done(((bf16[8,144,384]{2,1,0:T(8,128)(2,1)}), bf16[8,144,384]{2,1,0:T(8,128)(2,1)S(1)}, u32[]{:S(2)}, u32[]{:S(2)}) %all-to-all-start) | async-done | bytes 884768 | tf_op jit(solution)/shard_map/all_to_all | solution.py:728
  61.9 41.5 %shard_map.382 = (bf16[1024,128]{1,0:T(8,128)(2,1)S(1)}, f32[2048,256]{1,0:T(8,128)S(1)}, f32[2048,256]{1,0:T(8,128)}, f32[1024,128]{1,0:T(8,128)S(1)}, f32[2048...) custom-call(bf16[8,144,384]{2,1,0:T(8,128)(2,1)S(1)} %all-to-all-don, ...), custom_call_target="tpu_custom_call" | custom-call | tf_op jit(solution)/shard_map/pallas_call | solution.py:164
  103.4 1.3 copy-done.2
  107.8 12.3 %all_to_all.30 = bf16[8,128,128]{2,1,0:T(8,128)(2,1)S(1)} all-to-all(bf16[8,128,128]{2,1,0:T(8,128)(2,1)} %bitcast.141), channel_id=1, replica_groups=mesh['seq'=8,'tp'=4] {'seq'}, dimensions={0} | all-to-all | bytes 524288 | tf_op jit(solution)/shard_map/all_to_all | solution.py:728
  121.3 1.4 collective-permute-start.2
  122.8 4.3 %collective-permute-done.2 = bf16[128,768]{1,0:T(8,128)(2,1)S(1)} collective-permute-done((bf16[128,768]{1,0:T(8,128)(2,1)S(1)}, bf16[128,768]{1,0:T(8,128)(2,1)S(1)}, u32[]{:S(2)}, u32[]{:S(2)}) %collective-permute-start.2) | collective-permute-done | bytes 196640 | tf_op jit(solution)/shard_map/ppermute | solution.py:386
  127.2 1.7 collective-permute-done.3
  131.1 1.7 multiply_convert_fusion
  134.4 1.6 collective-permute-done.4
  136.1 1.4 collective-permute-start.5
  137.5 5.6 %collective-permute-done.5 = bf16[128,768]{1,0:T(8,128)(2,1)S(1)} collective-permute-done((bf16[128,768]{1,0:T(8,128)(2,1)S(1)}, bf16[128,768]{1,0:T(8,128)(2,1)S(1)}, u32[]{:S(2)}, u32[]{:S(2)}) %collective-permute-start.5) | collective-permute-done | bytes 196640 | tf_op jit(solution)/shard_map/ppermute | solution.py:386
  144.2 1.5 fusion.18
  146.8 4.2 %all-to-all-start.2 = ((bf16[8,128,128]{2,1,0:T(8,128)(2,1)}), bf16[8,128,128]{2,1,0:T(8,128)(2,1)S(1)}, u32[]{:S(2)}, u32[]{:S(2)}) async-start(bf16[8,128,128]{2,1,0:T(8,128)(2,1)} %bitcast_bitcast_fusion), calls=%async_computation.2 | async-start | bytes 524288 | tf_op jit(solution)/shard_map/all_to_all | solution.py:728
  151.1 1.9 fusion.61
  153.0 2.8 convolution_convert_fusion.3
  155.8 3.8 all-to-all-done.2
  159.9 1.6 convolution_convert_fusion.1
  163.4 1.6 pad_maximum_fusion.2
  165.0 1.5 add_convert_fusion
  166.5 4.5 %all-to-all-start.3 = ((bf16[8,192,768]{2,1,0:T(8,128)(2,1)}), bf16[8,192,768]{2,1,0:T(8,128)(2,1)}, u32[]{:S(2)}, u32[]{:S(2)}) async-start(bf16[8,192,768]{2,1,0:T(8,128)(2,1)} %pad_maximum_fusion.2), calls=%async_computation.3 | async-start | bytes 4718592 | tf_op jit(solution)/shard_map/all_to_all | solution.py:728
  175.4 43.4 %shard_map.383 = (bf16[8,144,384]{2,1,0:T(8,128)(2,1)}, f32[128,256]{1,0:T(8,128)S(1)}, f32[2,256]{1,0:T(2,128)S(1)}, f32[128,256]{1,0:T(8,128)S(1)}, f32[1,128]...) custom-call(bf16[8,144,384]{2,1,0:T(8,128)(2,1)S(1)} %all-to-all-done.x_ref.refs_0_.refs_9_.refs, ...), custom_call_target="tpu_custom_call" | custom-call | tf_op jit(solution)/shard_map/pallas_call | solution.py:346
  221.2 4.5 %all-to-all-done.3 = bf16[8,192,768]{2,1,0:T(8,128)(2,1)} async-done(((bf16[8,192,768]{2,1,0:T(8,128)(2,1)}), bf16[8,192,768]{2,1,0:T(8,128)(2,1)}, u32[]{:S(2)}, u32[]{:S(2)}) %all-to-all-start.3) | async-done | bytes 2359328 | tf_op jit(solution)/shard_map/all_to_all | solution.py:728
  225.7 4.2 %all-to-all-start.4 = ((bf16[8,48,768]{2,1,0:T(8,128)(2,1)}), bf16[8,48,768]{2,1,0:T(8,128)(2,1)}, u32[]{:S(2)}, u32[]{:S(2)}) async-start(bf16[8,48,768]{2,1,0:T(8,128)(2,1)} %bitcast.153), calls=%async_computation.4 | async-start | bytes 1179648 | tf_op jit(solution)/shard_map/all_to_all | solution.py:489
  230.3 2.4 shard_map.384
  232.7 1.7 collective-permute-done.10
  236.4 9.4 %all-to-all-done.4 = bf16[8,48,768]{2,1,0:T(8,128)(2,1)} async-done(((bf16[8,48,768]{2,1,0:T(8,128)(2,1)}), bf16[8,48,768]{2,1,0:T(8,128)(2,1)}, u32[]{:S(2)}, u32[]{:S(2)}) %all-to-all-start.4) | async-done | bytes 589856 | tf_op jit(solution)/shard_map/all_to_all | solution.py:489
  246.9 2.1 reduce_sum.187
  250.0 9.4 %collective-permute-done.12 = bf16[240,384]{1,0:T(8,128)(2,1)S(1)} collective-permute-done((bf16[240,384]{1,0:T(8,128)(2,1)S(1)}, bf16[240,384]{1,0:T(8,128)(2,1)S(1)}, u32[]{:S(2)}, u32[]{:S(2)}) %collective-permute-start.12) | collective-permute-done | bytes 184352 | tf_op jit(solution)/shard_map/ppermute | solution.py:386
  260.9 18.5 %collective-permute-done.13 = bf16[2,240,384]{2,1,0:T(8,128)(2,1)S(1)} collective-permute-done((bf16[2,240,384]{2,1,0:T(8,128)(2,1)}, bf16[2,240,384]{2,1,0:T(8,128)(2,1)S(1)}, u32[]{:S(2)}, u32[]{:S(2)}) %collective-permute-start.13) | collective-permute-done | bytes 368672 | tf_op jit(solution)/shard_map/ppermute | solution.py:386
  279.6 4.6 %all-to-all-start.5 = ((bf16[8,144,384]{2,1,0:T(8,128)(2,1)}), bf16[8,144,384]{2,1,0:T(8,128)(2,1)S(1)}, u32[]{:S(2)}, u32[]{:S(2)}) async-start(bf16[8,144,384]{2,1,0:T(8,128)(2,1)} %get-tuple-element.108.x_ref), calls=%async_computation.5 | async-start | bytes 1769472 | tf_op jit(solution)/shard_map/all_to_all | solution.py:666
  284.2 1.3 convert_add_fusion
  287.1 1.4 collective-permute-start.7
  289.9 2.2 collective-permute-start.14
  292.1 3.0 collective-permute-done.7
  295.1 1.7 fusion.43
  296.9 4.3 %collective-permute-done.15 = bf16[2,2,112,384]{3,2,1,0:T(8,128)(2,1)} collective-permute-done((bf16[2,2,112,384]{3,2,1,0:T(8,128)(2,1)}, bf16[2,2,112,384]{3,2,1,0:T(8,128)(2,1)}, u32[]{:S(2)}, u32[]{:S(2)}) %collective-permute-start.15) | collective-permute-done | bytes 344096 | tf_op jit(solution)/shard_map/ppermute | solution.py:386
  303.2 12.6 %collective-permute-done.14 = bf16[2,2,128,384]{3,2,1,0:T(8,128)(2,1)S(1)} collective-permute-done((bf16[2,2,128,384]{3,2,1,0:T(8,128)(2,1)S(1)}, bf16[2,2,128,384]{3,2,1,0:T(8,128)(2,1)S(1)}, u32[]{:S(2)}, u32[]{:S(2)}) %collective-permute-start.14) | collective-permute-done | bytes 393248 | tf_op jit(solution)/shard_map/ppermute | solution.py:386
  316.8 5.5 %all-to-all-done.5 = bf16[8,144,384]{2,1,0:T(8,128)(2,1)S(1)} async-done(((bf16[8,144,384]{2,1,0:T(8,128)(2,1)}), bf16[8,144,384]{2,1,0:T(8,128)(2,1)S(1)}, u32[]{:S(2)}, u32[]{:S(2)}) %all-to-all-start.5) | async-done | bytes 884768 | tf_op jit(solution)/shard_map/all_to_all | solution.py:666
  323.3 1.9 copy.102
  325.2 1.8 copy.101
  332.2 1.9 slice.180
  335.3 1.5 collective-permute-start.20
  337.8 1.7 slice_convert_fusion
  339.5 2.0 fusion.76
  341.5 3.0 copy.110
  344.5 3.0 copy.109
  348.1 3.1 collective-permute-done.20
  351.1 1.3 select_bitcast_fusion.5
  353.9 1.4 select_bitcast_fusion.3
  356.1 10.7 %collective-permute-done.16 = bf16[2,2,2,128,384]{4,3,2,1,0:T(8,128)(2,1)S(1)} collective-permute-done((bf16[2,2,2,128,384]{4,3,2,1,0:T(8,128)(2,1)}, bf16[2,2,2,128,384]{4,3,2,1,0:T(8,128)(2,1)S(1)}, u32[]{:S(2)}, u32[]{:S(2)}) %collective-permute-start.16) | collective-permute-done | bytes 786464 | tf_op jit(solution)/shard_map/ppermute | solution.py:386
  367.8 1.6 slice_bitcast_fusion
  369.3 1.7 multiply_reduce_fusion
  371.4 1.9 pad_maximum_fusion.1.b_ref
  373.6 2.0 pad_maximum_fusion.a_ref
  376.0 6.2 %shard_map.385 = (f32[768,768]{1,0:T(8,128)}, f32[768,768]{1,0:T(8,128)}, f32[768,768]{1,0:T(8,128)}, f32[768,1]{1,0:T(8,128)S(1)}, f32[3,2,64,256]{3,2,1,0:T(8,128)S(1)}, /*index=5*/f32[4,8,16,128]{3,2,1,0:T(8,128)S(1)}) custom-call(s32[1]{0:T(128)} %bitcast.9.me_ref, bf16[2,2,8,128,384]{4,3,2,1,0:T(8,128)(2,1)} %pad_maximum_fusion.a_ref, ...), custom_call_target="tpu_custom_call" | custom-call | tf_op jit(solution)/shard_map/pallas_call | solution.py:677
  (270 shorter events, 58.0 us)
Async XLA Ops:
  7.2 113.5 %copy-start = (bf16[768,768]{1,0:T(8,128)(2,1)S(1)}, bf16[768,768]{1,0:T(8,128)(2,1)}, u32[]{:S(2)}) copy-start(bf16[768,768]{1,0:T(8,128)(2,1)} %param.36) | copy-start | bytes 3538948
  7.2 8.0 %copy-start.3 = (bf16[768,768]{1,0:T(8,128)(2,1)S(1)}, bf16[768,768]{1,0:T(8,128)(2,1)}, u32[]{:S(2)}) copy-start(bf16[768,768]{1,0:T(8,128)(2,1)} %wq_ref.3) | copy-start | bytes 3538948
  7.2 8.0 %copy-start.16 = (bf16[1,128,768]{2,1,0:T(8,128)(2,1)S(1)}, bf16[1,128,768]{2,1,0:T(8,128)(2,1)}, u32[]{:S(2)}) copy-start(bf16[1,128,768]{2,1,0:T(8,128)(2,1)} %param.22) | copy-start | bytes 589828
  7.2 38.6 %all-gather.5.cloned.1.call-start = ((), (), s32[]{:S(2)}) async-start(), calls=%async_computation.6 | async-start | bytes 2088960 | tf_op jit(solution)/shard_map/all_gather | solution.py:743
  13.5 94.2 %all-gather.7.cloned.1.call-start = ((), (), s32[]{:S(2)}) async-start(), calls=%async_computation.7 | async-start | bytes 1769472 | tf_op jit(solution)/shard_map/all_gather | solution.py:768
  25.5 35.4 %all-to-all-start = ((bf16[8,144,384]{2,1,0:T(8,128)(2,1)}), bf16[8,144,384]{2,1,0:T(8,128)(2,1)S(1)}, u32[]{:S(2)}, u32[]{:S(2)}) async-start(bf16[8,144,384]{2,1,0:T(8,128)(2,1)} %copy-done.21), calls=%async_computation | async-start | bytes 1769472 | tf_op jit(solution)/shard_map/all_to_all | solution.py:728
  32.8 6.6 %collective-permute-start = (bf16[128,768]{1,0:T(8,128)(2,1)}, bf16[128,768]{1,0:T(8,128)(2,1)S(1)}, u32[]{:S(2)}, u32[]{:S(2)}) collective-permute-start(bf16[128,768]{1,0:T(8,128)(2,1)} %bitcast.154), channel_id=1, source_target_pairs={{0,2},{1,3},{2,0},{3,1},{4,6},{5,7},{6,4},{7,5},{8,10},{9,11},{10,... | collective-permute-start | bytes 589832 | tf_op jit(solution)/shard_map/ppermute | solution.py:386
  41.7 2.1 collective-permute-start.1
  45.8 74.6 %copy-start.65 = (f32[768]{0:T(1024)S(1)}, f32[768]{0:T(1024)}, u32[]{:S(2)}) copy-start(f32[768]{0:T(1024)} %param.37) | copy-start | bytes 9220
  45.9 74.6 %copy-start.66 = (f32[768]{0:T(1024)S(1)}, f32[768]{0:T(1024)}, u32[]{:S(2)}) copy-start(f32[768]{0:T(1024)} %param.38) | copy-start | bytes 9220
  107.8 12.7 %copy-start.23 = (f32[128,768]{1,0:T(8,128)S(1)}, f32[128,768]{1,0:T(8,128)}, u32[]{:S(2)}) copy-start(f32[128,768]{1,0:T(8,128)} %copy-done.22) | copy-start | bytes 1179652
  120.7 6.4 %copy-start.36 = (bf16[128,768]{1,0:T(8,128)(2,1)}, bf16[128,768]{1,0:T(8,128)(2,1)S(1)}, u32[]{:S(2)}) copy-start(bf16[128,768]{1,0:T(8,128)(2,1)S(1)} %fusion.17) | copy-start | bytes 589828
  120.8 8.2 %copy-start.52 = (bf16[768,512]{1,0:T(8,128)(2,1)S(1)}, bf16[768,512]{1,0:T(8,128)(2,1)}, u32[]{:S(2)}) copy-start(bf16[768,512]{1,0:T(8,128)(2,1)} %param.41) | copy-start | bytes 2359300
  121.2 22.1 %copy-start.30 = (f32[128,768]{1,0:T(8,128)}, f32[128,768]{1,0:T(8,128)S(1)}, u32[]{:S(2)}) copy-start(f32[128,768]{1,0:T(8,128)S(1)} %get-tuple-element.184) | copy-start | bytes 1179652
  121.3 8.2 %copy-start.50 = (bf16[128,768]{1,0:T(8,128)(2,1)}, bf16[128,768]{1,0:T(8,128)(2,1)S(1)}, u32[]{:S(2)}) copy-start(bf16[128,768]{1,0:T(8,128)(2,1)S(1)} %multiply_convert_fusion.2) | copy-start | bytes 589828
  121.3 5.7 %collective-permute-start.2 = (bf16[128,768]{1,0:T(8,128)(2,1)S(1)}, bf16[128,768]{1,0:T(8,128)(2,1)S(1)}, u32[]{:S(2)}, u32[]{:S(2)}) collective-permute-start(bf16[128,768]{1,0:T(8,128)(2,1)S(1)} %multiply_convert_fusion.2), channel_id=1, source_target_pairs={{0,2},{1,3},{2,0},{3,1},{4,6},{5,7},{6,4},{7,5},{8,10},{9,11},{10,... | collective-permute-start | bytes 589832 | tf_op jit(solution)/shard_map/ppermute | solution.py:386
  127.1 2.5 copy-start.61
  127.1 2.6 copy-start.49
  127.1 1.8 collective-permute-start.3
  134.1 9.1 %copy-start.35 = (bf16[1,128,768]{2,1,0:T(8,128)(2,1)S(1)}, bf16[1,128,768]{2,1,0:T(8,128)(2,1)}, u32[]{:S(2)}) copy-start(bf16[1,128,768]{2,1,0:T(8,128)(2,1)} %param.43) | copy-start | bytes 589828
  134.2 1.8 collective-permute-start.4
  136.1 7.0 %collective-permute-start.5 = (bf16[128,768]{1,0:T(8,128)(2,1)S(1)}, bf16[128,768]{1,0:T(8,128)(2,1)S(1)}, u32[]{:S(2)}, u32[]{:S(2)}) collective-permute-start(bf16[128,768]{1,0:T(8,128)(2,1)S(1)} %slice.282), channel_id=1, source_target_pairs={{0,2},{1,3},{2,0},{3,1},{4,6},{5,7},{6,4},{7,5},{8,10},{9,11},{10,... | collective-permute-start | bytes 589832 | tf_op jit(solution)/shard_map/ppermute | solution.py:386
  145.7 5.4 %copy-start.37 = (bf16[128,768]{1,0:T(8,128)(2,1)S(1)}, bf16[128,768]{1,0:T(8,128)(2,1)}, u32[]{:S(2)}) copy-start(bf16[128,768]{1,0:T(8,128)(2,1)} %copy-done.36) | copy-start | bytes 589828
  146.8 12.7 %all-to-all-start.2 = ((bf16[8,128,128]{2,1,0:T(8,128)(2,1)}), bf16[8,128,128]{2,1,0:T(8,128)(2,1)S(1)}, u32[]{:S(2)}, u32[]{:S(2)}) async-start(bf16[8,128,128]{2,1,0:T(8,128)(2,1)} %bitcast_bitcast_fusion), calls=%async_computation.2 | async-start | bytes 524288 | tf_op jit(solution)/shard_map/all_to_all | solution.py:728
  151.0 8.5 %copy-start.41 = (bf16[128,768]{1,0:T(8,128)(2,1)S(1)}, bf16[128,768]{1,0:T(8,128)(2,1)}, u32[]{:S(2)}) copy-start(bf16[128,768]{1,0:T(8,128)(2,1)} %get-tuple-element.81) | copy-start | bytes 589828
  151.0 8.5 %copy-start.44 = (bf16[128,768]{1,0:T(8,128)(2,1)S(1)}, bf16[128,768]{1,0:T(8,128)(2,1)}, u32[]{:S(2)}) copy-start(bf16[128,768]{1,0:T(8,128)(2,1)} %copy-done.43) | copy-start | bytes 589828
  155.8 5.8 %copy-start.51 = (bf16[128,768]{1,0:T(8,128)(2,1)S(1)}, bf16[128,768]{1,0:T(8,128)(2,1)}, u32[]{:S(2)}) copy-start(bf16[128,768]{1,0:T(8,128)(2,1)} %copy-done.50) | copy-start | bytes 589828
  159.6 2.1 copy-start.54
  159.6 2.1 copy-start.56
  159.6 2.1 copy-start.62
  159.6 2.1 copy-start.69
  161.5 3.4 collective-permute-start.8
  166.5 6.9 %copy-start.11 = (bf16[8,128,256]{2,1,0:T(8,128)(2,1)S(1)}, bf16[8,128,256]{2,1,0:T(8,128)(2,1)}, u32[]{:S(2)}) copy-start(bf16[8,128,256]{2,1,0:T(8,128)(2,1)} %copy-done.10) | copy-start | bytes 1572868
  166.5 6.9 %copy-start.13 = (f32[1024,128]{1,0:T(8,128)S(1)}, f32[1024,128]{1,0:T(8,128)}, u32[]{:S(2)}) copy-start(f32[1024,128]{1,0:T(8,128)} %copy-done.12) | copy-start | bytes 1572868
  166.5 59.2 %all-to-all-start.3 = ((bf16[8,192,768]{2,1,0:T(8,128)(2,1)}), bf16[8,192,768]{2,1,0:T(8,128)(2,1)}, u32[]{:S(2)}, u32[]{:S(2)}) async-start(bf16[8,192,768]{2,1,0:T(8,128)(2,1)} %pad_maximum_fusion.2), calls=%async_computation.3 | async-start | bytes 4718592 | tf_op jit(solution)/shard_map/all_to_all | solution.py:728
  172.2 48.0 %collective-permute-start.9 = (bf16[1,384,768]{2,1,0:T(8,128)(2,1)S(1)}, bf16[1,384,768]{2,1,0:T(8,128)(2,1)S(1)}, u32[]{:S(2)}, u32[]{:S(2)}) collective-permute-start(bf16[1,384,768]{2,1,0:T(8,128)(2,1)S(1)} %slice.164), channel_id=1, source_target_pairs={{0,2},{1,3},{2,0},{3,1},{4,6},{5,7},{6,4},{7,5},{8,10},{9,11},{10,... | collective-permute-start | bytes 1769480 | tf_op jit(solution)/shard_map/ppermute | solution.py:386
  175.4 44.8 %copy-start.32 = (bf16[2,384,768]{2,1,0:T(8,128)(2,1)S(1)}, bf16[2,384,768]{2,1,0:T(8,128)(2,1)}, u32[]{:S(2)}) copy-start(bf16[2,384,768]{2,1,0:T(8,128)(2,1)} %add_convert_fusion) | copy-start | bytes 3538948
  220.2 10.0 %copy-start.20 = (bf16[1024,768]{1,0:T(8,128)(2,1)S(1)}, bf16[1024,768]{1,0:T(8,128)(2,1)}, u32[]{:S(2)}) copy-start(bf16[1024,768]{1,0:T(8,128)(2,1)} %all-gather.7.cloned.1.call-done.n_ref) | copy-start | bytes 4718596
  220.2 10.0 %copy-start.26 = (f32[128,256]{1,0:T(8,128)S(1)}, f32[128,256]{1,0:T(8,128)}, u32[]{:S(2)}) copy-start(f32[128,256]{1,0:T(8,128)} %copy-done.25) | copy-start | bytes 393220
  220.2 10.0 %copy-start.28 = (f32[128,256]{1,0:T(8,128)S(1)}, f32[128,256]{1,0:T(8,128)}, u32[]{:S(2)}) copy-start(f32[128,256]{1,0:T(8,128)} %copy-done.27) | copy-start | bytes 393220
  225.7 20.1 %all-to-all-start.4 = ((bf16[8,48,768]{2,1,0:T(8,128)(2,1)}), bf16[8,48,768]{2,1,0:T(8,128)(2,1)}, u32[]{:S(2)}, u32[]{:S(2)}) async-start(bf16[8,48,768]{2,1,0:T(8,128)(2,1)} %bitcast.153), calls=%async_computation.4 | async-start | bytes 1179648 | tf_op jit(solution)/shard_map/all_to_all | solution.py:489
  229.9 102.3 %all-gather.9.cloned.1.call-start = ((), (), s32[]{:S(2)}) async-start(), calls=%async_computation.8 | async-start | bytes 3317760 | tf_op jit(solution)/shard_map/all_gather | solution.py:662
  232.7 1.7 collective-permute-start.10
  235.2 14.6 %collective-permute-start.11 = (bf16[1,240,384]{2,1,0:T(8,128)(2,1)}, bf16[1,240,384]{2,1,0:T(8,128)(2,1)S(1)}, u32[]{:S(2)}, u32[]{:S(2)}) collective-permute-start(bf16[1,240,384]{2,1,0:T(8,128)(2,1)} %slice.283), channel_id=1, source_target_pairs={{0,2},{1,3},{2,0},{3,1},{4,6},{5,7},{6,4},{7,5},{8,10},{9,11},{10,... | collective-permute-start | bytes 552968 | tf_op jit(solution)/shard_map/ppermute | solution.py:386
  249.0 11.1 %copy-start.48 = (bf16[512,768]{1,0:T(8,128)(2,1)S(1)}, bf16[512,768]{1,0:T(8,128)(2,1)}, u32[]{:S(2)}) copy-start(bf16[512,768]{1,0:T(8,128)(2,1)} %convolution_convert_fusion.3) | copy-start | bytes 2359300
  249.8 9.5 %collective-permute-start.12 = (bf16[240,384]{1,0:T(8,128)(2,1)S(1)}, bf16[240,384]{1,0:T(8,128)(2,1)S(1)}, u32[]{:S(2)}, u32[]{:S(2)}) collective-permute-start(bf16[240,384]{1,0:T(8,128)(2,1)S(1)} %fusion.58), channel_id=1, source_target_pairs={{0,16},{4,20},{8,24},{12,28},{16,0},{20,4},{24,8},{28,12},{1,17},{... | collective-permute-start | bytes 552968 | tf_op jit(solution)/shard_map/ppermute | solution.py:386
  260.1 19.3 %collective-permute-start.13 = (bf16[2,240,384]{2,1,0:T(8,128)(2,1)}, bf16[2,240,384]{2,1,0:T(8,128)(2,1)S(1)}, u32[]{:S(2)}, u32[]{:S(2)}) collective-permute-start(bf16[2,240,384]{2,1,0:T(8,128)(2,1)} %pad_maximum_fusion.14), channel_id=1, source_target_pairs={{0,8},{4,12},{8,0},{12,4},{16,24},{20,28},{24,16},{28,20},{1,9},{5... | collective-permute-start | bytes 1105928 | tf_op jit(solution)/shard_map/ppermute | solution.py:386
  260.9 23.3 %collective-permute-start.6 = (bf16[256,768]{1,0:T(8,128)(2,1)}, bf16[256,768]{1,0:T(8,128)(2,1)}, u32[]{:S(2)}, u32[]{:S(2)}) collective-permute-start(bf16[256,768]{1,0:T(8,128)(2,1)} %slice.160), channel_id=1, source_target_pairs={{0,1},{1,0},{2,3},{3,2},{4,5},{5,4},{6,7},{7,6},{8,9},{9,8},{10,11... | collective-permute-start | bytes 1179656 | tf_op jit(solution)/shard_map/ppermute | solution.py:386
  279.6 42.7 %all-to-all-start.5 = ((bf16[8,144,384]{2,1,0:T(8,128)(2,1)}), bf16[8,144,384]{2,1,0:T(8,128)(2,1)S(1)}, u32[]{:S(2)}, u32[]{:S(2)}) async-start(bf16[8,144,384]{2,1,0:T(8,128)(2,1)} %get-tuple-element.108.x_ref), calls=%async_computation.5 | async-start | bytes 1769472 | tf_op jit(solution)/shard_map/all_to_all | solution.py:666
  284.2 11.0 %copy-start.31 = (f32[128,768]{1,0:T(8,128)S(1)}, f32[128,768]{1,0:T(8,128)}, u32[]{:S(2)}) copy-start(f32[128,768]{1,0:T(8,128)} %copy-done.30) | copy-start | bytes 1179652
  287.1 8.0 %collective-permute-start.7 = (bf16[128,768]{1,0:T(8,128)(2,1)}, bf16[128,768]{1,0:T(8,128)(2,1)S(1)}, u32[]{:S(2)}, u32[]{:S(2)}) collective-permute-start(bf16[128,768]{1,0:T(8,128)(2,1)} %slice.281), channel_id=1, source_target_pairs={{0,2},{1,3},{2,0},{3,1},{4,6},{5,7},{6,4},{7,5},{8,10},{9,11},{10,... | collective-permute-start | bytes 589832 | tf_op jit(solution)/shard_map/ppermute | solution.py:386
  289.3 12.0 %collective-permute-start.15 = (bf16[2,2,112,384]{3,2,1,0:T(8,128)(2,1)}, bf16[2,2,112,384]{3,2,1,0:T(8,128)(2,1)}, u32[]{:S(2)}, u32[]{:S(2)}) collective-permute-start(bf16[2,2,112,384]{3,2,1,0:T(8,128)(2,1)} %slice.176), channel_id=1, source_target_pairs={{0,2},{1,3},{2,0},{3,1},{4,6},{5,7},{6,4},{7,5},{8,10},{9,11},{10,... | collective-permute-start | bytes 1032200 | tf_op jit(solution)/shard_map/ppermute | solution.py:386
  289.9 25.8 %collective-permute-start.14 = (bf16[2,2,128,384]{3,2,1,0:T(8,128)(2,1)S(1)}, bf16[2,2,128,384]{3,2,1,0:T(8,128)(2,1)S(1)}, u32[]{:S(2)}, u32[]{:S(2)}) collective-permute-start(bf16[2,2,128,384]{3,2,1,0:T(8,128)(2,1)S(1)} %slice.175), channel_id=1, source_target_pairs={{0,4},{4,0},{8,12},{12,8},{16,20},{20,16},{24,28},{28,24},{1,5},{5... | collective-permute-start | bytes 1179656 | tf_op jit(solution)/shard_map/ppermute | solution.py:386
  323.3 4.5 %copy-start.5 = (bf16[768,768]{1,0:T(8,128)(2,1)S(1)}, bf16[768,768]{1,0:T(8,128)(2,1)}, u32[]{:S(2)}) copy-start(bf16[768,768]{1,0:T(8,128)(2,1)} %wk_ref.3) | copy-start | bytes 3538948
  335.3 15.8 %collective-permute-start.20 = (bf16[384,768]{1,0:T(8,128)(2,1)}, bf16[384,768]{1,0:T(8,128)(2,1)}, u32[]{:S(2)}, u32[]{:S(2)}) collective-permute-start(bf16[384,768]{1,0:T(8,128)(2,1)} %bitcast.44), channel_id=1, source_target_pairs={{0,2},{1,3},{2,0},{3,1},{4,6},{5,7},{6,4},{7,5},{8,10},{9,11},{10,... | collective-permute-start | bytes 1769480 | tf_op jit(solution)/shard_map/ppermute | solution.py:386
  336.9 17.1 %collective-permute-start.18 = (bf16[2,2,2,112,384]{4,3,2,1,0:T(8,128)(2,1)}, bf16[2,2,2,112,384]{4,3,2,1,0:T(8,128)(2,1)}, u32[]{:S(2)}, u32[]{:S(2)}) collective-permute-start(bf16[2,2,2,112,384]{4,3,2,1,0:T(8,128)(2,1)} %pad_maximum_fusion.10), channel_id=1, source_target_pairs={{0,4},{4,0},{8,12},{12,8},{16,20},{20,16},{24,28},{28,24},{1,5},{5... | collective-permute-start | bytes 2064392 | tf_op jit(solution)/shard_map/ppermute | solution.py:386
  347.5 19.4 %collective-permute-start.16 = (bf16[2,2,2,128,384]{4,3,2,1,0:T(8,128)(2,1)}, bf16[2,2,2,128,384]{4,3,2,1,0:T(8,128)(2,1)S(1)}, u32[]{:S(2)}, u32[]{:S(2)}) collective-permute-start(bf16[2,2,2,128,384]{4,3,2,1,0:T(8,128)(2,1)} %pad_maximum_fusion.8), channel_id=1, source_target_pairs={{0,2},{1,3},{2,0},{3,1},{4,6},{5,7},{6,4},{7,5},{8,10},{9,11},{10,... | collective-permute-start | bytes 2359304 | tf_op jit(solution)/shard_map/ppermute | solution.py:386
  352.6 14.7 %collective-permute-start.21 = (bf16[2,384,768]{2,1,0:T(8,128)(2,1)S(1)}, bf16[2,384,768]{2,1,0:T(8,128)(2,1)S(1)}, u32[]{:S(2)}, u32[]{:S(2)}) collective-permute-start(bf16[2,384,768]{2,1,0:T(8,128)(2,1)S(1)} %pad_maximum_fusion.5), channel_id=1, source_target_pairs={{0,1},{1,0},{2,3},{3,2},{4,5},{5,4},{6,7},{7,6},{8,9},{9,8},{10,11... | collective-permute-start | bytes 3538952 | tf_op jit(solution)/shard_map/ppermute | solution.py:386
  355.4 11.5 %copy-start.33 = (bf16[2,2,2,128,384]{4,3,2,1,0:T(8,128)(2,1)S(1)}, bf16[2,2,2,128,384]{4,3,2,1,0:T(8,128)(2,1)}, u32[]{:S(2)}) copy-start(bf16[2,2,2,128,384]{4,3,2,1,0:T(8,128)(2,1)} %pad_maximum_fusion.8) | copy-start | bytes 2359300
  355.6 15.5 %collective-permute-start.19 = (bf16[2,2,2,2,112,384]{5,4,3,2,1,0:T(8,128)(2,1)S(1)}, bf16[2,2,2,2,112,384]{5,4,3,2,1,0:T(8,128)(2,1)S(1)}, u32[]{:S(2)}, u32[]{:S(2)}) collective-permute-start(bf16[2,2,2,2,112,384]{5,4,3,2,1,0:T(8,128)(2,1)S(1)} %pad_maximum_fusion.4), channel_id=1, source_target_pairs={{0,1},{1,0},{2,3},{3,2},{4,5},{5,4},{6,7},{7,6},{8,9},{9,8},{10,11... | collective-permute-start | bytes 4128776 | tf_op jit(solution)/shard_map/ppermute | solution.py:386
  367.2 6.0 %collective-permute-start.17 = (bf16[2,2,2,2,128,384]{5,4,3,2,1,0:T(8,128)(2,1)S(1)}, bf16[2,2,2,2,128,384]{5,4,3,2,1,0:T(8,128)(2,1)S(1)}, u32[]{:S(2)}, u32[]{:S(2)}) collective-permute-start(bf16[2,2,2,2,128,384]{5,4,3,2,1,0:T(8,128)(2,1)S(1)} %pad_maximum_fusion.3), channel_id=1, source_target_pairs={{0,1},{1,0},{2,3},{3,2},{4,5},{5,4},{6,7},{7,6},{8,9},{9,8},{10,11... | collective-permute-start | bytes 4718600 | tf_op jit(solution)/shard_map/ppermute | solution.py:386
  373.6 2.0 copy-start.6
  373.6 2.4 copy-start.9
  376.0 10.0 %copy-start.1 = (bf16[768,768]{1,0:T(8,128)(2,1)S(1)}, bf16[768,768]{1,0:T(8,128)(2,1)}, u32[]{:S(2)}) copy-start(bf16[768,768]{1,0:T(8,128)(2,1)} %param.36) | copy-start | bytes 3538948
  (37 other events, 41.3 us)
Sparse Core Ops, SparseCore 0:
  13.7 22.9 all-gather.4
  39.4 45.1 all-gather.6
  250.0 82.2 all-gather.8

commit v4 on v3

--- a/solution.py
+++ b/solution.py
@@ -6,6 +6,7 @@
 from jax.sharding import PartitionSpec as P
 from jax.experimental import pallas as pl
 from jax.experimental.pallas import tpu as pltpu
+from itertools import chain
 C0=0.7978845608028654
 C1=0.044715
 EPS=1e-6
@@ -82,10 +83,106 @@
 def pair_row(C,H,own_ref,k):
     return jnp.concatenate([own_ref[c,2*H+1:2*H+2,k*H:k*H+H] for c in range(C)],1)
 
-def fwd_kernel(C,H,x_ref,own_ref,
-               o_ref,z1_ref,p_ref,zc_ref,z1q_ref,zq_ref,us_ref,w1s_ref,
-               W1,B1,U,B2,TRI,BLK,S1,S2,X2,KK,BASE):
-    W=C*H; SB=B*C
+def mask_stack(C,H):
+    r=lax.broadcasted_iota(jnp.int32,(B*C,C*H),0)//B; c=lax.broadcasted_iota(jnp.int32,(B*C,C*H),1)//H
+    return r==c
+
+def fwd_pre(C,H,x,own_ref,BLK,gam,bet,S):
+    W=C*H
+    m16=lane_masks(C,H,B); m128=lane_masks(C,H,CH)
+    K=x[0,:CH,W:2*W]
+    Kst=expand(C,K,m16)
+    S["KST"][...]=Kst; S["QST"][...]=expand(C,x[0,:CH,:W],m16)
+    S["T"][...]=(bet+K.astype(F)-x[0,:CH,2*W:].astype(F))*gam
+    yield
+    R=rates(C,x,own_ref,H)
+    S["R"][...]=R
+    S["RP"][...]=pair_cols(C,H,R,m128)
+    yield
+    S["KK"][...]=((nt(Kst,Kst)+1.0)*BLK[...]).astype(LOW)
+    tst=expand(C,S["T"][...],m16)
+    S["TST"][...]=tst
+    S["CT"][...]=nn(tst,jnp.full((W,W),1.0/H,LOW))
+    yield
+
+def fwd_steps(C,H,S,W1,B1,U,B2,gam,z1_ref,p_ref,zc_ref,us_ref,w1s_ref,o,side,times):
+    W=C*H; SB=B*C; TALL=C*CH
+    m16=lane_masks(C,H,B)
+    ones=ones_of(C,H)
+    g2=gam*gam
+    Kst=S["KST"][...]
+    w1b=W1[...].astype(LOW); w1s_ref[o]=w1b
+    S["W1"][...]=w1b; S["B1"][...]=B1[...]; S["B2"][...]=B2[...]
+    b1r=tile_rows(C,B1[...],1)
+    uf=U[...]; ub=uf.astype(LOW); S["U"][...]=ub
+    b2=B2[...]
+    S["BASE"][...]=nn(Kst,w1b)
+    g2m=jnp.concatenate([jnp.broadcast_to(jnp.sum(jnp.where(m16[c][:1],g2,0.0),1,keepdims=True)*(1.0/H),(B,W)) for c in range(C)],0)
+    mst=mask_stack(C,H)
+    full=jnp.full((W,W),1.0/H,LOW)
+    I=W1.shape[1]
+    wide=lambda v: jnp.concatenate([v]*(I//W),1)
+    for j in range(NB):
+        sl=slice(B*j,B*j+B); st=slice(SB*j,SB*j+SB)
+        z1=S["BASE"][st]+b1r
+        if j>0: z1=z1-nn(S["KK"][st,:SB*j],S["S1"][:SB*j])
+        x2,g1=gelu2(z1)
+        x2b=x2.astype(LOW)
+        t=S["TST"][st]; ct=S["CT"][st]; rr=stack_col(C,S["R"][sl])
+        tU=nn(t,ub)
+        zc=jnp.where(mst,nt(x2b,ub)+b2,0.0)
+        zz=zc*zc; zg=zc*g2
+        AB=nn(jnp.concatenate([zg,zc],0),ub)
+        mm=nn(jnp.concatenate([zc,zz,zg,zz*g2,zc*t],0),full)
+        mu=mm[0:SB]; mzz=mm[SB:2*SB]; mzg=mm[2*SB:3*SB]; mzzg=mm[3*SB:4*SB]; mzt=mm[4*SB:]
+        s=lax.rsqrt(mzz-mu*mu+EPS)
+        m1=s*(mzg-mu*g2m)+ct
+        m2=s*(s*(mzzg-2.0*mu*mzg+mu*mu*g2m)+mzt-mu*ct)
+        ss=s*s
+        P=wide(ss)*(AB[:SB]-wide(m2)*AB[SB:])+wide(s)*tU
+        s1=(P*(g1*rr)).astype(LOW)
+        d2=ss*(zg-m2*zc)+s*t+jnp.where(mst,ss*mu*(m2-g2)-s*m1,0.0)
+        s2=d2*rr
+        s2b=s2.astype(LOW)
+        zc=collapse(C,zc-mu,m16)
+        S["S1"][st]=s1; S["S2"][st]=s2b; S["X2"][st]=x2b
+        z1_ref[TALL*o+SB*j:TALL*o+SB*j+SB]=z1; p_ref[TALL*o+SB*j:TALL*o+SB*j+SB]=P
+        zc_ref[CH*o+B*j:CH*o+B*j+B]=zc
+        us_ref[o,j]=ub
+        uf=uf-tn(s2b,x2b); ub=uf.astype(LOW)
+        b2=b2-jnp.sum(s2,0,keepdims=True)
+        for _ in range(times): next(side,None)
+    U[...]=uf; B2[...]=b2
+    S1v=S["S1"][...]
+    W1[...]=W1[...]-tn(Kst,S1v)
+    B1[...]=B1[...]-nn(sums_of(C),S1v)
+
+def fwd_query(C,H,S,x,TRI,gam,bet,o_ref,z1q_ref,zq_ref,o):
+    W=C*H; TALL=C*CH
+    m16=lane_masks(C,H,B)
+    ones=ones_of(C,H)
+    A1=((nt(S["QST"][...],S["KST"][...])+1.0)*TRI[...]).astype(LOW)
+    yield
+    z1q=nn(S["QST"][...],S["W1"][...])+tile_rows(C,S["B1"][...],NB)-nn(A1,S["S1"][...])
+    z1q_ref[TALL*o:TALL*o+TALL]=z1q
+    x2q=gelu1(z1q).astype(LOW)
+    yield
+    A2=((nt(x2q,S["X2"][...])+1.0)*TRI[...]).astype(LOW)
+    yield
+    zq=collapse(C,nt(x2q,S["U"][...])-nn(A2,S["S2"][...]),m16)+S["B2"][...]
+    zq=zq-nn(zq,ones)
+    zq_ref[CH*o:CH*o+CH]=zq
+    yield
+    yq=zq*lax.rsqrt(nn(zq*zq,ones)+EPS)
+    o_ref[CH*o:CH*o+CH]=(x[0,:CH,:W].astype(F)+yq*gam+bet).astype(LOW)
+    yield
+
+FSLOT=("TST","KST","QST","T","R","RP","KK","CT","W1","B1","U","B2","BASE","S1","S2","X2")
+
+def fwd_kernel(C,H,xa_ref,xb_ref,own_ref,o_ref,z1_ref,p_ref,zc_ref,z1q_ref,zq_ref,us_ref,w1s_ref,W1,B1,U,B2,TRI,BLK,*slots):
+    k=len(FSLOT)
+    even=dict(zip(FSLOT,slots[:k])); odd=dict(zip(FSLOT,slots[k:]))
+    gam=pair_row(C,H,own_ref,1); bet=pair_row(C,H,own_ref,2)
     @pl.when(pl.program_id(0)==0)
     def _():
         for c in range(C):
@@ -96,80 +193,32 @@
         raw=[own_ref[c,2*H+1:2*H+2,:H] for c in range(C)]
         B2[...]=jnp.concatenate([v-jnp.sum(v,1,keepdims=True)*(1.0/H) for v in raw],1)
         fill_masks(C,TRI,BLK,None)
-    m16=lane_masks(C,H,B); m128=lane_masks(C,H,CH)
-    ones=ones_of(C,H)
-    K=x_ref[0,:CH,W:2*W]
-    Kst=expand(C,K,m16); Qst=expand(C,x_ref[0,:CH,:W],m16)
-    gam=pair_row(C,H,own_ref,1); bet=pair_row(C,H,own_ref,2); g2=gam*gam
-    T=(bet+K.astype(F)-x_ref[0,:CH,2*W:].astype(F))*gam
-    R=rates(C,x_ref,own_ref,H)
-    RP=pair_cols(C,H,R,m128)
-    w1b=W1[...].astype(LOW); w1s_ref[0]=w1b
-    b1r=tile_rows(C,B1[...],1)
-    uf=U[...]; ub=uf.astype(LOW); u0=ub
-    b2=B2[...]; b20=b2
-    KK[...]=((nt(Kst,Kst)+1.0)*BLK[...]).astype(LOW)
-    BASE[...]=nn(Kst,w1b)
-    CT=nn(T,ones)
-    g2m=nn(jnp.broadcast_to(g2,(8,W)),ones)[0:1]
-    for j in range(NB):
-        sl=slice(B*j,B*j+B); st=slice(SB*j,SB*j+SB)
-        z1=BASE[st]+b1r
-        if j>0: z1=z1-nn(KK[st,:SB*j],S1[:SB*j])
-        x2,g1=gelu2(z1)
-        x2b=x2.astype(LOW)
-        zc=collapse(C,nt(x2b,ub),m16)+b2
-        t=T[sl]; zz=zc*zc; zg=zc*g2; ct=CT[sl]; rr=RP[sl]
-        mm=nn(jnp.concatenate([zc,zz,zg,zz*g2,zc*t],0),ones)
-        mu=mm[0:B]; mzz=mm[B:2*B]; mzg=mm[2*B:3*B]; mzzg=mm[3*B:4*B]; mzt=mm[4*B:]
-        s=lax.rsqrt(mzz-mu*mu+EPS)
-        m1=s*(mzg-mu*g2m)+ct
-        m2=s*(s*(mzzg-2.0*mu*mzg+mu*mu*g2m)+mzt-mu*ct)
-        zc=zc-mu
-        d2=s*(zc*s*(g2-m2)+(t-m1))
-        P=nn(expand(C,d2,m16),ub)
-        s1=(P*(g1*stack_col(C,R[sl]))).astype(LOW)
-        s2=d2*rr
-        s2b=expand(C,s2,m16).astype(LOW)
-        S1[st]=s1; S2[st]=s2b; X2[st]=x2b
-        z1_ref[st]=z1; p_ref[st]=P; zc_ref[sl]=zc
-        us_ref[0,j]=ub
-        uf=uf-tn(s2b,x2b); ub=uf.astype(LOW)
-        b2=b2-jnp.sum(s2,0,keepdims=True)
-    U[...]=uf; B2[...]=b2
-    S1v=S1[...]
-    W1[...]=W1[...]-tn(Kst,S1v)
-    B1[...]=B1[...]-nn(sums_of(C),S1v)
-    tri=TRI[...]
-    A1=(nt(Qst,Kst)+1.0)*tri
-    z1q=nn(Qst,w1b)+tile_rows(C,0.0+b1r_src(b1r,C),NB)-nn(A1,S1v)
-    x2q=gelu1(z1q).astype(LOW)
-    A2=(nt(x2q,X2[...])+1.0)*tri
-    zq=collapse(C,nt(x2q,u0)-nn(A2,S2[...]),m16)+b20
-    zq=zq-nn(zq,ones)
-    yq=zq*lax.rsqrt(nn(zq*zq,ones)+EPS)
-    o_ref[...]=(x_ref[0,:CH,:W].astype(F)+yq*gam+bet).astype(LOW)
-    z1q_ref[...]=z1q; zq_ref[...]=zq
-
-def b1r_src(b1r,C):
-    return jnp.concatenate([b1r[B*c:B*c+1] for c in range(C)],0)
+    for _ in fwd_pre(C,H,xa_ref,own_ref,BLK,gam,bet,even): pass
+    side=fwd_pre(C,H,xb_ref,own_ref,BLK,gam,bet,odd)
+    fwd_steps(C,H,even,W1,B1,U,B2,gam,z1_ref,p_ref,zc_ref,us_ref,w1s_ref,0,side,1)
+    for _ in side: pass
+    side=fwd_query(C,H,even,xa_ref,TRI,gam,bet,o_ref,z1q_ref,zq_ref,0)
+    fwd_steps(C,H,odd,W1,B1,U,B2,gam,z1_ref,p_ref,zc_ref,us_ref,w1s_ref,1,side,1)
+    for _ in side: pass
+    for _ in fwd_query(C,H,odd,xb_ref,TRI,gam,bet,o_ref,z1q_ref,zq_ref,1): pass
 
 def fwd_scan(x,own):
     n,tall,W=x.shape
     W//=3
-    C=own.shape[0]; I=own.shape[2]; H=W//C; L=n*CH
-    rows=lambda k,w: pl.BlockSpec((k,w),lambda i:(i,0))
+    C=own.shape[0]; I=own.shape[2]; H=W//C; L=n*CH; m=C*CH
+    rows=lambda k,w: pl.BlockSpec((2*k,w),lambda i:(i,0))
     sd=jax.ShapeDtypeStruct
     V=pltpu.VMEM
-    return pl.pallas_call(partial(fwd_kernel,C,H),grid=(n,),
-        in_specs=[pl.BlockSpec((1,tall,3*W),lambda i:(i,0,0)),pl.BlockSpec(own.shape,lambda i:(0,0,0))],
-        out_specs=[rows(CH,W),rows(C*CH,I),rows(C*CH,I),rows(CH,W),rows(C*CH,I),rows(CH,W),
-            pl.BlockSpec((1,NB,W,I),lambda i:(i,0,0,0)),pl.BlockSpec((1,W,I),lambda i:(i,0,0))],
+    kinds=dict(KST=V((m,W),LOW),QST=V((m,W),LOW),T=V((CH,W),F),R=V((CH,CH),F),RP=V((CH,W),F),KK=V((m,m),LOW),CT=V((m,W),F),TST=V((m,W),F),W1=V((W,I),LOW),
+        B1=V((C,I),F),U=V((W,I),LOW),B2=V((1,W),F),BASE=V((m,I),F),S1=V((m,I),LOW),S2=V((m,W),LOW),X2=V((m,I),LOW))
+    return pl.pallas_call(partial(fwd_kernel,C,H),grid=(n//2,),
+        in_specs=[pl.BlockSpec((1,tall,3*W),lambda i:(2*i,0,0)),pl.BlockSpec((1,tall,3*W),lambda i:(2*i+1,0,0)),pl.BlockSpec(own.shape,lambda i:(0,0,0))],
+        out_specs=[rows(CH,W),rows(m,I),rows(m,I),rows(CH,W),rows(m,I),rows(CH,W),
+            pl.BlockSpec((2,NB,W,I),lambda i:(i,0,0,0)),pl.BlockSpec((2,W,I),lambda i:(i,0,0))],
         out_shape=[sd((L,W),LOW),sd((C*L,I),F),sd((C*L,I),F),sd((L,W),F),sd((C*L,I),F),sd((L,W),F),sd((n,NB,W,I),LOW),sd((n,W,I),LOW)],
-        scratch_shapes=[V((W,I),F),V((C,I),F),V((W,I),F),V((1,W),F),V((C*CH,C*CH),F),V((C*CH,C*CH),F),
-            V((C*CH,I),LOW),V((C*CH,W),LOW),V((C*CH,I),LOW),V((C*CH,C*CH),LOW),V((C*CH,I),F)],
+        scratch_shapes=[V((W,I),F),V((C,I),F),V((W,I),F),V((1,W),F),V((m,m),F),V((m,m),F)]+[kinds[name] for name in FSLOT]*2,
         compiler_params=pltpu.CompilerParams(vmem_limit_bytes=48*1024*1024),
-    )(x,own)
+    )(x,x,own)
 
 SLOT=("BASE","DX2","X2","RG1","G1","RPG2","DS2Q","KK","YB","GB","DB","SB","M2B","RED","S2E","S1B","X2Q","DZQ","DZ1Q","DKQ","DQ","KST","QST","T0","RP","PG1","R")
 
@@ -350,6 +399,7 @@
         out_shape=[sd((n,tall,3*W),LOW),sd((W,I),F),sd((C,I),F),sd((W,I),F),sd((1,W),F),sd((1,W),F),sd((1,W),F),sd((1,CH),F)],
         scratch_shapes=[V((m,m),F),V((m,m),F),V((m,m),F),V((m,I),LOW),V((m,I),F),V((CH,W),F),V((CH,W),F)]+slot_shapes(C,W,I)*2,
         compiler_params=pltpu.CompilerParams(vmem_limit_bytes=48*1024*1024),
+        cost_estimate=pl.CostEstimate(flops=1000,bytes_accessed=1000,transcendentals=0),
     )(*ins,*ins,*ins,us,w1s,own)
 
 RATE_SCALE = 0.25
@@ -427,6 +477,28 @@
     return jnp.stack([jnp.where(upper, got, array), jnp.where(upper, array, got)])
 
 
+def params_kernel(f_ref, s_ref, fb_ref, sb_ref, g_ref, b_ref, r_ref, o_ref):
+    heads, head, inner = f_ref.shape
+    for i in range(heads):
+        o_ref[i, :head] = f_ref[i]
+        o_ref[i, head : 2 * head] = s_ref[i]
+        o_ref[i, 2 * head :] = jnp.zeros((8, inner), F)
+        o_ref[i, 2 * head : 2 * head + 1] = fb_ref[i : i + 1]
+        small = [ref[i : i + 1] for ref in (sb_ref, g_ref, b_ref)]
+        small.append(jnp.broadcast_to(r_ref[:, i : i + 1], (1, inner - 3 * head)))
+        o_ref[i, 2 * head + 1 : 2 * head + 2] = jnp.concatenate(small, 1)
+
+
+def pack_params(first_weight, *others):
+    heads, head, inner = first_weight.shape
+    return pl.pallas_call(
+        params_kernel,
+        in_specs=[pl.BlockSpec(memory_space=pltpu.VMEM)] * 7,
+        out_specs=pl.BlockSpec(memory_space=pltpu.VMEM),
+        out_shape=jax.ShapeDtypeStruct((heads, 2 * head + 8, inner), F),
+    )(first_weight, *others)
+
+
 def project_kernel(each, blocks, x_ref, g_ref, wq_ref, wk_ref, wv_ref, wr_ref, wg_ref, s_ref, n_ref, p_ref, LT):
     step = pl.program_id(0)
     rows, width = x_ref.shape
@@ -437,10 +509,8 @@
         x = x_ref[...].astype(F)
         scale = lax.rsqrt(jnp.sum(x * x, -1, keepdims=True) * (1.0 / width) + NORM_EPS)
         n_ref[...] = (x * scale * g_ref[...]).astype(LOW)
-        logits = nn(n_ref[...], wr_ref[...]).astype(LOW).astype(F)
-        heads = logits.shape[1]
-        logits = jnp.concatenate([logits, jnp.zeros((rows, 128 - heads), F)], 1)
-        LT[...] = logits.T
+        LT[...] = jnp.zeros_like(LT)
+        LT[: wr_ref.shape[0]] = nt(wr_ref[...], n_ref[...]).astype(LOW).astype(F)
 
     normed = n_ref[...]
     extra = s_ref.shape[1] - rows
@@ -463,7 +533,7 @@
 
 def project(x, gain, wq, wk, wv, wr, wg, seqs, each, extra):
     rows, width = x.shape
-    span = each * (width // wr.shape[1])
+    span = each * (width // wr.shape[0])
     blocks = width // span
     column = pl.BlockSpec((width, span), lambda s: (0, jnp.minimum(s, blocks - 1)))
     full = lambda *shape: pl.BlockSpec(shape, lambda s: (0,) * len(shape))
@@ -479,20 +549,108 @@
         ],
         out_shape=[sd((seqs, rows + extra, 3 * span), LOW), sd((rows, width), LOW), sd((rows, width), F)],
         scratch_shapes=[pltpu.VMEM((128, 128), F)],
-        compiler_params=pltpu.CompilerParams(vmem_limit_bytes=48 * 1024 * 1024),
+        compiler_params=pltpu.CompilerParams(vmem_limit_bytes=60 * 1024 * 1024),
     )(x, gain[None], wq, wk, wv, wr, wg)
 
 
-def summed(fed_parts, early):
+def tokens_kernel(each, blocks, x_ref, g_ref, m_ref, b_ref, d_ref, wq_ref, wk_ref, wv_ref, wr_ref, wg_ref, o_ref, ACC, LG):
+    step = pl.program_id(0)
+    rows, width = x_ref.shape
+    span = wq_ref.shape[1]
+    extra = b_ref.shape[1] - rows
+
+    @pl.when(step == 0)
+    def _():
+        ACC[...] = jnp.zeros_like(ACC)
+        LG[...] = jnp.zeros_like(LG)
+
+    @pl.when(step < blocks)
+    def _():
+        total = nt(d_ref[...], wg_ref[...])
+        for i, w_ref in enumerate((wq_ref, wk_ref, wv_ref)):
+            total = total + nt(b_ref[0, :rows, span * i : span * i + span], w_ref[...])
+        ACC[...] = ACC[...] + total
+        r = lax.broadcasted_iota(jnp.int32, (rows, extra), 0)
+        c = lax.broadcasted_iota(jnp.int32, (rows, extra), 1)
+        place = jnp.where((c < each) & (r == step * each + c), 1.0, 0.0)
+        LG[...] = LG[...] + nn(place, b_ref[0, rows:, :rows])
+
+    @pl.when(step == pl.num_programs(0) - 1)
+    def _():
+        heads = wr_ref.shape[0]
+        x = x_ref[...].astype(F)
+        scale = lax.rsqrt(jnp.sum(x * x, -1, keepdims=True) * (1.0 / width) + NORM_EPS)
+        grad = (ACC[...] + nn(LG[...].T[:, :heads], wr_ref[...])) * g_ref[...]
+        along = jnp.sum(x * grad, -1, keepdims=True) * (1.0 / width)
+        o_ref[...] = m_ref[...] + scale * (grad - x * (scale * scale * along))
+
+
+def tokens_back(x, gain, middle_grad, back, gate_low, wq, wk, wv, wr, wg, each):
+    rows, width = x.shape
+    seqs, tall, lanes = back.shape
+    span = lanes // 3
+    blocks = width // span
+    column = pl.BlockSpec((width, span), lambda s: (0, jnp.minimum(s, blocks - 1)))
+    full = lambda *shape: pl.BlockSpec(shape, lambda s: (0,) * len(shape))
+    return pl.pallas_call(
+        partial(tokens_kernel, each, blocks),
+        grid=(blocks,),
+        in_specs=[
+            full(rows, width), full(1, width), full(rows, width),
+            pl.BlockSpec((1, tall, lanes), lambda s: (s, 0, 0)),
+            pl.BlockSpec((rows, span), lambda s: (0, s)),
+            column, column, column, full(*wr.shape), column,
+        ],
+        out_specs=full(rows, width),
+        out_shape=jax.ShapeDtypeStruct((rows, width), F),
+        scratch_shapes=[pltpu.VMEM((rows, width), F), pltpu.VMEM((128, 128), F)],
+        compiler_params=pltpu.CompilerParams(vmem_limit_bytes=16 * 1024 * 1024),
+    )(x, gain[None], middle_grad, back, gate_low, wq, wk, wv, wr, wg)
+
+
+def feed_kernel(a_ref, b_ref, c_ref, g_ref, l_ref, d_ref):
+    unit = g_ref.shape[1]
+    g_ref[...] = a_ref[0, :unit].astype(F).T
+    l_ref[...] = b_ref[0, :unit].astype(F).T
+    half = unit // 2
+    for i in range(2):
+        d_ref[half * i : half * i + half] = c_ref[i, unit : unit + half].astype(F)
+
+
+def feed_outputs(fed, inner_units):
+    seqs, tall, width = fed.shape
+    steps = seqs // 2
+    unit = inner_units // steps
+    sd = jax.ShapeDtypeStruct
+    return pl.pallas_call(
+        feed_kernel,
+        grid=(steps,),
+        in_specs=[
+            pl.BlockSpec((1, tall, width), lambda i: (i, 0, 0)),
+            pl.BlockSpec((1, tall, width), lambda i: (i + steps, 0, 0)),
+            pl.BlockSpec((2, tall, width), lambda i: (i, 0, 0)),
+        ],
+        out_specs=[
+            pl.BlockSpec((width, unit), lambda i: (0, i)),
+            pl.BlockSpec((width, unit), lambda i: (0, i)),
+            pl.BlockSpec((unit, width), lambda i: (i, 0)),
+        ],
+        out_shape=[sd((width, inner_units), F)] * 2 + [sd((inner_units, width), F)],
+        compiler_params=pltpu.CompilerParams(vmem_limit_bytes=16 * 1024 * 1024),
+    )(fed, fed, fed)
+
+
+def swapped(array):
     seqs = lax.axis_size("seq")
-    early = early.reshape(seqs, -1, early.shape[-1])
-    early = lax.all_to_all(early, "seq", split_axis=0, concat_axis=0, tiled=True)
-    return jnp.concatenate(
-        [jnp.sum(fed_parts.astype(F), 0).astype(LOW), jnp.sum(early.astype(F), 0).astype(LOW)], 0
-    )
-
-
-def share_rows(every_normed, back_sent, state_g, vectors, fed_parts, early, heads, local_heads, head, weights_in):
+    array = array.reshape(seqs, -1, array.shape[-1])
+    return lax.all_to_all(array, "seq", split_axis=0, concat_axis=0, tiled=True)
+
+
+def summed(parts):
+    return jnp.sum(parts.astype(F), 0).astype(LOW)
+
+
+def share_rows(every_normed, back_sent, state_g, vectors, fed_parts, early, aside, heads, local_heads, head, weights_in):
     seqs, tps = lax.axis_size("seq"), lax.axis_size("tp")
     width = every_normed.shape[1]
     lanes = back_sent.shape[2]
@@ -501,7 +659,11 @@
     each = span // head
     first_g, first_bias_g, second_g, second_bias_g, gain_g, shift_g, bias_g = state_g
     inner = first_g.shape[1]
-    fed = lax.all_gather(summed(fed_parts, early), "seq", axis=0, tiled=False)
+    fed = lax.all_gather(summed(fed_parts), "seq", axis=0, tiled=False)
+    early = lax.all_gather(summed(swapped(early)), "seq", axis=0, tiled=True)
+    for mask in reversed(masks_of("tp")):
+        early = double(early, "tp", mask)
+    early = early.reshape(2, width, width).astype(F)
     back = lax.all_to_all(back_sent, "seq", split_axis=0, concat_axis=0, tiled=True)
     qkv_g = back_sent[:, :rows].reshape(seqs * rows, lanes)
     logit_g = back_sent[:, rows : rows + each, :rows].transpose(1, 0, 2).reshape(each, seqs * rows)
@@ -549,8 +711,10 @@
     rate_weight_grad = rest[:, :, :rate_rows].reshape(seqs * each, width)[:heads].T.astype(F)
     vectors = rest[:, :, rate_rows : rate_rows + vector_rows].reshape(seqs, 4, width)
     vectors = jnp.sum(vectors.astype(F), 0)
-    norm_gain_grad = jnp.sum(sum(weights[i] * weights_in[i].astype(F) for i in range(3)), -1)
-    return weights, states[:, :, :head], states[:, :, head], rate_weight_grad, vectors, fed, back, norm_gain_grad
+    grads = (weights[0], weights[1], weights[2], early[1])
+    norm_gain_grad = jnp.sum(sum(g * w.astype(F) for g, w in zip(grads, weights_in)), -1)
+    head_w = (states[:, 0, :head], jnp.swapaxes(states[:, 1, :head], 1, 2))
+    return weights, head_w, states[:, :, head], rate_weight_grad, vectors, fed, back, early, aside, norm_gain_grad
 
 
 def pack_kernel(head, me_ref, n_ref, x_ref, w_ref, wb_ref, u_ref, ub_ref, g_ref, s_ref, r_ref, v_ref, keep_ref, sent_ref, COL, UC, SMALL):
@@ -597,25 +761,44 @@
             out[row : row + 16, lane : lane + 128] = tile.astype(LOW)
 
 
-def last_kernel(seqs, each, heads, local_heads, me_ref, a_ref, b_ref, wq_ref, wk_ref, wv_ref,
-                q_ref, k_ref, v_ref, n_ref, s_ref, r_ref):
-    cut = a_ref.shape[3]
-    span = a_ref.shape[4] // 3
+def last_kernel(seqs, each, heads, local_heads, me_ref, *refs):
+    ours = lax.rem(pl.program_id(0), 2) == lax.rem(me_ref[0], 2)
+
+    @pl.when(ours)
+    def _():
+        last_part(seqs, each, heads, local_heads, me_ref, refs[0], refs[1], *refs[4:])
+
+    @pl.when(jnp.logical_not(ours))
+    def _():
+        last_part(seqs, each, heads, local_heads, me_ref, refs[2], refs[3], *refs[4:])
+
+
+def last_part(seqs, each, heads, local_heads, me_ref, a_ref, b_ref, wq_ref, wk_ref, wv_ref, wg_ref,
+              q_ref, k_ref, v_ref, n_ref, f_ref, s_ref, r_ref, out_ref, gate_ref, gate_n_ref, ST):
+    t = pl.program_id(0)
+    cut = a_ref.shape[2]
+    lanes = a_ref.shape[3]
+    span = lanes // 3
     below = q_ref.shape[0] - cut
+
+    def spot(s):
+        return s % 2, ((s >> 1) & 1) * 2 + (s >> 2)
+
     for s in range(seqs):
         if s * each >= heads:
             continue
-        x, q = s % 2, ((s >> 1) & 1) * 2 + (s >> 2)
+        x, q = spot(s)
         for i, o_ref in enumerate((q_ref, k_ref, v_ref)):
-            o_ref[:cut, span * s : span * s + span] = a_ref[0, 0, 4 * x + q, :, span * i : span * i + span].astype(F)
-            o_ref[cut:, span * s : span * s + span] = b_ref[0, x, 0, q, :below, span * i : span * i + span].astype(F)
+            o_ref[:cut, span * s : span * s + span] = a_ref[0, 4 * x + q, :, span * i : span * i + span].astype(F)
+            o_ref[cut:, span * s : span * s + span] = b_ref[x, 0, q, :below, span * i : span * i + span].astype(F)
     total = q_ref[...] * wq_ref[...].astype(F)
     for o_ref, w_ref in ((k_ref, wk_ref), (v_ref, wv_ref)):
         total = total + o_ref[...] * w_ref[...].astype(F)
     n_ref[...] = jnp.sum(total, -1, keepdims=True)
 
     def tile(x, q, n):
-        return b_ref[0, x, 0, q, below + 16 * (n // 3) : below + 16 * (n // 3) + 16, 128 * (n % 3) : 128 * (n % 3) + 128]
+        row, lane = below + 16 * (n // 3), 128 * (n % 3)
+        return b_ref[x, 0, q, row : row + 16, lane : lane + 128].astype(F)
 
     for i in range(local_heads):
         h = me_ref[0] * local_heads + i
@@ -625,14 +808,39 @@
         q = lax.rem(s // 2, 2) * 2 + s // 4
         for k in range(2):
             for j in range(2):
-                low = tile(x, q, k * 2 + j).astype(F)
-                high = tile(x, q, 4 + k * 2 + j).astype(F)
-                s_ref[i, k, :, 128 * j : 128 * j + 128] = jnp.where(upper, high, low)
+                ST[i, k, pl.ds(pl.multiple_of(16 * t, 16), 16), 128 * j : 128 * j + 128] = jnp.where(
+                    upper, tile(x, q, 4 + k * 2 + j), tile(x, q, k * 2 + j)
+                )
     for s in range(seqs):
-        r_ref[0, s] = tile(s % 2, ((s >> 1) & 1) * 2 + (s >> 2), 8).astype(F)
-
-
-def share_tiles(every_normed, back_sent, state_g, vectors, fed_parts, early, heads, local_heads, head, weights_in):
+        r_ref[0, s] = tile(*spot(s), 8)
+
+    first = below + 48
+    tall = out_ref.shape[0] // seqs
+
+    def square(o_ref):
+        for s in range(seqs):
+            x, q = spot(s)
+            for i in range(2):
+                row = first + tall * i
+                o_ref[tall * s : tall * s + tall, lanes * i : lanes * i + lanes] = b_ref[x, 0, q, row : row + tall].astype(F)
+
+    @pl.when(t == 3)
+    def _():
+        for i in range(local_heads):
+            f_ref[i] = ST[i, 0]
+            s_ref[i] = ST[i, 1]
+
+    @pl.when(t % 2 == 0)
+    def _():
+        square(out_ref)
+
+    @pl.when(t % 2 == 1)
+    def _():
+        square(gate_ref)
+        gate_n_ref[...] = jnp.sum(gate_ref[...] * wg_ref[...].astype(F), -1, keepdims=True)
+
+
+def share_tiles(every_normed, back_sent, state_g, vectors, fed_parts, early, aside, heads, local_heads, head, weights_in):
     seqs, tps = lax.axis_size("seq"), lax.axis_size("tp")
     width = every_normed.shape[1]
     lanes = back_sent.shape[2]
@@ -652,52 +860,60 @@
             pltpu.VMEM((each * head, inner), F),
             pltpu.VMEM((4, 16, 128), F),
         ],
-        compiler_params=pltpu.CompilerParams(vmem_limit_bytes=48 * 1024 * 1024),
+        compiler_params=pltpu.CompilerParams(vmem_limit_bytes=20 * 1024 * 1024),
     )(me, every_normed, back_sent, *state_g, vectors)
     late = late.astype(F) + flip(late_sent, "tp", 1).astype(F)
-    late, fed_parts = lax.optimization_barrier((late, fed_parts))
-    fed = summed(fed_parts, early)
+    fed = lax.all_gather(summed(fed_parts), "seq", axis=0, tiled=False)
     late = scatter_once(late, "tp", 2).astype(LOW)[0]
-    late, fed = lax.optimization_barrier((late, fed))
-    fed = lax.all_gather(fed, "seq", axis=0, tiled=False)
+    early = summed(swapped(early))
+    late = jnp.concatenate([late, early[:, :lanes], early[:, lanes:]], 0)
+    share = late.shape[0]
     late = double(late, "seq", 4)
     late = double(late, "seq", 2)
     late, back_sent = lax.optimization_barrier((late, back_sent))
     back = lax.all_to_all(back_sent, "seq", split_axis=0, concat_axis=0, tiled=True)
-    cut = 128
+    cut = 160
     part_a, part_b = late[:, :, :cut], late[:, :, cut:]
     part_a, part_b = double(part_a, "seq", 1), double(part_b, "tp", 2)
-    part_a, part_b, fed = lax.optimization_barrier((part_a, part_b, fed))
     part_a, part_b = double(part_a, "tp", 2), double(part_b, "seq", 1)
-    part_a, part_b = double(part_a, "tp", 1), double(part_b, "tp", 1)
-    part_a = part_a.reshape(2, 2, seqs, cut, lanes)
-    part_b = part_b.reshape(2, 2, 2, seqs // 2, share - cut, lanes)
+    part_a, part_b, fed, back, aside = lax.optimization_barrier((part_a, part_b, fed, back, aside))
+    part_a = part_a.reshape(2, seqs, cut, lanes)
+    part_b = part_b.reshape(2, 2, seqs // 2, share - cut, lanes)
+    got_a, got_b = flip(part_a, "tp", 1), flip(part_b, "tp", 1)
+    a_spec = pl.BlockSpec((1, seqs, cut, lanes), lambda t: (t // 2, 0, 0, 0))
+    b_spec = pl.BlockSpec((2, 1, seqs // 2, share - cut, lanes), lambda t: (0, t // 2, 0, 0, 0))
     square = pl.BlockSpec((here, width), lambda t: (t, 0))
-    sd = jax.ShapeDtypeStruct
-    *weights, norm_gain_grad, head_w, small = pl.pallas_call(
+    taller = pl.BlockSpec((2 * here, width), lambda t: (t // 2, 0))
+    *weights, norm_gain_grad, head_f, head_s, small, out_g, gate_g, gate_n = pl.pallas_call(
         partial(last_kernel, seqs, each, heads, local_heads),
         grid=(tps,),
         in_specs=[
             pl.BlockSpec(memory_space=pltpu.SMEM),
-            pl.BlockSpec((1, 1, seqs, cut, lanes), lambda t: (t % 2, t // 2, 0, 0, 0)),
-            pl.BlockSpec((1, 2, 1, seqs // 2, share - cut, lanes), lambda t: (t % 2, 0, t // 2, 0, 0, 0)),
-            square, square, square,
+            a_spec, b_spec, a_spec, b_spec, square, square, square, taller,
         ],
         out_specs=[
             square, square, square,
             pl.BlockSpec((here, 1), lambda t: (t, 0)),
-            pl.BlockSpec((local_heads, 2, head // tps, inner), lambda t: (0, 0, t, 0)),
+            pl.BlockSpec((local_heads, head, inner), lambda t: (0, 0, 0)),
+            pl.BlockSpec((local_heads, head, inner), lambda t: (0, 0, 0)),
             pl.BlockSpec((1, seqs, 16, 128), lambda t: (t, 0, 0, 0)),
+            taller, taller,
+            pl.BlockSpec((2 * here, 1), lambda t: (t // 2, 0)),
         ],
         out_shape=[sd((width, width), F)] * 3
-        + [sd((width, 1), F), sd((local_heads, 2, head, inner), F), sd((tps, seqs, 16, 128), F)],
+        + [sd((width, 1), F), sd((local_heads, head, inner), F), sd((local_heads, head, inner), F)]
+        + [sd((tps, seqs, 16, 128), F)]
+        + [sd((width, width), F)] * 2
+        + [sd((width, 1), F)],
+        scratch_shapes=[pltpu.VMEM((local_heads, 2, head, inner), F)],
         compiler_params=pltpu.CompilerParams(vmem_limit_bytes=48 * 1024 * 1024),
-    )(me, part_a, part_b, *weights_in)
+    )(me, part_a, part_b, got_a, got_b, *weights_in)
+    norm_gain_grad = norm_gain_grad + gate_n
     head_t = small[:, :, :2].transpose(1, 0, 2, 3).reshape(seqs * each, 2, inner)
     head_t = lax.dynamic_slice_in_dim(head_t, me[0] * local_heads, local_heads, 0)
     rate_weight_grad = small[:, :, 2:5].transpose(1, 0, 2, 3).reshape(seqs * each, width)[:heads].T
     vectors = jnp.sum(small[:, :, 5:10], 1).reshape(-1)[: 3 * width].reshape(3, width)
-    return weights, head_w, head_t, rate_weight_grad, vectors, fed, back, norm_gain_grad[:, 0]
+    return weights, (head_f, jnp.swapaxes(head_s, 1, 2)), head_t, rate_weight_grad, vectors, fed, back, (out_g, gate_g), aside, norm_gain_grad[:, 0]
 
 
 def on_device(
@@ -727,18 +943,8 @@
     def swap(array):
         return lax.all_to_all(array, "seq", split_axis=0, concat_axis=0, tiled=True)
 
-    tail = jnp.concatenate(
-        [second_bias, inner_gain, inner_bias, jnp.pad(rate_bias[:, None], ((0, 0), (0, inner - 3 * head - 1)))], -1
-    )
-    packed = jnp.concatenate(
-        [
-            first_weight,
-            jnp.swapaxes(second_weight, 1, 2),
-            first_bias[:, None],
-            tail[:, None],
-            jnp.zeros((local_heads, 6, inner), F),
-        ],
-        1,
+    packed = pack_params(
+        first_weight, jnp.swapaxes(second_weight, 1, 2), first_bias, second_bias, inner_gain, inner_bias, rate_bias[None]
     )
     every = lax.all_gather(packed, "tp", axis=0, tiled=True)
     own = lax.dynamic_slice_in_dim(every, jnp.minimum(rank * each, heads - each), each, 0)
@@ -750,7 +956,7 @@
     every_grad = gather_near(down_grad, "tp")
     if span % 128 == 0 and width % span == 0 and rows == 128:
         sent, normed, gate_pre = project(
-            tokens[0], norm_gain, query_weight, key_weight, value_weight, rate_weight, branch_gate, seqs, each, extra
+            tokens[0], norm_gain, query_weight, key_weight, value_weight, rate_weight.T, branch_gate, seqs, each, extra
         )
     else:
         normed = normed_val.astype(LOW)
@@ -788,7 +994,23 @@
     input_part = jnp.einsum("tf,df->td", gate_low, feed_gate, preferred_element_type=F) + jnp.einsum(
         "tf,df->td", linear_low, feed_linear, preferred_element_type=F
     )
-    feed_in_grad = scatter_near(input_part, "tp")
+    feed_down_grad = jnp.einsum("tf,td->fd", hidden, every_grad, preferred_element_type=F)
+    both_low = jnp.concatenate([gate_low, linear_low], 1)
+    feed_both_grad = jnp.einsum("tf,td->fd", both_low, every_in, preferred_element_type=F)
+    fed_parts = jnp.concatenate(
+        [
+            feed_both_grad.astype(LOW).reshape(seqs, -1, width),
+            feed_down_grad.astype(LOW).reshape(seqs, -1, width),
+        ],
+        1,
+    )
+    feed_in_grad = input_part
+    for mask in masks_of("tp"):
+        half = feed_in_grad.shape[0] // 2
+        arrived = flip(feed_in_grad[half:].astype(LOW), "tp", mask)
+        if mask == masks_of("tp")[-1]:
+            arrived, fed_parts = lax.optimization_barrier((arrived, fed_parts))
+        feed_in_grad = feed_in_grad[:half].astype(F) + arrived.astype(F)
     middle_part, feed_gain_grad = feed_pull(feed_in_grad)
     middle_grad = grad_out + middle_part
     out_low = middle_grad.astype(LOW)
@@ -801,9 +1023,6 @@
     second_out = scatter_near(second_part, "tp")
     result = (middle + second_out).astype(LOW)[None]
 
-    feed_down_grad = jnp.einsum("tf,td->fd", hidden, every_grad, preferred_element_type=F)
-    both_low = jnp.concatenate([gate_low, linear_low], 1)
-    feed_both_grad = jnp.einsum("tf,td->fd", both_low, every_in, preferred_element_type=F)
     gate_low_pre = gate_pre_grad.astype(LOW)
     out_low, gate_low_pre, out_grad_c = lax.optimization_barrier((out_low, gate_low_pre, out_grad_c))
     tps = lax.axis_size("tp")
@@ -829,49 +1048,47 @@
 
     early_sent = products(parts[half:]).astype(LOW)
     early = products(parts[:half]) + flip(early_sent, "tp", 1).astype(F)
-    fed_parts = jnp.concatenate(
-        [
-            feed_both_grad.astype(LOW).reshape(seqs, -1, width),
-            feed_down_grad.astype(LOW).reshape(seqs, -1, width),
-        ],
-        1,
-    )
     fed_parts, early, out_grad_c = lax.optimization_barrier((fed_parts, early.astype(LOW), out_grad_c))
     fed_parts = swap(fed_parts)
     for mask in masks_of("tp")[1:]:
         early = scatter_once(early, "tp", mask)
 
     back_sent, *state_g = bwd_scan(got, own, out_grad_c, *kept)
-    early, back_sent = lax.optimization_barrier((early.astype(LOW), back_sent))
+    early, fed_parts, back_sent = lax.optimization_barrier((early.astype(LOW), fed_parts, back_sent))
     vectors = jnp.stack([post_gain_grad, post_bias_grad, feed_gain_grad])
     share = share_tiles if each == 2 and tps == 4 and seqs == 8 else share_rows
-    weights, head_w, head_t, rate_weight_grad, vectors, fed, back, norm_gain_grad = share(
-        every_normed, back_sent, state_g, vectors, fed_parts, early, heads, local_heads, head,
-        (query_weight, key_weight, value_weight),
+    weights, head_w, head_t, rate_weight_grad, vectors, fed, back, early, result, norm_gain_grad = share(
+        every_normed, back_sent, state_g, vectors, fed_parts, early, result, heads, local_heads, head,
+        (query_weight, key_weight, value_weight, branch_gate),
     )
-    query_low = from_chains(back[:, :rows, :span])
-    keys_low = from_chains(back[:, :rows, span : 2 * span])
-    values_low = from_chains(back[:, :rows, 2 * span :])
-    logit_low = back[:, rows : rows + each, :rows].reshape(seqs * each, rows)[:heads].T
-
-    normed_grad = (
-        jnp.einsum("te,de->td", query_low, query_weight, preferred_element_type=F)
-        + jnp.einsum("te,de->td", keys_low, key_weight, preferred_element_type=F)
-        + jnp.einsum("te,de->td", values_low, value_weight, preferred_element_type=F)
-        + jnp.einsum("te,de->td", logit_low, rate_weight, preferred_element_type=F)
-        + jnp.einsum("te,de->td", gate_low_pre, branch_gate, preferred_element_type=F)
-    )
-    residual_part, unused = norm_pull(normed_grad)
-    tokens_grad = (middle_grad + residual_part)[None]
+    if span % 128 == 0 and width % span == 0 and rows == 128:
+        tokens_grad = tokens_back(
+            tokens[0], norm_gain, middle_grad, back, gate_low_pre,
+            query_weight, key_weight, value_weight, rate_weight.T, branch_gate, each,
+        )[None]
+    else:
+        query_low = from_chains(back[:, :rows, :span])
+        keys_low = from_chains(back[:, :rows, span : 2 * span])
+        values_low = from_chains(back[:, :rows, 2 * span :])
+        logit_low = back[:, rows : rows + each, :rows].reshape(seqs * each, rows)[:heads].T
+
+        normed_grad = (
+            jnp.einsum("te,de->td", query_low, query_weight, preferred_element_type=F)
+            + jnp.einsum("te,de->td", keys_low, key_weight, preferred_element_type=F)
+            + jnp.einsum("te,de->td", values_low, value_weight, preferred_element_type=F)
+            + jnp.einsum("te,de->td", logit_low, rate_weight, preferred_element_type=F)
+            + jnp.einsum("te,de->td", gate_low_pre, branch_gate, preferred_element_type=F)
+        )
+        residual_part, unused = norm_pull(normed_grad)
+        tokens_grad = (middle_grad + residual_part)[None]
     inner_units = feed_gate.shape[1]
-    both = fed[:, : 2 * inner_units // seqs].reshape(2, inner_units, width).astype(F)
-    down = fed[:, 2 * inner_units // seqs : 3 * inner_units // seqs].reshape(inner_units, width).astype(F)
-    early = fed[:, 3 * inner_units // seqs :].reshape(-1, width)
-    for mask in reversed(masks_of("tp")):
-        early = double(early, "tp", mask)
-    early = early.reshape(2, width, width).astype(F)
+    if 2 * inner_units // seqs % 128 == 0:
+        fed_grads = feed_outputs(fed, inner_units)
+    else:
+        both = fed[:, : 2 * inner_units // seqs].reshape(2, inner_units, width).astype(F)
+        down = fed[:, 2 * inner_units // seqs : 3 * inner_units // seqs].reshape(inner_units, width).astype(F)
+        fed_grads = (both[0].T, both[1].T, down)
     norm_gain_grad = norm_gain_grad + jnp.sum(rate_weight_grad * rate_weight.astype(F), -1)
-    norm_gain_grad = norm_gain_grad + jnp.sum(early[1] * branch_gate.astype(F), -1)
     norm_gain_grad = norm_gain_grad / norm_gain
     tail_sum = head_t[:, 1]
     return (
@@ -883,9 +1100,9 @@
         weights[2],
         rate_weight_grad,
         tail_sum[:, 3 * head],
-        head_w[:, 0],
+        head_w[0],
         head_t[:, 0],
-        jnp.swapaxes(head_w[:, 1], 1, 2),
+        head_w[1],
         tail_sum[:, :head],
         tail_sum[:, head : 2 * head],
         tail_sum[:, 2 * head : 3 * head],
@@ -894,9 +1111,7 @@
         vectors[0],
         vectors[1],
         vectors[2],
-        both[0].T,
-        both[1].T,
-        down,
+        *fed_grads,
     )
 
 

time: 395 us -> 354 us (0.90)
  local copies, waits for them, and re-layouts: 51.1 us -> 14.3 us
  other arithmetic: 37.5 us -> 17.8 us
  Pallas kernels: 99.6 us -> 111 us
  waiting for transfers between devices: 121 us -> 129 us
    ppermute x22 -> x20, waiting for transfers between devices: 83.5 us -> 99.8 us  [flip(): return lax.ppermute(array, axis, [(i, i ^ mask) for i in range(peers)])]
    unnamed x145 -> x85, local copies, waits for them, and re-layouts: 19.4 us -> 6.8 us
    squeeze x3 -> x0, local copies, waits for them, and re-layouts: 7.6 us -> none  [the longest x1 3.02 us: on_device(): both[1]]
    another operation x16 -> x12, other arithmetic: 11.2 us -> 5.25 us  [double(): jnp.stack([jnp.where(upper, got, array), jnp.where(upper, array, got)])]
    pallas_call x1 -> x4, Pallas kernels: 41.5 us -> 47.2 us  [the longest x1 38 us: fwd_scan(): pl.pallas_call(partial(fwd_kernel, C, H), grid=(n // 2,), in_specs=[pl.Bl...]
    transpose x5 -> x0, local copies, waits for them, and re-layouts: 5.65 us -> none  [the longest x4 4.86 us: from_chains(): return array.transpose(1, 0, 2).reshape(rows, seqs * span)[:, :width]]
    all_to_all x1, waiting for transfers between devices: 5.49 us -> 0.01 us  [share_tiles(): lax.all_to_all(back_sent, 'seq', split_axis=0, concat_axis=0, tiled=True)]
    slice x5 -> x3, local copies, waits for them, and re-layouts: 5.08 us -> 0.07 us  [the longest x2 0.06 us: on_device(): arrived = flip(feed_in_grad[half:].astype(LOW), 'tp', mask)]
  transfers between devices with their start and end apart: 30 -> 28, of which waited for: 20 -> 17; matrix products, arithmetic and copies ran while one was open for 15% -> 7% of each run, Pallas kernels for 24% -> 27%
where the time goes in v4:
time: 354 us; the launch traced here: 352 us
  waiting for transfers between devices  129 us (36%)
  Pallas kernels  111 us (31%)
  starting transfers between devices  40.5 us (11%)
  other arithmetic  17.8 us (5%)
  between operations  14.7 us (4%)
  local copies, waits for them, and re-layouts  14.3 us (4%)
  blocking collectives  12.7 us (4%)
  matrix products  12.7 us (4%)
    ppermute x20, waiting for transfers between devices, flip(): return lax.ppermute(array, axis, [(i, i ^ mask) for i in range(peers)])  99.8 us
    pallas_call x1, Pallas kernels, bwd_scan(): pl.pallas_call(partial(bwd_kernel, C, H, n // 2), grid=(n // 2,), in_spec...  43.5 us
    pallas_call x1, Pallas kernels, fwd_scan(): pl.pallas_call(partial(fwd_kernel, C, H), grid=(n // 2,), in_specs=[pl.Bl...  38 us
    all_to_all x3, waiting for transfers between devices, swap(): return lax.all_to_all(array, 'seq', split_axis=0, concat_axis=0, tiled=True)  19.9 us
    ppermute x20, starting transfers between devices, flip(): return lax.ppermute(array, axis, [(i, i ^ mask) for i in range(peers)])  16.7 us
    all_to_all x3, starting transfers between devices, swap(): return lax.all_to_all(array, 'seq', split_axis=0, concat_axis=0, tiled=True)  16.2 us
    all_to_all x1, blocking collectives, swap(): return lax.all_to_all(array, 'seq', split_axis=0, concat_axis=0, tiled=True)  12.7 us
    pallas_call x1, Pallas kernels, share_tiles(): pl.pallas_call(partial(last_kernel, seqs, each, heads, local_heads), grid...  10.1 us
  transfers between devices with their start and end apart: 28, of which 17 were waited for; matrix products, arithmetic and copies ran while one was open for 7% of the time, Pallas kernels for 27%

profile of v4, /device:TPU:0, one launch (start us, length us, event | category | flops | bytes accessed | tf_op | source)
XLA Modules:
  0.0 352.5 jit_solution(7103557901657488639)
XLA Ops:
  7.3 2.0 shard_map.382
  9.3 1.3 broadcast_in_dim.28.g_ref
  10.6 7.4 %shard_map.381 = (bf16[8,144,384]{2,1,0:T(8,128)(2,1)}, bf16[128,768]{1,0:T(8,128)(2,1)}, f32[128,768]{1,0:T(8,128)}) custom-call(bf16[128,768]{1,0:T(8,128)(2,1)} %bitcast.96, f32[1,768]{1,0:T(1,128)} %broadcast_in_dim.28.g_ref, bf16[768,768]{1,0:T(8,128)(2,1)} %refs_4_.1, bf16[768,768]{1,0:T(8,128)(2,1)} %refs_5_.1, bf16[768,768]{1,0:T(8,128)(2,1)} %refs_6_.1, ...), custom_call_target="tpu_custom_call" | custom-call | tf_op jit(solution)/shard_map/pallas_call | solution.py:541
  18.0 7.4 %all-to-all-start = ((bf16[8,144,384]{2,1,0:T(8,128)(2,1)}), bf16[8,144,384]{2,1,0:T(8,128)(2,1)S(1)}, u32[]{:S(2)}, u32[]{:S(2)}) async-start(bf16[8,144,384]{2,1,0:T(8,128)(2,1)} %get-tuple-element.79), calls=%async_computation | async-start | bytes 1769472 | tf_op jit(solution)/shard_map/all_to_all | solution.py:944
  25.4 1.6 collective-permute-start
  27.0 8.8 %collective-permute-done = bf16[128,768]{1,0:T(8,128)(2,1)S(1)} collective-permute-done((bf16[128,768]{1,0:T(8,128)(2,1)S(1)}, bf16[128,768]{1,0:T(8,128)(2,1)S(1)}, u32[]{:S(2)}, u32[]{:S(2)}) %collective-permute-start) | collective-permute-done | bytes 196640 | tf_op jit(solution)/shard_map/ppermute | solution.py:436
  35.9 1.7 collective-permute-done.1
  37.6 0.9 pad_maximum_fusion.6
  38.6 1.0 constant_dynamic-slice_fusion.2.own_ref.refs_29_
  39.6 8.2 %all-to-all-done.xa_ref.xb_ref.refs_0_.refs_9_.refs_18_ = bf16[8,144,384]{2,1,0:T(8,128)(2,1)S(1)} async-done(((bf16[8,144,384]{2,1,0:T(8,128)(2,1)}), bf16[8,144,384]{2,1,0:T(8,128)(2,1)S(1)}, u32[]{:S(2)}, u32[]{:S(2)}) %all-to-all-start) | async-done | bytes 884768 | tf_op jit(solution)/shard_map/all_to_all | solution.py:944
  47.7 38.0 %shard_map.383 = (bf16[1024,128]{1,0:T(8,128)(2,1)S(1)}, f32[2048,256]{1,0:T(8,128)S(1)}, f32[2048,256]{1,0:T(8,128)}, f32[1024,128]{1,0:T(8,128)S(1)}, f32[2048...) custom-call(bf16[8,144,384]{2,1,0:T(8,128)(2,1)S(1)} %all-to-all-don, ...), custom_call_target="tpu_custom_call" | custom-call | tf_op jit(solution)/shard_map/pallas_call | solution.py:214
  85.7 1.3 copy-done.3
  88.6 12.7 %all_to_all.30 = bf16[8,128,128]{2,1,0:T(8,128)(2,1)S(1)} all-to-all(bf16[8,128,128]{2,1,0:T(8,128)(2,1)} %bitcast.99), channel_id=1, replica_groups=mesh['seq'=8,'tp'=4] {'seq'}, dimensions={0} | all-to-all | bytes 524288 | tf_op jit(solution)/shard_map/all_to_all | solution.py:944
  102.6 1.6 collective-permute-start.2
  104.2 4.2 %collective-permute-done.2 = bf16[128,768]{1,0:T(8,128)(2,1)S(1)} collective-permute-done((bf16[128,768]{1,0:T(8,128)(2,1)S(1)}, bf16[128,768]{1,0:T(8,128)(2,1)S(1)}, u32[]{:S(2)}, u32[]{:S(2)}) %collective-permute-start.2) | collective-permute-done | bytes 196640 | tf_op jit(solution)/shard_map/ppermute | solution.py:436
  109.1 1.1 collective-permute-done.3
  110.8 1.0 multiply_convert_fusion
  113.9 1.0 collective-permute-done.4
  115.0 1.6 collective-permute-start.5
  116.6 1.0 convolution_convert_fusion
  117.6 1.6 pad_maximum_fusion
  119.2 2.9 collective-permute-done.5
  122.2 0.9 fusion.65
  123.1 1.5 fusion.17
  125.8 4.2 %all-to-all-start.2 = ((bf16[8,128,128]{2,1,0:T(8,128)(2,1)}), bf16[8,128,128]{2,1,0:T(8,128)(2,1)S(1)}, u32[]{:S(2)}, u32[]{:S(2)}) async-start(bf16[8,128,128]{2,1,0:T(8,128)(2,1)} %bitcast_bitcast_fusion), calls=%async_computation.2 | async-start | bytes 524288 | tf_op jit(solution)/shard_map/all_to_all | solution.py:944
  130.0 0.9 fusion.53
  130.9 2.8 convolution_convert_fusion.2
  133.7 4.8 %all-to-all-done.2 = bf16[8,128,128]{2,1,0:T(8,128)(2,1)S(1)} async-done(((bf16[8,128,128]{2,1,0:T(8,128)(2,1)}), bf16[8,128,128]{2,1,0:T(8,128)(2,1)S(1)}, u32[]{:S(2)}, u32[]{:S(2)}) %all-to-all-start.2) | async-done | bytes 262176 | tf_op jit(solution)/shard_map/all_to_all | solution.py:944
  138.8 1.5 convolution_convert_fusion.1
  140.3 2.8 collective-permute-done.6
  143.2 1.5 add_convert_fusion
  144.7 4.6 %all-to-all-start.3 = ((bf16[8,192,768]{2,1,0:T(8,128)(2,1)}), bf16[8,192,768]{2,1,0:T(8,128)(2,1)}, u32[]{:S(2)}, u32[]{:S(2)}) async-start(bf16[8,192,768]{2,1,0:T(8,128)(2,1)} %pad_maximum_fusion), calls=%async_computation.3 | async-start | bytes 4718592 | tf_op jit(solution)/shard_map/all_to_all | solution.py:944
  149.3 1.2 slice.110
  150.5 1.6 collective-permute-start.7
  152.1 43.5 %shard_map.384 = (bf16[8,144,384]{2,1,0:T(8,128)(2,1)}, f32[128,256]{1,0:T(8,128)S(1)}, f32[2,256]{1,0:T(2,128)S(1)}, f32[128,256]{1,0:T(8,128)S(1)}, f32[1,128]...) custom-call(bf16[8,144,384]{2,1,0:T(8,128)(2,1)S(1)} %all-to-all-done.xa_ref.xb_ref.refs_0_.refs, ...), custom_call_target="tpu_custom_call" | custom-call | flops 1000 | bytes 1000 | tf_op jit(solution)/shard_map/pallas_call | solution.py:395
  195.7 1.0 add_convert_fusion.1
  196.6 6.9 %all-to-all-done.3 = bf16[8,192,768]{2,1,0:T(8,128)(2,1)} async-done(((bf16[8,192,768]{2,1,0:T(8,128)(2,1)}), bf16[8,192,768]{2,1,0:T(8,128)(2,1)}, u32[]{:S(2)}, u32[]{:S(2)}) %all-to-all-start.3) | async-done | bytes 2359328 | tf_op jit(solution)/shard_map/all_to_all | solution.py:944
  203.5 2.4 shard_map.385
  206.0 3.6 %all-to-all-start.4 = ((bf16[8,48,768]{2,1,0:T(8,128)(2,1)}), bf16[8,48,768]{2,1,0:T(8,128)(2,1)S(1)}, u32[]{:S(2)}, u32[]{:S(2)}) async-start(bf16[8,48,768]{2,1,0:T(8,128)(2,1)} %bitcast.106), calls=%async_computation.4 | async-start | bytes 1179648 | tf_op jit(solution)/shard_map/all_to_all | solution.py:646
  209.8 1.6 collective-permute-start.9
  211.4 5.5 %collective-permute-done.9 = bf16[1,240,384]{2,1,0:T(8,128)(2,1)S(1)} collective-permute-done((bf16[1,240,384]{2,1,0:T(8,128)(2,1)S(1)}, bf16[1,240,384]{2,1,0:T(8,128)(2,1)S(1)}, u32[]{:S(2)}, u32[]{:S(2)}) %collective-permute-start.9) | collective-permute-done | bytes 184352 | tf_op jit(solution)/shard_map/ppermute | solution.py:436
  216.9 9.5 %all-to-all-done.4 = bf16[8,48,768]{2,1,0:T(8,128)(2,1)S(1)} async-done(((bf16[8,48,768]{2,1,0:T(8,128)(2,1)}), bf16[8,48,768]{2,1,0:T(8,128)(2,1)S(1)}, u32[]{:S(2)}, u32[]{:S(2)}) %all-to-all-start.4) | async-done | bytes 589856 | tf_op jit(solution)/shard_map/all_to_all | solution.py:646
  226.6 2.8 reduce_sum.157
  229.4 10.6 %collective-permute-done.10 = bf16[336,384]{1,0:T(8,128)(2,1)S(1)} collective-permute-done((bf16[336,384]{1,0:T(8,128)(2,1)S(1)}, bf16[336,384]{1,0:T(8,128)(2,1)S(1)}, u32[]{:S(2)}, u32[]{:S(2)}) %collective-permute-start.10) | collective-permute-done | bytes 258080 | tf_op jit(solution)/shard_map/ppermute | solution.py:436
  240.3 21.1 %collective-permute-done.11 = bf16[2,336,384]{2,1,0:T(8,128)(2,1)S(1)} collective-permute-done((bf16[2,336,384]{2,1,0:T(8,128)(2,1)S(1)}, bf16[2,336,384]{2,1,0:T(8,128)(2,1)S(1)}, u32[]{:S(2)}, u32[]{:S(2)}) %collective-permute-start.11) | collective-permute-done | bytes 516128 | tf_op jit(solution)/shard_map/ppermute | solution.py:436
  261.7 0.8 slice.115
  262.5 1.5 collective-permute-start.12
  264.0 1.5 collective-permute-start.14
  266.4 3.8 %all-to-all-start.5 = ((bf16[8,144,384]{2,1,0:T(8,128)(2,1)}), bf16[8,144,384]{2,1,0:T(8,128)(2,1)S(1)}, u32[]{:S(2)}, u32[]{:S(2)}) async-start(bf16[8,144,384]{2,1,0:T(8,128)(2,1)} %get-tuple-element.116.x_ref), calls=%async_computation.5 | async-start | bytes 1769472 | tf_op jit(solution)/shard_map/all_to_all | solution.py:874
  270.2 22.4 %collective-permute-done.12 = bf16[2,2,160,384]{3,2,1,0:T(8,128)(2,1)} collective-permute-done((bf16[2,2,160,384]{3,2,1,0:T(8,128)(2,1)}, bf16[2,2,160,384]{3,2,1,0:T(8,128)(2,1)}, u32[]{:S(2)}, u32[]{:S(2)}) %collective-permute-start.12) | collective-permute-done | bytes 491552 | tf_op jit(solution)/shard_map/ppermute | solution.py:436
  292.6 1.1 select_bitcast_fusion.9
  293.9 1.6 collective-permute-start.13
  295.5 1.2 select_bitcast_fusion.5
  296.8 2.1 collective-permute-start.15
  298.9 1.1 convert_add_fusion
  300.0 0.9 collective-permute-start.17
  300.9 16.3 %collective-permute-done.17 = bf16[128,768]{1,0:T(8,128)(2,1)S(1)} collective-permute-done((bf16[128,768]{1,0:T(8,128)(2,1)S(1)}, bf16[128,768]{1,0:T(8,128)(2,1)S(1)}, u32[]{:S(2)}, u32[]{:S(2)}) %collective-permute-start.17) | collective-permute-done | bytes 196640 | tf_op jit(solution)/shard_map/ppermute | solution.py:436
  318.2 1.6 pad_maximum_fusion.2
  319.8 1.3 collective-permute-done.15
  322.3 1.8 copy-done.2
  324.1 2.7 shard_map.388
  326.9 0.9 copy-done.6
  328.3 4.5 %shard_map.386 = f32[128,768]{1,0:T(8,128)} custom-call(bf16[128,768]{1,0:T(8,128)(2,1)S(1)} %bitcast.97, f32[1,768]{1,0:T(1,128)S(1)} %copy-done.18, f32[128,768]{1,0:T(8,128)S(1)} %copy-done.13, bf16[8,144,384]{2,1,0:T(8,128)(2,1)S(1)} %all-to-all-done.5.b_ref, bf16[128,768]{1,0:T(8,128)(2,1)S(1)} %copy-done.15, bf16[768,768]{1,0:T(8,128)(2,1)S(1)} %copy-done.4, ...), custom_call_target="tpu_custom_call" | custom-call | tf_op jit(solution)/shard_map/pallas_call | solution.py:595
  332.8 10.1 %shard_map.387 = (f32[768,768]{1,0:T(8,128)}, f32[768,768]{1,0:T(8,128)}, f32[768,768]{1,0:T(8,128)}, f32[768,1]{1,0:T(8,128)S(1)}, f32[3,64,256]{2,1,0:T(8,128)...) custom-call(s32[1]{0:T(128)} %bitcast.me_ref, ...), custom_call_target="tpu_custom_call" | custom-call | tf_op jit(solution)/shard_map/pallas_call | solution.py:887
  (174 shorter events, 15.7 us)
Async XLA Ops:
  7.2 94.8 %copy-start = (bf16[768,768]{1,0:T(8,128)(2,1)S(1)}, bf16[768,768]{1,0:T(8,128)(2,1)}, u32[]{:S(2)}) copy-start(bf16[768,768]{1,0:T(8,128)(2,1)} %param.36) | copy-start | bytes 3538948
  7.2 31.4 %all-gather.5.cloned.1.call-start = ((), (), s32[]{:S(2)}) async-start(), calls=%async_computation.6 | async-start | bytes 2088960 | tf_op jit(solution)/shard_map/all_gather | solution.py:949
  9.3 79.3 %all-gather.7.cloned.1.call-start = ((), (), s32[]{:S(2)}) async-start(), calls=%async_computation.7 | async-start | bytes 1769472 | tf_op jit(solution)/shard_map/all_gather | solution.py:974
  18.0 7.4 %copy-start.24 = (bf16[1,128,768]{2,1,0:T(8,128)(2,1)S(1)}, bf16[1,128,768]{2,1,0:T(8,128)(2,1)}, u32[]{:S(2)}) copy-start(bf16[1,128,768]{2,1,0:T(8,128)(2,1)} %param.43) | copy-start | bytes 589828
  18.0 29.7 %all-to-all-start = ((bf16[8,144,384]{2,1,0:T(8,128)(2,1)}), bf16[8,144,384]{2,1,0:T(8,128)(2,1)S(1)}, u32[]{:S(2)}, u32[]{:S(2)}) async-start(bf16[8,144,384]{2,1,0:T(8,128)(2,1)} %get-tuple-element.79), calls=%async_computation | async-start | bytes 1769472 | tf_op jit(solution)/shard_map/all_to_all | solution.py:944
  25.4 10.4 %collective-permute-start = (bf16[128,768]{1,0:T(8,128)(2,1)S(1)}, bf16[128,768]{1,0:T(8,128)(2,1)S(1)}, u32[]{:S(2)}, u32[]{:S(2)}) collective-permute-start(bf16[128,768]{1,0:T(8,128)(2,1)S(1)} %bitcast.107), channel_id=1, source_target_pairs={{0,2},{1,3},{2,0},{3,1},{4,6},{5,7},{6,4},{7,5},{8,10},{9,11},{10,... | collective-permute-start | bytes 589832 | tf_op jit(solution)/shard_map/ppermute | solution.py:436
  35.9 1.8 collective-permute-start.1
  39.6 62.1 %copy-start.38 = (f32[768]{0:T(1024)S(1)}, f32[768]{0:T(1024)}, u32[]{:S(2)}) copy-start(f32[768]{0:T(1024)} %param.37) | copy-start | bytes 9220
  39.6 62.1 %copy-start.40 = (f32[768]{0:T(1024)S(1)}, f32[768]{0:T(1024)}, u32[]{:S(2)}) copy-start(f32[768]{0:T(1024)} %param.38) | copy-start | bytes 9220
  88.6 13.1 %copy-start.35 = (f32[128,768]{1,0:T(8,128)S(1)}, f32[128,768]{1,0:T(8,128)}, u32[]{:S(2)}) copy-start(f32[128,768]{1,0:T(8,128)} %get-tuple-element.85) | copy-start | bytes 1179652
  88.6 13.4 %copy-start.10 = (bf16[1,128,768]{2,1,0:T(8,128)(2,1)S(1)}, bf16[1,128,768]{2,1,0:T(8,128)(2,1)}, u32[]{:S(2)}) copy-start(bf16[1,128,768]{2,1,0:T(8,128)(2,1)} %param.22) | copy-start | bytes 589828
  102.0 6.4 %copy-start.26 = (bf16[128,768]{1,0:T(8,128)(2,1)}, bf16[128,768]{1,0:T(8,128)(2,1)S(1)}, u32[]{:S(2)}) copy-start(bf16[128,768]{1,0:T(8,128)(2,1)S(1)} %fusion.16) | copy-start | bytes 589828
  102.0 6.5 %copy-start.23 = (bf16[512,768]{1,0:T(8,128)(2,1)S(1)}, bf16[512,768]{1,0:T(8,128)(2,1)}, u32[]{:S(2)}) copy-start(bf16[512,768]{1,0:T(8,128)(2,1)} %pad_maximum_fusion.6) | copy-start | bytes 2359300
  102.0 6.5 %copy-start.33 = (bf16[512,768]{1,0:T(8,128)(2,1)S(1)}, bf16[512,768]{1,0:T(8,128)(2,1)}, u32[]{:S(2)}) copy-start(bf16[512,768]{1,0:T(8,128)(2,1)} %param.42) | copy-start | bytes 2359300
  102.4 19.8 %copy-start.19 = (f32[128,768]{1,0:T(8,128)}, f32[128,768]{1,0:T(8,128)S(1)}, u32[]{:S(2)}) copy-start(f32[128,768]{1,0:T(8,128)S(1)} %get-tuple-element.181) | copy-start | bytes 1179652
  102.6 7.6 %copy-start.32 = (bf16[768,512]{1,0:T(8,128)(2,1)S(1)}, bf16[768,512]{1,0:T(8,128)(2,1)}, u32[]{:S(2)}) copy-start(bf16[768,512]{1,0:T(8,128)(2,1)} %param.40) | copy-start | bytes 2359300
  102.6 5.7 %collective-permute-start.2 = (bf16[128,768]{1,0:T(8,128)(2,1)S(1)}, bf16[128,768]{1,0:T(8,128)(2,1)S(1)}, u32[]{:S(2)}, u32[]{:S(2)}) collective-permute-start(bf16[128,768]{1,0:T(8,128)(2,1)S(1)} %multiply_convert_fusion.2), channel_id=1, source_target_pairs={{0,2},{1,3},{2,0},{3,1},{4,6},{5,7},{6,4},{7,5},{8,10},{9,11},{10,... | collective-permute-start | bytes 589832 | tf_op jit(solution)/shard_map/ppermute | solution.py:436
  108.4 1.8 collective-permute-start.3
  109.1 1.7 copy-start.34
  111.8 1.5 copy-start.41
  113.2 1.8 collective-permute-start.4
  115.0 7.0 %collective-permute-start.5 = (bf16[128,768]{1,0:T(8,128)(2,1)S(1)}, bf16[128,768]{1,0:T(8,128)(2,1)S(1)}, u32[]{:S(2)}, u32[]{:S(2)}) collective-permute-start(bf16[128,768]{1,0:T(8,128)(2,1)S(1)} %slice.197), channel_id=1, source_target_pairs={{0,2},{1,3},{2,0},{3,1},{4,6},{5,7},{6,4},{7,5},{8,10},{9,11},{10,... | collective-permute-start | bytes 589832 | tf_op jit(solution)/shard_map/ppermute | solution.py:436
  117.6 4.6 %copy-start.25 = (bf16[1,128,768]{2,1,0:T(8,128)(2,1)S(1)}, bf16[1,128,768]{2,1,0:T(8,128)(2,1)}, u32[]{:S(2)}) copy-start(bf16[1,128,768]{2,1,0:T(8,128)(2,1)} %param.43) | copy-start | bytes 589828
  124.6 5.4 %copy-start.27 = (bf16[128,768]{1,0:T(8,128)(2,1)S(1)}, bf16[128,768]{1,0:T(8,128)(2,1)}, u32[]{:S(2)}) copy-start(bf16[128,768]{1,0:T(8,128)(2,1)} %copy-done.26) | copy-start | bytes 589828
  124.6 5.4 %copy-start.31 = (bf16[128,768]{1,0:T(8,128)(2,1)S(1)}, bf16[128,768]{1,0:T(8,128)(2,1)}, u32[]{:S(2)}) copy-start(bf16[128,768]{1,0:T(8,128)(2,1)} %get-tuple-element.81) | copy-start | bytes 589828
  125.8 12.7 %all-to-all-start.2 = ((bf16[8,128,128]{2,1,0:T(8,128)(2,1)}), bf16[8,128,128]{2,1,0:T(8,128)(2,1)S(1)}, u32[]{:S(2)}, u32[]{:S(2)}) async-start(bf16[8,128,128]{2,1,0:T(8,128)(2,1)} %bitcast_bitcast_fusion), calls=%async_computation.2 | async-start | bytes 524288 | tf_op jit(solution)/shard_map/all_to_all | solution.py:944
  130.0 8.5 %copy-start.14 = (bf16[128,768]{1,0:T(8,128)(2,1)S(1)}, bf16[128,768]{1,0:T(8,128)(2,1)}, u32[]{:S(2)}) copy-start(bf16[128,768]{1,0:T(8,128)(2,1)} %get-tuple-element.90.d_ref) | copy-start | bytes 589828
  130.0 8.5 %copy-start.29 = (bf16[128,768]{1,0:T(8,128)(2,1)S(1)}, bf16[128,768]{1,0:T(8,128)(2,1)}, u32[]{:S(2)}) copy-start(bf16[128,768]{1,0:T(8,128)(2,1)} %copy-done.28) | copy-start | bytes 589828
  140.3 2.9 collective-permute-start.6
  144.7 58.8 %all-to-all-start.3 = ((bf16[8,192,768]{2,1,0:T(8,128)(2,1)}), bf16[8,192,768]{2,1,0:T(8,128)(2,1)}, u32[]{:S(2)}, u32[]{:S(2)}) async-start(bf16[8,192,768]{2,1,0:T(8,128)(2,1)} %pad_maximum_fusion), calls=%async_computation.3 | async-start | bytes 4718592 | tf_op jit(solution)/shard_map/all_to_all | solution.py:944
  149.3 2.8 copy-start.9
  150.5 45.2 %collective-permute-start.7 = (bf16[1,384,768]{2,1,0:T(8,128)(2,1)S(1)}, bf16[1,384,768]{2,1,0:T(8,128)(2,1)S(1)}, u32[]{:S(2)}, u32[]{:S(2)}) collective-permute-start(bf16[1,384,768]{2,1,0:T(8,128)(2,1)S(1)} %slice.110), channel_id=1, source_target_pairs={{0,2},{1,3},{2,0},{3,1},{4,6},{5,7},{6,4},{7,5},{8,10},{9,11},{10,... | collective-permute-start | bytes 1769480 | tf_op jit(solution)/shard_map/ppermute | solution.py:436
  152.1 43.5 %copy-start.22 = (bf16[2,384,768]{2,1,0:T(8,128)(2,1)S(1)}, bf16[2,384,768]{2,1,0:T(8,128)(2,1)}, u32[]{:S(2)}) copy-start(bf16[2,384,768]{2,1,0:T(8,128)(2,1)} %add_convert_fusion) | copy-start | bytes 3538948
  195.6 7.9 %copy-start.12 = (bf16[1024,768]{1,0:T(8,128)(2,1)S(1)}, bf16[1024,768]{1,0:T(8,128)(2,1)}, u32[]{:S(2)}) copy-start(bf16[1024,768]{1,0:T(8,128)(2,1)} %all-gather.7.cloned.1.call-done.n_ref) | copy-start | bytes 4718596
  205.9 3.7 %collective-permute-start.8 = (bf16[2,240,384]{2,1,0:T(8,128)(2,1)S(1)}, bf16[2,240,384]{2,1,0:T(8,128)(2,1)S(1)}, u32[]{:S(2)}, u32[]{:S(2)}) collective-permute-start(bf16[2,240,384]{2,1,0:T(8,128)(2,1)S(1)} %get-tuple-element.112), channel_id=1, source_target_pairs={{0,1},{1,0},{2,3},{3,2},{4,5},{5,4},{6,7},{7,6},{8,9},{9,8},{10,11... | collective-permute-start | bytes 1105928 | tf_op jit(solution)/shard_map/ppermute | solution.py:436
  206.0 20.3 %all-to-all-start.4 = ((bf16[8,48,768]{2,1,0:T(8,128)(2,1)}), bf16[8,48,768]{2,1,0:T(8,128)(2,1)S(1)}, u32[]{:S(2)}, u32[]{:S(2)}) async-start(bf16[8,48,768]{2,1,0:T(8,128)(2,1)} %bitcast.106), calls=%async_computation.4 | async-start | bytes 1179648 | tf_op jit(solution)/shard_map/all_to_all | solution.py:646
  209.6 112.1 %all-gather.9.cloned.1.call-start = ((), (), s32[]{:S(2)}) async-start(), calls=%async_computation.8 | async-start | bytes 2654208 | tf_op jit(solution)/shard_map/all_gather | solution.py:866
  209.8 7.0 %collective-permute-start.9 = (bf16[1,240,384]{2,1,0:T(8,128)(2,1)S(1)}, bf16[1,240,384]{2,1,0:T(8,128)(2,1)S(1)}, u32[]{:S(2)}, u32[]{:S(2)}) collective-permute-start(bf16[1,240,384]{2,1,0:T(8,128)(2,1)S(1)} %slice.198), channel_id=1, source_target_pairs={{0,2},{1,3},{2,0},{3,1},{4,6},{5,7},{6,4},{7,5},{8,10},{9,11},{10,... | collective-permute-start | bytes 552968 | tf_op jit(solution)/shard_map/ppermute | solution.py:436
  226.5 13.5 %collective-permute-start.10 = (bf16[336,384]{1,0:T(8,128)(2,1)S(1)}, bf16[336,384]{1,0:T(8,128)(2,1)S(1)}, u32[]{:S(2)}, u32[]{:S(2)}) collective-permute-start(bf16[336,384]{1,0:T(8,128)(2,1)S(1)} %pad_maximum_fusion.11), channel_id=1, source_target_pairs={{0,16},{4,20},{8,24},{12,28},{16,0},{20,4},{24,8},{28,12},{1,17},{... | collective-permute-start | bytes 774152 | tf_op jit(solution)/shard_map/ppermute | solution.py:436
  240.2 21.3 %collective-permute-start.11 = (bf16[2,336,384]{2,1,0:T(8,128)(2,1)S(1)}, bf16[2,336,384]{2,1,0:T(8,128)(2,1)S(1)}, u32[]{:S(2)}, u32[]{:S(2)}) collective-permute-start(bf16[2,336,384]{2,1,0:T(8,128)(2,1)S(1)} %pad_maximum_fusion.8), channel_id=1, source_target_pairs={{0,8},{4,12},{8,0},{12,4},{16,24},{20,28},{24,16},{28,20},{1,9},{5... | collective-permute-start | bytes 1548296 | tf_op jit(solution)/shard_map/ppermute | solution.py:436
  261.6 4.0 %copy-start.30 = (bf16[512,768]{1,0:T(8,128)(2,1)S(1)}, bf16[512,768]{1,0:T(8,128)(2,1)}, u32[]{:S(2)}) copy-start(bf16[512,768]{1,0:T(8,128)(2,1)} %convolution_convert_fusion.2) | copy-start | bytes 2359300
  262.5 30.1 %collective-permute-start.12 = (bf16[2,2,160,384]{3,2,1,0:T(8,128)(2,1)}, bf16[2,2,160,384]{3,2,1,0:T(8,128)(2,1)}, u32[]{:S(2)}, u32[]{:S(2)}) collective-permute-start(bf16[2,2,160,384]{3,2,1,0:T(8,128)(2,1)} %slice.115), channel_id=1, source_target_pairs={{0,4},{4,0},{8,12},{12,8},{16,20},{20,16},{24,28},{28,24},{1,5},{5... | collective-permute-start | bytes 1474568 | tf_op jit(solution)/shard_map/ppermute | solution.py:436
  264.0 31.4 %collective-permute-start.14 = (bf16[2,2,176,384]{3,2,1,0:T(8,128)(2,1)S(1)}, bf16[2,2,176,384]{3,2,1,0:T(8,128)(2,1)}, u32[]{:S(2)}, u32[]{:S(2)}) collective-permute-start(bf16[2,2,176,384]{3,2,1,0:T(8,128)(2,1)S(1)} %slice.116), channel_id=1, source_target_pairs={{0,2},{1,3},{2,0},{3,1},{4,6},{5,7},{6,4},{7,5},{8,10},{9,11},{10,... | collective-permute-start | bytes 1622024 | tf_op jit(solution)/shard_map/ppermute | solution.py:436
  266.4 32.6 %collective-permute-start.16 = (bf16[256,768]{1,0:T(8,128)(2,1)}, bf16[256,768]{1,0:T(8,128)(2,1)}, u32[]{:S(2)}, u32[]{:S(2)}) collective-permute-start(bf16[256,768]{1,0:T(8,128)(2,1)} %slice.118), channel_id=1, source_target_pairs={{0,1},{1,0},{2,3},{3,2},{4,5},{5,4},{6,7},{7,6},{8,9},{9,8},{10,11... | collective-permute-start | bytes 1179656 | tf_op jit(solution)/shard_map/ppermute | solution.py:436
  266.4 55.3 %all-to-all-start.5 = ((bf16[8,144,384]{2,1,0:T(8,128)(2,1)}), bf16[8,144,384]{2,1,0:T(8,128)(2,1)S(1)}, u32[]{:S(2)}, u32[]{:S(2)}) async-start(bf16[8,144,384]{2,1,0:T(8,128)(2,1)} %get-tuple-element.116.x_ref), calls=%async_computation.5 | async-start | bytes 1769472 | tf_op jit(solution)/shard_map/all_to_all | solution.py:874
  293.9 24.1 %collective-permute-start.13 = (bf16[2,2,2,160,384]{4,3,2,1,0:T(8,128)(2,1)S(1)}, bf16[2,2,2,160,384]{4,3,2,1,0:T(8,128)(2,1)S(1)}, u32[]{:S(2)}, u32[]{:S(2)}) collective-permute-start(bf16[2,2,2,160,384]{4,3,2,1,0:T(8,128)(2,1)S(1)} %pad_maximum_fusion.5), channel_id=1, source_target_pairs={{0,2},{1,3},{2,0},{3,1},{4,6},{5,7},{6,4},{7,5},{8,10},{9,11},{10,... | collective-permute-start | bytes 2949128 | tf_op jit(solution)/shard_map/ppermute | solution.py:436
  296.6 20.6 %copy-start.20 = (f32[128,768]{1,0:T(8,128)S(1)}, f32[128,768]{1,0:T(8,128)}, u32[]{:S(2)}) copy-start(f32[128,768]{1,0:T(8,128)} %copy-done.19) | copy-start | bytes 1179652
  296.8 24.4 %collective-permute-start.15 = (bf16[2,2,2,176,384]{4,3,2,1,0:T(8,128)(2,1)S(1)}, bf16[2,2,2,176,384]{4,3,2,1,0:T(8,128)(2,1)S(1)}, u32[]{:S(2)}, u32[]{:S(2)}) collective-permute-start(bf16[2,2,2,176,384]{4,3,2,1,0:T(8,128)(2,1)S(1)} %pad_maximum_fusion.3), channel_id=1, source_target_pairs={{0,4},{4,0},{8,12},{12,8},{16,20},{20,16},{24,28},{28,24},{1,5},{5... | collective-permute-start | bytes 3244040 | tf_op jit(solution)/shard_map/ppermute | solution.py:436
  300.0 17.2 %collective-permute-start.17 = (bf16[128,768]{1,0:T(8,128)(2,1)S(1)}, bf16[128,768]{1,0:T(8,128)(2,1)S(1)}, u32[]{:S(2)}, u32[]{:S(2)}) collective-permute-start(bf16[128,768]{1,0:T(8,128)(2,1)S(1)} %slice.196), channel_id=1, source_target_pairs={{0,2},{1,3},{2,0},{3,1},{4,6},{5,7},{6,4},{7,5},{8,10},{9,11},{10,... | collective-permute-start | bytes 589832 | tf_op jit(solution)/shard_map/ppermute | solution.py:436
  321.7 5.2 %copy-start.21 = (bf16[2,2,2,2,176,384]{5,4,3,2,1,0:T(8,128)(2,1)}, bf16[2,2,2,2,176,384]{5,4,3,2,1,0:T(8,128)(2,1)S(1)}, u32[]{:S(2)}) copy-start(bf16[2,2,2,2,176,384]{5,4,3,2,1,0:T(8,128)(2,1)S(1)} %pad_maximum_fusion.1) | copy-start | bytes 6488068
  321.7 11.1 %collective-permute-start.19 = (bf16[2,2,4,176,384]{4,3,2,1,0:T(8,128)(2,1)S(1)}, bf16[2,2,4,176,384]{4,3,2,1,0:T(8,128)(2,1)}, u32[]{:S(2)}, u32[]{:S(2)}) collective-permute-start(bf16[2,2,4,176,384]{4,3,2,1,0:T(8,128)(2,1)S(1)} %bitcast.102), channel_id=1, source_target_pairs={{0,1},{1,0},{2,3},{3,2},{4,5},{5,4},{6,7},{7,6},{8,9},{9,8},{10,11... | collective-permute-start | bytes 6488072 | tf_op jit(solution)/shard_map/ppermute | solution.py:436
  321.8 11.0 %collective-permute-start.18 = (bf16[2,8,160,384]{3,2,1,0:T(8,128)(2,1)}, bf16[2,8,160,384]{3,2,1,0:T(8,128)(2,1)}, u32[]{:S(2)}, u32[]{:S(2)}) collective-permute-start(bf16[2,8,160,384]{3,2,1,0:T(8,128)(2,1)} %bitcast.104), channel_id=1, source_target_pairs={{0,1},{1,0},{2,3},{3,2},{4,5},{5,4},{6,7},{7,6},{8,9},{9,8},{10,11... | collective-permute-start | bytes 5898248 | tf_op jit(solution)/shard_map/ppermute | solution.py:436
  322.3 1.8 copy-start.2
  324.1 2.8 copy-start.4
  324.1 2.8 copy-start.5
  324.1 3.7 %copy-start.6 = (bf16[768,768]{1,0:T(8,128)(2,1)S(1)}, bf16[768,768]{1,0:T(8,128)(2,1)}, u32[]{:S(2)}) copy-start(bf16[768,768]{1,0:T(8,128)(2,1)} %refs_6_.1) | copy-start | bytes 3538948
  324.1 4.0 %copy-start.7 = (bf16[768,768]{1,0:T(8,128)(2,1)S(1)}, bf16[768,768]{1,0:T(8,128)(2,1)}, u32[]{:S(2)}) copy-start(bf16[768,768]{1,0:T(8,128)(2,1)} %refs_7_.1) | copy-start | bytes 3538948
  324.1 4.0 %copy-start.11 = (bf16[1,128,768]{2,1,0:T(8,128)(2,1)S(1)}, bf16[1,128,768]{2,1,0:T(8,128)(2,1)}, u32[]{:S(2)}) copy-start(bf16[1,128,768]{2,1,0:T(8,128)(2,1)} %param.22) | copy-start | bytes 589828
  324.1 4.1 %copy-start.13 = (f32[128,768]{1,0:T(8,128)S(1)}, f32[128,768]{1,0:T(8,128)}, u32[]{:S(2)}) copy-start(f32[128,768]{1,0:T(8,128)} %get-tuple-element.145.m_ref) | copy-start | bytes 1179652
  324.1 4.2 %copy-start.15 = (bf16[128,768]{1,0:T(8,128)(2,1)S(1)}, bf16[128,768]{1,0:T(8,128)(2,1)}, u32[]{:S(2)}) copy-start(bf16[128,768]{1,0:T(8,128)(2,1)} %get-tuple-element.90.d_ref) | copy-start | bytes 589828
  324.1 4.2 %copy-start.17 = (bf16[768,12]{0,1:T(8,128)(2,1)S(1)}, bf16[768,12]{0,1:T(8,128)(2,1)}, u32[]{:S(2)}) copy-start(bf16[768,12]{0,1:T(8,128)(2,1)} %param.27) | copy-start | bytes 55300
  324.1 4.2 %copy-start.18 = (f32[1,768]{1,0:T(1,128)S(1)}, f32[1,768]{1,0:T(1,128)}, u32[]{:S(2)}) copy-start(f32[1,768]{1,0:T(1,128)} %broadcast_in_dim.28.g_ref) | copy-start | bytes 9220
  332.8 13.1 %copy-start.1 = (bf16[768,768]{1,0:T(8,128)(2,1)S(1)}, bf16[768,768]{1,0:T(8,128)(2,1)}, u32[]{:S(2)}) copy-start(bf16[768,768]{1,0:T(8,128)(2,1)} %param.36) | copy-start | bytes 3538948
  342.9 2.4 copy-start.39
  (6 other events, 6.3 us)
Sparse Core Ops, SparseCore 0:
  10.2 26.6 all-gather.4
  39.6 43.8 all-gather.6
  229.5 78.8 all-gather.8

commit v5 on v4

--- a/solution.py
+++ b/solution.py
@@ -863,14 +863,14 @@
         compiler_params=pltpu.CompilerParams(vmem_limit_bytes=20 * 1024 * 1024),
     )(me, every_normed, back_sent, *state_g, vectors)
     late = late.astype(F) + flip(late_sent, "tp", 1).astype(F)
-    fed = lax.all_gather(summed(fed_parts), "seq", axis=0, tiled=False)
     late = scatter_once(late, "tp", 2).astype(LOW)[0]
     early = summed(swapped(early))
     late = jnp.concatenate([late, early[:, :lanes], early[:, lanes:]], 0)
     share = late.shape[0]
     late = double(late, "seq", 4)
+    late, fed = lax.optimization_barrier((late, summed(fed_parts)))
+    fed = lax.all_gather(fed, "seq", axis=0, tiled=False)
     late = double(late, "seq", 2)
-    late, back_sent = lax.optimization_barrier((late, back_sent))
     back = lax.all_to_all(back_sent, "seq", split_axis=0, concat_axis=0, tiled=True)
     cut = 160
     part_a, part_b = late[:, :, :cut], late[:, :, cut:]

time: 354 us -> 349 us (0.986)
  waiting for transfers between devices: 129 us -> 123 us
    ppermute x20, waiting for transfers between devices: 99.8 us -> 93.2 us  [flip(): return lax.ppermute(array, axis, [(i, i ^ mask) for i in range(peers)])]
  transfers between devices with their start and end apart: 28 -> 28, of which waited for: 17 -> 17; matrix products, arithmetic and copies ran while one was open for 7% -> 7% of each run, Pallas kernels for 27% -> 28%
where the time goes in v5:
time: 349 us; the launch traced here: 348 us
  waiting for transfers between devices  123 us (35%)
  Pallas kernels  111 us (32%)
  starting transfers between devices  42.4 us (12%)
  other arithmetic  18.7 us (5%)
  between operations  14.7 us (4%)
  local copies, waits for them, and re-layouts  13.4 us (4%)
  blocking collectives  12.7 us (4%)
  matrix products  12.7 us (4%)
    ppermute x20, waiting for transfers between devices, flip(): return lax.ppermute(array, axis, [(i, i ^ mask) for i in range(peers)])  93.2 us
    pallas_call x1, Pallas kernels, bwd_scan(): pl.pallas_call(partial(bwd_kernel, C, H, n // 2), grid=(n // 2,), in_spec...  43.5 us
    pallas_call x1, Pallas kernels, fwd_scan(): pl.pallas_call(partial(fwd_kernel, C, H), grid=(n // 2,), in_specs=[pl.Bl...  38 us
    all_to_all x3, waiting for transfers between devices, swap(): return lax.all_to_all(array, 'seq', split_axis=0, concat_axis=0, tiled=True)  19.9 us
    ppermute x20, starting transfers between devices, flip(): return lax.ppermute(array, axis, [(i, i ^ mask) for i in range(peers)])  18.7 us
    all_to_all x3, starting transfers between devices, swap(): return lax.all_to_all(array, 'seq', split_axis=0, concat_axis=0, tiled=True)  16.2 us
    all_to_all x1, blocking collectives, swap(): return lax.all_to_all(array, 'seq', split_axis=0, concat_axis=0, tiled=True)  12.7 us
    pallas_call x1, Pallas kernels, share_tiles(): pl.pallas_call(partial(last_kernel, seqs, each, heads, local_heads), grid...  10.1 us
  transfers between devices with their start and end apart: 28, of which 17 were waited for; matrix products, arithmetic and copies ran while one was open for 7% of the time, Pallas kernels for 28%

profile of v5, /device:TPU:0, one launch (start us, length us, event | category | flops | bytes accessed | tf_op | source)
XLA Modules:
  0.0 347.9 jit_solution(15918783837214405581)
XLA Ops:
  7.3 2.0 shard_map.382
  9.3 1.3 broadcast_in_dim.28.g_ref
  10.6 7.4 %shard_map.381 = (bf16[8,144,384]{2,1,0:T(8,128)(2,1)}, bf16[128,768]{1,0:T(8,128)(2,1)}, f32[128,768]{1,0:T(8,128)}) custom-call(bf16[128,768]{1,0:T(8,128)(2,1)} %bitcast.96, f32[1,768]{1,0:T(1,128)} %broadcast_in_dim.28.g_ref, bf16[768,768]{1,0:T(8,128)(2,1)} %refs_4_.1, bf16[768,768]{1,0:T(8,128)(2,1)} %refs_5_.1, bf16[768,768]{1,0:T(8,128)(2,1)} %refs_6_.1, ...), custom_call_target="tpu_custom_call" | custom-call | tf_op jit(solution)/shard_map/pallas_call | solution.py:541
  18.0 7.4 %all-to-all-start = ((bf16[8,144,384]{2,1,0:T(8,128)(2,1)}), bf16[8,144,384]{2,1,0:T(8,128)(2,1)S(1)}, u32[]{:S(2)}, u32[]{:S(2)}) async-start(bf16[8,144,384]{2,1,0:T(8,128)(2,1)} %get-tuple-element.79), calls=%async_computation | async-start | bytes 1769472 | tf_op jit(solution)/shard_map/all_to_all | solution.py:944
  25.4 1.6 collective-permute-start
  27.0 8.8 %collective-permute-done = bf16[128,768]{1,0:T(8,128)(2,1)S(1)} collective-permute-done((bf16[128,768]{1,0:T(8,128)(2,1)S(1)}, bf16[128,768]{1,0:T(8,128)(2,1)S(1)}, u32[]{:S(2)}, u32[]{:S(2)}) %collective-permute-start) | collective-permute-done | bytes 196640 | tf_op jit(solution)/shard_map/ppermute | solution.py:436
  35.9 1.7 collective-permute-done.1
  37.6 0.9 pad_maximum_fusion.5
  38.6 1.0 constant_dynamic-slice_fusion.2.own_ref.refs_29_
  39.6 8.2 %all-to-all-done.xa_ref.xb_ref.refs_0_.refs_9_.refs_18_ = bf16[8,144,384]{2,1,0:T(8,128)(2,1)S(1)} async-done(((bf16[8,144,384]{2,1,0:T(8,128)(2,1)}), bf16[8,144,384]{2,1,0:T(8,128)(2,1)S(1)}, u32[]{:S(2)}, u32[]{:S(2)}) %all-to-all-start) | async-done | bytes 884768 | tf_op jit(solution)/shard_map/all_to_all | solution.py:944
  47.7 38.0 %shard_map.383 = (bf16[1024,128]{1,0:T(8,128)(2,1)S(1)}, f32[2048,256]{1,0:T(8,128)S(1)}, f32[2048,256]{1,0:T(8,128)}, f32[1024,128]{1,0:T(8,128)S(1)}, f32[2048...) custom-call(bf16[8,144,384]{2,1,0:T(8,128)(2,1)S(1)} %all-to-all-don, ...), custom_call_target="tpu_custom_call" | custom-call | tf_op jit(solution)/shard_map/pallas_call | solution.py:214
  85.7 1.3 copy-done.3
  87.1 0.8 copy-done.8
  88.6 12.7 %all_to_all.30 = bf16[8,128,128]{2,1,0:T(8,128)(2,1)S(1)} all-to-all(bf16[8,128,128]{2,1,0:T(8,128)(2,1)} %bitcast.99), channel_id=1, replica_groups=mesh['seq'=8,'tp'=4] {'seq'}, dimensions={0} | all-to-all | bytes 524288 | tf_op jit(solution)/shard_map/all_to_all | solution.py:944
  102.6 1.6 collective-permute-start.2
  104.2 4.2 %collective-permute-done.2 = bf16[128,768]{1,0:T(8,128)(2,1)S(1)} collective-permute-done((bf16[128,768]{1,0:T(8,128)(2,1)S(1)}, bf16[128,768]{1,0:T(8,128)(2,1)S(1)}, u32[]{:S(2)}, u32[]{:S(2)}) %collective-permute-start.2) | collective-permute-done | bytes 196640 | tf_op jit(solution)/shard_map/ppermute | solution.py:436
  109.1 1.1 collective-permute-done.3
  110.8 1.0 multiply_convert_fusion
  113.9 1.0 collective-permute-done.4
  115.0 1.6 collective-permute-start.5
  116.6 1.0 convolution_convert_fusion
  117.6 1.6 pad_maximum_fusion
  119.2 2.9 collective-permute-done.5
  122.2 0.9 fusion.65
  123.1 1.5 fusion.17
  125.8 4.2 %all-to-all-start.2 = ((bf16[8,128,128]{2,1,0:T(8,128)(2,1)}), bf16[8,128,128]{2,1,0:T(8,128)(2,1)S(1)}, u32[]{:S(2)}, u32[]{:S(2)}) async-start(bf16[8,128,128]{2,1,0:T(8,128)(2,1)} %bitcast_bitcast_fusion), calls=%async_computation.2 | async-start | bytes 524288 | tf_op jit(solution)/shard_map/all_to_all | solution.py:944
  130.0 0.9 fusion.53
  130.9 2.8 convolution_convert_fusion.2
  133.7 4.8 %all-to-all-done.2 = bf16[8,128,128]{2,1,0:T(8,128)(2,1)S(1)} async-done(((bf16[8,128,128]{2,1,0:T(8,128)(2,1)}), bf16[8,128,128]{2,1,0:T(8,128)(2,1)S(1)}, u32[]{:S(2)}, u32[]{:S(2)}) %all-to-all-start.2) | async-done | bytes 262176 | tf_op jit(solution)/shard_map/all_to_all | solution.py:944
  138.8 1.5 convolution_convert_fusion.1
  140.3 2.8 collective-permute-done.6
  143.2 1.5 add_convert_fusion
  144.7 4.6 %all-to-all-start.3 = ((bf16[8,192,768]{2,1,0:T(8,128)(2,1)}), bf16[8,192,768]{2,1,0:T(8,128)(2,1)}, u32[]{:S(2)}, u32[]{:S(2)}) async-start(bf16[8,192,768]{2,1,0:T(8,128)(2,1)} %pad_maximum_fusion), calls=%async_computation.3 | async-start | bytes 4718592 | tf_op jit(solution)/shard_map/all_to_all | solution.py:944
  149.3 1.2 slice.110
  150.5 1.6 collective-permute-start.7
  152.1 43.5 %shard_map.384 = (bf16[8,144,384]{2,1,0:T(8,128)(2,1)}, f32[128,256]{1,0:T(8,128)S(1)}, f32[2,256]{1,0:T(2,128)S(1)}, f32[128,256]{1,0:T(8,128)S(1)}, f32[1,128]...) custom-call(bf16[8,144,384]{2,1,0:T(8,128)(2,1)S(1)} %all-to-all-done.xa_ref.xb_ref.refs_0_.refs, ...), custom_call_target="tpu_custom_call" | custom-call | flops 1000 | bytes 1000 | tf_op jit(solution)/shard_map/pallas_call | solution.py:395
  195.7 1.0 add_convert_fusion.1
  196.6 6.9 %all-to-all-done.3 = bf16[8,192,768]{2,1,0:T(8,128)(2,1)} async-done(((bf16[8,192,768]{2,1,0:T(8,128)(2,1)}), bf16[8,192,768]{2,1,0:T(8,128)(2,1)}, u32[]{:S(2)}, u32[]{:S(2)}) %all-to-all-start.3) | async-done | bytes 2359328 | tf_op jit(solution)/shard_map/all_to_all | solution.py:944
  203.5 2.4 shard_map.385
  206.0 3.6 %all-to-all-start.4 = ((bf16[8,48,768]{2,1,0:T(8,128)(2,1)}), bf16[8,48,768]{2,1,0:T(8,128)(2,1)S(1)}, u32[]{:S(2)}, u32[]{:S(2)}) async-start(bf16[8,48,768]{2,1,0:T(8,128)(2,1)} %bitcast.106), calls=%async_computation.4 | async-start | bytes 1179648 | tf_op jit(solution)/shard_map/all_to_all | solution.py:646
  209.8 1.6 collective-permute-start.9
  211.4 5.5 %collective-permute-done.9 = bf16[1,240,384]{2,1,0:T(8,128)(2,1)S(1)} collective-permute-done((bf16[1,240,384]{2,1,0:T(8,128)(2,1)S(1)}, bf16[1,240,384]{2,1,0:T(8,128)(2,1)S(1)}, u32[]{:S(2)}, u32[]{:S(2)}) %collective-permute-start.9) | collective-permute-done | bytes 184352 | tf_op jit(solution)/shard_map/ppermute | solution.py:436
  216.9 9.5 %all-to-all-done.4 = bf16[8,48,768]{2,1,0:T(8,128)(2,1)S(1)} async-done(((bf16[8,48,768]{2,1,0:T(8,128)(2,1)}), bf16[8,48,768]{2,1,0:T(8,128)(2,1)S(1)}, u32[]{:S(2)}, u32[]{:S(2)}) %all-to-all-start.4) | async-done | bytes 589856 | tf_op jit(solution)/shard_map/all_to_all | solution.py:646
  226.6 2.8 reduce_sum.157
  229.4 10.6 %collective-permute-done.10 = bf16[336,384]{1,0:T(8,128)(2,1)S(1)} collective-permute-done((bf16[336,384]{1,0:T(8,128)(2,1)S(1)}, bf16[336,384]{1,0:T(8,128)(2,1)S(1)}, u32[]{:S(2)}, u32[]{:S(2)}) %collective-permute-start.10) | collective-permute-done | bytes 258080 | tf_op jit(solution)/shard_map/ppermute | solution.py:436
  240.3 19.9 %collective-permute-done.11 = bf16[2,336,384]{2,1,0:T(8,128)(2,1)S(1)} collective-permute-done((bf16[2,336,384]{2,1,0:T(8,128)(2,1)S(1)}, bf16[2,336,384]{2,1,0:T(8,128)(2,1)S(1)}, u32[]{:S(2)}, u32[]{:S(2)}) %collective-permute-start.11) | collective-permute-done | bytes 516128 | tf_op jit(solution)/shard_map/ppermute | solution.py:436
  260.3 0.8 pad_maximum_fusion.9
  261.1 2.2 collective-permute-start.12
  263.4 1.8 collective-permute-start.14
  266.0 3.8 %all-to-all-start.5 = ((bf16[8,144,384]{2,1,0:T(8,128)(2,1)}), bf16[8,144,384]{2,1,0:T(8,128)(2,1)S(1)}, u32[]{:S(2)}, u32[]{:S(2)}) async-start(bf16[8,144,384]{2,1,0:T(8,128)(2,1)} %get-tuple-element.103.x_ref), calls=%async_computation.5 | async-start | bytes 1769472 | tf_op jit(solution)/shard_map/all_to_all | solution.py:874
  269.8 6.7 %collective-permute-done.12 = bf16[2,2,160,384]{3,2,1,0:T(8,128)(2,1)} collective-permute-done((bf16[2,2,160,384]{3,2,1,0:T(8,128)(2,1)}, bf16[2,2,160,384]{3,2,1,0:T(8,128)(2,1)}, u32[]{:S(2)}, u32[]{:S(2)}) %collective-permute-start.12) | collective-permute-done | bytes 491552 | tf_op jit(solution)/shard_map/ppermute | solution.py:436
  276.5 1.2 select_bitcast_fusion.9
  278.3 1.3 select_bitcast_fusion.5
  279.7 3.4 collective-permute-start.15
  283.0 1.1 convert_add_fusion
  284.1 1.8 collective-permute-start.17
  286.0 13.7 %collective-permute-done.17 = bf16[128,768]{1,0:T(8,128)(2,1)S(1)} collective-permute-done((bf16[128,768]{1,0:T(8,128)(2,1)S(1)}, bf16[128,768]{1,0:T(8,128)(2,1)S(1)}, u32[]{:S(2)}, u32[]{:S(2)}) %collective-permute-start.17) | collective-permute-done | bytes 196640 | tf_op jit(solution)/shard_map/ppermute | solution.py:436
  300.6 1.6 pad_maximum_fusion.2
  302.2 14.4 %collective-permute-done.15 = bf16[2,2,2,176,384]{4,3,2,1,0:T(8,128)(2,1)S(1)} collective-permute-done((bf16[2,2,2,176,384]{4,3,2,1,0:T(8,128)(2,1)S(1)}, bf16[2,2,2,176,384]{4,3,2,1,0:T(8,128)(2,1)S(1)}, u32[]{:S(2)}, u32[]{:S(2)}) %collective-permute-start.15) | collective-permute-done | bytes 1081376 | tf_op jit(solution)/shard_map/ppermute | solution.py:436
  317.7 1.8 copy-done.2
  319.6 2.7 shard_map.388
  322.3 0.9 copy-done.6
  323.7 4.5 %shard_map.386 = f32[128,768]{1,0:T(8,128)} custom-call(bf16[128,768]{1,0:T(8,128)(2,1)S(1)} %bitcast.97, f32[1,768]{1,0:T(1,128)S(1)} %copy-done.18, f32[128,768]{1,0:T(8,128)S(1)} %copy-done.13, bf16[8,144,384]{2,1,0:T(8,128)(2,1)S(1)} %all-to-all-done.5.b_ref, bf16[128,768]{1,0:T(8,128)(2,1)S(1)} %copy-done.15, bf16[768,768]{1,0:T(8,128)(2,1)S(1)} %copy-done.4, ...), custom_call_target="tpu_custom_call" | custom-call | tf_op jit(solution)/shard_map/pallas_call | solution.py:595
  328.2 10.1 %shard_map.387 = (f32[768,768]{1,0:T(8,128)}, f32[768,768]{1,0:T(8,128)}, f32[768,768]{1,0:T(8,128)}, f32[768,1]{1,0:T(8,128)S(1)}, f32[3,64,256]{2,1,0:T(8,128)...) custom-call(s32[1]{0:T(128)} %bitcast.me_ref, ...), custom_call_target="tpu_custom_call" | custom-call | tf_op jit(solution)/shard_map/pallas_call | solution.py:887
  (173 shorter events, 15.1 us)
Async XLA Ops:
  7.2 94.8 %copy-start = (bf16[768,768]{1,0:T(8,128)(2,1)S(1)}, bf16[768,768]{1,0:T(8,128)(2,1)}, u32[]{:S(2)}) copy-start(bf16[768,768]{1,0:T(8,128)(2,1)} %param.36) | copy-start | bytes 3538948
  7.2 31.4 %all-gather.5.cloned.1.call-start = ((), (), s32[]{:S(2)}) async-start(), calls=%async_computation.6 | async-start | bytes 2088960 | tf_op jit(solution)/shard_map/all_gather | solution.py:949
  9.3 79.3 %all-gather.7.cloned.1.call-start = ((), (), s32[]{:S(2)}) async-start(), calls=%async_computation.7 | async-start | bytes 1769472 | tf_op jit(solution)/shard_map/all_gather | solution.py:974
  18.0 7.4 %copy-start.24 = (bf16[1,128,768]{2,1,0:T(8,128)(2,1)S(1)}, bf16[1,128,768]{2,1,0:T(8,128)(2,1)}, u32[]{:S(2)}) copy-start(bf16[1,128,768]{2,1,0:T(8,128)(2,1)} %param.43) | copy-start | bytes 589828
  18.0 29.7 %all-to-all-start = ((bf16[8,144,384]{2,1,0:T(8,128)(2,1)}), bf16[8,144,384]{2,1,0:T(8,128)(2,1)S(1)}, u32[]{:S(2)}, u32[]{:S(2)}) async-start(bf16[8,144,384]{2,1,0:T(8,128)(2,1)} %get-tuple-element.79), calls=%async_computation | async-start | bytes 1769472 | tf_op jit(solution)/shard_map/all_to_all | solution.py:944
  25.4 10.4 %collective-permute-start = (bf16[128,768]{1,0:T(8,128)(2,1)S(1)}, bf16[128,768]{1,0:T(8,128)(2,1)S(1)}, u32[]{:S(2)}, u32[]{:S(2)}) collective-permute-start(bf16[128,768]{1,0:T(8,128)(2,1)S(1)} %bitcast.107), channel_id=1, source_target_pairs={{0,2},{1,3},{2,0},{3,1},{4,6},{5,7},{6,4},{7,5},{8,10},{9,11},{10,... | collective-permute-start | bytes 589832 | tf_op jit(solution)/shard_map/ppermute | solution.py:436
  35.9 1.8 collective-permute-start.1
  39.6 62.1 %copy-start.38 = (f32[768]{0:T(1024)S(1)}, f32[768]{0:T(1024)}, u32[]{:S(2)}) copy-start(f32[768]{0:T(1024)} %param.37) | copy-start | bytes 9220
  39.6 62.1 %copy-start.40 = (f32[768]{0:T(1024)S(1)}, f32[768]{0:T(1024)}, u32[]{:S(2)}) copy-start(f32[768]{0:T(1024)} %param.38) | copy-start | bytes 9220
  88.6 13.1 %copy-start.35 = (f32[128,768]{1,0:T(8,128)S(1)}, f32[128,768]{1,0:T(8,128)}, u32[]{:S(2)}) copy-start(f32[128,768]{1,0:T(8,128)} %get-tuple-element.85) | copy-start | bytes 1179652
  88.6 13.4 %copy-start.10 = (bf16[1,128,768]{2,1,0:T(8,128)(2,1)S(1)}, bf16[1,128,768]{2,1,0:T(8,128)(2,1)}, u32[]{:S(2)}) copy-start(bf16[1,128,768]{2,1,0:T(8,128)(2,1)} %param.22) | copy-start | bytes 589828
  102.0 6.4 %copy-start.26 = (bf16[128,768]{1,0:T(8,128)(2,1)}, bf16[128,768]{1,0:T(8,128)(2,1)S(1)}, u32[]{:S(2)}) copy-start(bf16[128,768]{1,0:T(8,128)(2,1)S(1)} %fusion.16) | copy-start | bytes 589828
  102.0 6.5 %copy-start.23 = (bf16[512,768]{1,0:T(8,128)(2,1)S(1)}, bf16[512,768]{1,0:T(8,128)(2,1)}, u32[]{:S(2)}) copy-start(bf16[512,768]{1,0:T(8,128)(2,1)} %pad_maximum_fusion.5) | copy-start | bytes 2359300
  102.0 6.5 %copy-start.33 = (bf16[512,768]{1,0:T(8,128)(2,1)S(1)}, bf16[512,768]{1,0:T(8,128)(2,1)}, u32[]{:S(2)}) copy-start(bf16[512,768]{1,0:T(8,128)(2,1)} %param.42) | copy-start | bytes 2359300
  102.4 19.8 %copy-start.19 = (f32[128,768]{1,0:T(8,128)}, f32[128,768]{1,0:T(8,128)S(1)}, u32[]{:S(2)}) copy-start(f32[128,768]{1,0:T(8,128)S(1)} %get-tuple-element.181) | copy-start | bytes 1179652
  102.6 7.6 %copy-start.32 = (bf16[768,512]{1,0:T(8,128)(2,1)S(1)}, bf16[768,512]{1,0:T(8,128)(2,1)}, u32[]{:S(2)}) copy-start(bf16[768,512]{1,0:T(8,128)(2,1)} %param.40) | copy-start | bytes 2359300
  102.6 5.7 %collective-permute-start.2 = (bf16[128,768]{1,0:T(8,128)(2,1)S(1)}, bf16[128,768]{1,0:T(8,128)(2,1)S(1)}, u32[]{:S(2)}, u32[]{:S(2)}) collective-permute-start(bf16[128,768]{1,0:T(8,128)(2,1)S(1)} %multiply_convert_fusion.2), channel_id=1, source_target_pairs={{0,2},{1,3},{2,0},{3,1},{4,6},{5,7},{6,4},{7,5},{8,10},{9,11},{10,... | collective-permute-start | bytes 589832 | tf_op jit(solution)/shard_map/ppermute | solution.py:436
  108.4 1.8 collective-permute-start.3
  109.1 1.7 copy-start.34
  111.8 1.5 copy-start.41
  113.2 1.8 collective-permute-start.4
  115.0 7.0 %collective-permute-start.5 = (bf16[128,768]{1,0:T(8,128)(2,1)S(1)}, bf16[128,768]{1,0:T(8,128)(2,1)S(1)}, u32[]{:S(2)}, u32[]{:S(2)}) collective-permute-start(bf16[128,768]{1,0:T(8,128)(2,1)S(1)} %slice.193), channel_id=1, source_target_pairs={{0,2},{1,3},{2,0},{3,1},{4,6},{5,7},{6,4},{7,5},{8,10},{9,11},{10,... | collective-permute-start | bytes 589832 | tf_op jit(solution)/shard_map/ppermute | solution.py:436
  117.6 4.6 %copy-start.25 = (bf16[1,128,768]{2,1,0:T(8,128)(2,1)S(1)}, bf16[1,128,768]{2,1,0:T(8,128)(2,1)}, u32[]{:S(2)}) copy-start(bf16[1,128,768]{2,1,0:T(8,128)(2,1)} %param.43) | copy-start | bytes 589828
  124.6 5.4 %copy-start.27 = (bf16[128,768]{1,0:T(8,128)(2,1)S(1)}, bf16[128,768]{1,0:T(8,128)(2,1)}, u32[]{:S(2)}) copy-start(bf16[128,768]{1,0:T(8,128)(2,1)} %copy-done.26) | copy-start | bytes 589828
  124.6 5.4 %copy-start.31 = (bf16[128,768]{1,0:T(8,128)(2,1)S(1)}, bf16[128,768]{1,0:T(8,128)(2,1)}, u32[]{:S(2)}) copy-start(bf16[128,768]{1,0:T(8,128)(2,1)} %get-tuple-element.81) | copy-start | bytes 589828
  125.8 12.7 %all-to-all-start.2 = ((bf16[8,128,128]{2,1,0:T(8,128)(2,1)}), bf16[8,128,128]{2,1,0:T(8,128)(2,1)S(1)}, u32[]{:S(2)}, u32[]{:S(2)}) async-start(bf16[8,128,128]{2,1,0:T(8,128)(2,1)} %bitcast_bitcast_fusion), calls=%async_computation.2 | async-start | bytes 524288 | tf_op jit(solution)/shard_map/all_to_all | solution.py:944
  130.0 8.5 %copy-start.14 = (bf16[128,768]{1,0:T(8,128)(2,1)S(1)}, bf16[128,768]{1,0:T(8,128)(2,1)}, u32[]{:S(2)}) copy-start(bf16[128,768]{1,0:T(8,128)(2,1)} %get-tuple-element.90.d_ref) | copy-start | bytes 589828
  130.0 8.5 %copy-start.29 = (bf16[128,768]{1,0:T(8,128)(2,1)S(1)}, bf16[128,768]{1,0:T(8,128)(2,1)}, u32[]{:S(2)}) copy-start(bf16[128,768]{1,0:T(8,128)(2,1)} %copy-done.28) | copy-start | bytes 589828
  140.3 2.9 collective-permute-start.6
  144.7 58.8 %all-to-all-start.3 = ((bf16[8,192,768]{2,1,0:T(8,128)(2,1)}), bf16[8,192,768]{2,1,0:T(8,128)(2,1)}, u32[]{:S(2)}, u32[]{:S(2)}) async-start(bf16[8,192,768]{2,1,0:T(8,128)(2,1)} %pad_maximum_fusion), calls=%async_computation.3 | async-start | bytes 4718592 | tf_op jit(solution)/shard_map/all_to_all | solution.py:944
  149.3 2.8 copy-start.9
  150.5 45.2 %collective-permute-start.7 = (bf16[1,384,768]{2,1,0:T(8,128)(2,1)S(1)}, bf16[1,384,768]{2,1,0:T(8,128)(2,1)S(1)}, u32[]{:S(2)}, u32[]{:S(2)}) collective-permute-start(bf16[1,384,768]{2,1,0:T(8,128)(2,1)S(1)} %slice.110), channel_id=1, source_target_pairs={{0,2},{1,3},{2,0},{3,1},{4,6},{5,7},{6,4},{7,5},{8,10},{9,11},{10,... | collective-permute-start | bytes 1769480 | tf_op jit(solution)/shard_map/ppermute | solution.py:436
  152.1 43.5 %copy-start.22 = (bf16[2,384,768]{2,1,0:T(8,128)(2,1)S(1)}, bf16[2,384,768]{2,1,0:T(8,128)(2,1)}, u32[]{:S(2)}) copy-start(bf16[2,384,768]{2,1,0:T(8,128)(2,1)} %add_convert_fusion) | copy-start | bytes 3538948
  195.6 7.9 %copy-start.12 = (bf16[1024,768]{1,0:T(8,128)(2,1)S(1)}, bf16[1024,768]{1,0:T(8,128)(2,1)}, u32[]{:S(2)}) copy-start(bf16[1024,768]{1,0:T(8,128)(2,1)} %all-gather.7.cloned.1.call-done.n_ref) | copy-start | bytes 4718596
  205.9 3.7 %collective-permute-start.8 = (bf16[2,240,384]{2,1,0:T(8,128)(2,1)S(1)}, bf16[2,240,384]{2,1,0:T(8,128)(2,1)S(1)}, u32[]{:S(2)}, u32[]{:S(2)}) collective-permute-start(bf16[2,240,384]{2,1,0:T(8,128)(2,1)S(1)} %get-tuple-element.112), channel_id=1, source_target_pairs={{0,1},{1,0},{2,3},{3,2},{4,5},{5,4},{6,7},{7,6},{8,9},{9,8},{10,11... | collective-permute-start | bytes 1105928 | tf_op jit(solution)/shard_map/ppermute | solution.py:436
  206.0 20.3 %all-to-all-start.4 = ((bf16[8,48,768]{2,1,0:T(8,128)(2,1)}), bf16[8,48,768]{2,1,0:T(8,128)(2,1)S(1)}, u32[]{:S(2)}, u32[]{:S(2)}) async-start(bf16[8,48,768]{2,1,0:T(8,128)(2,1)} %bitcast.106), calls=%async_computation.4 | async-start | bytes 1179648 | tf_op jit(solution)/shard_map/all_to_all | solution.py:646
  209.6 107.5 %all-gather.9.cloned.1.call-start = ((), (), s32[]{:S(2)}) async-start(), calls=%async_computation.8 | async-start | bytes 2654208 | tf_op jit(solution)/shard_map/all_gather | solution.py:872
  209.8 7.0 %collective-permute-start.9 = (bf16[1,240,384]{2,1,0:T(8,128)(2,1)S(1)}, bf16[1,240,384]{2,1,0:T(8,128)(2,1)S(1)}, u32[]{:S(2)}, u32[]{:S(2)}) collective-permute-start(bf16[1,240,384]{2,1,0:T(8,128)(2,1)S(1)} %slice.194), channel_id=1, source_target_pairs={{0,2},{1,3},{2,0},{3,1},{4,6},{5,7},{6,4},{7,5},{8,10},{9,11},{10,... | collective-permute-start | bytes 552968 | tf_op jit(solution)/shard_map/ppermute | solution.py:436
  226.5 13.5 %collective-permute-start.10 = (bf16[336,384]{1,0:T(8,128)(2,1)S(1)}, bf16[336,384]{1,0:T(8,128)(2,1)S(1)}, u32[]{:S(2)}, u32[]{:S(2)}) collective-permute-start(bf16[336,384]{1,0:T(8,128)(2,1)S(1)} %pad_maximum_fusion.12), channel_id=1, source_target_pairs={{0,16},{4,20},{8,24},{12,28},{16,0},{20,4},{24,8},{28,12},{1,17},{... | collective-permute-start | bytes 774152 | tf_op jit(solution)/shard_map/ppermute | solution.py:436
  240.2 20.0 %collective-permute-start.11 = (bf16[2,336,384]{2,1,0:T(8,128)(2,1)S(1)}, bf16[2,336,384]{2,1,0:T(8,128)(2,1)S(1)}, u32[]{:S(2)}, u32[]{:S(2)}) collective-permute-start(bf16[2,336,384]{2,1,0:T(8,128)(2,1)S(1)} %pad_maximum_fusion.8), channel_id=1, source_target_pairs={{0,8},{4,12},{8,0},{12,4},{16,24},{20,28},{24,16},{28,20},{1,9},{5... | collective-permute-start | bytes 1548296 | tf_op jit(solution)/shard_map/ppermute | solution.py:436
  260.3 4.9 %copy-start.30 = (bf16[512,768]{1,0:T(8,128)(2,1)S(1)}, bf16[512,768]{1,0:T(8,128)(2,1)}, u32[]{:S(2)}) copy-start(bf16[512,768]{1,0:T(8,128)(2,1)} %convolution_convert_fusion.2) | copy-start | bytes 2359300
  261.1 15.4 %collective-permute-start.12 = (bf16[2,2,160,384]{3,2,1,0:T(8,128)(2,1)}, bf16[2,2,160,384]{3,2,1,0:T(8,128)(2,1)}, u32[]{:S(2)}, u32[]{:S(2)}) collective-permute-start(bf16[2,2,160,384]{3,2,1,0:T(8,128)(2,1)} %pad_maximum_fusion.9), channel_id=1, source_target_pairs={{0,4},{4,0},{8,12},{12,8},{16,20},{20,16},{24,28},{28,24},{1,5},{5... | collective-permute-start | bytes 1474568 | tf_op jit(solution)/shard_map/ppermute | solution.py:436
  263.4 14.8 %collective-permute-start.14 = (bf16[2,2,176,384]{3,2,1,0:T(8,128)(2,1)S(1)}, bf16[2,2,176,384]{3,2,1,0:T(8,128)(2,1)}, u32[]{:S(2)}, u32[]{:S(2)}) collective-permute-start(bf16[2,2,176,384]{3,2,1,0:T(8,128)(2,1)S(1)} %pad_maximum_fusion.7), channel_id=1, source_target_pairs={{0,2},{1,3},{2,0},{3,1},{4,6},{5,7},{6,4},{7,5},{8,10},{9,11},{10,... | collective-permute-start | bytes 1622024 | tf_op jit(solution)/shard_map/ppermute | solution.py:436
  266.0 17.1 %collective-permute-start.16 = (bf16[256,768]{1,0:T(8,128)(2,1)}, bf16[256,768]{1,0:T(8,128)(2,1)}, u32[]{:S(2)}, u32[]{:S(2)}) collective-permute-start(bf16[256,768]{1,0:T(8,128)(2,1)} %slice.118), channel_id=1, source_target_pairs={{0,1},{1,0},{2,3},{3,2},{4,5},{5,4},{6,7},{7,6},{8,9},{9,8},{10,11... | collective-permute-start | bytes 1179656 | tf_op jit(solution)/shard_map/ppermute | solution.py:436
  266.0 51.1 %all-to-all-start.5 = ((bf16[8,144,384]{2,1,0:T(8,128)(2,1)}), bf16[8,144,384]{2,1,0:T(8,128)(2,1)S(1)}, u32[]{:S(2)}, u32[]{:S(2)}) async-start(bf16[8,144,384]{2,1,0:T(8,128)(2,1)} %get-tuple-element.103.x_ref), calls=%async_computation.5 | async-start | bytes 1769472 | tf_op jit(solution)/shard_map/all_to_all | solution.py:874
  277.9 22.5 %collective-permute-start.13 = (bf16[2,2,2,160,384]{4,3,2,1,0:T(8,128)(2,1)S(1)}, bf16[2,2,2,160,384]{4,3,2,1,0:T(8,128)(2,1)S(1)}, u32[]{:S(2)}, u32[]{:S(2)}) collective-permute-start(bf16[2,2,2,160,384]{4,3,2,1,0:T(8,128)(2,1)S(1)} %pad_maximum_fusion.4), channel_id=1, source_target_pairs={{0,2},{1,3},{2,0},{3,1},{4,6},{5,7},{6,4},{7,5},{8,10},{9,11},{10,... | collective-permute-start | bytes 2949128 | tf_op jit(solution)/shard_map/ppermute | solution.py:436
  279.5 20.1 %copy-start.20 = (f32[128,768]{1,0:T(8,128)S(1)}, f32[128,768]{1,0:T(8,128)}, u32[]{:S(2)}) copy-start(f32[128,768]{1,0:T(8,128)} %copy-done.19) | copy-start | bytes 1179652
  279.7 36.9 %collective-permute-start.15 = (bf16[2,2,2,176,384]{4,3,2,1,0:T(8,128)(2,1)S(1)}, bf16[2,2,2,176,384]{4,3,2,1,0:T(8,128)(2,1)S(1)}, u32[]{:S(2)}, u32[]{:S(2)}) collective-permute-start(bf16[2,2,2,176,384]{4,3,2,1,0:T(8,128)(2,1)S(1)} %pad_maximum_fusion.3), channel_id=1, source_target_pairs={{0,4},{4,0},{8,12},{12,8},{16,20},{20,16},{24,28},{28,24},{1,5},{5... | collective-permute-start | bytes 3244040 | tf_op jit(solution)/shard_map/ppermute | solution.py:436
  284.1 15.5 %collective-permute-start.17 = (bf16[128,768]{1,0:T(8,128)(2,1)S(1)}, bf16[128,768]{1,0:T(8,128)(2,1)S(1)}, u32[]{:S(2)}, u32[]{:S(2)}) collective-permute-start(bf16[128,768]{1,0:T(8,128)(2,1)S(1)} %slice.192), channel_id=1, source_target_pairs={{0,2},{1,3},{2,0},{3,1},{4,6},{5,7},{6,4},{7,5},{8,10},{9,11},{10,... | collective-permute-start | bytes 589832 | tf_op jit(solution)/shard_map/ppermute | solution.py:436
  317.1 5.2 %copy-start.21 = (bf16[2,2,2,2,176,384]{5,4,3,2,1,0:T(8,128)(2,1)}, bf16[2,2,2,2,176,384]{5,4,3,2,1,0:T(8,128)(2,1)S(1)}, u32[]{:S(2)}) copy-start(bf16[2,2,2,2,176,384]{5,4,3,2,1,0:T(8,128)(2,1)S(1)} %pad_maximum_fusion.1) | copy-start | bytes 6488068
  317.1 11.1 %collective-permute-start.19 = (bf16[2,2,4,176,384]{4,3,2,1,0:T(8,128)(2,1)S(1)}, bf16[2,2,4,176,384]{4,3,2,1,0:T(8,128)(2,1)}, u32[]{:S(2)}, u32[]{:S(2)}) collective-permute-start(bf16[2,2,4,176,384]{4,3,2,1,0:T(8,128)(2,1)S(1)} %bitcast.102), channel_id=1, source_target_pairs={{0,1},{1,0},{2,3},{3,2},{4,5},{5,4},{6,7},{7,6},{8,9},{9,8},{10,11... | collective-permute-start | bytes 6488072 | tf_op jit(solution)/shard_map/ppermute | solution.py:436
  317.2 11.0 %collective-permute-start.18 = (bf16[2,8,160,384]{3,2,1,0:T(8,128)(2,1)}, bf16[2,8,160,384]{3,2,1,0:T(8,128)(2,1)}, u32[]{:S(2)}, u32[]{:S(2)}) collective-permute-start(bf16[2,8,160,384]{3,2,1,0:T(8,128)(2,1)} %bitcast.104), channel_id=1, source_target_pairs={{0,1},{1,0},{2,3},{3,2},{4,5},{5,4},{6,7},{7,6},{8,9},{9,8},{10,11... | collective-permute-start | bytes 5898248 | tf_op jit(solution)/shard_map/ppermute | solution.py:436
  317.7 1.8 copy-start.2
  319.5 2.8 copy-start.4
  319.5 2.8 copy-start.5
  319.5 3.7 %copy-start.6 = (bf16[768,768]{1,0:T(8,128)(2,1)S(1)}, bf16[768,768]{1,0:T(8,128)(2,1)}, u32[]{:S(2)}) copy-start(bf16[768,768]{1,0:T(8,128)(2,1)} %refs_6_.1) | copy-start | bytes 3538948
  319.5 4.0 %copy-start.7 = (bf16[768,768]{1,0:T(8,128)(2,1)S(1)}, bf16[768,768]{1,0:T(8,128)(2,1)}, u32[]{:S(2)}) copy-start(bf16[768,768]{1,0:T(8,128)(2,1)} %refs_7_.1) | copy-start | bytes 3538948
  319.5 4.0 %copy-start.11 = (bf16[1,128,768]{2,1,0:T(8,128)(2,1)S(1)}, bf16[1,128,768]{2,1,0:T(8,128)(2,1)}, u32[]{:S(2)}) copy-start(bf16[1,128,768]{2,1,0:T(8,128)(2,1)} %param.22) | copy-start | bytes 589828
  319.5 4.1 %copy-start.13 = (f32[128,768]{1,0:T(8,128)S(1)}, f32[128,768]{1,0:T(8,128)}, u32[]{:S(2)}) copy-start(f32[128,768]{1,0:T(8,128)} %get-tuple-element.145.m_ref) | copy-start | bytes 1179652
  319.5 4.2 %copy-start.15 = (bf16[128,768]{1,0:T(8,128)(2,1)S(1)}, bf16[128,768]{1,0:T(8,128)(2,1)}, u32[]{:S(2)}) copy-start(bf16[128,768]{1,0:T(8,128)(2,1)} %get-tuple-element.90.d_ref) | copy-start | bytes 589828
  319.5 4.2 %copy-start.17 = (bf16[768,12]{0,1:T(8,128)(2,1)S(1)}, bf16[768,12]{0,1:T(8,128)(2,1)}, u32[]{:S(2)}) copy-start(bf16[768,12]{0,1:T(8,128)(2,1)} %param.27) | copy-start | bytes 55300
  319.6 4.2 %copy-start.18 = (f32[1,768]{1,0:T(1,128)S(1)}, f32[1,768]{1,0:T(1,128)}, u32[]{:S(2)}) copy-start(f32[1,768]{1,0:T(1,128)} %broadcast_in_dim.28.g_ref) | copy-start | bytes 9220
  328.2 13.1 %copy-start.1 = (bf16[768,768]{1,0:T(8,128)(2,1)S(1)}, bf16[768,768]{1,0:T(8,128)(2,1)}, u32[]{:S(2)}) copy-start(bf16[768,768]{1,0:T(8,128)(2,1)} %param.36) | copy-start | bytes 3538948
  338.3 2.4 copy-start.39
  (6 other events, 6.3 us)
Sparse Core Ops, SparseCore 0:
  10.2 26.6 all-gather.4
  39.6 43.8 all-gather.6
  240.3 70.4 all-gather.8

commit v6 on v5

--- a/solution.py
+++ b/solution.py
@@ -508,7 +508,7 @@
     def _():
         x = x_ref[...].astype(F)
         scale = lax.rsqrt(jnp.sum(x * x, -1, keepdims=True) * (1.0 / width) + NORM_EPS)
-        n_ref[...] = (x * scale * g_ref[...]).astype(LOW)
+        n_ref[...] = (x * scale * g_ref[...][None]).astype(LOW)
         LT[...] = jnp.zeros_like(LT)
         LT[: wr_ref.shape[0]] = nt(wr_ref[...], n_ref[...]).astype(LOW).astype(F)
 
@@ -541,7 +541,7 @@
     return pl.pallas_call(
         partial(project_kernel, each, blocks),
         grid=(seqs,),
-        in_specs=[full(rows, width), full(1, width), column, column, column, full(*wr.shape), column],
+        in_specs=[full(rows, width), full(width), column, column, column, full(*wr.shape), column],
         out_specs=[
             pl.BlockSpec((1, rows + extra, 3 * span), lambda s: (s, 0, 0)),
             full(rows, width),
@@ -550,7 +550,7 @@
         out_shape=[sd((seqs, rows + extra, 3 * span), LOW), sd((rows, width), LOW), sd((rows, width), F)],
         scratch_shapes=[pltpu.VMEM((128, 128), F)],
         compiler_params=pltpu.CompilerParams(vmem_limit_bytes=60 * 1024 * 1024),
-    )(x, gain[None], wq, wk, wv, wr, wg)
+    )(x, gain, wq, wk, wv, wr, wg)
 
 
 def tokens_kernel(each, blocks, x_ref, g_ref, m_ref, b_ref, d_ref, wq_ref, wk_ref, wv_ref, wr_ref, wg_ref, o_ref, ACC, LG):
@@ -580,7 +580,7 @@
         heads = wr_ref.shape[0]
         x = x_ref[...].astype(F)
         scale = lax.rsqrt(jnp.sum(x * x, -1, keepdims=True) * (1.0 / width) + NORM_EPS)
-        grad = (ACC[...] + nn(LG[...].T[:, :heads], wr_ref[...])) * g_ref[...]
+        grad = (ACC[...] + nn(LG[...].T[:, :heads], wr_ref[...])) * g_ref[...][None]
         along = jnp.sum(x * grad, -1, keepdims=True) * (1.0 / width)
         o_ref[...] = m_ref[...] + scale * (grad - x * (scale * scale * along))
 
@@ -596,7 +596,7 @@
         partial(tokens_kernel, each, blocks),
         grid=(blocks,),
         in_specs=[
-            full(rows, width), full(1, width), full(rows, width),
+            full(rows, width), full(width), full(rows, width),
             pl.BlockSpec((1, tall, lanes), lambda s: (s, 0, 0)),
             pl.BlockSpec((rows, span), lambda s: (0, s)),
             column, column, column, full(*wr.shape), column,
@@ -605,7 +605,7 @@
         out_shape=jax.ShapeDtypeStruct((rows, width), F),
         scratch_shapes=[pltpu.VMEM((rows, width), F), pltpu.VMEM((128, 128), F)],
         compiler_params=pltpu.CompilerParams(vmem_limit_bytes=16 * 1024 * 1024),
-    )(x, gain[None], middle_grad, back, gate_low, wq, wk, wv, wr, wg)
+    )(x, gain, middle_grad, back, gate_low, wq, wk, wv, wr, wg)
 
 
 def feed_kernel(a_ref, b_ref, c_ref, g_ref, l_ref, d_ref):

time: 349 us -> 348 us (level)
  no operation moved by 1% of the time
where the time goes in v6:
time: 348 us; the launch traced here: 347 us
  waiting for transfers between devices  123 us (35%)
  Pallas kernels  111 us (32%)
  starting transfers between devices  42.5 us (12%)
  other arithmetic  18.7 us (5%)
  between operations  14.7 us (4%)
  blocking collectives  12.7 us (4%)
  matrix products  12.7 us (4%)
  local copies, waits for them, and re-layouts  12.1 us (3%)
    ppermute x20, waiting for transfers between devices, flip(): return lax.ppermute(array, axis, [(i, i ^ mask) for i in range(peers)])  94.2 us
    pallas_call x1, Pallas kernels, bwd_scan(): pl.pallas_call(partial(bwd_kernel, C, H, n // 2), grid=(n // 2,), in_spec...  43.5 us
    pallas_call x1, Pallas kernels, fwd_scan(): pl.pallas_call(partial(fwd_kernel, C, H), grid=(n // 2,), in_specs=[pl.Bl...  38 us
    all_to_all x3, waiting for transfers between devices, swap(): return lax.all_to_all(array, 'seq', split_axis=0, concat_axis=0, tiled=True)  18.8 us
    ppermute x20, starting transfers between devices, flip(): return lax.ppermute(array, axis, [(i, i ^ mask) for i in range(peers)])  18.7 us
    all_to_all x3, starting transfers between devices, swap(): return lax.all_to_all(array, 'seq', split_axis=0, concat_axis=0, tiled=True)  16.2 us
    all_to_all x1, blocking collectives, swap(): return lax.all_to_all(array, 'seq', split_axis=0, concat_axis=0, tiled=True)  12.7 us
    pallas_call x1, Pallas kernels, share_tiles(): pl.pallas_call(partial(last_kernel, seqs, each, heads, local_heads), grid...  10.1 us
  transfers between devices with their start and end apart: 28, of which 17 were waited for; matrix products, arithmetic and copies ran while one was open for 7% of the time, Pallas kernels for 28%

profile of v6, /device:TPU:0, one launch (start us, length us, event | category | flops | bytes accessed | tf_op | source)
XLA Modules:
  0.0 346.6 jit_solution(15107646178100774718)
XLA Ops:
  7.3 2.0 shard_map.382
  9.3 7.4 %shard_map.381 = (bf16[8,144,384]{2,1,0:T(8,128)(2,1)}, bf16[128,768]{1,0:T(8,128)(2,1)}, f32[128,768]{1,0:T(8,128)}) custom-call(bf16[128,768]{1,0:T(8,128)(2,1)} %bitcast.96, f32[768]{0:T(1024)} %g_ref.5, bf16[768,768]{1,0:T(8,128)(2,1)} %refs_4_.1, bf16[768,768]{1,0:T(8,128)(2,1)} %refs_5_.1, bf16[768,768]{1,0:T(8,128)(2,1)} %refs_6_.1, ...), custom_call_target="tpu_custom_call" | custom-call | tf_op jit(solution)/shard_map/pallas_call | solution.py:541
  16.8 7.4 %all-to-all-start = ((bf16[8,144,384]{2,1,0:T(8,128)(2,1)}), bf16[8,144,384]{2,1,0:T(8,128)(2,1)S(1)}, u32[]{:S(2)}, u32[]{:S(2)}) async-start(bf16[8,144,384]{2,1,0:T(8,128)(2,1)} %get-tuple-element.79), calls=%async_computation | async-start | bytes 1769472 | tf_op jit(solution)/shard_map/all_to_all | solution.py:944
  24.2 1.6 collective-permute-start
  25.7 9.9 %collective-permute-done = bf16[128,768]{1,0:T(8,128)(2,1)S(1)} collective-permute-done((bf16[128,768]{1,0:T(8,128)(2,1)S(1)}, bf16[128,768]{1,0:T(8,128)(2,1)S(1)}, u32[]{:S(2)}, u32[]{:S(2)}) %collective-permute-start) | collective-permute-done | bytes 196640 | tf_op jit(solution)/shard_map/ppermute | solution.py:436
  35.8 1.7 collective-permute-done.1
  37.5 0.9 pad_maximum_fusion.5
  38.4 1.0 constant_dynamic-slice_fusion.2.own_ref.refs_29_
  39.4 7.1 %all-to-all-done.xa_ref.xb_ref.refs_0_.refs_9_.refs_18_ = bf16[8,144,384]{2,1,0:T(8,128)(2,1)S(1)} async-done(((bf16[8,144,384]{2,1,0:T(8,128)(2,1)}), bf16[8,144,384]{2,1,0:T(8,128)(2,1)S(1)}, u32[]{:S(2)}, u32[]{:S(2)}) %all-to-all-start) | async-done | bytes 884768 | tf_op jit(solution)/shard_map/all_to_all | solution.py:944
  46.5 38.0 %shard_map.383 = (bf16[1024,128]{1,0:T(8,128)(2,1)S(1)}, f32[2048,256]{1,0:T(8,128)S(1)}, f32[2048,256]{1,0:T(8,128)}, f32[1024,128]{1,0:T(8,128)S(1)}, f32[2048...) custom-call(bf16[8,144,384]{2,1,0:T(8,128)(2,1)S(1)} %all-to-all-don, ...), custom_call_target="tpu_custom_call" | custom-call | tf_op jit(solution)/shard_map/pallas_call | solution.py:214
  84.5 1.3 copy-done.3
  85.8 0.8 copy-done.8
  87.3 12.7 %all_to_all.30 = bf16[8,128,128]{2,1,0:T(8,128)(2,1)S(1)} all-to-all(bf16[8,128,128]{2,1,0:T(8,128)(2,1)} %bitcast.99), channel_id=1, replica_groups=mesh['seq'=8,'tp'=4] {'seq'}, dimensions={0} | all-to-all | bytes 524288 | tf_op jit(solution)/shard_map/all_to_all | solution.py:944
  101.4 1.6 collective-permute-start.2
  103.0 4.1 %collective-permute-done.2 = bf16[128,768]{1,0:T(8,128)(2,1)S(1)} collective-permute-done((bf16[128,768]{1,0:T(8,128)(2,1)S(1)}, bf16[128,768]{1,0:T(8,128)(2,1)S(1)}, u32[]{:S(2)}, u32[]{:S(2)}) %collective-permute-start.2) | collective-permute-done | bytes 196640 | tf_op jit(solution)/shard_map/ppermute | solution.py:436
  107.9 1.1 collective-permute-done.3
  109.6 1.0 multiply_convert_fusion
  112.7 1.0 collective-permute-done.4
  113.8 1.6 collective-permute-start.5
  115.4 1.0 convolution_convert_fusion
  116.4 1.6 pad_maximum_fusion
  118.0 2.8 collective-permute-done.5
  121.0 0.9 fusion.65
  121.9 1.5 fusion.17
  124.5 4.2 %all-to-all-start.2 = ((bf16[8,128,128]{2,1,0:T(8,128)(2,1)}), bf16[8,128,128]{2,1,0:T(8,128)(2,1)S(1)}, u32[]{:S(2)}, u32[]{:S(2)}) async-start(bf16[8,128,128]{2,1,0:T(8,128)(2,1)} %bitcast_bitcast_fusion), calls=%async_computation.2 | async-start | bytes 524288 | tf_op jit(solution)/shard_map/all_to_all | solution.py:944
  128.8 0.9 fusion.53
  129.7 2.8 convolution_convert_fusion.2
  132.4 4.8 %all-to-all-done.2 = bf16[8,128,128]{2,1,0:T(8,128)(2,1)S(1)} async-done(((bf16[8,128,128]{2,1,0:T(8,128)(2,1)}), bf16[8,128,128]{2,1,0:T(8,128)(2,1)S(1)}, u32[]{:S(2)}, u32[]{:S(2)}) %all-to-all-start.2) | async-done | bytes 262176 | tf_op jit(solution)/shard_map/all_to_all | solution.py:944
  137.6 1.5 convolution_convert_fusion.1
  139.1 2.8 collective-permute-done.6
  141.9 1.5 add_convert_fusion
  143.5 4.6 %all-to-all-start.3 = ((bf16[8,192,768]{2,1,0:T(8,128)(2,1)}), bf16[8,192,768]{2,1,0:T(8,128)(2,1)}, u32[]{:S(2)}, u32[]{:S(2)}) async-start(bf16[8,192,768]{2,1,0:T(8,128)(2,1)} %pad_maximum_fusion), calls=%async_computation.3 | async-start | bytes 4718592 | tf_op jit(solution)/shard_map/all_to_all | solution.py:944
  148.1 1.2 slice.110
  149.3 1.6 collective-permute-start.7
  150.9 43.5 %shard_map.384 = (bf16[8,144,384]{2,1,0:T(8,128)(2,1)}, f32[128,256]{1,0:T(8,128)S(1)}, f32[2,256]{1,0:T(2,128)S(1)}, f32[128,256]{1,0:T(8,128)S(1)}, f32[1,128]...) custom-call(bf16[8,144,384]{2,1,0:T(8,128)(2,1)S(1)} %all-to-all-done.xa_ref.xb_ref.refs_0_.refs, ...), custom_call_target="tpu_custom_call" | custom-call | flops 1000 | bytes 1000 | tf_op jit(solution)/shard_map/pallas_call | solution.py:395
  194.5 1.0 add_convert_fusion.1
  195.4 6.9 %all-to-all-done.3 = bf16[8,192,768]{2,1,0:T(8,128)(2,1)} async-done(((bf16[8,192,768]{2,1,0:T(8,128)(2,1)}), bf16[8,192,768]{2,1,0:T(8,128)(2,1)}, u32[]{:S(2)}, u32[]{:S(2)}) %all-to-all-start.3) | async-done | bytes 2359328 | tf_op jit(solution)/shard_map/all_to_all | solution.py:944
  202.3 2.4 shard_map.385
  204.8 3.6 %all-to-all-start.4 = ((bf16[8,48,768]{2,1,0:T(8,128)(2,1)}), bf16[8,48,768]{2,1,0:T(8,128)(2,1)S(1)}, u32[]{:S(2)}, u32[]{:S(2)}) async-start(bf16[8,48,768]{2,1,0:T(8,128)(2,1)} %bitcast.106), calls=%async_computation.4 | async-start | bytes 1179648 | tf_op jit(solution)/shard_map/all_to_all | solution.py:646
  208.6 1.6 collective-permute-start.9
  210.2 5.4 %collective-permute-done.9 = bf16[1,240,384]{2,1,0:T(8,128)(2,1)S(1)} collective-permute-done((bf16[1,240,384]{2,1,0:T(8,128)(2,1)S(1)}, bf16[1,240,384]{2,1,0:T(8,128)(2,1)S(1)}, u32[]{:S(2)}, u32[]{:S(2)}) %collective-permute-start.9) | collective-permute-done | bytes 184352 | tf_op jit(solution)/shard_map/ppermute | solution.py:436
  215.7 9.5 %all-to-all-done.4 = bf16[8,48,768]{2,1,0:T(8,128)(2,1)S(1)} async-done(((bf16[8,48,768]{2,1,0:T(8,128)(2,1)}), bf16[8,48,768]{2,1,0:T(8,128)(2,1)S(1)}, u32[]{:S(2)}, u32[]{:S(2)}) %all-to-all-start.4) | async-done | bytes 589856 | tf_op jit(solution)/shard_map/all_to_all | solution.py:646
  225.4 2.8 reduce_sum.157
  228.2 10.6 %collective-permute-done.10 = bf16[336,384]{1,0:T(8,128)(2,1)S(1)} collective-permute-done((bf16[336,384]{1,0:T(8,128)(2,1)S(1)}, bf16[336,384]{1,0:T(8,128)(2,1)S(1)}, u32[]{:S(2)}, u32[]{:S(2)}) %collective-permute-start.10) | collective-permute-done | bytes 258080 | tf_op jit(solution)/shard_map/ppermute | solution.py:436
  239.1 19.9 %collective-permute-done.11 = bf16[2,336,384]{2,1,0:T(8,128)(2,1)S(1)} collective-permute-done((bf16[2,336,384]{2,1,0:T(8,128)(2,1)S(1)}, bf16[2,336,384]{2,1,0:T(8,128)(2,1)S(1)}, u32[]{:S(2)}, u32[]{:S(2)}) %collective-permute-start.11) | collective-permute-done | bytes 516128 | tf_op jit(solution)/shard_map/ppermute | solution.py:436
  259.1 0.8 pad_maximum_fusion.9
  259.9 2.2 collective-permute-start.12
  262.2 1.8 collective-permute-start.14
  264.0 0.8 slice.118
  264.7 3.8 %all-to-all-start.5 = ((bf16[8,144,384]{2,1,0:T(8,128)(2,1)}), bf16[8,144,384]{2,1,0:T(8,128)(2,1)S(1)}, u32[]{:S(2)}, u32[]{:S(2)}) async-start(bf16[8,144,384]{2,1,0:T(8,128)(2,1)} %get-tuple-element.103.x_ref), calls=%async_computation.5 | async-start | bytes 1769472 | tf_op jit(solution)/shard_map/all_to_all | solution.py:874
  268.6 6.6 %collective-permute-done.12 = bf16[2,2,160,384]{3,2,1,0:T(8,128)(2,1)} collective-permute-done((bf16[2,2,160,384]{3,2,1,0:T(8,128)(2,1)}, bf16[2,2,160,384]{3,2,1,0:T(8,128)(2,1)}, u32[]{:S(2)}, u32[]{:S(2)}) %collective-permute-start.12) | collective-permute-done | bytes 491552 | tf_op jit(solution)/shard_map/ppermute | solution.py:436
  275.2 1.2 select_bitcast_fusion.9
  277.1 1.3 select_bitcast_fusion.5
  278.5 3.4 collective-permute-start.15
  281.8 1.1 convert_add_fusion
  282.9 1.7 collective-permute-start.17
  284.7 13.7 %collective-permute-done.17 = bf16[128,768]{1,0:T(8,128)(2,1)S(1)} collective-permute-done((bf16[128,768]{1,0:T(8,128)(2,1)S(1)}, bf16[128,768]{1,0:T(8,128)(2,1)S(1)}, u32[]{:S(2)}, u32[]{:S(2)}) %collective-permute-start.17) | collective-permute-done | bytes 196640 | tf_op jit(solution)/shard_map/ppermute | solution.py:436
  299.4 1.6 pad_maximum_fusion.2
  301.0 14.4 %collective-permute-done.15 = bf16[2,2,2,176,384]{4,3,2,1,0:T(8,128)(2,1)S(1)} collective-permute-done((bf16[2,2,2,176,384]{4,3,2,1,0:T(8,128)(2,1)S(1)}, bf16[2,2,2,176,384]{4,3,2,1,0:T(8,128)(2,1)S(1)}, u32[]{:S(2)}, u32[]{:S(2)}) %collective-permute-start.15) | collective-permute-done | bytes 1081376 | tf_op jit(solution)/shard_map/ppermute | solution.py:436
  316.5 1.8 copy-done.2
  318.3 2.7 shard_map.388
  321.1 0.9 copy-done.6
  322.5 4.5 %shard_map.386 = f32[128,768]{1,0:T(8,128)} custom-call(bf16[128,768]{1,0:T(8,128)(2,1)S(1)} %bitcast.97, f32[768]{0:T(1024)S(1)} %copy-done.18, f32[128,768]{1,0:T(8,128)S(1)} %copy-done.13, bf16[8,144,384]{2,1,0:T(8,128)(2,1)S(1)} %all-to-all-done.5.b_ref, bf16[128,768]{1,0:T(8,128)(2,1)S(1)} %copy-done.15, bf16[768,768]{1,0:T(8,128)(2,1)S(1)} %copy-done.4, ...), custom_call_target="tpu_custom_call" | custom-call | tf_op jit(solution)/shard_map/pallas_call | solution.py:595
  327.0 10.1 %shard_map.387 = (f32[768,768]{1,0:T(8,128)}, f32[768,768]{1,0:T(8,128)}, f32[768,768]{1,0:T(8,128)}, f32[768,1]{1,0:T(8,128)S(1)}, f32[3,64,256]{2,1,0:T(8,128)...) custom-call(s32[1]{0:T(128)} %bitcast.me_ref, ...), custom_call_target="tpu_custom_call" | custom-call | tf_op jit(solution)/shard_map/pallas_call | solution.py:887
  (170 shorter events, 14.5 us)
Async XLA Ops:
  7.2 93.5 %copy-start = (bf16[768,768]{1,0:T(8,128)(2,1)S(1)}, bf16[768,768]{1,0:T(8,128)(2,1)}, u32[]{:S(2)}) copy-start(bf16[768,768]{1,0:T(8,128)(2,1)} %param.36) | copy-start | bytes 3538948
  7.2 31.2 %all-gather.5.cloned.1.call-start = ((), (), s32[]{:S(2)}) async-start(), calls=%async_computation.6 | async-start | bytes 2088960 | tf_op jit(solution)/shard_map/all_gather | solution.py:949
  9.3 78.1 %all-gather.7.cloned.1.call-start = ((), (), s32[]{:S(2)}) async-start(), calls=%async_computation.7 | async-start | bytes 1769472 | tf_op jit(solution)/shard_map/all_gather | solution.py:974
  16.7 7.4 %copy-start.24 = (bf16[1,128,768]{2,1,0:T(8,128)(2,1)S(1)}, bf16[1,128,768]{2,1,0:T(8,128)(2,1)}, u32[]{:S(2)}) copy-start(bf16[1,128,768]{2,1,0:T(8,128)(2,1)} %param.43) | copy-start | bytes 589828
  16.8 29.7 %all-to-all-start = ((bf16[8,144,384]{2,1,0:T(8,128)(2,1)}), bf16[8,144,384]{2,1,0:T(8,128)(2,1)S(1)}, u32[]{:S(2)}, u32[]{:S(2)}) async-start(bf16[8,144,384]{2,1,0:T(8,128)(2,1)} %get-tuple-element.79), calls=%async_computation | async-start | bytes 1769472 | tf_op jit(solution)/shard_map/all_to_all | solution.py:944
  24.2 11.5 %collective-permute-start = (bf16[128,768]{1,0:T(8,128)(2,1)S(1)}, bf16[128,768]{1,0:T(8,128)(2,1)S(1)}, u32[]{:S(2)}, u32[]{:S(2)}) collective-permute-start(bf16[128,768]{1,0:T(8,128)(2,1)S(1)} %bitcast.107), channel_id=1, source_target_pairs={{0,2},{1,3},{2,0},{3,1},{4,6},{5,7},{6,4},{7,5},{8,10},{9,11},{10,... | collective-permute-start | bytes 589832 | tf_op jit(solution)/shard_map/ppermute | solution.py:436
  35.7 1.8 collective-permute-start.1
  39.4 61.1 %copy-start.38 = (f32[768]{0:T(1024)S(1)}, f32[768]{0:T(1024)}, u32[]{:S(2)}) copy-start(f32[768]{0:T(1024)} %param.37) | copy-start | bytes 9220
  39.4 61.1 %copy-start.39 = (f32[768]{0:T(1024)S(1)}, f32[768]{0:T(1024)}, u32[]{:S(2)}) copy-start(f32[768]{0:T(1024)} %param.38) | copy-start | bytes 9220
  87.3 13.1 %copy-start.35 = (f32[128,768]{1,0:T(8,128)S(1)}, f32[128,768]{1,0:T(8,128)}, u32[]{:S(2)}) copy-start(f32[128,768]{1,0:T(8,128)} %get-tuple-element.85) | copy-start | bytes 1179652
  87.3 13.4 %copy-start.10 = (bf16[1,128,768]{2,1,0:T(8,128)(2,1)S(1)}, bf16[1,128,768]{2,1,0:T(8,128)(2,1)}, u32[]{:S(2)}) copy-start(bf16[1,128,768]{2,1,0:T(8,128)(2,1)} %param.22) | copy-start | bytes 589828
  100.7 6.4 %copy-start.26 = (bf16[128,768]{1,0:T(8,128)(2,1)}, bf16[128,768]{1,0:T(8,128)(2,1)S(1)}, u32[]{:S(2)}) copy-start(bf16[128,768]{1,0:T(8,128)(2,1)S(1)} %fusion.16) | copy-start | bytes 589828
  100.8 6.5 %copy-start.23 = (bf16[512,768]{1,0:T(8,128)(2,1)S(1)}, bf16[512,768]{1,0:T(8,128)(2,1)}, u32[]{:S(2)}) copy-start(bf16[512,768]{1,0:T(8,128)(2,1)} %pad_maximum_fusion.5) | copy-start | bytes 2359300
  100.8 6.5 %copy-start.33 = (bf16[512,768]{1,0:T(8,128)(2,1)S(1)}, bf16[512,768]{1,0:T(8,128)(2,1)}, u32[]{:S(2)}) copy-start(bf16[512,768]{1,0:T(8,128)(2,1)} %param.42) | copy-start | bytes 2359300
  101.2 19.8 %copy-start.19 = (f32[128,768]{1,0:T(8,128)}, f32[128,768]{1,0:T(8,128)S(1)}, u32[]{:S(2)}) copy-start(f32[128,768]{1,0:T(8,128)S(1)} %get-tuple-element.181) | copy-start | bytes 1179652
  101.4 7.6 %copy-start.32 = (bf16[768,512]{1,0:T(8,128)(2,1)S(1)}, bf16[768,512]{1,0:T(8,128)(2,1)}, u32[]{:S(2)}) copy-start(bf16[768,512]{1,0:T(8,128)(2,1)} %param.40) | copy-start | bytes 2359300
  101.4 5.7 %collective-permute-start.2 = (bf16[128,768]{1,0:T(8,128)(2,1)S(1)}, bf16[128,768]{1,0:T(8,128)(2,1)S(1)}, u32[]{:S(2)}, u32[]{:S(2)}) collective-permute-start(bf16[128,768]{1,0:T(8,128)(2,1)S(1)} %multiply_convert_fusion.2), channel_id=1, source_target_pairs={{0,2},{1,3},{2,0},{3,1},{4,6},{5,7},{6,4},{7,5},{8,10},{9,11},{10,... | collective-permute-start | bytes 589832 | tf_op jit(solution)/shard_map/ppermute | solution.py:436
  107.1 1.8 collective-permute-start.3
  107.9 1.7 copy-start.34
  110.6 1.5 copy-start.40
  111.9 1.8 collective-permute-start.4
  113.8 7.0 %collective-permute-start.5 = (bf16[128,768]{1,0:T(8,128)(2,1)S(1)}, bf16[128,768]{1,0:T(8,128)(2,1)S(1)}, u32[]{:S(2)}, u32[]{:S(2)}) collective-permute-start(bf16[128,768]{1,0:T(8,128)(2,1)S(1)} %slice.193), channel_id=1, source_target_pairs={{0,2},{1,3},{2,0},{3,1},{4,6},{5,7},{6,4},{7,5},{8,10},{9,11},{10,... | collective-permute-start | bytes 589832 | tf_op jit(solution)/shard_map/ppermute | solution.py:436
  116.4 4.6 %copy-start.25 = (bf16[1,128,768]{2,1,0:T(8,128)(2,1)S(1)}, bf16[1,128,768]{2,1,0:T(8,128)(2,1)}, u32[]{:S(2)}) copy-start(bf16[1,128,768]{2,1,0:T(8,128)(2,1)} %param.43) | copy-start | bytes 589828
  121.9 1.5 copy-start.28
  123.4 5.4 %copy-start.27 = (bf16[128,768]{1,0:T(8,128)(2,1)S(1)}, bf16[128,768]{1,0:T(8,128)(2,1)}, u32[]{:S(2)}) copy-start(bf16[128,768]{1,0:T(8,128)(2,1)} %copy-done.26) | copy-start | bytes 589828
  123.4 5.4 %copy-start.31 = (bf16[128,768]{1,0:T(8,128)(2,1)S(1)}, bf16[128,768]{1,0:T(8,128)(2,1)}, u32[]{:S(2)}) copy-start(bf16[128,768]{1,0:T(8,128)(2,1)} %get-tuple-element.81) | copy-start | bytes 589828
  124.5 12.7 %all-to-all-start.2 = ((bf16[8,128,128]{2,1,0:T(8,128)(2,1)}), bf16[8,128,128]{2,1,0:T(8,128)(2,1)S(1)}, u32[]{:S(2)}, u32[]{:S(2)}) async-start(bf16[8,128,128]{2,1,0:T(8,128)(2,1)} %bitcast_bitcast_fusion), calls=%async_computation.2 | async-start | bytes 524288 | tf_op jit(solution)/shard_map/all_to_all | solution.py:944
  128.7 8.5 %copy-start.14 = (bf16[128,768]{1,0:T(8,128)(2,1)S(1)}, bf16[128,768]{1,0:T(8,128)(2,1)}, u32[]{:S(2)}) copy-start(bf16[128,768]{1,0:T(8,128)(2,1)} %get-tuple-element.90.d_ref) | copy-start | bytes 589828
  128.7 8.5 %copy-start.29 = (bf16[128,768]{1,0:T(8,128)(2,1)S(1)}, bf16[128,768]{1,0:T(8,128)(2,1)}, u32[]{:S(2)}) copy-start(bf16[128,768]{1,0:T(8,128)(2,1)} %copy-done.28) | copy-start | bytes 589828
  139.0 2.9 collective-permute-start.6
  143.5 58.8 %all-to-all-start.3 = ((bf16[8,192,768]{2,1,0:T(8,128)(2,1)}), bf16[8,192,768]{2,1,0:T(8,128)(2,1)}, u32[]{:S(2)}, u32[]{:S(2)}) async-start(bf16[8,192,768]{2,1,0:T(8,128)(2,1)} %pad_maximum_fusion), calls=%async_computation.3 | async-start | bytes 4718592 | tf_op jit(solution)/shard_map/all_to_all | solution.py:944
  148.1 2.8 copy-start.9
  149.3 45.2 %collective-permute-start.7 = (bf16[1,384,768]{2,1,0:T(8,128)(2,1)S(1)}, bf16[1,384,768]{2,1,0:T(8,128)(2,1)S(1)}, u32[]{:S(2)}, u32[]{:S(2)}) collective-permute-start(bf16[1,384,768]{2,1,0:T(8,128)(2,1)S(1)} %slice.110), channel_id=1, source_target_pairs={{0,2},{1,3},{2,0},{3,1},{4,6},{5,7},{6,4},{7,5},{8,10},{9,11},{10,... | collective-permute-start | bytes 1769480 | tf_op jit(solution)/shard_map/ppermute | solution.py:436
  150.9 43.6 %copy-start.22 = (bf16[2,384,768]{2,1,0:T(8,128)(2,1)S(1)}, bf16[2,384,768]{2,1,0:T(8,128)(2,1)}, u32[]{:S(2)}) copy-start(bf16[2,384,768]{2,1,0:T(8,128)(2,1)} %add_convert_fusion) | copy-start | bytes 3538948
  194.5 7.8 %copy-start.12 = (bf16[1024,768]{1,0:T(8,128)(2,1)S(1)}, bf16[1024,768]{1,0:T(8,128)(2,1)}, u32[]{:S(2)}) copy-start(bf16[1024,768]{1,0:T(8,128)(2,1)} %all-gather.7.cloned.1.call-done.n_ref) | copy-start | bytes 4718596
  204.7 3.7 %collective-permute-start.8 = (bf16[2,240,384]{2,1,0:T(8,128)(2,1)S(1)}, bf16[2,240,384]{2,1,0:T(8,128)(2,1)S(1)}, u32[]{:S(2)}, u32[]{:S(2)}) collective-permute-start(bf16[2,240,384]{2,1,0:T(8,128)(2,1)S(1)} %get-tuple-element.112), channel_id=1, source_target_pairs={{0,1},{1,0},{2,3},{3,2},{4,5},{5,4},{6,7},{7,6},{8,9},{9,8},{10,11... | collective-permute-start | bytes 1105928 | tf_op jit(solution)/shard_map/ppermute | solution.py:436
  204.8 20.3 %all-to-all-start.4 = ((bf16[8,48,768]{2,1,0:T(8,128)(2,1)}), bf16[8,48,768]{2,1,0:T(8,128)(2,1)S(1)}, u32[]{:S(2)}, u32[]{:S(2)}) async-start(bf16[8,48,768]{2,1,0:T(8,128)(2,1)} %bitcast.106), calls=%async_computation.4 | async-start | bytes 1179648 | tf_op jit(solution)/shard_map/all_to_all | solution.py:646
  208.4 107.5 %all-gather.9.cloned.1.call-start = ((), (), s32[]{:S(2)}) async-start(), calls=%async_computation.8 | async-start | bytes 2654208 | tf_op jit(solution)/shard_map/all_gather | solution.py:872
  208.6 7.0 %collective-permute-start.9 = (bf16[1,240,384]{2,1,0:T(8,128)(2,1)S(1)}, bf16[1,240,384]{2,1,0:T(8,128)(2,1)S(1)}, u32[]{:S(2)}, u32[]{:S(2)}) collective-permute-start(bf16[1,240,384]{2,1,0:T(8,128)(2,1)S(1)} %slice.194), channel_id=1, source_target_pairs={{0,2},{1,3},{2,0},{3,1},{4,6},{5,7},{6,4},{7,5},{8,10},{9,11},{10,... | collective-permute-start | bytes 552968 | tf_op jit(solution)/shard_map/ppermute | solution.py:436
  225.3 13.5 %collective-permute-start.10 = (bf16[336,384]{1,0:T(8,128)(2,1)S(1)}, bf16[336,384]{1,0:T(8,128)(2,1)S(1)}, u32[]{:S(2)}, u32[]{:S(2)}) collective-permute-start(bf16[336,384]{1,0:T(8,128)(2,1)S(1)} %pad_maximum_fusion.12), channel_id=1, source_target_pairs={{0,16},{4,20},{8,24},{12,28},{16,0},{20,4},{24,8},{28,12},{1,17},{... | collective-permute-start | bytes 774152 | tf_op jit(solution)/shard_map/ppermute | solution.py:436
  239.0 20.0 %collective-permute-start.11 = (bf16[2,336,384]{2,1,0:T(8,128)(2,1)S(1)}, bf16[2,336,384]{2,1,0:T(8,128)(2,1)S(1)}, u32[]{:S(2)}, u32[]{:S(2)}) collective-permute-start(bf16[2,336,384]{2,1,0:T(8,128)(2,1)S(1)} %pad_maximum_fusion.8), channel_id=1, source_target_pairs={{0,8},{4,12},{8,0},{12,4},{16,24},{20,28},{24,16},{28,20},{1,9},{5... | collective-permute-start | bytes 1548296 | tf_op jit(solution)/shard_map/ppermute | solution.py:436
  259.1 4.9 %copy-start.30 = (bf16[512,768]{1,0:T(8,128)(2,1)S(1)}, bf16[512,768]{1,0:T(8,128)(2,1)}, u32[]{:S(2)}) copy-start(bf16[512,768]{1,0:T(8,128)(2,1)} %convolution_convert_fusion.2) | copy-start | bytes 2359300
  259.9 15.3 %collective-permute-start.12 = (bf16[2,2,160,384]{3,2,1,0:T(8,128)(2,1)}, bf16[2,2,160,384]{3,2,1,0:T(8,128)(2,1)}, u32[]{:S(2)}, u32[]{:S(2)}) collective-permute-start(bf16[2,2,160,384]{3,2,1,0:T(8,128)(2,1)} %pad_maximum_fusion.9), channel_id=1, source_target_pairs={{0,4},{4,0},{8,12},{12,8},{16,20},{20,16},{24,28},{28,24},{1,5},{5... | collective-permute-start | bytes 1474568 | tf_op jit(solution)/shard_map/ppermute | solution.py:436
  262.2 14.9 %collective-permute-start.14 = (bf16[2,2,176,384]{3,2,1,0:T(8,128)(2,1)S(1)}, bf16[2,2,176,384]{3,2,1,0:T(8,128)(2,1)}, u32[]{:S(2)}, u32[]{:S(2)}) collective-permute-start(bf16[2,2,176,384]{3,2,1,0:T(8,128)(2,1)S(1)} %pad_maximum_fusion.7), channel_id=1, source_target_pairs={{0,2},{1,3},{2,0},{3,1},{4,6},{5,7},{6,4},{7,5},{8,10},{9,11},{10,... | collective-permute-start | bytes 1622024 | tf_op jit(solution)/shard_map/ppermute | solution.py:436
  264.7 17.1 %collective-permute-start.16 = (bf16[256,768]{1,0:T(8,128)(2,1)}, bf16[256,768]{1,0:T(8,128)(2,1)}, u32[]{:S(2)}, u32[]{:S(2)}) collective-permute-start(bf16[256,768]{1,0:T(8,128)(2,1)} %slice.118), channel_id=1, source_target_pairs={{0,1},{1,0},{2,3},{3,2},{4,5},{5,4},{6,7},{7,6},{8,9},{9,8},{10,11... | collective-permute-start | bytes 1179656 | tf_op jit(solution)/shard_map/ppermute | solution.py:436
  264.7 51.1 %all-to-all-start.5 = ((bf16[8,144,384]{2,1,0:T(8,128)(2,1)}), bf16[8,144,384]{2,1,0:T(8,128)(2,1)S(1)}, u32[]{:S(2)}, u32[]{:S(2)}) async-start(bf16[8,144,384]{2,1,0:T(8,128)(2,1)} %get-tuple-element.103.x_ref), calls=%async_computation.5 | async-start | bytes 1769472 | tf_op jit(solution)/shard_map/all_to_all | solution.py:874
  276.6 22.6 %collective-permute-start.13 = (bf16[2,2,2,160,384]{4,3,2,1,0:T(8,128)(2,1)S(1)}, bf16[2,2,2,160,384]{4,3,2,1,0:T(8,128)(2,1)S(1)}, u32[]{:S(2)}, u32[]{:S(2)}) collective-permute-start(bf16[2,2,2,160,384]{4,3,2,1,0:T(8,128)(2,1)S(1)} %pad_maximum_fusion.4), channel_id=1, source_target_pairs={{0,2},{1,3},{2,0},{3,1},{4,6},{5,7},{6,4},{7,5},{8,10},{9,11},{10,... | collective-permute-start | bytes 2949128 | tf_op jit(solution)/shard_map/ppermute | solution.py:436
  278.3 20.1 %copy-start.20 = (f32[128,768]{1,0:T(8,128)S(1)}, f32[128,768]{1,0:T(8,128)}, u32[]{:S(2)}) copy-start(f32[128,768]{1,0:T(8,128)} %copy-done.19) | copy-start | bytes 1179652
  278.5 36.9 %collective-permute-start.15 = (bf16[2,2,2,176,384]{4,3,2,1,0:T(8,128)(2,1)S(1)}, bf16[2,2,2,176,384]{4,3,2,1,0:T(8,128)(2,1)S(1)}, u32[]{:S(2)}, u32[]{:S(2)}) collective-permute-start(bf16[2,2,2,176,384]{4,3,2,1,0:T(8,128)(2,1)S(1)} %pad_maximum_fusion.3), channel_id=1, source_target_pairs={{0,4},{4,0},{8,12},{12,8},{16,20},{20,16},{24,28},{28,24},{1,5},{5... | collective-permute-start | bytes 3244040 | tf_op jit(solution)/shard_map/ppermute | solution.py:436
  282.9 15.5 %collective-permute-start.17 = (bf16[128,768]{1,0:T(8,128)(2,1)S(1)}, bf16[128,768]{1,0:T(8,128)(2,1)S(1)}, u32[]{:S(2)}, u32[]{:S(2)}) collective-permute-start(bf16[128,768]{1,0:T(8,128)(2,1)S(1)} %slice.192), channel_id=1, source_target_pairs={{0,2},{1,3},{2,0},{3,1},{4,6},{5,7},{6,4},{7,5},{8,10},{9,11},{10,... | collective-permute-start | bytes 589832 | tf_op jit(solution)/shard_map/ppermute | solution.py:436
  315.9 5.2 %copy-start.21 = (bf16[2,2,2,2,176,384]{5,4,3,2,1,0:T(8,128)(2,1)}, bf16[2,2,2,2,176,384]{5,4,3,2,1,0:T(8,128)(2,1)S(1)}, u32[]{:S(2)}) copy-start(bf16[2,2,2,2,176,384]{5,4,3,2,1,0:T(8,128)(2,1)S(1)} %pad_maximum_fusion.1) | copy-start | bytes 6488068
  315.9 11.1 %collective-permute-start.19 = (bf16[2,2,4,176,384]{4,3,2,1,0:T(8,128)(2,1)S(1)}, bf16[2,2,4,176,384]{4,3,2,1,0:T(8,128)(2,1)}, u32[]{:S(2)}, u32[]{:S(2)}) collective-permute-start(bf16[2,2,4,176,384]{4,3,2,1,0:T(8,128)(2,1)S(1)} %bitcast.102), channel_id=1, source_target_pairs={{0,1},{1,0},{2,3},{3,2},{4,5},{5,4},{6,7},{7,6},{8,9},{9,8},{10,11... | collective-permute-start | bytes 6488072 | tf_op jit(solution)/shard_map/ppermute | solution.py:436
  316.0 11.0 %collective-permute-start.18 = (bf16[2,8,160,384]{3,2,1,0:T(8,128)(2,1)}, bf16[2,8,160,384]{3,2,1,0:T(8,128)(2,1)}, u32[]{:S(2)}, u32[]{:S(2)}) collective-permute-start(bf16[2,8,160,384]{3,2,1,0:T(8,128)(2,1)} %bitcast.104), channel_id=1, source_target_pairs={{0,1},{1,0},{2,3},{3,2},{4,5},{5,4},{6,7},{7,6},{8,9},{9,8},{10,11... | collective-permute-start | bytes 5898248 | tf_op jit(solution)/shard_map/ppermute | solution.py:436
  316.5 1.8 copy-start.2
  318.3 2.8 copy-start.4
  318.3 2.8 copy-start.5
  318.3 3.7 %copy-start.6 = (bf16[768,768]{1,0:T(8,128)(2,1)S(1)}, bf16[768,768]{1,0:T(8,128)(2,1)}, u32[]{:S(2)}) copy-start(bf16[768,768]{1,0:T(8,128)(2,1)} %refs_6_.1) | copy-start | bytes 3538948
  318.3 4.0 %copy-start.7 = (bf16[768,768]{1,0:T(8,128)(2,1)S(1)}, bf16[768,768]{1,0:T(8,128)(2,1)}, u32[]{:S(2)}) copy-start(bf16[768,768]{1,0:T(8,128)(2,1)} %refs_7_.1) | copy-start | bytes 3538948
  318.3 4.0 %copy-start.11 = (bf16[1,128,768]{2,1,0:T(8,128)(2,1)S(1)}, bf16[1,128,768]{2,1,0:T(8,128)(2,1)}, u32[]{:S(2)}) copy-start(bf16[1,128,768]{2,1,0:T(8,128)(2,1)} %param.22) | copy-start | bytes 589828
  318.3 4.1 %copy-start.13 = (f32[128,768]{1,0:T(8,128)S(1)}, f32[128,768]{1,0:T(8,128)}, u32[]{:S(2)}) copy-start(f32[128,768]{1,0:T(8,128)} %get-tuple-element.145.m_ref) | copy-start | bytes 1179652
  318.3 4.2 %copy-start.15 = (bf16[128,768]{1,0:T(8,128)(2,1)S(1)}, bf16[128,768]{1,0:T(8,128)(2,1)}, u32[]{:S(2)}) copy-start(bf16[128,768]{1,0:T(8,128)(2,1)} %get-tuple-element.90.d_ref) | copy-start | bytes 589828
  318.3 4.2 %copy-start.17 = (bf16[768,12]{0,1:T(8,128)(2,1)S(1)}, bf16[768,12]{0,1:T(8,128)(2,1)}, u32[]{:S(2)}) copy-start(bf16[768,12]{0,1:T(8,128)(2,1)} %param.27) | copy-start | bytes 55300
  318.3 4.2 %copy-start.18 = (f32[768]{0:T(1024)S(1)}, f32[768]{0:T(1024)}, u32[]{:S(2)}) copy-start(f32[768]{0:T(1024)} %g_ref.5) | copy-start | bytes 9220
  327.0 13.1 %copy-start.1 = (bf16[768,768]{1,0:T(8,128)(2,1)S(1)}, bf16[768,768]{1,0:T(8,128)(2,1)}, u32[]{:S(2)}) copy-start(bf16[768,768]{1,0:T(8,128)(2,1)} %param.36) | copy-start | bytes 3538948
  (5 other events, 4.8 us)
Sparse Core Ops, SparseCore 0:
  10.2 27.1 all-gather.4
  40.2 44.7 all-gather.6
  239.1 70.4 all-gather.8
